TPU v7x, 32 devices: a whole 2x2x4 slice. The times are simulated.
32 devices in a mesh: groups: 2 (over y), blk: 16 (over z, x, core).
Axes of the slice: x: 2, y: 2, z: 4, core: 2. Of those that a mesh axis runs over, the one named last changes fastest.
Arguments:
- image_embeds: bfloat16 [4096, 1152], P(('groups', 'blk')), parts along dimension 0, may hold values from -100 to 100
- text_embeds: bfloat16 [4096, 1152], P(('groups', 'blk')), parts along dimension 0, may hold values from -20 to 20
- log_temp: float32 [1], replicated, may hold values from 3.7 to 4.6
- bias: float32 [1], replicated, may hold values from -3.5 to -1.5
Outputs:
- grad_image: bfloat16 [4096, 1152], P(('groups', 'blk')), parts along dimension 0
- grad_text: bfloat16 [4096, 1152], P(('groups', 'blk')), parts along dimension 0
- grad_temp: float32 [2], P('groups'), parts along dimension 0
- grad_bias: float32 [2], P('groups'), parts along dimension 0
There are 2 independent parts, one for each index of `groups`. A program takes and returns all parts, laid end to end along the dimension named above; an argument that names none is the same for every part. Nothing has to cross between parts.
All inputs are finite; a program needn't handle non-finite values.
Results may differ from a plain program's by a relative error of at most 0.0034.
Values may be sent and summed in bfloat16 or wider, within the bound.
No kernel may reach another device: no remote copies, remote signals or barrier semaphores. Data moves between devices by JAX's collectives and lax.ppermute only.
A program may use at most 64 MiB of HBM per device.

v0:
```python
import jax
import jax.numpy as jnp
from jax import lax
from jax.sharding import PartitionSpec as P

REPL = 8


def shifted(x, axis, by):
    count = lax.axis_size(axis)
    return lax.ppermute(x, axis, [(i, (i + by) % count) for i in range(count)])


def unit_rows(values):
    wide = values.astype(jnp.float32)
    inverse = lax.rsqrt(jnp.sum(wide * wide, axis=1, keepdims=True) + 1e-06)
    return (wide * inverse, inverse)


def pair_tile(panel, row_ids, piece, start, temp, shift_b):
    cosine = lax.dot_general(
        panel, piece, (((1,), (1,)), ((), ())), preferred_element_type=jnp.float32
    )
    scaled = temp * cosine
    logits = scaled + shift_b
    col_ids = start + jnp.arange(piece.shape[0], dtype=jnp.int32)
    sign = jnp.where(row_ids[:, None] == col_ids[None, :], 1.0, -1.0)
    grads = -sign * jax.nn.sigmoid(-sign * logits)
    grads_b = grads.astype(jnp.bfloat16)
    img_part = jnp.dot(grads_b, piece, preferred_element_type=jnp.float32)
    txt_part = lax.dot_general(
        grads_b, panel, (((0,), (0,)), ((), ())), preferred_element_type=jnp.float32
    )
    return (img_part, txt_part, jnp.sum(grads), jnp.sum(grads * scaled))


def shards(image_embeds, text_embeds, log_temp, bias):
    rows, width = image_embeds.shape
    count = lax.axis_size("blk")
    me = lax.axis_index("blk")
    unit_img, inv_img = unit_rows(image_embeds)
    unit_txt, inv_txt = unit_rows(text_embeds)
    img_b = unit_img.astype(jnp.bfloat16)
    txt_b = unit_txt.astype(jnp.bfloat16)
    temp = jnp.exp(log_temp[0])
    shift_b = bias[0]
    zero = jnp.zeros((), jnp.float32)
    local_ids = jnp.arange(rows, dtype=jnp.int32)
    pieces = [img_b]
    moving = img_b
    for offset in range(1, REPL):
        moving = shifted(moving, "blk", 1)
        pieces.append(moving)
    panel = jnp.concatenate(pieces, axis=0)
    row_ids = jnp.concatenate(
        [(me - offset) % count * rows + local_ids for offset in range(REPL)], axis=0
    )
    back_start = txt_b[rows:]
    turns = count // REPL

    def loop_step(step, state):
        panel_acc, sum_g, sum_gl, fwd_text, fwd_grad, back_text, back_grad = state
        anchor = (me - step * REPL) % count
        part = pair_tile(panel, row_ids, fwd_text, anchor * rows, temp, shift_b)
        panel_acc = panel_acc + part[0]
        fwd_grad = fwd_grad + part[1]
        sum_g = sum_g + part[2]
        sum_gl = sum_gl + part[3]
        fwd_text = shifted(fwd_text, "blk", REPL)
        fwd_grad = shifted(fwd_grad, "blk", REPL)
        return (panel_acc, sum_g, sum_gl, fwd_text, fwd_grad, back_text, back_grad)

    init = (
        jnp.zeros((REPL * rows, width), jnp.float32),
        zero,
        zero,
        txt_b,
        jnp.zeros(txt_b.shape, jnp.float32),
        back_start,
        jnp.zeros(back_start.shape, jnp.float32),
    )
    state = lax.fori_loop(0, turns, loop_step, init)
    panel_acc, sum_g, sum_gl = (state[0], state[1], state[2])
    txt_acc = jnp.concatenate([state[4], state[6]], axis=0)
    img_acc = panel_acc[(REPL - 1) * rows :]
    for rank in range(1, REPL):
        img_acc = shifted(img_acc, "blk", -1)
        slot = REPL - 1 - rank
        img_acc = img_acc + panel_acc[slot * rows : (slot + 1) * rows]
    total_g, total_gl = lax.psum((sum_g, sum_gl), "blk")
    d_img = temp * img_acc
    d_txt = temp * txt_acc
    grad_image = (
        (d_img - unit_img * jnp.sum(unit_img * d_img, axis=1, keepdims=True)) * inv_img
    ).astype(jnp.bfloat16)
    grad_text = (
        (d_txt - unit_txt * jnp.sum(unit_txt * d_txt, axis=1, keepdims=True)) * inv_txt
    ).astype(jnp.bfloat16)
    pairs = float(rows * count) * float(rows * count)
    grad_temp = jnp.reshape(total_gl / pairs, (1,))
    grad_bias = jnp.reshape(total_g / pairs, (1,))
    return (grad_image, grad_text, grad_temp, grad_bias)


def solution(mesh):
    in_specs = (P(("groups", "blk"), None), P(("groups", "blk"), None), P(), P())
    out_specs = (P(("groups", "blk"), None), P(("groups", "blk"), None), P("groups"), P("groups"))
    return jax.shard_map(shards, mesh=mesh, in_specs=in_specs, out_specs=out_specs, check_vma=False)
```

profile of v0, /device:TPU:0, one launch (start us, length us, event | category | flops | bytes accessed | tf_op | source)
XLA Modules:
  0.0 270.0 jit_solution(17287317738334260586)
XLA Ops:
  0.6 1.1 fusion.18
  1.7 1.8 constant_dynamic-update-slice_fusion.8
  4.1 9.3 %collective-permute-done.2 = bf16[128,1152]{1,0:T(8,128)(2,1)S(1)} collective-permute-done((bf16[128,1152]{1,0:T(8,128)(2,1)S(1)}, bf16[128,1152]{1,0:T(8,128)(2,1)S(1)}, u32[]{:S(2)}, u32[]{:S(2)}) %collective-permute-start.2) | collective-permute-done | bytes 294944 | tf_op jit(solution)/shard_map/ppermute | solution.py:11
  14.1 1.1 fusion.13
  15.2 7.0 %collective-permute-done.3 = bf16[128,1152]{1,0:T(8,128)(2,1)S(1)} collective-permute-done((bf16[128,1152]{1,0:T(8,128)(2,1)S(1)}, bf16[128,1152]{1,0:T(8,128)(2,1)S(1)}, u32[]{:S(2)}, u32[]{:S(2)}) %collective-permute-start.3) | collective-permute-done | bytes 294944 | tf_op jit(solution)/shard_map/ppermute | solution.py:11
  22.2 8.8 %collective-permute-done.4 = bf16[128,1152]{1,0:T(8,128)(2,1)S(1)} collective-permute-done((bf16[128,1152]{1,0:T(8,128)(2,1)S(1)}, bf16[128,1152]{1,0:T(8,128)(2,1)S(1)}, u32[]{:S(2)}, u32[]{:S(2)}) %collective-permute-start.4) | collective-permute-done | bytes 294944 | tf_op jit(solution)/shard_map/ppermute | solution.py:11
  31.1 1.1 fusion.8
  32.1 7.8 %collective-permute-done.5 = bf16[128,1152]{1,0:T(8,128)(2,1)S(1)} collective-permute-done((bf16[128,1152]{1,0:T(8,128)(2,1)S(1)}, bf16[128,1152]{1,0:T(8,128)(2,1)S(1)}, u32[]{:S(2)}, u32[]{:S(2)}) %collective-permute-start.5) | collective-permute-done | bytes 294944 | tf_op jit(solution)/shard_map/ppermute | solution.py:11
  39.9 0.8 constant_dynamic-update-slice_fusion.7
  41.4 7.4 %collective-permute-done.6 = bf16[128,1152]{1,0:T(8,128)(2,1)S(1)} collective-permute-done((bf16[128,1152]{1,0:T(8,128)(2,1)S(1)}, bf16[128,1152]{1,0:T(8,128)(2,1)S(1)}, u32[]{:S(2)}, u32[]{:S(2)}) %collective-permute-start.6) | collective-permute-done | bytes 294944 | tf_op jit(solution)/shard_map/ppermute | solution.py:11
  49.5 0.7 constant_dynamic-update-slice_fusion.4
  50.2 7.4 %collective-permute-done.7 = bf16[128,1152]{1,0:T(8,128)(2,1)S(1)} collective-permute-done((bf16[128,1152]{1,0:T(8,128)(2,1)S(1)}, bf16[128,1152]{1,0:T(8,128)(2,1)S(1)}, u32[]{:S(2)}, u32[]{:S(2)}) %collective-permute-start.7) | collective-permute-done | bytes 294944 | tf_op jit(solution)/shard_map/ppermute | solution.py:11
  59.1 7.5 %collective-permute-done.8 = bf16[128,1152]{1,0:T(8,128)(2,1)S(1)} collective-permute-done((bf16[128,1152]{1,0:T(8,128)(2,1)S(1)}, bf16[128,1152]{1,0:T(8,128)(2,1)S(1)}, u32[]{:S(2)}, u32[]{:S(2)}) %collective-permute-start.8) | collective-permute-done | bytes 294944 | tf_op jit(solution)/shard_map/ppermute | solution.py:11
  66.5 0.8 constant_dynamic-update-slice_fusion.1
  67.3 77.7 %while.24 = (s32[]{:T(128)}, f32[1024,1152]{1,0:T(8,128)}, f32[]{:T(128)}, f32[]{:T(128)}, bf16[128,1152]{1,0:T(8,128)(2,1)S(1)}, /*index=5*/f32[128,1152]{1,0:T...) while((s32[]{:T(128)}, f32[1024,1152]{1,0:T(8,128)}, ...), condition=%wide.region_5.6_spmd.clone, body=%wide.region_2.5_spmd.clone.sunk | while | flops 912801920 | bytes 21641660 | solution.py:82
  67.4 3.9 %multiply_reduce_fusion.2 = (f32[]{:T(128)}, f32[]{:T(128)}, f32[1024,128]{1,0:T(8,128)S(1)}) fusion(f32[]{:T(128)} %get-tuple-element.458, s32[128]{0:T(128)S(1)} %iota_add_fusion.2, s32[1024]{0:T(1024)S(1)} %get-tuple-element.454, bf16[1024,1152]{1,0:T(8,128)(2,1)} %get-tuple-element.457, bf16[128,1152]{1,0:T(8,128)(2,1)S(1)} %copy.33, ...), kind=kOutput, calls=%fused_computation.3.clone.1 | convolution fusion | flops 303693824 | bytes 3183120 | tf_op jit(solution)/shard_map/while/body/eval_jaxpr/dot_general | solution.py:21
  71.3 3.1 %convolution_add_fusion.5 = f32[128,1152]{1,0:T(8,128)S(1)} fusion(f32[128,1152]{1,0:T(8,128)S(1)} %get-tuple-element.436, bf16[1024,1152]{1,0:T(8,128)(2,1)} %get-tuple-element.457, f32[1024,128]{1,0:T(8,128)S(1)} %get-tuple-element.411, f32[]{:T(128)} %get-tuple-element.458, s32[128]{0:T(128)S(1)} %iota_add_fusion.2, s32[1024]{0:T(1024)S(1)} %get-tuple-element.454), kind=kOutput, calls=%fused_computation.1.clone.1 | convolution fusion | flops 303448064 | bytes 4067844 | tf_op jit(solution)/shard_map/while/body/eval_jaxpr/dot_general | solution.py:31
  74.6 2.9 %collective-permute-start = (bf16[128,1152]{1,0:T(8,128)(2,1)S(1)}, bf16[128,1152]{1,0:T(8,128)(2,1)S(1)}, u32[]{:S(2)}, u32[]{:S(2)}) collective-permute-start(bf16[128,1152]{1,0:T(8,128)(2,1)S(1)} %copy.33), channel_id=1, source_target_pairs={{0,8},{1,9},{2,10},{3,11},{4,12},{5,13},{6,14},{7,15},{8,0},{9,1},... | collective-permute-start | bytes 884744 | tf_op jit(solution)/shard_map/while/body/eval_jaxpr/ppermute | solution.py:11
  78.9 3.6 %convolution_add_fusion.4 = f32[1024,1152]{1,0:T(8,128)} fusion(bf16[128,1152]{1,0:T(8,128)(2,1)S(1)} %copy.33, f32[1024,1152]{1,0:T(8,128)} %get-tuple-element.432, pred[]{:T(512)S(6)} %compare.12, f32[1024,128]{1,0:T(8,128)S(1)} %get-tuple-element.411, f32[]{:T(128)} %get-tuple-element.458, s32[128]{0:T(128)S(1)} %iota_add_fusion.2, ...), kind=kOutput, calls=%fused_computation.clone.1 | convolution fusion | flops 305659904 | bytes 10260997 | tf_op jit(solution)/shard_map/while/body/eval_jaxpr/dot_general | solution.py:30
  82.5 18.5 %collective-permute-done = bf16[128,1152]{1,0:T(8,128)(2,1)S(1)} collective-permute-done((bf16[128,1152]{1,0:T(8,128)(2,1)S(1)}, bf16[128,1152]{1,0:T(8,128)(2,1)S(1)}, u32[]{:S(2)}, u32[]{:S(2)}) %collective-permute-start) | collective-permute-done | bytes 294944 | tf_op jit(solution)/shard_map/while/body/eval_jaxpr/ppermute | solution.py:11
  101.1 3.9 %multiply_reduce_fusion.2 = (f32[]{:T(128)}, f32[]{:T(128)}, f32[1024,128]{1,0:T(8,128)S(1)}) fusion(f32[]{:T(128)} %get-tuple-element.458, s32[128]{0:T(128)S(1)} %iota_add_fusion.2, s32[1024]{0:T(1024)S(1)} %get-tuple-element.454, bf16[1024,1152]{1,0:T(8,128)(2,1)} %get-tuple-element.457, bf16[128,1152]{1,0:T(8,128)(2,1)S(1)} %copy.33, ...), kind=kOutput, calls=%fused_computation.3.clone.1 | convolution fusion | flops 303693824 | bytes 3183120 | tf_op jit(solution)/shard_map/while/body/eval_jaxpr/dot_general | solution.py:21
  105.0 3.1 %convolution_add_fusion.5 = f32[128,1152]{1,0:T(8,128)S(1)} fusion(f32[128,1152]{1,0:T(8,128)S(1)} %get-tuple-element.436, bf16[1024,1152]{1,0:T(8,128)(2,1)} %get-tuple-element.457, f32[1024,128]{1,0:T(8,128)S(1)} %get-tuple-element.411, f32[]{:T(128)} %get-tuple-element.458, s32[128]{0:T(128)S(1)} %iota_add_fusion.2, s32[1024]{0:T(1024)S(1)} %get-tuple-element.454), kind=kOutput, calls=%fused_computation.1.clone.1 | convolution fusion | flops 303448064 | bytes 4067844 | tf_op jit(solution)/shard_map/while/body/eval_jaxpr/dot_general | solution.py:31
  108.2 2.9 %collective-permute-start = (bf16[128,1152]{1,0:T(8,128)(2,1)S(1)}, bf16[128,1152]{1,0:T(8,128)(2,1)S(1)}, u32[]{:S(2)}, u32[]{:S(2)}) collective-permute-start(bf16[128,1152]{1,0:T(8,128)(2,1)S(1)} %copy.33), channel_id=1, source_target_pairs={{0,8},{1,9},{2,10},{3,11},{4,12},{5,13},{6,14},{7,15},{8,0},{9,1},... | collective-permute-start | bytes 884744 | tf_op jit(solution)/shard_map/while/body/eval_jaxpr/ppermute | solution.py:11
  112.5 6.0 %convolution_add_fusion.4 = f32[1024,1152]{1,0:T(8,128)} fusion(bf16[128,1152]{1,0:T(8,128)(2,1)S(1)} %copy.33, f32[1024,1152]{1,0:T(8,128)} %get-tuple-element.432, pred[]{:T(512)S(6)} %compare.12, f32[1024,128]{1,0:T(8,128)S(1)} %get-tuple-element.411, f32[]{:T(128)} %get-tuple-element.458, s32[128]{0:T(128)S(1)} %iota_add_fusion.2, ...), kind=kOutput, calls=%fused_computation.clone.1 | convolution fusion | flops 305659904 | bytes 10260997 | tf_op jit(solution)/shard_map/while/body/eval_jaxpr/dot_general | solution.py:30
  118.5 26.5 %collective-permute-done = bf16[128,1152]{1,0:T(8,128)(2,1)S(1)} collective-permute-done((bf16[128,1152]{1,0:T(8,128)(2,1)S(1)}, bf16[128,1152]{1,0:T(8,128)(2,1)S(1)}, u32[]{:S(2)}, u32[]{:S(2)}) %collective-permute-start) | collective-permute-done | bytes 294944 | tf_op jit(solution)/shard_map/while/body/eval_jaxpr/ppermute | solution.py:11
  145.0 1.1 slice.24
  146.1 7.0 %collective-permute-start.9 = (f32[128,1152]{1,0:T(8,128)S(1)}, f32[128,1152]{1,0:T(8,128)S(1)}, u32[]{:S(2)}, u32[]{:S(2)}) collective-permute-start(f32[128,1152]{1,0:T(8,128)S(1)} %slice.24), channel_id=1, source_target_pairs={{0,15},{1,0},{2,1},{3,2},{4,3},{5,4},{6,5},{7,6},{8,7},{9,8},{10,9... | collective-permute-start | bytes 1769480 | tf_op jit(solution)/shard_map/ppermute | solution.py:11
  153.1 7.4 %collective-permute-done.9 = f32[128,1152]{1,0:T(8,128)S(1)} collective-permute-done((f32[128,1152]{1,0:T(8,128)S(1)}, f32[128,1152]{1,0:T(8,128)S(1)}, u32[]{:S(2)}, u32[]{:S(2)}) %collective-permute-start.9) | collective-permute-done | bytes 589856 | tf_op jit(solution)/shard_map/ppermute | solution.py:11
  160.5 1.2 slice_add_fusion.5
  161.7 4.7 %collective-permute-start.10 = (f32[128,1152]{1,0:T(8,128)S(1)}, f32[128,1152]{1,0:T(8,128)S(1)}, u32[]{:S(2)}, u32[]{:S(2)}) collective-permute-start(f32[128,1152]{1,0:T(8,128)S(1)} %slice_add_fusion.5), channel_id=1, source_target_pairs={{0,15},{1,0},{2,1},{3,2},{4,3},{5,4},{6,5},{7,6},{8,7},{9,8},{10,9... | collective-permute-start | bytes 1769480 | tf_op jit(solution)/shard_map/ppermute | solution.py:11
  166.4 7.4 %collective-permute-done.10 = f32[128,1152]{1,0:T(8,128)S(1)} collective-permute-done((f32[128,1152]{1,0:T(8,128)S(1)}, f32[128,1152]{1,0:T(8,128)S(1)}, u32[]{:S(2)}, u32[]{:S(2)}) %collective-permute-start.10) | collective-permute-done | bytes 589856 | tf_op jit(solution)/shard_map/ppermute | solution.py:11
  173.8 1.2 slice_add_fusion.4
  174.9 4.7 %collective-permute-start.11 = (f32[128,1152]{1,0:T(8,128)S(1)}, f32[128,1152]{1,0:T(8,128)S(1)}, u32[]{:S(2)}, u32[]{:S(2)}) collective-permute-start(f32[128,1152]{1,0:T(8,128)S(1)} %slice_add_fusion.4), channel_id=1, source_target_pairs={{0,15},{1,0},{2,1},{3,2},{4,3},{5,4},{6,5},{7,6},{8,7},{9,8},{10,9... | collective-permute-start | bytes 1769480 | tf_op jit(solution)/shard_map/ppermute | solution.py:11
  179.6 7.4 %collective-permute-done.11 = f32[128,1152]{1,0:T(8,128)S(1)} collective-permute-done((f32[128,1152]{1,0:T(8,128)S(1)}, f32[128,1152]{1,0:T(8,128)S(1)}, u32[]{:S(2)}, u32[]{:S(2)}) %collective-permute-start.11) | collective-permute-done | bytes 589856 | tf_op jit(solution)/shard_map/ppermute | solution.py:11
  187.0 1.2 slice_add_fusion.3
  188.2 4.7 %collective-permute-start.12 = (f32[128,1152]{1,0:T(8,128)S(1)}, f32[128,1152]{1,0:T(8,128)S(1)}, u32[]{:S(2)}, u32[]{:S(2)}) collective-permute-start(f32[128,1152]{1,0:T(8,128)S(1)} %slice_add_fusion.3), channel_id=1, source_target_pairs={{0,15},{1,0},{2,1},{3,2},{4,3},{5,4},{6,5},{7,6},{8,7},{9,8},{10,9... | collective-permute-start | bytes 1769480 | tf_op jit(solution)/shard_map/ppermute | solution.py:11
  192.8 7.4 %collective-permute-done.12 = f32[128,1152]{1,0:T(8,128)S(1)} collective-permute-done((f32[128,1152]{1,0:T(8,128)S(1)}, f32[128,1152]{1,0:T(8,128)S(1)}, u32[]{:S(2)}, u32[]{:S(2)}) %collective-permute-start.12) | collective-permute-done | bytes 589856 | tf_op jit(solution)/shard_map/ppermute | solution.py:11
  200.2 1.2 slice_add_fusion.2
  201.4 4.7 %collective-permute-start.13 = (f32[128,1152]{1,0:T(8,128)S(1)}, f32[128,1152]{1,0:T(8,128)S(1)}, u32[]{:S(2)}, u32[]{:S(2)}) collective-permute-start(f32[128,1152]{1,0:T(8,128)S(1)} %slice_add_fusion.2), channel_id=1, source_target_pairs={{0,15},{1,0},{2,1},{3,2},{4,3},{5,4},{6,5},{7,6},{8,7},{9,8},{10,9... | collective-permute-start | bytes 1769480 | tf_op jit(solution)/shard_map/ppermute | solution.py:11
  206.1 7.4 %collective-permute-done.13 = f32[128,1152]{1,0:T(8,128)S(1)} collective-permute-done((f32[128,1152]{1,0:T(8,128)S(1)}, f32[128,1152]{1,0:T(8,128)S(1)}, u32[]{:S(2)}, u32[]{:S(2)}) %collective-permute-start.13) | collective-permute-done | bytes 589856 | tf_op jit(solution)/shard_map/ppermute | solution.py:11
  213.5 1.2 slice_add_fusion.1
  214.6 4.7 %collective-permute-start.14 = (f32[128,1152]{1,0:T(8,128)S(1)}, f32[128,1152]{1,0:T(8,128)S(1)}, u32[]{:S(2)}, u32[]{:S(2)}) collective-permute-start(f32[128,1152]{1,0:T(8,128)S(1)} %slice_add_fusion.1), channel_id=1, source_target_pairs={{0,15},{1,0},{2,1},{3,2},{4,3},{5,4},{6,5},{7,6},{8,7},{9,8},{10,9... | collective-permute-start | bytes 1769480 | tf_op jit(solution)/shard_map/ppermute | solution.py:11
  219.3 35.1 %all-reduce = (f32[]{:T(128)}, f32[]{:T(128)}) all-reduce(f32[]{:T(128)} %get-tuple-element.274, f32[]{:T(128)} %get-tuple-element.275), channel_id=1, replica_groups=mesh['groups'=2,'blk'=16] {'blk'}, use_global_device_ids=true, to_apply=%region_8.9 | all-reduce | flops 2 | bytes 16 | tf_op jit(solution)/shard_map/psum | solution.py:90
  255.7 1.2 slice_add_fusion
  257.2 0.9 fusion.12
  258.2 6.2 %collective-permute-done.15 = f32[128,1152]{1,0:T(8,128)S(1)} collective-permute-done((f32[128,1152]{1,0:T(8,128)S(1)}, f32[128,1152]{1,0:T(8,128)S(1)}, u32[]{:S(2)}, u32[]{:S(2)}) %collective-permute-start.15) | collective-permute-done | bytes 589856 | tf_op jit(solution)/shard_map/ppermute | solution.py:11
  264.4 1.3 fusion.14
  265.7 2.0 fusion.17
  (39 shorter events, 4.0 us)
Async XLA Ops:
  3.5 9.8 %collective-permute-start.2 = (bf16[128,1152]{1,0:T(8,128)(2,1)S(1)}, bf16[128,1152]{1,0:T(8,128)(2,1)S(1)}, u32[]{:S(2)}, u32[]{:S(2)}) collective-permute-start(bf16[128,1152]{1,0:T(8,128)(2,1)S(1)} %get-tuple-element.339), channel_id=1, source_target_pairs={{0,1},{1,2},{2,3},{3,4},{4,5},{5,6},{6,7},{7,8},{8,9},{9,10},{10,1... | collective-permute-start | bytes 884744 | tf_op jit(solution)/shard_map/ppermute | solution.py:11
  13.4 8.8 %collective-permute-start.3 = (bf16[128,1152]{1,0:T(8,128)(2,1)S(1)}, bf16[128,1152]{1,0:T(8,128)(2,1)S(1)}, u32[]{:S(2)}, u32[]{:S(2)}) collective-permute-start(bf16[128,1152]{1,0:T(8,128)(2,1)S(1)} %collective-permute-done.2), channel_id=1, source_target_pairs={{0,1},{1,2},{2,3},{3,4},{4,5},{5,6},{6,7},{7,8},{8,9},{9,10},{10,1... | collective-permute-start | bytes 884744 | tf_op jit(solution)/shard_map/ppermute | solution.py:11
  22.2 8.8 %collective-permute-start.4 = (bf16[128,1152]{1,0:T(8,128)(2,1)S(1)}, bf16[128,1152]{1,0:T(8,128)(2,1)S(1)}, u32[]{:S(2)}, u32[]{:S(2)}) collective-permute-start(bf16[128,1152]{1,0:T(8,128)(2,1)S(1)} %collective-permute-done.3), channel_id=1, source_target_pairs={{0,1},{1,2},{2,3},{3,4},{4,5},{5,6},{6,7},{7,8},{8,9},{9,10},{10,1... | collective-permute-start | bytes 884744 | tf_op jit(solution)/shard_map/ppermute | solution.py:11
  31.1 8.8 %collective-permute-start.5 = (bf16[128,1152]{1,0:T(8,128)(2,1)S(1)}, bf16[128,1152]{1,0:T(8,128)(2,1)S(1)}, u32[]{:S(2)}, u32[]{:S(2)}) collective-permute-start(bf16[128,1152]{1,0:T(8,128)(2,1)S(1)} %collective-permute-done.4), channel_id=1, source_target_pairs={{0,1},{1,2},{2,3},{3,4},{4,5},{5,6},{6,7},{7,8},{8,9},{9,10},{10,1... | collective-permute-start | bytes 884744 | tf_op jit(solution)/shard_map/ppermute | solution.py:11
  39.9 8.8 %collective-permute-start.6 = (bf16[128,1152]{1,0:T(8,128)(2,1)S(1)}, bf16[128,1152]{1,0:T(8,128)(2,1)S(1)}, u32[]{:S(2)}, u32[]{:S(2)}) collective-permute-start(bf16[128,1152]{1,0:T(8,128)(2,1)S(1)} %collective-permute-done.5), channel_id=1, source_target_pairs={{0,1},{1,2},{2,3},{3,4},{4,5},{5,6},{6,7},{7,8},{8,9},{9,10},{10,1... | collective-permute-start | bytes 884744 | tf_op jit(solution)/shard_map/ppermute | solution.py:11
  48.7 8.8 %collective-permute-start.7 = (bf16[128,1152]{1,0:T(8,128)(2,1)S(1)}, bf16[128,1152]{1,0:T(8,128)(2,1)S(1)}, u32[]{:S(2)}, u32[]{:S(2)}) collective-permute-start(bf16[128,1152]{1,0:T(8,128)(2,1)S(1)} %collective-permute-done.6), channel_id=1, source_target_pairs={{0,1},{1,2},{2,3},{3,4},{4,5},{5,6},{6,7},{7,8},{8,9},{9,10},{10,1... | collective-permute-start | bytes 884744 | tf_op jit(solution)/shard_map/ppermute | solution.py:11
  57.6 8.9 %collective-permute-start.8 = (bf16[128,1152]{1,0:T(8,128)(2,1)S(1)}, bf16[128,1152]{1,0:T(8,128)(2,1)S(1)}, u32[]{:S(2)}, u32[]{:S(2)}) collective-permute-start(bf16[128,1152]{1,0:T(8,128)(2,1)S(1)} %collective-permute-done.7), channel_id=1, source_target_pairs={{0,1},{1,2},{2,3},{3,4},{4,5},{5,6},{6,7},{7,8},{8,9},{9,10},{10,1... | collective-permute-start | bytes 884744 | tf_op jit(solution)/shard_map/ppermute | solution.py:11
  74.5 26.5 %collective-permute-start.1 = (f32[128,1152]{1,0:T(8,128)S(1)}, f32[128,1152]{1,0:T(8,128)S(1)}, u32[]{:S(2)}, u32[]{:S(2)}) collective-permute-start(f32[128,1152]{1,0:T(8,128)S(1)} %convolution_add_fusion.5), channel_id=1, source_target_pairs={{0,8},{1,9},{2,10},{3,11},{4,12},{5,13},{6,14},{7,15},{8,0},{9,1},... | collective-permute-start | bytes 1769480 | tf_op jit(solution)/shard_map/while/body/eval_jaxpr/ppermute | solution.py:11
  74.6 26.5 %collective-permute-start = (bf16[128,1152]{1,0:T(8,128)(2,1)S(1)}, bf16[128,1152]{1,0:T(8,128)(2,1)S(1)}, u32[]{:S(2)}, u32[]{:S(2)}) collective-permute-start(bf16[128,1152]{1,0:T(8,128)(2,1)S(1)} %copy.33), channel_id=1, source_target_pairs={{0,8},{1,9},{2,10},{3,11},{4,12},{5,13},{6,14},{7,15},{8,0},{9,1},... | collective-permute-start | bytes 884744 | tf_op jit(solution)/shard_map/while/body/eval_jaxpr/ppermute | solution.py:11
  108.1 36.9 %collective-permute-start.1 = (f32[128,1152]{1,0:T(8,128)S(1)}, f32[128,1152]{1,0:T(8,128)S(1)}, u32[]{:S(2)}, u32[]{:S(2)}) collective-permute-start(f32[128,1152]{1,0:T(8,128)S(1)} %convolution_add_fusion.5), channel_id=1, source_target_pairs={{0,8},{1,9},{2,10},{3,11},{4,12},{5,13},{6,14},{7,15},{8,0},{9,1},... | collective-permute-start | bytes 1769480 | tf_op jit(solution)/shard_map/while/body/eval_jaxpr/ppermute | solution.py:11
  108.2 36.8 %collective-permute-start = (bf16[128,1152]{1,0:T(8,128)(2,1)S(1)}, bf16[128,1152]{1,0:T(8,128)(2,1)S(1)}, u32[]{:S(2)}, u32[]{:S(2)}) collective-permute-start(bf16[128,1152]{1,0:T(8,128)(2,1)S(1)} %copy.33), channel_id=1, source_target_pairs={{0,8},{1,9},{2,10},{3,11},{4,12},{5,13},{6,14},{7,15},{8,0},{9,1},... | collective-permute-start | bytes 884744 | tf_op jit(solution)/shard_map/while/body/eval_jaxpr/ppermute | solution.py:11
  146.1 14.4 %collective-permute-start.9 = (f32[128,1152]{1,0:T(8,128)S(1)}, f32[128,1152]{1,0:T(8,128)S(1)}, u32[]{:S(2)}, u32[]{:S(2)}) collective-permute-start(f32[128,1152]{1,0:T(8,128)S(1)} %slice.24), channel_id=1, source_target_pairs={{0,15},{1,0},{2,1},{3,2},{4,3},{5,4},{6,5},{7,6},{8,7},{9,8},{10,9... | collective-permute-start | bytes 1769480 | tf_op jit(solution)/shard_map/ppermute | solution.py:11
  161.7 12.1 %collective-permute-start.10 = (f32[128,1152]{1,0:T(8,128)S(1)}, f32[128,1152]{1,0:T(8,128)S(1)}, u32[]{:S(2)}, u32[]{:S(2)}) collective-permute-start(f32[128,1152]{1,0:T(8,128)S(1)} %slice_add_fusion.5), channel_id=1, source_target_pairs={{0,15},{1,0},{2,1},{3,2},{4,3},{5,4},{6,5},{7,6},{8,7},{9,8},{10,9... | collective-permute-start | bytes 1769480 | tf_op jit(solution)/shard_map/ppermute | solution.py:11
  174.9 12.1 %collective-permute-start.11 = (f32[128,1152]{1,0:T(8,128)S(1)}, f32[128,1152]{1,0:T(8,128)S(1)}, u32[]{:S(2)}, u32[]{:S(2)}) collective-permute-start(f32[128,1152]{1,0:T(8,128)S(1)} %slice_add_fusion.4), channel_id=1, source_target_pairs={{0,15},{1,0},{2,1},{3,2},{4,3},{5,4},{6,5},{7,6},{8,7},{9,8},{10,9... | collective-permute-start | bytes 1769480 | tf_op jit(solution)/shard_map/ppermute | solution.py:11
  188.2 68.8 %copy-start.1 = (bf16[128,1152]{1,0:T(8,128)(2,1)S(1)}, bf16[128,1152]{1,0:T(8,128)(2,1)}, u32[]{:S(2)}) copy-start(bf16[128,1152]{1,0:T(8,128)(2,1)} %param.7) | copy-start | bytes 884740
  188.2 12.1 %collective-permute-start.12 = (f32[128,1152]{1,0:T(8,128)S(1)}, f32[128,1152]{1,0:T(8,128)S(1)}, u32[]{:S(2)}, u32[]{:S(2)}) collective-permute-start(f32[128,1152]{1,0:T(8,128)S(1)} %slice_add_fusion.3), channel_id=1, source_target_pairs={{0,15},{1,0},{2,1},{3,2},{4,3},{5,4},{6,5},{7,6},{8,7},{9,8},{10,9... | collective-permute-start | bytes 1769480 | tf_op jit(solution)/shard_map/ppermute | solution.py:11
  201.4 12.1 %collective-permute-start.13 = (f32[128,1152]{1,0:T(8,128)S(1)}, f32[128,1152]{1,0:T(8,128)S(1)}, u32[]{:S(2)}, u32[]{:S(2)}) collective-permute-start(f32[128,1152]{1,0:T(8,128)S(1)} %slice_add_fusion.2), channel_id=1, source_target_pairs={{0,15},{1,0},{2,1},{3,2},{4,3},{5,4},{6,5},{7,6},{8,7},{9,8},{10,9... | collective-permute-start | bytes 1769480 | tf_op jit(solution)/shard_map/ppermute | solution.py:11
  214.6 49.7 %copy-start = (bf16[128,1152]{1,0:T(8,128)(2,1)S(1)}, bf16[128,1152]{1,0:T(8,128)(2,1)}, u32[]{:S(2)}) copy-start(bf16[128,1152]{1,0:T(8,128)(2,1)} %param.6) | copy-start | bytes 884740
  214.6 41.1 %collective-permute-start.14 = (f32[128,1152]{1,0:T(8,128)S(1)}, f32[128,1152]{1,0:T(8,128)S(1)}, u32[]{:S(2)}, u32[]{:S(2)}) collective-permute-start(f32[128,1152]{1,0:T(8,128)S(1)} %slice_add_fusion.1), channel_id=1, source_target_pairs={{0,15},{1,0},{2,1},{3,2},{4,3},{5,4},{6,5},{7,6},{8,7},{9,8},{10,9... | collective-permute-start | bytes 1769480 | tf_op jit(solution)/shard_map/ppermute | solution.py:11
  256.9 7.5 %collective-permute-start.15 = (f32[128,1152]{1,0:T(8,128)S(1)}, f32[128,1152]{1,0:T(8,128)S(1)}, u32[]{:S(2)}, u32[]{:S(2)}) collective-permute-start(f32[128,1152]{1,0:T(8,128)S(1)} %slice_add_fusion), channel_id=1, source_target_pairs={{0,15},{1,0},{2,1},{3,2},{4,3},{5,4},{6,5},{7,6},{8,7},{9,8},{10,9... | collective-permute-start | bytes 1769480 | tf_op jit(solution)/shard_map/ppermute | solution.py:11
where the time goes:
time: 271 us; the launch traced here: 270 us
  waiting for transfers between devices  143 us (53%)
  starting transfers between devices  36.8 us (14%)
  blocking collectives  35.1 us (13%)
  matrix products  23.7 us (9%)
  other arithmetic  16.7 us (6%)
  local copies, waits for them, and re-layouts  6.39 us (2%)
  between operations  5.05 us (2%)
  loops' own time  2.86 us (1%)
    ppermute x18, waiting for transfers between devices, shifted(): return lax.ppermute(x, axis, [(i, (i + by) % count) for i in range(count)])  143 us
    ppermute x18, starting transfers between devices, shifted(): return lax.ppermute(x, axis, [(i, (i + by) % count) for i in range(count)])  36.8 us
    psum x1, blocking collectives, shards(): total_g, total_gl = lax.psum((sum_g, sum_gl), 'blk')  35.1 us
    dot_general x2, matrix products, pair_tile(): img_part = jnp.dot(grads_b, piece, preferred_element_type=jnp.float32)  9.58 us
    dot_general x2, matrix products, pair_tile(): lax.dot_general(panel, piece, (((1,), (1,)), ((), ())), preferred_element...  7.87 us
    add x6, other arithmetic, shards(): img_acc = img_acc + panel_acc[slot * rows:(slot + 1) * rows]  7.04 us
    dot_general x2, matrix products, pair_tile(): lax.dot_general(grads_b, panel, (((0,), (0,)), ((), ())), preferred_eleme...  6.27 us
  transfers between devices with their start and end apart: 18, of which 15 were waited for; matrix products, arithmetic and copies ran while one was open for 6% of the time, Pallas kernels for 0%

commit v1 on v0

v1 whole, which is shorter than its diff:
```python
import functools

import jax
import jax.numpy as jnp
from jax import lax
from jax.experimental import pallas as pl
from jax.experimental.pallas import tpu as pltpu
from jax.sharding import PartitionSpec as P

VMEM_BYTES = 48 * 1024 * 1024


def swapped(x, bit):
    count = lax.axis_size("blk")
    return lax.ppermute(x, "blk", [(i, i ^ bit) for i in range(count)])


def gathered(block, bits):
    blocks = [block]
    for bit in bits:
        blocks = blocks + [swapped(b, bit) for b in blocks]
    return blocks


def unit_rows(values):
    wide = values.astype(jnp.float32)
    inverse = lax.rsqrt(jnp.sum(wide * wide, axis=1, keepdims=True) + 1e-06)
    return (wide * inverse, inverse)


def lane_sums(values):
    rows = jnp.sum(values.reshape(values.shape[0] // 8, 8, values.shape[1]), axis=0)
    total = rows[:, :128]
    for start in range(128, values.shape[1], 128):
        total = total + rows[:, start : start + 128]
    return total


def tile_kernel(n_img, n_txt, rows, *refs):
    imgs = refs[:n_img]
    txts = refs[n_img : n_img + n_txt]
    log_temp, bias = refs[n_img + n_txt : n_img + n_txt + 2]
    img_keep, img_send, txt_keep, txt_send, sums = refs[n_img + n_txt + 2 : n_img + n_txt + 7]
    img_b, txt_b, grad_b = refs[n_img + n_txt + 7 :]
    for k in range(n_img):
        img_b[k * rows : (k + 1) * rows] = unit_rows(imgs[k][...])[0].astype(jnp.bfloat16)
    for k in range(n_txt):
        txt_b[k * rows : (k + 1) * rows] = unit_rows(txts[k][...])[0].astype(jnp.bfloat16)
    temp = jnp.exp(log_temp[...])
    shift_b = bias[...]
    sum_g = jnp.zeros((8, 128), jnp.float32)
    sum_gl = jnp.zeros((8, 128), jnp.float32)
    step = 2 * rows
    half = n_img // 2 * rows
    for start in range(0, n_img * rows, step):
        panel = img_b[start : start + step]
        cosine = lax.dot_general(
            panel, txt_b[...], (((1,), (1,)), ((), ())), preferred_element_type=jnp.float32
        )
        scaled = temp * cosine
        logits = scaled + shift_b
        if start == 0:
            at_row = lax.broadcasted_iota(jnp.int32, logits.shape, 0)
            at_col = lax.broadcasted_iota(jnp.int32, logits.shape, 1)
            own = jnp.logical_and(at_row == at_col, at_row < rows)
            sign = jnp.where(own, 1.0, -1.0)
            grads = -sign * jax.nn.sigmoid(-sign * logits)
        else:
            grads = jax.nn.sigmoid(logits)
        sum_g = sum_g + lane_sums(grads)
        sum_gl = sum_gl + lane_sums(grads * scaled)
        grads_b = grads.astype(jnp.bfloat16)
        grad_b[start : start + step] = grads_b
        part = jnp.dot(grads_b, txt_b[...], preferred_element_type=jnp.float32)
        if start < half:
            img_keep[start : start + step] = part
        else:
            img_send[start - half : start - half + step] = part.astype(jnp.bfloat16)
    sums[0:8] = sum_g
    sums[8:16] = sum_gl
    half = n_txt // 2 * rows
    for start in range(0, n_txt * rows, step):
        part = lax.dot_general(
            grad_b[:, start : start + step],
            img_b[...],
            (((0,), (0,)), ((), ())),
            preferred_element_type=jnp.float32,
        )
        if start < half:
            txt_keep[start : start + step] = part
        else:
            txt_send[start - half : start - half + step] = part.astype(jnp.bfloat16)


def tile_call(imgs, txts, log_temp, bias):
    rows, width = imgs[0].shape
    n_img, n_txt = len(imgs), len(txts)
    half_img, half_txt = n_img // 2 * rows, n_txt // 2 * rows
    pairs = n_img * n_txt * rows * rows
    return pl.pallas_call(
        functools.partial(tile_kernel, n_img, n_txt, rows),
        out_shape=(
            jax.ShapeDtypeStruct((half_img, width), jnp.float32),
            jax.ShapeDtypeStruct((half_img, width), jnp.bfloat16),
            jax.ShapeDtypeStruct((half_txt, width), jnp.float32),
            jax.ShapeDtypeStruct((half_txt, width), jnp.bfloat16),
            jax.ShapeDtypeStruct((16, 128), jnp.float32),
        ),
        in_specs=[pl.BlockSpec(memory_space=pltpu.VMEM)] * (n_img + n_txt + 2),
        out_specs=[pl.BlockSpec(memory_space=pltpu.VMEM)] * 5,
        scratch_shapes=[
            pltpu.VMEM((n_img * rows, width), jnp.bfloat16),
            pltpu.VMEM((n_txt * rows, width), jnp.bfloat16),
            pltpu.VMEM((n_img * rows, n_txt * rows), jnp.bfloat16),
        ],
        compiler_params=pltpu.CompilerParams(vmem_limit_bytes=VMEM_BYTES),
        cost_estimate=pl.CostEstimate(
            flops=6 * pairs * width, bytes_accessed=0, transcendentals=2 * pairs
        ),
    )(*imgs, *txts, log_temp, bias)


def finish_kernel(value, keep, recv, log_temp, out):
    unit, inverse = unit_rows(value[...])
    grad = jnp.exp(log_temp[...]) * (keep[...] + recv[...].astype(jnp.float32))
    along = jnp.sum(unit * grad, axis=1, keepdims=True)
    out[...] = ((grad - unit * along) * inverse).astype(jnp.bfloat16)


def finish_call(value, keep, recv, log_temp):
    return pl.pallas_call(
        finish_kernel,
        out_shape=jax.ShapeDtypeStruct(value.shape, jnp.bfloat16),
        compiler_params=pltpu.CompilerParams(vmem_limit_bytes=VMEM_BYTES),
    )(value, keep, recv, log_temp)


def halved(keep, send, bits):
    for place, bit in enumerate(bits):
        recv = swapped(send, bit)
        if place == len(bits) - 1:
            return keep, recv
        half = keep.shape[0] // 2
        send = (keep[half:] + recv[half:].astype(jnp.float32)).astype(jnp.bfloat16)
        keep = keep[:half] + recv[:half].astype(jnp.float32)


def shards(image_embeds, text_embeds, log_temp, bias):
    rows, width = image_embeds.shape
    count = lax.axis_size("blk")
    depth = count.bit_length() - 1
    all_bits = [1 << place for place in range(depth)]
    split = 1 + depth // 2
    img_bits = all_bits[1:split]
    txt_bits = all_bits[:1] + all_bits[split:]
    temp_in = log_temp.reshape(1, 1)
    txts = gathered(text_embeds, txt_bits[::-1])
    imgs = gathered(image_embeds, img_bits[::-1])
    img_keep, img_send, txt_keep, txt_send, sums = tile_call(imgs, txts, temp_in, bias.reshape(1, 1))
    txt_keep, txt_recv = halved(txt_keep, txt_send, txt_bits)
    img_keep, img_recv = halved(img_keep, img_send, img_bits)
    for bit in all_bits:
        sums = sums + swapped(sums, bit)
    grad_text = finish_call(text_embeds, txt_keep, txt_recv, temp_in)
    grad_image = finish_call(image_embeds, img_keep, img_recv, temp_in)
    pairs = float(rows * count) * float(rows * count)
    grad_bias = jnp.reshape(jnp.sum(sums[:8]) / pairs, (1,))
    grad_temp = jnp.reshape(jnp.sum(sums[8:]) / pairs, (1,))
    return (grad_image, grad_text, grad_temp, grad_bias)


def solution(mesh):
    in_specs = (P(("groups", "blk"), None), P(("groups", "blk"), None), P(), P())
    out_specs = (P(("groups", "blk"), None), P(("groups", "blk"), None), P("groups"), P("groups"))
    return jax.shard_map(shards, mesh=mesh, in_specs=in_specs, out_specs=out_specs, check_vma=False)
```

time: 271 us -> 66.8 us (0.25)
  waiting for transfers between devices: 143 us -> 37.1 us
  blocking collectives: 35.1 us -> 0 us
  matrix products: 23.7 us -> 0 us
  starting transfers between devices: 36.8 us -> 16.1 us
  other arithmetic: 16.7 us -> 0.88 us
  Pallas kernels: 0 us -> 4.98 us
  local copies, waits for them, and re-layouts: 6.39 us -> 1.94 us
  loops' own time: 2.86 us -> 0 us
    ppermute x18 -> x14, waiting for transfers between devices: 143 us -> 37.1 us  [swapped(): return lax.ppermute(x, 'blk', [(i, i ^ bit) for i in range(count)])]
    psum x1 -> x0, blocking collectives: 35.1 us -> none  [shards(): total_g, total_gl = lax.psum((sum_g, sum_gl), 'blk')]
    dot_general x6 -> x0, matrix products: 23.7 us -> none  [the longest x2 9.58 us: pair_tile(): img_part = jnp.dot(grads_b, piece, preferred_element_type=jnp.float32)]
    ppermute x18 -> x14, starting transfers between devices: 36.8 us -> 16.1 us  [swapped(): return lax.ppermute(x, 'blk', [(i, i ^ bit) for i in range(count)])]
    add x8 -> x4, other arithmetic: 7.05 us -> 0.01 us  [shards(): sums = sums + swapped(sums, bit)]
    pallas_call x0 -> x3, Pallas kernels: none -> 4.98 us  [the longest x1 2.93 us: tile_call(): pl.pallas_call(functools.partial(tile_kernel, n_img, n_txt, rows), out_sh...]
    convert_element_type x3 -> x2, other arithmetic: 4.05 us -> 0.26 us  [halved(): send = (keep[half:] + recv[half:].astype(jnp.float32)).astype(jnp.bfloat16)]
    reduce_sum x4 -> x1, other arithmetic: 3.74 us -> 0.6 us  [shards(): grad_bias = jnp.reshape(jnp.sum(sums[:8]) / pairs, (1,))]
  transfers between devices with their start and end apart: 18 -> 14, of which waited for: 15 -> 8; matrix products, arithmetic and copies ran while one was open for 6% -> 1% of each run, Pallas kernels for 0% -> 2%
where the time goes in v1:
time: 66.8 us; the launch traced here: 66.6 us
  waiting for transfers between devices  37.1 us (56%)
  starting transfers between devices  16.1 us (24%)
  between operations  5.58 us (8%)
  Pallas kernels  4.98 us (7%)
  local copies, waits for them, and re-layouts  1.94 us (3%)
  other arithmetic  0.88 us (1%)
    ppermute x14, waiting for transfers between devices, swapped(): return lax.ppermute(x, 'blk', [(i, i ^ bit) for i in range(count)])  37.1 us
    ppermute x14, starting transfers between devices, swapped(): return lax.ppermute(x, 'blk', [(i, i ^ bit) for i in range(count)])  16.1 us
    pallas_call x1, Pallas kernels, tile_call(): pl.pallas_call(functools.partial(tile_kernel, n_img, n_txt, rows), out_sh...  2.93 us
    pallas_call x2, Pallas kernels, finish_call(): pl.pallas_call(finish_kernel, out_shape=jax.ShapeDtypeStruct(value.shape,...  2.05 us
    unnamed x8, local copies, waits for them, and re-layouts  1.94 us
  transfers between devices with their start and end apart: 14, of which 8 were waited for; matrix products, arithmetic and copies ran while one was open for 1% of the time, Pallas kernels for 2%

profile of v1, /device:TPU:0, one launch (start us, length us, event | category | flops | bytes accessed | tf_op | source)
XLA Modules:
  0.0 66.6 jit_solution(18117400913796413420)
XLA Ops:
  0.6 3.1 %collective-permute-start = (bf16[128,1152]{1,0:T(8,128)(2,1)}, bf16[128,1152]{1,0:T(8,128)(2,1)S(1)}, u32[]{:S(2)}, u32[]{:S(2)}) collective-permute-start(bf16[128,1152]{1,0:T(8,128)(2,1)} %value.2), channel_id=1, source_target_pairs={{0,4},{1,5},{2,6},{3,7},{4,0},{5,1},{6,2},{7,3},{8,12},{9,13},{10,... | collective-permute-start | bytes 884744 | tf_op jit(solution)/shard_map/ppermute | solution.py:15
  3.7 2.6 %collective-permute-start.3 = (bf16[128,1152]{1,0:T(8,128)(2,1)}, bf16[128,1152]{1,0:T(8,128)(2,1)S(1)}, u32[]{:S(2)}, u32[]{:S(2)}) collective-permute-start(bf16[128,1152]{1,0:T(8,128)(2,1)} %value.3), channel_id=1, source_target_pairs={{0,8},{1,9},{2,10},{3,11},{4,12},{5,13},{6,14},{7,15},{8,0},{9,1},... | collective-permute-start | bytes 884744 | tf_op jit(solution)/shard_map/ppermute | solution.py:15
  6.3 1.5 %collective-permute-start.1 = (bf16[128,1152]{1,0:T(8,128)(2,1)}, bf16[128,1152]{1,0:T(8,128)(2,1)S(1)}, u32[]{:S(2)}, u32[]{:S(2)}) collective-permute-start(bf16[128,1152]{1,0:T(8,128)(2,1)} %value.2), channel_id=1, source_target_pairs={{0,2},{1,3},{2,0},{3,1},{4,6},{5,7},{6,4},{7,5},{8,10},{9,11},{10,... | collective-permute-start | bytes 884744 | tf_op jit(solution)/shard_map/ppermute | solution.py:15
  7.8 0.0 collective-permute-start.4
  7.8 9.3 %collective-permute-done.refs_1_ = bf16[128,1152]{1,0:T(8,128)(2,1)S(1)} collective-permute-done((bf16[128,1152]{1,0:T(8,128)(2,1)}, bf16[128,1152]{1,0:T(8,128)(2,1)S(1)}, u32[]{:S(2)}, u32[]{:S(2)}) %collective-permute-start) | collective-permute-done | bytes 294944 | tf_op jit(solution)/shard_map/ppermute | solution.py:15
  17.1 1.7 %collective-permute-start.2 = (bf16[128,1152]{1,0:T(8,128)(2,1)S(1)}, bf16[128,1152]{1,0:T(8,128)(2,1)S(1)}, u32[]{:S(2)}, u32[]{:S(2)}) collective-permute-start(bf16[128,1152]{1,0:T(8,128)(2,1)S(1)} %collective-permute-done.refs_1_), channel_id=1, source_target_pairs={{0,2},{1,3},{2,0},{3,1},{4,6},{5,7},{6,4},{7,5},{8,10},{9,11},{10,... | collective-permute-start | bytes 884744 | tf_op jit(solution)/shard_map/ppermute | solution.py:15
  18.8 0.9 %collective-permute-done.3.refs_5_ = bf16[128,1152]{1,0:T(8,128)(2,1)S(1)} collective-permute-done((bf16[128,1152]{1,0:T(8,128)(2,1)}, bf16[128,1152]{1,0:T(8,128)(2,1)S(1)}, u32[]{:S(2)}, u32[]{:S(2)}) %collective-permute-start.3) | collective-permute-done | bytes 294944 | tf_op jit(solution)/shard_map/ppermute | solution.py:15
  19.7 0.0 collective-permute-start.5
  21.0 0.0 collective-permute-done.1.refs_2_
  21.0 0.0 collective-permute-done.4.refs_6_
  21.0 4.4 %collective-permute-done.2.refs_3_ = bf16[128,1152]{1,0:T(8,128)(2,1)S(1)} collective-permute-done((bf16[128,1152]{1,0:T(8,128)(2,1)S(1)}, bf16[128,1152]{1,0:T(8,128)(2,1)S(1)}, u32[]{:S(2)}, u32[]{:S(2)}) %collective-permute-start.2) | collective-permute-done | bytes 294944 | tf_op jit(solution)/shard_map/ppermute | solution.py:15
  25.3 0.0 collective-permute-done.5.refs_7_
  25.3 0.0 copy-start
  25.3 1.0 %copy-done = bf16[128,1152]{1,0:T(8,128)(2,1)S(1)} copy-done((bf16[128,1152]{1,0:T(8,128)(2,1)S(1)}, bf16[128,1152]{1,0:T(8,128)(2,1)}, u32[]{:S(2)}) %copy-start) | copy-done | bytes 294936
  26.3 0.0 copy-start.2
  26.3 1.0 %copy-done.2 = bf16[128,1152]{1,0:T(8,128)(2,1)S(1)} copy-done((bf16[128,1152]{1,0:T(8,128)(2,1)S(1)}, bf16[128,1152]{1,0:T(8,128)(2,1)}, u32[]{:S(2)}) %copy-start.2) | copy-done | bytes 294936
  27.3 2.9 %shard_map.75 = (f32[256,1152]{1,0:T(8,128)S(1)}, bf16[256,1152]{1,0:T(8,128)(2,1)S(1)}, f32[256,1152]{1,0:T(8,128)S(1)}, bf16[256,1152]{1,0:T(8,128)(2,1)S(1)}, f32[16,128]{1,0:T(8,128)S(1)}) custom-call(bf16[128,1152]{1,0:T(8,128)(2,1)S(1)} %copy-done, bf16[128,1152]{1,0:T(8,128)(2,1)S(1)} %collective-permute-done.refs_1_, ...), custom_call_target="tpu_custom_call" | custom-call | flops 1811939328 | tf_op jit(solution)/shard_map/pallas_call | solution.py:100
  30.2 1.4 %collective-permute-start.6 = (bf16[256,1152]{1,0:T(8,128)(2,1)S(1)}, bf16[256,1152]{1,0:T(8,128)(2,1)S(1)}, u32[]{:S(2)}, u32[]{:S(2)}) collective-permute-start(bf16[256,1152]{1,0:T(8,128)(2,1)S(1)} %get-tuple-element.10), channel_id=1, source_target_pairs={{0,2},{1,3},{2,0},{3,1},{4,6},{5,7},{6,4},{7,5},{8,10},{9,11},{10,... | collective-permute-start | bytes 1769480 | tf_op jit(solution)/shard_map/ppermute | solution.py:15
  31.6 0.0 collective-permute-start.8
  31.6 12.3 %collective-permute-done.6 = bf16[256,1152]{1,0:T(8,128)(2,1)S(1)} collective-permute-done((bf16[256,1152]{1,0:T(8,128)(2,1)S(1)}, bf16[256,1152]{1,0:T(8,128)(2,1)S(1)}, u32[]{:S(2)}, u32[]{:S(2)}) %collective-permute-start.6) | collective-permute-done | bytes 589856 | tf_op jit(solution)/shard_map/ppermute | solution.py:15
  43.9 0.1 add_convert_fusion.1
  44.0 0.1 collective-permute-start.7
  44.1 0.0 collective-permute-done.8
  44.1 0.0 copy-start.1
  44.1 0.1 add_convert_fusion
  44.2 0.0 copy-start.3
  44.2 2.6 %collective-permute-start.9 = (bf16[128,1152]{1,0:T(8,128)(2,1)S(1)}, bf16[128,1152]{1,0:T(8,128)(2,1)S(1)}, u32[]{:S(2)}, u32[]{:S(2)}) collective-permute-start(bf16[128,1152]{1,0:T(8,128)(2,1)S(1)} %get-tuple-element.16), channel_id=1, source_target_pairs={{0,8},{1,9},{2,10},{3,11},{4,12},{5,13},{6,14},{7,15},{8,0},{9,1},... | collective-permute-start | bytes 884744 | tf_op jit(solution)/shard_map/ppermute | solution.py:15
  46.9 0.0 collective-permute-start.10
  46.9 1.2 %collective-permute-done.10 = f32[16,128]{1,0:T(8,128)S(1)} collective-permute-done((f32[16,128]{1,0:T(8,128)S(1)}, f32[16,128]{1,0:T(8,128)S(1)}, u32[]{:S(2)}, u32[]{:S(2)}) %collective-permute-start.10) | collective-permute-done | bytes 8224 | tf_op jit(solution)/shard_map/ppermute | solution.py:15
  48.0 1.5 %collective-permute-start.11 = (f32[16,128]{1,0:T(8,128)S(1)}, f32[16,128]{1,0:T(8,128)S(1)}, u32[]{:S(2)}, u32[]{:S(2)}) collective-permute-start(f32[16,128]{1,0:T(8,128)S(1)} %add.28), channel_id=1, source_target_pairs={{0,2},{1,3},{2,0},{3,1},{4,6},{5,7},{6,4},{7,5},{8,10},{9,11},{10,... | collective-permute-start | bytes 24584 | tf_op jit(solution)/shard_map/ppermute | solution.py:15
  49.5 2.2 %collective-permute-done.11 = f32[16,128]{1,0:T(8,128)S(1)} collective-permute-done((f32[16,128]{1,0:T(8,128)S(1)}, f32[16,128]{1,0:T(8,128)S(1)}, u32[]{:S(2)}, u32[]{:S(2)}) %collective-permute-start.11) | collective-permute-done | bytes 8224 | tf_op jit(solution)/shard_map/ppermute | solution.py:15
  51.7 0.0 collective-permute-start.12
  51.7 4.1 %collective-permute-done.12 = f32[16,128]{1,0:T(8,128)S(1)} collective-permute-done((f32[16,128]{1,0:T(8,128)S(1)}, f32[16,128]{1,0:T(8,128)S(1)}, u32[]{:S(2)}, u32[]{:S(2)}) %collective-permute-start.12) | collective-permute-done | bytes 8224 | tf_op jit(solution)/shard_map/ppermute | solution.py:15
  55.8 1.7 %collective-permute-start.13 = (f32[16,128]{1,0:T(8,128)S(1)}, f32[16,128]{1,0:T(8,128)S(1)}, u32[]{:S(2)}, u32[]{:S(2)}) collective-permute-start(f32[16,128]{1,0:T(8,128)S(1)} %add.30), channel_id=1, source_target_pairs={{0,8},{1,9},{2,10},{3,11},{4,12},{5,13},{6,14},{7,15},{8,0},{9,1},... | collective-permute-start | bytes 24584 | tf_op jit(solution)/shard_map/ppermute | solution.py:15
  57.4 2.9 %collective-permute-done.13 = f32[16,128]{1,0:T(8,128)S(1)} collective-permute-done((f32[16,128]{1,0:T(8,128)S(1)}, f32[16,128]{1,0:T(8,128)S(1)}, u32[]{:S(2)}, u32[]{:S(2)}) %collective-permute-start.13) | collective-permute-done | bytes 8224 | tf_op jit(solution)/shard_map/ppermute | solution.py:15
  60.4 0.6 slice_reduce_fusion
  62.3 0.0 collective-permute-done.7.recv
  62.3 0.0 copy-done.1
  62.3 1.0 %shard_map.76 = bf16[128,1152]{1,0:T(8,128)(2,1)} custom-call(bf16[128,1152]{1,0:T(8,128)(2,1)S(1)} %copy-done.1, f32[128,1152]{1,0:T(8,128)S(1)} %get-tuple-element.19.keep, bf16[128,1152]{1,0:T(8,128)(2,1)S(1)} %collective-permute-done.7.recv, f32[1,1]{1,0:T(1,128)} %bitcast.5.log_temp), custom_call_target="tpu_custom_call" | custom-call | tf_op jit(solution)/shard_map/pallas_call | solution.py:131
  63.3 0.0 collective-permute-done.9.recv
  63.3 0.0 copy-done.3
  63.3 1.0 %shard_map.77 = bf16[128,1152]{1,0:T(8,128)(2,1)} custom-call(bf16[128,1152]{1,0:T(8,128)(2,1)S(1)} %copy-done.3, f32[128,1152]{1,0:T(8,128)S(1)} %get-tuple-element.17.keep, bf16[128,1152]{1,0:T(8,128)(2,1)S(1)} %collective-permute-done.9.recv, f32[1,1]{1,0:T(1,128)} %bitcast.6.log_temp), custom_call_target="tpu_custom_call" | custom-call | tf_op jit(solution)/shard_map/pallas_call | solution.py:131
  (4 shorter events, 0.0 us)
Async XLA Ops:
  0.6 16.5 %collective-permute-start = (bf16[128,1152]{1,0:T(8,128)(2,1)}, bf16[128,1152]{1,0:T(8,128)(2,1)S(1)}, u32[]{:S(2)}, u32[]{:S(2)}) collective-permute-start(bf16[128,1152]{1,0:T(8,128)(2,1)} %value.2), channel_id=1, source_target_pairs={{0,4},{1,5},{2,6},{3,7},{4,0},{5,1},{6,2},{7,3},{8,12},{9,13},{10,... | collective-permute-start | bytes 884744 | tf_op jit(solution)/shard_map/ppermute | solution.py:15
  3.7 15.9 %collective-permute-start.3 = (bf16[128,1152]{1,0:T(8,128)(2,1)}, bf16[128,1152]{1,0:T(8,128)(2,1)S(1)}, u32[]{:S(2)}, u32[]{:S(2)}) collective-permute-start(bf16[128,1152]{1,0:T(8,128)(2,1)} %value.3), channel_id=1, source_target_pairs={{0,8},{1,9},{2,10},{3,11},{4,12},{5,13},{6,14},{7,15},{8,0},{9,1},... | collective-permute-start | bytes 884744 | tf_op jit(solution)/shard_map/ppermute | solution.py:15
  6.3 14.7 %collective-permute-start.1 = (bf16[128,1152]{1,0:T(8,128)(2,1)}, bf16[128,1152]{1,0:T(8,128)(2,1)S(1)}, u32[]{:S(2)}, u32[]{:S(2)}) collective-permute-start(bf16[128,1152]{1,0:T(8,128)(2,1)} %value.2), channel_id=1, source_target_pairs={{0,2},{1,3},{2,0},{3,1},{4,6},{5,7},{6,4},{7,5},{8,10},{9,11},{10,... | collective-permute-start | bytes 884744 | tf_op jit(solution)/shard_map/ppermute | solution.py:15
  7.8 13.2 %collective-permute-start.4 = (bf16[128,1152]{1,0:T(8,128)(2,1)}, bf16[128,1152]{1,0:T(8,128)(2,1)S(1)}, u32[]{:S(2)}, u32[]{:S(2)}) collective-permute-start(bf16[128,1152]{1,0:T(8,128)(2,1)} %value.3), channel_id=1, source_target_pairs={{0,1},{1,0},{2,3},{3,2},{4,5},{5,4},{6,7},{7,6},{8,9},{9,8},{10,11... | collective-permute-start | bytes 884744 | tf_op jit(solution)/shard_map/ppermute | solution.py:15
  17.1 8.2 %collective-permute-start.2 = (bf16[128,1152]{1,0:T(8,128)(2,1)S(1)}, bf16[128,1152]{1,0:T(8,128)(2,1)S(1)}, u32[]{:S(2)}, u32[]{:S(2)}) collective-permute-start(bf16[128,1152]{1,0:T(8,128)(2,1)S(1)} %collective-permute-done.refs_1_), channel_id=1, source_target_pairs={{0,2},{1,3},{2,0},{3,1},{4,6},{5,7},{6,4},{7,5},{8,10},{9,11},{10,... | collective-permute-start | bytes 884744 | tf_op jit(solution)/shard_map/ppermute | solution.py:15
  19.7 5.7 %collective-permute-start.5 = (bf16[128,1152]{1,0:T(8,128)(2,1)S(1)}, bf16[128,1152]{1,0:T(8,128)(2,1)S(1)}, u32[]{:S(2)}, u32[]{:S(2)}) collective-permute-start(bf16[128,1152]{1,0:T(8,128)(2,1)S(1)} %collective-permute-done.3.refs_5_), channel_id=1, source_target_pairs={{0,1},{1,0},{2,3},{3,2},{4,5},{5,4},{6,7},{7,6},{8,9},{9,8},{10,11... | collective-permute-start | bytes 884744 | tf_op jit(solution)/shard_map/ppermute | solution.py:15
  25.3 1.0 %copy-start = (bf16[128,1152]{1,0:T(8,128)(2,1)S(1)}, bf16[128,1152]{1,0:T(8,128)(2,1)}, u32[]{:S(2)}) copy-start(bf16[128,1152]{1,0:T(8,128)(2,1)} %value.2) | copy-start | bytes 884740
  26.3 1.0 %copy-start.2 = (bf16[128,1152]{1,0:T(8,128)(2,1)S(1)}, bf16[128,1152]{1,0:T(8,128)(2,1)}, u32[]{:S(2)}) copy-start(bf16[128,1152]{1,0:T(8,128)(2,1)} %value.3) | copy-start | bytes 884740
  30.2 13.7 %collective-permute-start.6 = (bf16[256,1152]{1,0:T(8,128)(2,1)S(1)}, bf16[256,1152]{1,0:T(8,128)(2,1)S(1)}, u32[]{:S(2)}, u32[]{:S(2)}) collective-permute-start(bf16[256,1152]{1,0:T(8,128)(2,1)S(1)} %get-tuple-element.10), channel_id=1, source_target_pairs={{0,2},{1,3},{2,0},{3,1},{4,6},{5,7},{6,4},{7,5},{8,10},{9,11},{10,... | collective-permute-start | bytes 1769480 | tf_op jit(solution)/shard_map/ppermute | solution.py:15
  31.6 12.5 %collective-permute-start.8 = (bf16[256,1152]{1,0:T(8,128)(2,1)S(1)}, bf16[256,1152]{1,0:T(8,128)(2,1)S(1)}, u32[]{:S(2)}, u32[]{:S(2)}) collective-permute-start(bf16[256,1152]{1,0:T(8,128)(2,1)S(1)} %get-tuple-element.12), channel_id=1, source_target_pairs={{0,1},{1,0},{2,3},{3,2},{4,5},{5,4},{6,7},{7,6},{8,9},{9,8},{10,11... | collective-permute-start | bytes 1769480 | tf_op jit(solution)/shard_map/ppermute | solution.py:15
  44.0 18.3 %collective-permute-start.7 = (bf16[128,1152]{1,0:T(8,128)(2,1)S(1)}, bf16[128,1152]{1,0:T(8,128)(2,1)S(1)}, u32[]{:S(2)}, u32[]{:S(2)}) collective-permute-start(bf16[128,1152]{1,0:T(8,128)(2,1)S(1)} %get-tuple-element.18), channel_id=1, source_target_pairs={{0,4},{1,5},{2,6},{3,7},{4,0},{5,1},{6,2},{7,3},{8,12},{9,13},{10,... | collective-permute-start | bytes 884744 | tf_op jit(solution)/shard_map/ppermute | solution.py:15
  44.1 18.2 %copy-start.1 = (bf16[128,1152]{1,0:T(8,128)(2,1)S(1)}, bf16[128,1152]{1,0:T(8,128)(2,1)}, u32[]{:S(2)}) copy-start(bf16[128,1152]{1,0:T(8,128)(2,1)} %value.2) | copy-start | bytes 884740
  44.2 19.1 %copy-start.3 = (bf16[128,1152]{1,0:T(8,128)(2,1)S(1)}, bf16[128,1152]{1,0:T(8,128)(2,1)}, u32[]{:S(2)}) copy-start(bf16[128,1152]{1,0:T(8,128)(2,1)} %value.3) | copy-start | bytes 884740
  44.2 19.1 %collective-permute-start.9 = (bf16[128,1152]{1,0:T(8,128)(2,1)S(1)}, bf16[128,1152]{1,0:T(8,128)(2,1)S(1)}, u32[]{:S(2)}, u32[]{:S(2)}) collective-permute-start(bf16[128,1152]{1,0:T(8,128)(2,1)S(1)} %get-tuple-element.16), channel_id=1, source_target_pairs={{0,8},{1,9},{2,10},{3,11},{4,12},{5,13},{6,14},{7,15},{8,0},{9,1},... | collective-permute-start | bytes 884744 | tf_op jit(solution)/shard_map/ppermute | solution.py:15
  46.9 1.2 %collective-permute-start.10 = (f32[16,128]{1,0:T(8,128)S(1)}, f32[16,128]{1,0:T(8,128)S(1)}, u32[]{:S(2)}, u32[]{:S(2)}) collective-permute-start(f32[16,128]{1,0:T(8,128)S(1)} %get-tuple-element.13), channel_id=1, source_target_pairs={{0,1},{1,0},{2,3},{3,2},{4,5},{5,4},{6,7},{7,6},{8,9},{9,8},{10,11... | collective-permute-start | bytes 24584 | tf_op jit(solution)/shard_map/ppermute | solution.py:15
  48.0 3.7 %collective-permute-start.11 = (f32[16,128]{1,0:T(8,128)S(1)}, f32[16,128]{1,0:T(8,128)S(1)}, u32[]{:S(2)}, u32[]{:S(2)}) collective-permute-start(f32[16,128]{1,0:T(8,128)S(1)} %add.28), channel_id=1, source_target_pairs={{0,2},{1,3},{2,0},{3,1},{4,6},{5,7},{6,4},{7,5},{8,10},{9,11},{10,... | collective-permute-start | bytes 24584 | tf_op jit(solution)/shard_map/ppermute | solution.py:15
  51.7 4.1 %collective-permute-start.12 = (f32[16,128]{1,0:T(8,128)S(1)}, f32[16,128]{1,0:T(8,128)S(1)}, u32[]{:S(2)}, u32[]{:S(2)}) collective-permute-start(f32[16,128]{1,0:T(8,128)S(1)} %add.29), channel_id=1, source_target_pairs={{0,4},{1,5},{2,6},{3,7},{4,0},{5,1},{6,2},{7,3},{8,12},{9,13},{10,... | collective-permute-start | bytes 24584 | tf_op jit(solution)/shard_map/ppermute | solution.py:15
  55.8 4.5 %collective-permute-start.13 = (f32[16,128]{1,0:T(8,128)S(1)}, f32[16,128]{1,0:T(8,128)S(1)}, u32[]{:S(2)}, u32[]{:S(2)}) collective-permute-start(f32[16,128]{1,0:T(8,128)S(1)} %add.30), channel_id=1, source_target_pairs={{0,8},{1,9},{2,10},{3,11},{4,12},{5,13},{6,14},{7,15},{8,0},{9,1},... | collective-permute-start | bytes 24584 | tf_op jit(solution)/shard_map/ppermute | solution.py:15

commit v2 on v1

v2 whole, which is shorter than its diff:
```python
import functools

import jax
import jax.numpy as jnp
from jax import lax
from jax.experimental import pallas as pl
from jax.experimental.pallas import tpu as pltpu
from jax.sharding import PartitionSpec as P

VMEM_BYTES = 48 * 1024 * 1024


def swapped(x, bit):
    count = lax.axis_size("blk")
    return lax.ppermute(x, "blk", [(i, i ^ bit) for i in range(count)])


def after(value, *others):
    return pl.pallas_call(
        lambda *refs: None,
        out_shape=jax.ShapeDtypeStruct(value.shape, value.dtype),
        in_specs=[pl.BlockSpec(memory_space=pl.ANY)] * (1 + len(others)),
        out_specs=pl.BlockSpec(memory_space=pl.ANY),
        input_output_aliases={0: 0},
    )(value, *others)


def unit_rows(values):
    wide = values.astype(jnp.float32)
    inverse = lax.rsqrt(jnp.sum(wide * wide, axis=1, keepdims=True) + 1e-06)
    return (wide * inverse, inverse)


def lane_sums(values):
    rows = jnp.sum(values.reshape(values.shape[0] // 8, 8, values.shape[1]), axis=0)
    total = rows[:, :128]
    for start in range(128, values.shape[1], 128):
        total = total + rows[:, start : start + 128]
    return total


def own_kernel(value, unit, inverse, *pieces):
    scaled, inv = unit_rows(value[...])
    unit[...] = scaled
    inverse[...] = jnp.broadcast_to(inv, inverse.shape)
    store_pieces(scaled, pieces)


def other_kernel(value, *pieces):
    store_pieces(unit_rows(value[...])[0], pieces)


def store_pieces(values, pieces):
    size = values.shape[0] // len(pieces)
    for place, piece in enumerate(pieces):
        piece[...] = values[place * size : (place + 1) * size].astype(jnp.bfloat16)


def unit_call(value, count, own):
    rows, width = value.shape
    outs = [jax.ShapeDtypeStruct((rows // count, width), jnp.bfloat16)] * count
    if own:
        wide = jax.ShapeDtypeStruct((rows, width), jnp.float32)
        outs = [wide, jax.ShapeDtypeStruct((rows, 128), jnp.float32)] + outs
    return pl.pallas_call(
        own_kernel if own else other_kernel,
        out_shape=outs,
        cost_estimate=pl.CostEstimate(
            flops=4 * rows * width, bytes_accessed=4 * rows * width, transcendentals=rows
        ),
    )(value)


def gathered(value, bits, count):
    raw = [swapped(value, bit) for bit in bits]
    unit, inverse, *own = unit_call(value, count, True)
    blocks = {0: own}
    for place in range(len(bits)):
        blocks[1 << place] = unit_call(raw[place], count, False)
    for offset in range(1 << len(bits)):
        if offset not in blocks:
            high = 1 << (offset.bit_length() - 1)
            low = offset & -offset
            lasts = [high] + [low] * (count - 1)
            blocks[offset] = [
                swapped(blocks[offset ^ last][place], bits[last.bit_length() - 1])
                for place, last in enumerate(lasts)
            ]
    return unit, inverse, [blocks[offset] for offset in range(1 << len(bits))]


def tile_kernel(img_places, txt_places, rows, *refs):
    n_img, n_txt = len(img_places), len(txt_places)
    taken = 0
    sources = []
    for places in (img_places, txt_places):
        pieces = sum(places)
        sources.append(refs[taken : taken + pieces])
        taken += pieces
    log_temp, bias = refs[taken : taken + 2]
    img_parts = refs[taken + 2 : taken + 2 + n_img]
    txt_parts = refs[taken + 2 + n_img : taken + 2 + n_img + n_txt]
    sums, img_b, txt_b, grad_b = refs[taken + 2 + n_img + n_txt :]
    for group, held in zip(sources, (img_b, txt_b)):
        start = 0
        for piece in group:
            end = start + piece.shape[0]
            held[start:end] = piece[...]
            start = end
    temp = jnp.exp(log_temp[...])
    shift_b = bias[...]
    sum_g = jnp.zeros((8, 128), jnp.float32)
    sum_gl = jnp.zeros((8, 128), jnp.float32)
    step = 2 * rows
    for start in range(0, n_img * rows, step):
        panel = img_b[start : start + step]
        cosine = lax.dot_general(
            panel, txt_b[...], (((1,), (1,)), ((), ())), preferred_element_type=jnp.float32
        )
        scaled = temp * cosine
        logits = scaled + shift_b
        if start == 0:
            at_row = lax.broadcasted_iota(jnp.int32, logits.shape, 0)
            at_col = lax.broadcasted_iota(jnp.int32, logits.shape, 1)
            own = jnp.logical_and(at_row == at_col, at_row < rows)
            sign = jnp.where(own, 1.0, -1.0)
            grads = -sign * jax.nn.sigmoid(-sign * logits)
        else:
            grads = jax.nn.sigmoid(logits)
        sum_g = sum_g + lane_sums(grads)
        sum_gl = sum_gl + lane_sums(grads * scaled)
        grads_b = grads.astype(jnp.bfloat16)
        grad_b[start : start + step] = grads_b
        part = jnp.dot(grads_b, txt_b[...], preferred_element_type=jnp.float32)
        for at in range(start // rows, (start + step) // rows):
            out = img_parts[at]
            out[...] = part[at * rows - start : (at + 1) * rows - start].astype(out.dtype)
    sums[0:8] = sum_g
    sums[8:16] = sum_gl
    for start in range(0, n_txt * rows, step):
        part = lax.dot_general(
            grad_b[:, start : start + step],
            img_b[...],
            (((0,), (0,)), ((), ())),
            preferred_element_type=jnp.float32,
        )
        for at in range(start // rows, (start + step) // rows):
            out = txt_parts[at]
            out[...] = part[at * rows - start : (at + 1) * rows - start].astype(out.dtype)


def tile_call(imgs, txts, log_temp, bias):
    rows = sum(piece.shape[0] for piece in imgs[0])
    width = imgs[0][0].shape[1]
    n_img, n_txt = len(imgs), len(txts)
    flat = [piece for block in imgs + txts for piece in block]
    pairs = n_img * n_txt * rows * rows

    def outs(count):
        kinds = [jnp.float32] * (count // 2) + [jnp.bfloat16] * (count // 2)
        return [jax.ShapeDtypeStruct((rows, width), kind) for kind in kinds]

    results = pl.pallas_call(
        functools.partial(
            tile_kernel, [len(block) for block in imgs], [len(block) for block in txts], rows
        ),
        out_shape=outs(n_img) + outs(n_txt) + [jax.ShapeDtypeStruct((16, 128), jnp.float32)],
        in_specs=[pl.BlockSpec(memory_space=pltpu.VMEM)] * (len(flat) + 2),
        out_specs=[pl.BlockSpec(memory_space=pltpu.VMEM)] * (n_img + n_txt + 1),
        scratch_shapes=[
            pltpu.VMEM((n_img * rows, width), jnp.bfloat16),
            pltpu.VMEM((n_txt * rows, width), jnp.bfloat16),
            pltpu.VMEM((n_img * rows, n_txt * rows), jnp.bfloat16),
        ],
        compiler_params=pltpu.CompilerParams(vmem_limit_bytes=VMEM_BYTES),
        cost_estimate=pl.CostEstimate(
            flops=6 * pairs * width, bytes_accessed=0, transcendentals=2 * pairs
        ),
    )(*flat, log_temp, bias)
    return results[:n_img], results[n_img:-1], results[-1]


def finish_kernel(unit, inverse, log_temp, keep, *refs):
    total = keep[...]
    for recv in refs[:-1]:
        total = total + recv[...].astype(jnp.float32)
    grad = jnp.exp(log_temp[...]) * total
    along = jnp.sum(unit[...] * grad, axis=1, keepdims=True)
    refs[-1][...] = ((grad - unit[...] * along) * inverse[:, :1]).astype(jnp.bfloat16)


def finish_call(unit, inverse, log_temp, keep, recvs):
    return pl.pallas_call(
        finish_kernel,
        out_shape=jax.ShapeDtypeStruct(keep.shape, jnp.bfloat16),
        compiler_params=pltpu.CompilerParams(vmem_limit_bytes=VMEM_BYTES),
    )(unit, inverse, log_temp, keep, *recvs)


def add_kernel(keep, recv, *refs):
    refs[-1][...] = (keep[...] + recv[...].astype(jnp.float32)).astype(refs[-1].dtype)


def add_call(keep, recv, dtype, others):
    rest = [pl.BlockSpec(memory_space=pl.ANY)] * len(others)
    return pl.pallas_call(
        add_kernel,
        out_shape=jax.ShapeDtypeStruct(keep.shape, dtype),
        in_specs=[pl.BlockSpec(memory_space=pltpu.VMEM)] * 2 + rest,
        out_specs=pl.BlockSpec(memory_space=pltpu.VMEM),
    )(keep, recv, *others)


def returned(parts, bits, others):
    parts = dict(enumerate(parts))
    recvs = []
    for place in reversed(range(len(bits))):
        arrived = {}
        for offset in range(1, 1 << place):
            send = parts.pop(offset | 1 << place).astype(jnp.bfloat16)
            arrived[offset] = swapped(send, bits[place])
        for offset, recv in arrived.items():
            dtype = jnp.float32 if offset < 1 << place - 1 else jnp.bfloat16
            parts[offset] = add_call(parts[offset], recv, dtype, others)
        send = parts.pop(1 << place).astype(jnp.bfloat16)
        if arrived:
            send = after(send, *[parts[offset] for offset in arrived])
            others = [parts[max(arrived)]]
        recvs.append(swapped(send, bits[place]))
    return parts[0], recvs, others


def shards(image_embeds, text_embeds, log_temp, bias):
    rows, width = image_embeds.shape
    count = lax.axis_size("blk")
    depth = count.bit_length() - 1
    all_bits = [1 << place for place in range(depth)]
    split = 1 + depth // 2
    img_bits = all_bits[1:split][::-1]
    txt_bits = (all_bits[:1] + all_bits[split:])[::-1]
    temp_in = log_temp.reshape(1, 1)
    unit_txt, inv_txt, txts = gathered(text_embeds, txt_bits, 1)
    unit_img, inv_img, imgs = gathered(image_embeds, img_bits, 2)
    img_parts, txt_parts, sums = tile_call(imgs, txts, temp_in, bias.reshape(1, 1))
    txt_keep, txt_recvs, others = returned(txt_parts, txt_bits, [])
    img_keep, img_recvs, others = returned(img_parts, img_bits, others)
    for bit in all_bits:
        sums = sums + swapped(sums, bit)
    grad_text = finish_call(unit_txt, inv_txt, temp_in, txt_keep, txt_recvs)
    grad_image = finish_call(unit_img, inv_img, temp_in, img_keep, img_recvs)
    pairs = float(rows * count) * float(rows * count)
    grad_bias = jnp.reshape(jnp.sum(sums[:8]) / pairs, (1,))
    grad_temp = jnp.reshape(jnp.sum(sums[8:]) / pairs, (1,))
    return (grad_image, grad_text, grad_temp, grad_bias)


def solution(mesh):
    in_specs = (P(("groups", "blk"), None), P(("groups", "blk"), None), P(), P())
    out_specs = (P(("groups", "blk"), None), P(("groups", "blk"), None), P("groups"), P("groups"))
    return jax.shard_map(shards, mesh=mesh, in_specs=in_specs, out_specs=out_specs, check_vma=False)
```

time: 66.8 us -> 84.2 us (1.26)
  Pallas kernels: 4.98 us -> 19.8 us
  waiting for transfers between devices: 37.1 us -> 25.6 us
  local copies, waits for them, and re-layouts: 1.94 us -> 11.2 us
  starting transfers between devices: 16.1 us -> 20.9 us
    pallas_call x3 -> x13, Pallas kernels: 4.98 us -> 19.8 us  [the longest x6 11.5 us: unit_call(): pl.pallas_call(own_kernel if own else other_kernel, out_shape=outs, cost_...]
    ppermute x14 -> x17, waiting for transfers between devices: 37.1 us -> 25.6 us  [swapped(): return lax.ppermute(x, 'blk', [(i, i ^ bit) for i in range(count)])]
    unnamed x8 -> x48, local copies, waits for them, and re-layouts: 1.94 us -> 11.2 us
    ppermute x14 -> x17, starting transfers between devices: 16.1 us -> 20.9 us  [swapped(): return lax.ppermute(x, 'blk', [(i, i ^ bit) for i in range(count)])]
  transfers between devices with their start and end apart: 14 -> 17, of which waited for: 8 -> 7; matrix products, arithmetic and copies ran while one was open for 1% -> 1% of each run, Pallas kernels for 2% -> 17%
where the time goes in v2:
time: 84.2 us; the launch traced here: 83.7 us
  waiting for transfers between devices  25.6 us (30%)
  starting transfers between devices  20.9 us (25%)
  Pallas kernels  19.8 us (24%)
  local copies, waits for them, and re-layouts  11.2 us (13%)
  between operations  5.68 us (7%)
    ppermute x17, waiting for transfers between devices, swapped(): return lax.ppermute(x, 'blk', [(i, i ^ bit) for i in range(count)])  25.6 us
    ppermute x17, starting transfers between devices, swapped(): return lax.ppermute(x, 'blk', [(i, i ^ bit) for i in range(count)])  20.9 us
    pallas_call x6, Pallas kernels, unit_call(): pl.pallas_call(own_kernel if own else other_kernel, out_shape=outs, cost_...  11.5 us
    unnamed x48, local copies, waits for them, and re-layouts  11.2 us
    pallas_call x2, Pallas kernels, add_call(): pl.pallas_call(add_kernel, out_shape=jax.ShapeDtypeStruct(keep.shape, dty...  3.83 us
    pallas_call x1, Pallas kernels, tile_call(): pl.pallas_call(functools.partial(tile_kernel, [len(block) for block in im...  2.58 us
    pallas_call x2, Pallas kernels, finish_call(): pl.pallas_call(finish_kernel, out_shape=jax.ShapeDtypeStruct(keep.shape,...  1.91 us
  transfers between devices with their start and end apart: 17, of which 7 were waited for; matrix products, arithmetic and copies ran while one was open for 1% of the time, Pallas kernels for 17%

profile of v2, /device:TPU:0, one launch (start us, length us, event | category | flops | bytes accessed | tf_op | source)
XLA Modules:
  0.0 83.7 jit_solution(6773093204632474752)
XLA Ops:
  0.6 4.1 %collective-permute-start.4 = (bf16[128,1152]{1,0:T(8,128)(2,1)}, bf16[128,1152]{1,0:T(8,128)(2,1)S(1)}, u32[]{:S(2)}, u32[]{:S(2)}) collective-permute-start(bf16[128,1152]{1,0:T(8,128)(2,1)} %value.3), channel_id=1, source_target_pairs={{0,8},{1,9},{2,10},{3,11},{4,12},{5,13},{6,14},{7,15},{8,0},{9,1},... | collective-permute-start | bytes 884744 | tf_op jit(solution)/shard_map/ppermute | solution.py:15
  4.7 1.5 %collective-permute-start.1 = (bf16[128,1152]{1,0:T(8,128)(2,1)}, bf16[128,1152]{1,0:T(8,128)(2,1)S(1)}, u32[]{:S(2)}, u32[]{:S(2)}) collective-permute-start(bf16[128,1152]{1,0:T(8,128)(2,1)} %value.2), channel_id=1, source_target_pairs={{0,2},{1,3},{2,0},{3,1},{4,6},{5,7},{6,4},{7,5},{8,10},{9,11},{10,... | collective-permute-start | bytes 884744 | tf_op jit(solution)/shard_map/ppermute | solution.py:15
  6.2 1.6 %collective-permute-start = (bf16[128,1152]{1,0:T(8,128)(2,1)}, bf16[128,1152]{1,0:T(8,128)(2,1)S(1)}, u32[]{:S(2)}, u32[]{:S(2)}) collective-permute-start(bf16[128,1152]{1,0:T(8,128)(2,1)} %value.2), channel_id=1, source_target_pairs={{0,4},{1,5},{2,6},{3,7},{4,0},{5,1},{6,2},{7,3},{8,12},{9,13},{10,... | collective-permute-start | bytes 884744 | tf_op jit(solution)/shard_map/ppermute | solution.py:15
  7.8 0.0 collective-permute-start.5
  7.8 10.6 %collective-permute-done.4.value = bf16[128,1152]{1,0:T(8,128)(2,1)S(1)} collective-permute-done((bf16[128,1152]{1,0:T(8,128)(2,1)}, bf16[128,1152]{1,0:T(8,128)(2,1)S(1)}, u32[]{:S(2)}, u32[]{:S(2)}) %collective-permute-start.4) | collective-permute-done | bytes 294944 | tf_op jit(solution)/shard_map/ppermute | solution.py:15
  18.4 0.7 copy-done.21
  19.1 1.8 %shard_map.79.refs_9_ = bf16[128,1152]{1,0:T(8,128)(2,1)} custom-call(bf16[128,1152]{1,0:T(8,128)(2,1)} %copy-done.21), custom_call_target="tpu_custom_call" | custom-call | flops 589824 | bytes 589824 | tf_op jit(solution)/shard_map/pallas_call | solution.py:65
  20.9 0.0 collective-permute-start.6
  20.9 0.7 copy-done.20
  21.6 1.8 %shard_map.77 = (bf16[64,1152]{1,0:T(8,128)(2,1)}, bf16[64,1152]{1,0:T(8,128)(2,1)}) custom-call(bf16[128,1152]{1,0:T(8,128)(2,1)} %copy-done.20), custom_call_target="tpu_custom_call" | custom-call | flops 589824 | bytes 589824 | tf_op jit(solution)/shard_map/pallas_call | solution.py:65
  23.4 0.8 collective-permute-start.3
  24.2 0.7 copy-done.19
  24.9 1.8 %shard_map.76 = (bf16[64,1152]{1,0:T(8,128)(2,1)}, bf16[64,1152]{1,0:T(8,128)(2,1)}) custom-call(bf16[128,1152]{1,0:T(8,128)(2,1)} %copy-done.19), custom_call_target="tpu_custom_call" | custom-call | flops 589824 | bytes 589824 | tf_op jit(solution)/shard_map/pallas_call | solution.py:65
  26.7 1.4 %collective-permute-start.2 = (bf16[64,1152]{1,0:T(8,128)(2,1)}, bf16[64,1152]{1,0:T(8,128)(2,1)S(1)}, u32[]{:S(2)}, u32[]{:S(2)}) collective-permute-start(bf16[64,1152]{1,0:T(8,128)(2,1)} %get-tuple-element.28.refs_2_), channel_id=1, source_target_pairs={{0,2},{1,3},{2,0},{3,1},{4,6},{5,7},{6,4},{7,5},{8,10},{9,11},{10,... | collective-permute-start | bytes 442376 | tf_op jit(solution)/shard_map/ppermute | solution.py:15
  29.5 2.1 %shard_map.75 = (f32[128,1152]{1,0:T(8,128)}, f32[128,128]{1,0:T(8,128)}, bf16[64,1152]{1,0:T(8,128)(2,1)}, bf16[64,1152]{1,0:T(8,128)(2,1)}) custom-call(bf16[128,1152]{1,0:T(8,128)(2,1)} %value.2), custom_call_target="tpu_custom_call" | custom-call | flops 589824 | bytes 589824 | tf_op jit(solution)/shard_map/pallas_call | solution.py:65
  31.7 2.1 %shard_map.78 = (f32[128,1152]{1,0:T(8,128)}, f32[128,128]{1,0:T(8,128)}, bf16[128,1152]{1,0:T(8,128)(2,1)}) custom-call(bf16[128,1152]{1,0:T(8,128)(2,1)} %value.3), custom_call_target="tpu_custom_call" | custom-call | flops 589824 | bytes 589824 | tf_op jit(solution)/shard_map/pallas_call | solution.py:65
  33.8 0.7 copy-done.18
  34.5 1.8 %shard_map.80.refs_10_ = bf16[128,1152]{1,0:T(8,128)(2,1)} custom-call(bf16[128,1152]{1,0:T(8,128)(2,1)} %copy-done.18), custom_call_target="tpu_custom_call" | custom-call | flops 589824 | bytes 589824 | tf_op jit(solution)/shard_map/pallas_call | solution.py:65
  36.4 1.0 %copy-done.7 = bf16[128,1152]{1,0:T(8,128)(2,1)S(1)} copy-done((bf16[128,1152]{1,0:T(8,128)(2,1)S(1)}, bf16[128,1152]{1,0:T(8,128)(2,1)}, u32[]{:S(2)}) %copy-start.7) | copy-done | bytes 294936
  37.3 0.9 %copy-done.15 = bf16[64,1152]{1,0:T(8,128)(2,1)S(1)} copy-done((bf16[64,1152]{1,0:T(8,128)(2,1)S(1)}, bf16[64,1152]{1,0:T(8,128)(2,1)}, u32[]{:S(2)}) %copy-start.15) | copy-done | bytes 147480
  38.2 0.9 %copy-done.16 = bf16[64,1152]{1,0:T(8,128)(2,1)S(1)} copy-done((bf16[64,1152]{1,0:T(8,128)(2,1)S(1)}, bf16[64,1152]{1,0:T(8,128)(2,1)}, u32[]{:S(2)}) %copy-start.16) | copy-done | bytes 147480
  39.1 2.6 %shard_map.81 = (f32[128,1152]{1,0:T(8,128)S(1)}, f32[128,1152]{1,0:T(8,128)S(1)}, bf16[128,1152]{1,0:T(8,128)(2,1)S(1)}, bf16[128,1152]{1,0:T(8,128)(2,1)S(1)},...) custom-call(bf16[64,1152]{1,0:T(8,128)(2,1)S(1)} %copy-done.15, ...), custom_call_target="tpu_custom_call" | custom-call | flops 1811939328 | tf_op jit(solution)/shard_map/pallas_call | solution.py:163
  41.7 0.8 copy-done.2
  42.5 0.8 copy-done.3
  43.4 0.7 copy-done.4
  44.1 0.7 copy-done.5
  44.8 0.6 collective-permute-start.7
  45.4 1.0 %collective-permute-done.8.recv = bf16[128,1152]{1,0:T(8,128)(2,1)S(1)} collective-permute-done((bf16[128,1152]{1,0:T(8,128)(2,1)S(1)}, bf16[128,1152]{1,0:T(8,128)(2,1)S(1)}, u32[]{:S(2)}, u32[]{:S(2)}) %collective-permute-start.8) | collective-permute-done | bytes 294944 | tf_op jit(solution)/shard_map/ppermute | solution.py:15
  46.4 0.7 copy-done.23
  47.1 1.9 %shard_map.82.refs_0_.refs_1_ = bf16[128,1152]{1,0:T(8,128)(2,1)} custom-call(f32[128,1152]{1,0:T(8,128)} %copy-done.2, bf16[128,1152]{1,0:T(8,128)(2,1)} %copy-done.23), custom_call_target="tpu_custom_call" | custom-call | tf_op jit(solution)/shard_map/pallas_call | solution.py:206
  49.0 5.2 %collective-permute-done.7.recv = bf16[128,1152]{1,0:T(8,128)(2,1)S(1)} collective-permute-done((bf16[128,1152]{1,0:T(8,128)(2,1)S(1)}, bf16[128,1152]{1,0:T(8,128)(2,1)S(1)}, u32[]{:S(2)}, u32[]{:S(2)}) %collective-permute-start.7) | collective-permute-done | bytes 294944 | tf_op jit(solution)/shard_map/ppermute | solution.py:15
  54.2 0.7 copy-done.22
  54.9 1.9 %shard_map.83.refs_1_ = bf16[128,1152]{1,0:T(8,128)(2,1)} custom-call(f32[128,1152]{1,0:T(8,128)} %copy-done.3, bf16[128,1152]{1,0:T(8,128)(2,1)} %copy-done.22, bf16[128,1152]{1,0:T(8,128)(2,1)} %shard_map.82.refs_0_.refs_1_), custom_call_target="tpu_custom_call" | custom-call | tf_op jit(solution)/shard_map/pallas_call | solution.py:206
  56.9 0.6 collective-permute-start.9
  57.4 1.2 %collective-permute-start.10 = (bf16[128,1152]{1,0:T(8,128)(2,1)}, bf16[128,1152]{1,0:T(8,128)(2,1)S(1)}, u32[]{:S(2)}, u32[]{:S(2)}) collective-permute-start(bf16[128,1152]{1,0:T(8,128)(2,1)} %shard_map.83.refs_1_), channel_id=1, source_target_pairs={{0,4},{1,5},{2,6},{3,7},{4,0},{5,1},{6,2},{7,3},{8,12},{9,13},{10,... | collective-permute-start | bytes 884744 | tf_op jit(solution)/shard_map/ppermute | solution.py:15
  58.7 1.0 %copy-done.17 = bf16[128,1152]{1,0:T(8,128)(2,1)S(1)} copy-done((bf16[128,1152]{1,0:T(8,128)(2,1)S(1)}, bf16[128,1152]{1,0:T(8,128)(2,1)}, u32[]{:S(2)}) %copy-start.17) | copy-done | bytes 294936
  59.7 2.1 %collective-permute-start.12 = (bf16[128,1152]{1,0:T(8,128)(2,1)S(1)}, bf16[128,1152]{1,0:T(8,128)(2,1)S(1)}, u32[]{:S(2)}, u32[]{:S(2)}) collective-permute-start(bf16[128,1152]{1,0:T(8,128)(2,1)S(1)} %copy-done.17), channel_id=1, source_target_pairs={{0,8},{1,9},{2,10},{3,11},{4,12},{5,13},{6,14},{7,15},{8,0},{9,1},... | collective-permute-start | bytes 884744 | tf_op jit(solution)/shard_map/ppermute | solution.py:15
  61.7 1.2 %collective-permute-done.13 = f32[16,128]{1,0:T(8,128)S(1)} collective-permute-done((f32[16,128]{1,0:T(8,128)S(1)}, f32[16,128]{1,0:T(8,128)S(1)}, u32[]{:S(2)}, u32[]{:S(2)}) %collective-permute-start.13) | collective-permute-done | bytes 8224 | tf_op jit(solution)/shard_map/ppermute | solution.py:15
  62.9 1.4 %collective-permute-start.14 = (f32[16,128]{1,0:T(8,128)S(1)}, f32[16,128]{1,0:T(8,128)S(1)}, u32[]{:S(2)}, u32[]{:S(2)}) collective-permute-start(f32[16,128]{1,0:T(8,128)S(1)} %add.12), channel_id=1, source_target_pairs={{0,2},{1,3},{2,0},{3,1},{4,6},{5,7},{6,4},{7,5},{8,10},{9,11},{10,... | collective-permute-start | bytes 24584 | tf_op jit(solution)/shard_map/ppermute | solution.py:15
  64.3 2.3 %collective-permute-done.14 = f32[16,128]{1,0:T(8,128)S(1)} collective-permute-done((f32[16,128]{1,0:T(8,128)S(1)}, f32[16,128]{1,0:T(8,128)S(1)}, u32[]{:S(2)}, u32[]{:S(2)}) %collective-permute-start.14) | collective-permute-done | bytes 8224 | tf_op jit(solution)/shard_map/ppermute | solution.py:15
  66.6 2.0 %collective-permute-start.15 = (f32[16,128]{1,0:T(8,128)S(1)}, f32[16,128]{1,0:T(8,128)S(1)}, u32[]{:S(2)}, u32[]{:S(2)}) collective-permute-start(f32[16,128]{1,0:T(8,128)S(1)} %add.13), channel_id=1, source_target_pairs={{0,4},{1,5},{2,6},{3,7},{4,0},{5,1},{6,2},{7,3},{8,12},{9,13},{10,... | collective-permute-start | bytes 24584 | tf_op jit(solution)/shard_map/ppermute | solution.py:15
  68.6 3.7 %collective-permute-done.15 = f32[16,128]{1,0:T(8,128)S(1)} collective-permute-done((f32[16,128]{1,0:T(8,128)S(1)}, f32[16,128]{1,0:T(8,128)S(1)}, u32[]{:S(2)}, u32[]{:S(2)}) %collective-permute-start.15) | collective-permute-done | bytes 8224 | tf_op jit(solution)/shard_map/ppermute | solution.py:15
  72.3 3.6 %collective-permute-start.16 = (f32[16,128]{1,0:T(8,128)S(1)}, f32[16,128]{1,0:T(8,128)S(1)}, u32[]{:S(2)}, u32[]{:S(2)}) collective-permute-start(f32[16,128]{1,0:T(8,128)S(1)} %add.14), channel_id=1, source_target_pairs={{0,8},{1,9},{2,10},{3,11},{4,12},{5,13},{6,14},{7,15},{8,0},{9,1},... | collective-permute-start | bytes 24584 | tf_op jit(solution)/shard_map/ppermute | solution.py:15
  75.9 1.6 %collective-permute-done.16 = f32[16,128]{1,0:T(8,128)S(1)} collective-permute-done((f32[16,128]{1,0:T(8,128)S(1)}, f32[16,128]{1,0:T(8,128)S(1)}, u32[]{:S(2)}, u32[]{:S(2)}) %collective-permute-start.16) | collective-permute-done | bytes 8224 | tf_op jit(solution)/shard_map/ppermute | solution.py:15
  77.5 0.6 slice_reduce_fusion
  79.5 1.0 %shard_map.85 = bf16[128,1152]{1,0:T(8,128)(2,1)} custom-call(f32[128,1152]{1,0:T(8,128)S(1)} %copy-done.1, f32[128,128]{1,0:T(8,128)S(1)} %copy-done.9, f32[1,1]{1,0:T(1,128)} %bitcast.5.log_temp, f32[128,1152]{1,0:T(8,128)S(1)} %get-tuple-element.33.keep, bf16[128,1152]{1,0:T(8,128)(2,1)S(1)} %collective-permute-done.9.refs_0_, ...), custom_call_target="tpu_custom_call" | custom-call | tf_op jit(solution)/shard_map/pallas_call | solution.py:193
  80.4 0.1 copy-done
  80.5 1.0 %shard_map.87 = bf16[128,1152]{1,0:T(8,128)(2,1)} custom-call(f32[128,1152]{1,0:T(8,128)S(1)} %copy-done, f32[128,128]{1,0:T(8,128)S(1)} %copy-done.8, f32[1,1]{1,0:T(1,128)} %bitcast.6.log_temp, f32[128,1152]{1,0:T(8,128)S(1)} %get-tuple-element.41.keep, bf16[128,1152]{1,0:T(8,128)(2,1)S(1)} %collective-permute-done.11.refs_0_, ...), custom_call_target="tpu_custom_call" | custom-call | tf_op jit(solution)/shard_map/pallas_call | solution.py:193
  (52 shorter events, 0.1 us)
Async XLA Ops:
  0.6 17.8 %collective-permute-start.4 = (bf16[128,1152]{1,0:T(8,128)(2,1)}, bf16[128,1152]{1,0:T(8,128)(2,1)S(1)}, u32[]{:S(2)}, u32[]{:S(2)}) collective-permute-start(bf16[128,1152]{1,0:T(8,128)(2,1)} %value.3), channel_id=1, source_target_pairs={{0,8},{1,9},{2,10},{3,11},{4,12},{5,13},{6,14},{7,15},{8,0},{9,1},... | collective-permute-start | bytes 884744 | tf_op jit(solution)/shard_map/ppermute | solution.py:15
  4.7 16.2 %collective-permute-start.1 = (bf16[128,1152]{1,0:T(8,128)(2,1)}, bf16[128,1152]{1,0:T(8,128)(2,1)S(1)}, u32[]{:S(2)}, u32[]{:S(2)}) collective-permute-start(bf16[128,1152]{1,0:T(8,128)(2,1)} %value.2), channel_id=1, source_target_pairs={{0,2},{1,3},{2,0},{3,1},{4,6},{5,7},{6,4},{7,5},{8,10},{9,11},{10,... | collective-permute-start | bytes 884744 | tf_op jit(solution)/shard_map/ppermute | solution.py:15
  6.2 18.0 %collective-permute-start = (bf16[128,1152]{1,0:T(8,128)(2,1)}, bf16[128,1152]{1,0:T(8,128)(2,1)S(1)}, u32[]{:S(2)}, u32[]{:S(2)}) collective-permute-start(bf16[128,1152]{1,0:T(8,128)(2,1)} %value.2), channel_id=1, source_target_pairs={{0,4},{1,5},{2,6},{3,7},{4,0},{5,1},{6,2},{7,3},{8,12},{9,13},{10,... | collective-permute-start | bytes 884744 | tf_op jit(solution)/shard_map/ppermute | solution.py:15
  7.8 25.9 %collective-permute-start.5 = (bf16[128,1152]{1,0:T(8,128)(2,1)}, bf16[128,1152]{1,0:T(8,128)(2,1)S(1)}, u32[]{:S(2)}, u32[]{:S(2)}) collective-permute-start(bf16[128,1152]{1,0:T(8,128)(2,1)} %value.3), channel_id=1, source_target_pairs={{0,1},{1,0},{2,3},{3,2},{4,5},{5,4},{6,7},{7,6},{8,9},{9,8},{10,11... | collective-permute-start | bytes 884744 | tf_op jit(solution)/shard_map/ppermute | solution.py:15
  18.4 0.7 copy-start.21
  20.9 15.4 %collective-permute-start.6 = (bf16[128,1152]{1,0:T(8,128)(2,1)}, bf16[128,1152]{1,0:T(8,128)(2,1)S(1)}, u32[]{:S(2)}, u32[]{:S(2)}) collective-permute-start(bf16[128,1152]{1,0:T(8,128)(2,1)} %shard_map.79.refs_9_), channel_id=1, source_target_pairs={{0,1},{1,0},{2,3},{3,2},{4,5},{5,4},{6,7},{7,6},{8,9},{9,8},{10,11... | collective-permute-start | bytes 884744 | tf_op jit(solution)/shard_map/ppermute | solution.py:15
  20.9 0.7 copy-start.20
  23.4 12.9 %collective-permute-start.3 = (bf16[64,1152]{1,0:T(8,128)(2,1)}, bf16[64,1152]{1,0:T(8,128)(2,1)S(1)}, u32[]{:S(2)}, u32[]{:S(2)}) collective-permute-start(bf16[64,1152]{1,0:T(8,128)(2,1)} %get-tuple-element.31.refs_5_), channel_id=1, source_target_pairs={{0,4},{1,5},{2,6},{3,7},{4,0},{5,1},{6,2},{7,3},{8,12},{9,13},{10,... | collective-permute-start | bytes 442376 | tf_op jit(solution)/shard_map/ppermute | solution.py:15
  24.2 0.7 copy-start.19
  26.7 9.6 %collective-permute-start.2 = (bf16[64,1152]{1,0:T(8,128)(2,1)}, bf16[64,1152]{1,0:T(8,128)(2,1)S(1)}, u32[]{:S(2)}, u32[]{:S(2)}) collective-permute-start(bf16[64,1152]{1,0:T(8,128)(2,1)} %get-tuple-element.28.refs_2_), channel_id=1, source_target_pairs={{0,2},{1,3},{2,0},{3,1},{4,6},{5,7},{6,4},{7,5},{8,10},{9,11},{10,... | collective-permute-start | bytes 442376 | tf_op jit(solution)/shard_map/ppermute | solution.py:15
  29.5 6.8 %copy-start.13 = (bf16[64,1152]{1,0:T(8,128)(2,1)S(1)}, bf16[64,1152]{1,0:T(8,128)(2,1)}, u32[]{:S(2)}) copy-start(bf16[64,1152]{1,0:T(8,128)(2,1)} %get-tuple-element.28.refs_2_) | copy-start | bytes 442372
  29.5 6.8 %copy-start.14 = (bf16[64,1152]{1,0:T(8,128)(2,1)S(1)}, bf16[64,1152]{1,0:T(8,128)(2,1)}, u32[]{:S(2)}) copy-start(bf16[64,1152]{1,0:T(8,128)(2,1)} %get-tuple-element.29.refs_3_) | copy-start | bytes 442372
  31.6 4.7 %copy-start.11 = (bf16[64,1152]{1,0:T(8,128)(2,1)S(1)}, bf16[64,1152]{1,0:T(8,128)(2,1)}, u32[]{:S(2)}) copy-start(bf16[64,1152]{1,0:T(8,128)(2,1)} %get-tuple-element.30.refs_4_) | copy-start | bytes 442372
  31.6 4.7 %copy-start.12 = (bf16[64,1152]{1,0:T(8,128)(2,1)S(1)}, bf16[64,1152]{1,0:T(8,128)(2,1)}, u32[]{:S(2)}) copy-start(bf16[64,1152]{1,0:T(8,128)(2,1)} %get-tuple-element.31.refs_5_) | copy-start | bytes 442372
  33.7 2.6 %copy-start.6 = (bf16[128,1152]{1,0:T(8,128)(2,1)S(1)}, bf16[128,1152]{1,0:T(8,128)(2,1)}, u32[]{:S(2)}) copy-start(bf16[128,1152]{1,0:T(8,128)(2,1)} %shard_map.79.refs_9_) | copy-start | bytes 884740
  33.7 2.6 %copy-start.10 = (bf16[128,1152]{1,0:T(8,128)(2,1)S(1)}, bf16[128,1152]{1,0:T(8,128)(2,1)}, u32[]{:S(2)}) copy-start(bf16[128,1152]{1,0:T(8,128)(2,1)} %get-tuple-element.32.refs_8_) | copy-start | bytes 884740
  33.7 0.7 copy-start.18
  36.4 1.0 %copy-start.7 = (bf16[128,1152]{1,0:T(8,128)(2,1)S(1)}, bf16[128,1152]{1,0:T(8,128)(2,1)}, u32[]{:S(2)}) copy-start(bf16[128,1152]{1,0:T(8,128)(2,1)} %shard_map.80.refs_10_) | copy-start | bytes 884740
  37.3 0.9 %copy-start.15 = (bf16[64,1152]{1,0:T(8,128)(2,1)S(1)}, bf16[64,1152]{1,0:T(8,128)(2,1)}, u32[]{:S(2)}) copy-start(bf16[64,1152]{1,0:T(8,128)(2,1)} %get-tuple-element.26.refs_0_) | copy-start | bytes 442372
  38.2 0.9 %copy-start.16 = (bf16[64,1152]{1,0:T(8,128)(2,1)S(1)}, bf16[64,1152]{1,0:T(8,128)(2,1)}, u32[]{:S(2)}) copy-start(bf16[64,1152]{1,0:T(8,128)(2,1)} %get-tuple-element.27.refs_1_) | copy-start | bytes 442372
  41.7 0.8 copy-start.2
  42.5 0.8 %copy-start.3 = (f32[128,1152]{1,0:T(8,128)}, f32[128,1152]{1,0:T(8,128)S(1)}, u32[]{:S(2)}) copy-start(f32[128,1152]{1,0:T(8,128)S(1)} %get-tuple-element.35.keep) | copy-start | bytes 1769476
  43.4 0.7 copy-start.4
  44.1 0.7 copy-start.5
  44.8 1.6 %collective-permute-start.8 = (bf16[128,1152]{1,0:T(8,128)(2,1)S(1)}, bf16[128,1152]{1,0:T(8,128)(2,1)S(1)}, u32[]{:S(2)}, u32[]{:S(2)}) collective-permute-start(bf16[128,1152]{1,0:T(8,128)(2,1)S(1)} %get-tuple-element.38), channel_id=1, source_target_pairs={{0,1},{1,0},{2,3},{3,2},{4,5},{5,4},{6,7},{7,6},{8,9},{9,8},{10,11... | collective-permute-start | bytes 884744 | tf_op jit(solution)/shard_map/ppermute | solution.py:15
  44.8 9.4 %collective-permute-start.7 = (bf16[128,1152]{1,0:T(8,128)(2,1)S(1)}, bf16[128,1152]{1,0:T(8,128)(2,1)S(1)}, u32[]{:S(2)}, u32[]{:S(2)}) collective-permute-start(bf16[128,1152]{1,0:T(8,128)(2,1)S(1)} %get-tuple-element.36), channel_id=1, source_target_pairs={{0,2},{1,3},{2,0},{3,1},{4,6},{5,7},{6,4},{7,5},{8,10},{9,11},{10,... | collective-permute-start | bytes 884744 | tf_op jit(solution)/shard_map/ppermute | solution.py:15
  46.4 0.7 copy-start.23
  54.2 0.7 copy-start.22
  56.9 22.6 %copy-start.1 = (f32[128,1152]{1,0:T(8,128)S(1)}, f32[128,1152]{1,0:T(8,128)}, u32[]{:S(2)}) copy-start(f32[128,1152]{1,0:T(8,128)} %get-tuple-element.24.unit) | copy-start | bytes 1769476
  56.9 22.6 %collective-permute-start.9 = (bf16[128,1152]{1,0:T(8,128)(2,1)}, bf16[128,1152]{1,0:T(8,128)(2,1)S(1)}, u32[]{:S(2)}, u32[]{:S(2)}) collective-permute-start(bf16[128,1152]{1,0:T(8,128)(2,1)} %shard_map.84), channel_id=1, source_target_pairs={{0,2},{1,3},{2,0},{3,1},{4,6},{5,7},{6,4},{7,5},{8,10},{9,11},{10,... | collective-permute-start | bytes 884744 | tf_op jit(solution)/shard_map/ppermute | solution.py:15
  57.4 22.0 %collective-permute-start.10 = (bf16[128,1152]{1,0:T(8,128)(2,1)}, bf16[128,1152]{1,0:T(8,128)(2,1)S(1)}, u32[]{:S(2)}, u32[]{:S(2)}) collective-permute-start(bf16[128,1152]{1,0:T(8,128)(2,1)} %shard_map.83.refs_1_), channel_id=1, source_target_pairs={{0,4},{1,5},{2,6},{3,7},{4,0},{5,1},{6,2},{7,3},{8,12},{9,13},{10,... | collective-permute-start | bytes 884744 | tf_op jit(solution)/shard_map/ppermute | solution.py:15
  58.7 1.0 %copy-start.17 = (bf16[128,1152]{1,0:T(8,128)(2,1)S(1)}, bf16[128,1152]{1,0:T(8,128)(2,1)}, u32[]{:S(2)}) copy-start(bf16[128,1152]{1,0:T(8,128)(2,1)} %shard_map.82.refs_0_.refs_1_) | copy-start | bytes 884740
  58.7 20.8 %copy-start.9 = (f32[128,128]{1,0:T(8,128)S(1)}, f32[128,128]{1,0:T(8,128)}, u32[]{:S(2)}) copy-start(f32[128,128]{1,0:T(8,128)} %get-tuple-element.25.inverse) | copy-start | bytes 196612
  58.7 21.7 %collective-permute-start.11 = (bf16[128,1152]{1,0:T(8,128)(2,1)}, bf16[128,1152]{1,0:T(8,128)(2,1)S(1)}, u32[]{:S(2)}, u32[]{:S(2)}) collective-permute-start(bf16[128,1152]{1,0:T(8,128)(2,1)} %shard_map.86), channel_id=1, source_target_pairs={{0,1},{1,0},{2,3},{3,2},{4,5},{5,4},{6,7},{7,6},{8,9},{9,8},{10,11... | collective-permute-start | bytes 884744 | tf_op jit(solution)/shard_map/ppermute | solution.py:15
  59.7 20.8 %collective-permute-start.12 = (bf16[128,1152]{1,0:T(8,128)(2,1)S(1)}, bf16[128,1152]{1,0:T(8,128)(2,1)S(1)}, u32[]{:S(2)}, u32[]{:S(2)}) collective-permute-start(bf16[128,1152]{1,0:T(8,128)(2,1)S(1)} %copy-done.17), channel_id=1, source_target_pairs={{0,8},{1,9},{2,10},{3,11},{4,12},{5,13},{6,14},{7,15},{8,0},{9,1},... | collective-permute-start | bytes 884744 | tf_op jit(solution)/shard_map/ppermute | solution.py:15
  61.7 1.2 %collective-permute-start.13 = (f32[16,128]{1,0:T(8,128)S(1)}, f32[16,128]{1,0:T(8,128)S(1)}, u32[]{:S(2)}, u32[]{:S(2)}) collective-permute-start(f32[16,128]{1,0:T(8,128)S(1)} %get-tuple-element.43), channel_id=1, source_target_pairs={{0,1},{1,0},{2,3},{3,2},{4,5},{5,4},{6,7},{7,6},{8,9},{9,8},{10,11... | collective-permute-start | bytes 24584 | tf_op jit(solution)/shard_map/ppermute | solution.py:15
  62.9 3.7 %collective-permute-start.14 = (f32[16,128]{1,0:T(8,128)S(1)}, f32[16,128]{1,0:T(8,128)S(1)}, u32[]{:S(2)}, u32[]{:S(2)}) collective-permute-start(f32[16,128]{1,0:T(8,128)S(1)} %add.12), channel_id=1, source_target_pairs={{0,2},{1,3},{2,0},{3,1},{4,6},{5,7},{6,4},{7,5},{8,10},{9,11},{10,... | collective-permute-start | bytes 24584 | tf_op jit(solution)/shard_map/ppermute | solution.py:15
  66.6 5.8 %collective-permute-start.15 = (f32[16,128]{1,0:T(8,128)S(1)}, f32[16,128]{1,0:T(8,128)S(1)}, u32[]{:S(2)}, u32[]{:S(2)}) collective-permute-start(f32[16,128]{1,0:T(8,128)S(1)} %add.13), channel_id=1, source_target_pairs={{0,4},{1,5},{2,6},{3,7},{4,0},{5,1},{6,2},{7,3},{8,12},{9,13},{10,... | collective-permute-start | bytes 24584 | tf_op jit(solution)/shard_map/ppermute | solution.py:15
  72.3 5.2 %collective-permute-start.16 = (f32[16,128]{1,0:T(8,128)S(1)}, f32[16,128]{1,0:T(8,128)S(1)}, u32[]{:S(2)}, u32[]{:S(2)}) collective-permute-start(f32[16,128]{1,0:T(8,128)S(1)} %add.14), channel_id=1, source_target_pairs={{0,8},{1,9},{2,10},{3,11},{4,12},{5,13},{6,14},{7,15},{8,0},{9,1},... | collective-permute-start | bytes 24584 | tf_op jit(solution)/shard_map/ppermute | solution.py:15
  79.5 1.1 %copy-start = (f32[128,1152]{1,0:T(8,128)S(1)}, f32[128,1152]{1,0:T(8,128)}, u32[]{:S(2)}) copy-start(f32[128,1152]{1,0:T(8,128)} %get-tuple-element.39.unit) | copy-start | bytes 1769476
  79.5 1.1 %copy-start.8 = (f32[128,128]{1,0:T(8,128)S(1)}, f32[128,128]{1,0:T(8,128)}, u32[]{:S(2)}) copy-start(f32[128,128]{1,0:T(8,128)} %get-tuple-element.40.inverse) | copy-start | bytes 196612

commit v3 on v2

--- a/solution.py
+++ b/solution.py
@@ -7,7 +7,12 @@
 from jax.experimental.pallas import tpu as pltpu
 from jax.sharding import PartitionSpec as P
 
-VMEM_BYTES = 48 * 1024 * 1024
+TILE_VMEM = 32 * 1024 * 1024
+SMALL_VMEM = 4 * 1024 * 1024
+FINISH_COST = 100
+LANDED_COST = 100_000_000_000
+VMEM = pl.BlockSpec(memory_space=pltpu.VMEM)
+ANY = pl.BlockSpec(memory_space=pl.ANY)
 
 
 def swapped(x, bit):
@@ -15,13 +20,15 @@
     return lax.ppermute(x, "blk", [(i, i ^ bit) for i in range(count)])
 
 
-def after(value, *others):
+def after(value, *others, cost=0):
     return pl.pallas_call(
         lambda *refs: None,
         out_shape=jax.ShapeDtypeStruct(value.shape, value.dtype),
-        in_specs=[pl.BlockSpec(memory_space=pl.ANY)] * (1 + len(others)),
-        out_specs=pl.BlockSpec(memory_space=pl.ANY),
+        in_specs=[ANY] * (1 + len(others)),
+        out_specs=ANY,
         input_output_aliases={0: 0},
+        cost_estimate=pl.CostEstimate(flops=cost, bytes_accessed=0, transcendentals=0),
+        compiler_params=pltpu.CompilerParams(vmem_limit_bytes=SMALL_VMEM),
     )(value, *others)
 
 
@@ -39,54 +46,84 @@
     return total
 
 
-def own_kernel(value, unit, inverse, *pieces):
+def own_kernel(value, *refs):
+    unit, inverse = refs[-2:]
     scaled, inv = unit_rows(value[...])
     unit[...] = scaled
     inverse[...] = jnp.broadcast_to(inv, inverse.shape)
-    store_pieces(scaled, pieces)
-
-
-def other_kernel(value, *pieces):
-    store_pieces(unit_rows(value[...])[0], pieces)
-
-
-def store_pieces(values, pieces):
-    size = values.shape[0] // len(pieces)
-    for place, piece in enumerate(pieces):
-        piece[...] = values[place * size : (place + 1) * size].astype(jnp.bfloat16)
-
-
-def unit_call(value, count, own):
+
+
+def piece_kernel(count, value, *refs):
+    unit = unit_rows(value[...])[0].astype(jnp.bfloat16)
+    size = value.shape[0] // count
+    for place, piece in enumerate(refs[-count:]):
+        piece[...] = unit[place * size : (place + 1) * size]
+
+
+def unit_call(kernel, value, outs, others):
+    return pl.pallas_call(
+        kernel,
+        out_shape=outs,
+        in_specs=[VMEM] + [ANY] * len(others),
+        out_specs=[VMEM] * len(outs),
+        compiler_params=pltpu.CompilerParams(vmem_limit_bytes=SMALL_VMEM),
+        cost_estimate=pl.CostEstimate(
+            flops=4 * value.size, bytes_accessed=4 * value.size, transcendentals=value.shape[0]
+        ),
+    )(value, *others)
+
+
+def unit_pieces(value, count, others):
     rows, width = value.shape
     outs = [jax.ShapeDtypeStruct((rows // count, width), jnp.bfloat16)] * count
-    if own:
-        wide = jax.ShapeDtypeStruct((rows, width), jnp.float32)
-        outs = [wide, jax.ShapeDtypeStruct((rows, 128), jnp.float32)] + outs
-    return pl.pallas_call(
-        own_kernel if own else other_kernel,
-        out_shape=outs,
-        cost_estimate=pl.CostEstimate(
-            flops=4 * rows * width, bytes_accessed=4 * rows * width, transcendentals=rows
-        ),
-    )(value)
-
-
-def gathered(value, bits, count):
-    raw = [swapped(value, bit) for bit in bits]
-    unit, inverse, *own = unit_call(value, count, True)
-    blocks = {0: own}
-    for place in range(len(bits)):
-        blocks[1 << place] = unit_call(raw[place], count, False)
+    return unit_call(functools.partial(piece_kernel, count), value, outs, others)
+
+
+def unit_wide(value, others):
+    wide = jax.ShapeDtypeStruct(value.shape, jnp.float32)
+    inverse = jax.ShapeDtypeStruct((value.shape[0], 128), jnp.float32)
+    return unit_call(own_kernel, value, [wide, inverse], others)
+
+
+def piece_of(block, place, count):
+    if len(block) == count:
+        return block[place]
+    size = block[0].shape[0] // count
+    return block[0][place * size : (place + 1) * size]
+
+
+def forwarded(blocks, bits, count):
     for offset in range(1 << len(bits)):
         if offset not in blocks:
             high = 1 << (offset.bit_length() - 1)
             low = offset & -offset
             lasts = [high] + [low] * (count - 1)
             blocks[offset] = [
-                swapped(blocks[offset ^ last][place], bits[last.bit_length() - 1])
+                swapped(piece_of(blocks[offset ^ last], place, count), bits[last.bit_length() - 1])
                 for place, last in enumerate(lasts)
             ]
-    return unit, inverse, [blocks[offset] for offset in range(1 << len(bits))]
+    return [blocks[offset] for offset in range(1 << len(bits))]
+
+
+def gathered(image, text, img_bits, txt_bits):
+    img_raw = [swapped(image, bit) for bit in img_bits]
+    txt_raw = swapped(text, txt_bits[0])
+    imgs, txts = {}, {}
+    others = []
+    for place in reversed(range(1, len(img_bits))):
+        imgs[1 << place] = others = unit_pieces(img_raw[place], 2, others[:1])
+    txts[0] = unit_pieces(text, 1, others[:1])
+    imgs[0] = unit_pieces(image, 1, txts[0])
+    for place in range(1, len(txt_bits)):
+        txts[1 << place] = [swapped(txts[0][0], txt_bits[place])]
+    imgs[1] = unit_pieces(img_raw[0], 2, imgs[0])
+    txts[1] = unit_pieces(txt_raw, 1, imgs[1][:1])
+    imgs = forwarded(imgs, img_bits, 2)
+    txts = forwarded(txts, txt_bits, 1)
+    landed = after(imgs[-1][0], *imgs[-1][1:], cost=LANDED_COST)
+    imgs[-1][0] = landed
+    txts[-1][0] = after(txts[-1][0], landed)
+    return imgs, txts
 
 
 def tile_kernel(img_places, txt_places, rows, *refs):
@@ -165,14 +202,14 @@
             tile_kernel, [len(block) for block in imgs], [len(block) for block in txts], rows
         ),
         out_shape=outs(n_img) + outs(n_txt) + [jax.ShapeDtypeStruct((16, 128), jnp.float32)],
-        in_specs=[pl.BlockSpec(memory_space=pltpu.VMEM)] * (len(flat) + 2),
-        out_specs=[pl.BlockSpec(memory_space=pltpu.VMEM)] * (n_img + n_txt + 1),
+        in_specs=[VMEM] * (len(flat) + 2),
+        out_specs=[VMEM] * (n_img + n_txt + 1),
         scratch_shapes=[
             pltpu.VMEM((n_img * rows, width), jnp.bfloat16),
             pltpu.VMEM((n_txt * rows, width), jnp.bfloat16),
             pltpu.VMEM((n_img * rows, n_txt * rows), jnp.bfloat16),
         ],
-        compiler_params=pltpu.CompilerParams(vmem_limit_bytes=VMEM_BYTES),
+        compiler_params=pltpu.CompilerParams(vmem_limit_bytes=TILE_VMEM),
         cost_estimate=pl.CostEstimate(
             flops=6 * pairs * width, bytes_accessed=0, transcendentals=2 * pairs
         ),
@@ -180,39 +217,58 @@
     return results[:n_img], results[n_img:-1], results[-1]
 
 
-def finish_kernel(unit, inverse, log_temp, keep, *refs):
+def finish_kernel(count, *refs):
+    unit, inverse, log_temp, keep = refs[:4]
     total = keep[...]
-    for recv in refs[:-1]:
+    for recv in refs[4 : 4 + count]:
         total = total + recv[...].astype(jnp.float32)
     grad = jnp.exp(log_temp[...]) * total
     along = jnp.sum(unit[...] * grad, axis=1, keepdims=True)
-    refs[-1][...] = ((grad - unit[...] * along) * inverse[:, :1]).astype(jnp.bfloat16)
-
-
-def finish_call(unit, inverse, log_temp, keep, recvs):
+    out, token = refs[-2:]
+    out[...] = ((grad - unit[...] * along) * inverse[:, :1]).astype(jnp.bfloat16)
+    token[...] = jnp.zeros(token.shape, jnp.float32)
+
+
+def finish_call(unit, inverse, log_temp, keep, recvs, others):
     return pl.pallas_call(
-        finish_kernel,
-        out_shape=jax.ShapeDtypeStruct(keep.shape, jnp.bfloat16),
-        compiler_params=pltpu.CompilerParams(vmem_limit_bytes=VMEM_BYTES),
-    )(unit, inverse, log_temp, keep, *recvs)
-
-
-def add_kernel(keep, recv, *refs):
-    refs[-1][...] = (keep[...] + recv[...].astype(jnp.float32)).astype(refs[-1].dtype)
-
-
-def add_call(keep, recv, dtype, others):
-    rest = [pl.BlockSpec(memory_space=pl.ANY)] * len(others)
+        functools.partial(finish_kernel, len(recvs)),
+        out_shape=(
+            jax.ShapeDtypeStruct(keep.shape, jnp.bfloat16),
+            jax.ShapeDtypeStruct((8, 128), jnp.float32),
+        ),
+        in_specs=[VMEM] * (4 + len(recvs)) + [ANY] * len(others),
+        out_specs=[VMEM] * 2,
+        compiler_params=pltpu.CompilerParams(vmem_limit_bytes=SMALL_VMEM),
+        cost_estimate=pl.CostEstimate(
+            flops=FINISH_COST * keep.size, bytes_accessed=0, transcendentals=0
+        ),
+    )(unit, inverse, log_temp, keep, *recvs, *others)
+
+
+def add_kernel(keep, recv, sums, sums_recv, *refs):
+    refs[-2][...] = (keep[...] + recv[...].astype(jnp.float32)).astype(refs[-2].dtype)
+    refs[-1][...] = sums[...] + sums_recv[...]
+
+
+def add_call(keep, recv, dtype, sums, bit, others):
     return pl.pallas_call(
         add_kernel,
-        out_shape=jax.ShapeDtypeStruct(keep.shape, dtype),
-        in_specs=[pl.BlockSpec(memory_space=pltpu.VMEM)] * 2 + rest,
-        out_specs=pl.BlockSpec(memory_space=pltpu.VMEM),
-    )(keep, recv, *others)
-
-
-def returned(parts, bits, others):
+        out_shape=(
+            jax.ShapeDtypeStruct(keep.shape, dtype),
+            jax.ShapeDtypeStruct(sums.shape, sums.dtype),
+        ),
+        in_specs=[VMEM] * 4 + [ANY] * len(others),
+        out_specs=[VMEM] * 2,
+        compiler_params=pltpu.CompilerParams(vmem_limit_bytes=SMALL_VMEM),
+        cost_estimate=pl.CostEstimate(
+            flops=keep.size, bytes_accessed=keep.size, transcendentals=0
+        ),
+    )(keep, recv, sums, swapped(sums, bit), *others)
+
+
+def returned(parts, bits, sums, sum_bits, wait, others):
     parts = dict(enumerate(parts))
+    sum_bits = list(sum_bits)
     recvs = []
     for place in reversed(range(len(bits))):
         arrived = {}
@@ -221,13 +277,19 @@
             arrived[offset] = swapped(send, bits[place])
         for offset, recv in arrived.items():
             dtype = jnp.float32 if offset < 1 << place - 1 else jnp.bfloat16
-            parts[offset] = add_call(parts[offset], recv, dtype, others)
+            if sum_bits:
+                parts[offset], sums = add_call(
+                    parts[offset], recv, dtype, sums, sum_bits.pop(0), others
+                )
+            else:
+                parts[offset] = (parts[offset] + recv.astype(jnp.float32)).astype(dtype)
         send = parts.pop(1 << place).astype(jnp.bfloat16)
         if arrived:
-            send = after(send, *[parts[offset] for offset in arrived])
             others = [parts[max(arrived)]]
+            if wait:
+                send = after(send, *[parts[offset] for offset in arrived])
         recvs.append(swapped(send, bits[place]))
-    return parts[0], recvs, others
+    return parts[0], recvs, sums, sum_bits, others
 
 
 def shards(image_embeds, text_embeds, log_temp, bias):
@@ -239,15 +301,16 @@
     img_bits = all_bits[1:split][::-1]
     txt_bits = (all_bits[:1] + all_bits[split:])[::-1]
     temp_in = log_temp.reshape(1, 1)
-    unit_txt, inv_txt, txts = gathered(text_embeds, txt_bits, 1)
-    unit_img, inv_img, imgs = gathered(image_embeds, img_bits, 2)
+    imgs, txts = gathered(image_embeds, text_embeds, img_bits, txt_bits)
     img_parts, txt_parts, sums = tile_call(imgs, txts, temp_in, bias.reshape(1, 1))
-    txt_keep, txt_recvs, others = returned(txt_parts, txt_bits, [])
-    img_keep, img_recvs, others = returned(img_parts, img_bits, others)
-    for bit in all_bits:
+    unit_img, inv_img = unit_wide(image_embeds, [sums])
+    unit_txt, inv_txt = unit_wide(text_embeds, [sums])
+    txt_keep, txt_recvs, sums, left, others = returned(txt_parts, txt_bits, sums, all_bits, False, [])
+    img_keep, img_recvs, sums, left, others = returned(img_parts, img_bits, sums, left, True, others)
+    for bit in left:
         sums = sums + swapped(sums, bit)
-    grad_text = finish_call(unit_txt, inv_txt, temp_in, txt_keep, txt_recvs)
-    grad_image = finish_call(unit_img, inv_img, temp_in, img_keep, img_recvs)
+    grad_text, done = finish_call(unit_txt, inv_txt, temp_in, txt_keep, txt_recvs, [])
+    grad_image, done = finish_call(unit_img, inv_img, temp_in, img_keep, img_recvs, [done])
     pairs = float(rows * count) * float(rows * count)
     grad_bias = jnp.reshape(jnp.sum(sums[:8]) / pairs, (1,))
     grad_temp = jnp.reshape(jnp.sum(sums[8:]) / pairs, (1,))

time: 84.2 us -> 66.8 us (0.79)
  Pallas kernels: 19.8 us -> 8.36 us
  local copies, waits for them, and re-layouts: 11.2 us -> 2.89 us
  waiting for transfers between devices: 25.6 us -> 31.2 us
  starting transfers between devices: 20.9 us -> 17.9 us
    pallas_call x10 -> x11, Pallas kernels: 17.2 us -> 5.08 us  [the longest x2 3.95 us: finish_call(): pl.pallas_call(functools.partial(finish_kernel, len(recvs)), out_shape=(j...]
    unnamed x48 -> x12, local copies, waits for them, and re-layouts: 11.2 us -> 2.89 us
    ppermute x17, waiting for transfers between devices: 25.6 us -> 31.2 us  [swapped(): return lax.ppermute(x, 'blk', [(i, i ^ bit) for i in range(count)])]
    ppermute x17, starting transfers between devices: 20.9 us -> 17.9 us  [swapped(): return lax.ppermute(x, 'blk', [(i, i ^ bit) for i in range(count)])]
  transfers between devices with their start and end apart: 17 -> 17, of which waited for: 7 -> 8; matrix products, arithmetic and copies ran while one was open for 1% -> 1% of each run, Pallas kernels for 17% -> 5%
where the time goes in v3:
time: 66.8 us; the launch traced here: 66.6 us
  waiting for transfers between devices  31.2 us (47%)
  starting transfers between devices  17.9 us (27%)
  Pallas kernels  8.36 us (13%)
  between operations  5.62 us (8%)
  local copies, waits for them, and re-layouts  2.89 us (4%)
    ppermute x17, waiting for transfers between devices, swapped(): return lax.ppermute(x, 'blk', [(i, i ^ bit) for i in range(count)])  31.2 us
    ppermute x17, starting transfers between devices, swapped(): return lax.ppermute(x, 'blk', [(i, i ^ bit) for i in range(count)])  17.9 us
    pallas_call x2, Pallas kernels, finish_call(): pl.pallas_call(functools.partial(finish_kernel, len(recvs)), out_shape=(j...  3.95 us
    pallas_call x1, Pallas kernels, tile_call(): pl.pallas_call(functools.partial(tile_kernel, [len(block) for block in im...  3.27 us
    unnamed x12, local copies, waits for them, and re-layouts  2.89 us
  transfers between devices with their start and end apart: 17, of which 8 were waited for; matrix products, arithmetic and copies ran while one was open for 1% of the time, Pallas kernels for 5%

profile of v3, /device:TPU:0, one launch (start us, length us, event | category | flops | bytes accessed | tf_op | source)
XLA Modules:
  0.0 66.6 jit_solution(13024076324283378663)
XLA Ops:
  0.6 3.0 %collective-permute-start = (bf16[128,1152]{1,0:T(8,128)(2,1)}, bf16[128,1152]{1,0:T(8,128)(2,1)S(1)}, u32[]{:S(2)}, u32[]{:S(2)}) collective-permute-start(bf16[128,1152]{1,0:T(8,128)(2,1)} %value.6), channel_id=1, source_target_pairs={{0,2},{1,3},{2,0},{3,1},{4,6},{5,7},{6,4},{7,5},{8,10},{9,11},{10,... | collective-permute-start | bytes 884744 | tf_op jit(solution)/shard_map/ppermute | solution.py:20
  3.6 1.6 %collective-permute-start.1 = (bf16[128,1152]{1,0:T(8,128)(2,1)}, bf16[128,1152]{1,0:T(8,128)(2,1)S(1)}, u32[]{:S(2)}, u32[]{:S(2)}) collective-permute-start(bf16[128,1152]{1,0:T(8,128)(2,1)} %value.6), channel_id=1, source_target_pairs={{0,4},{1,5},{2,6},{3,7},{4,0},{5,1},{6,2},{7,3},{8,12},{9,13},{10,... | collective-permute-start | bytes 884744 | tf_op jit(solution)/shard_map/ppermute | solution.py:20
  5.2 2.6 %collective-permute-start.4 = (bf16[128,1152]{1,0:T(8,128)(2,1)}, bf16[128,1152]{1,0:T(8,128)(2,1)S(1)}, u32[]{:S(2)}, u32[]{:S(2)}) collective-permute-start(bf16[128,1152]{1,0:T(8,128)(2,1)} %value.7), channel_id=1, source_target_pairs={{0,8},{1,9},{2,10},{3,11},{4,12},{5,13},{6,14},{7,15},{8,0},{9,1},... | collective-permute-start | bytes 884744 | tf_op jit(solution)/shard_map/ppermute | solution.py:20
  7.8 3.1 %collective-permute-done.value = bf16[128,1152]{1,0:T(8,128)(2,1)S(1)} collective-permute-done((bf16[128,1152]{1,0:T(8,128)(2,1)}, bf16[128,1152]{1,0:T(8,128)(2,1)S(1)}, u32[]{:S(2)}, u32[]{:S(2)}) %collective-permute-start) | collective-permute-done | bytes 294944 | tf_op jit(solution)/shard_map/ppermute | solution.py:20
  10.9 0.1 shard_map.75
  11.0 1.9 %collective-permute-start.3 = (bf16[64,1152]{1,0:T(8,128)(2,1)S(1)}, bf16[64,1152]{1,0:T(8,128)(2,1)S(1)}, u32[]{:S(2)}, u32[]{:S(2)}) collective-permute-start(bf16[64,1152]{1,0:T(8,128)(2,1)S(1)} %get-tuple-element.31.refs_4_), channel_id=1, source_target_pairs={{0,4},{1,5},{2,6},{3,7},{4,0},{5,1},{6,2},{7,3},{8,12},{9,13},{10,... | collective-permute-start | bytes 442376 | tf_op jit(solution)/shard_map/ppermute | solution.py:20
  12.9 0.1 shard_map.76.refs_0_.refs_7_
  13.1 0.8 %copy-done = bf16[128,1152]{1,0:T(8,128)(2,1)S(1)} copy-done((bf16[128,1152]{1,0:T(8,128)(2,1)S(1)}, bf16[128,1152]{1,0:T(8,128)(2,1)}, u32[]{:S(2)}) %copy-start) | copy-done | bytes 294936
  13.9 0.1 shard_map.77.refs_0_
  14.0 6.1 %collective-permute-done.1.value = bf16[128,1152]{1,0:T(8,128)(2,1)S(1)} collective-permute-done((bf16[128,1152]{1,0:T(8,128)(2,1)}, bf16[128,1152]{1,0:T(8,128)(2,1)S(1)}, u32[]{:S(2)}, u32[]{:S(2)}) %collective-permute-start.1) | collective-permute-done | bytes 294944 | tf_op jit(solution)/shard_map/ppermute | solution.py:20
  20.1 0.1 shard_map.78
  20.3 0.1 collective-permute-start.2
  21.7 0.1 collective-permute-start.5
  21.8 0.0 collective-permute-done.4.value
  21.8 0.1 shard_map.80.refs_8_
  21.9 0.6 collective-permute-start.6
  22.5 0.0 collective-permute-done.3.refs_1_.refs_6_
  22.5 3.0 %collective-permute-done.2.refs_0_ = bf16[64,1152]{1,0:T(8,128)(2,1)S(1)} collective-permute-done((bf16[64,1152]{1,0:T(8,128)(2,1)S(1)}, bf16[64,1152]{1,0:T(8,128)(2,1)S(1)}, u32[]{:S(2)}, u32[]{:S(2)}) %collective-permute-start.2) | collective-permute-done | bytes 147488 | tf_op jit(solution)/shard_map/ppermute | solution.py:20
  25.5 0.0 collective-permute-done.6.refs_0_
  25.5 0.0 collective-permute-done.5.refs_9_
  25.5 3.3 %shard_map.82 = (f32[128,1152]{1,0:T(8,128)S(1)}, f32[128,1152]{1,0:T(8,128)S(1)}, bf16[128,1152]{1,0:T(8,128)(2,1)S(1)}, bf16[128,1152]{1,0:T(8,128)(2,1)S(1)},...) custom-call(bf16[128,1152]{1,0:T(8,128)(2,1)S(1)} %shard_map.77.refs, ...), custom_call_target="tpu_custom_call" | custom-call | flops 1811939328 | tf_op jit(solution)/shard_map/pallas_call | solution.py:200
  28.8 0.5 collective-permute-start.7
  29.3 1.2 %collective-permute-done.9.sums_recv = f32[16,128]{1,0:T(8,128)S(1)} collective-permute-done((f32[16,128]{1,0:T(8,128)S(1)}, f32[16,128]{1,0:T(8,128)S(1)}, u32[]{:S(2)}, u32[]{:S(2)}) %collective-permute-start.9) | collective-permute-done | bytes 8224 | tf_op jit(solution)/shard_map/ppermute | solution.py:20
  30.5 0.1 shard_map.84
  30.5 1.5 %collective-permute-start.10 = (f32[16,128]{1,0:T(8,128)S(1)}, f32[16,128]{1,0:T(8,128)S(1)}, u32[]{:S(2)}, u32[]{:S(2)}) collective-permute-start(f32[16,128]{1,0:T(8,128)S(1)} %get-tuple-element.41.sums), channel_id=1, source_target_pairs={{0,2},{1,3},{2,0},{3,1},{4,6},{5,7},{6,4},{7,5},{8,10},{9,11},{10,... | collective-permute-start | bytes 24584 | tf_op jit(solution)/shard_map/ppermute | solution.py:20
  32.1 1.3 %collective-permute-start.14 = (bf16[128,1152]{1,0:T(8,128)(2,1)S(1)}, bf16[128,1152]{1,0:T(8,128)(2,1)}, u32[]{:S(2)}, u32[]{:S(2)}) collective-permute-start(bf16[128,1152]{1,0:T(8,128)(2,1)S(1)} %get-tuple-element.42.refs_0_), channel_id=1, source_target_pairs={{0,8},{1,9},{2,10},{3,11},{4,12},{5,13},{6,14},{7,15},{8,0},{9,1},... | collective-permute-start | bytes 884744 | tf_op jit(solution)/shard_map/ppermute | solution.py:20
  33.4 4.9 %collective-permute-done.7.recv = bf16[128,1152]{1,0:T(8,128)(2,1)S(1)} collective-permute-done((bf16[128,1152]{1,0:T(8,128)(2,1)S(1)}, bf16[128,1152]{1,0:T(8,128)(2,1)S(1)}, u32[]{:S(2)}, u32[]{:S(2)}) %collective-permute-start.7) | collective-permute-done | bytes 294944 | tf_op jit(solution)/shard_map/ppermute | solution.py:20
  38.3 0.1 collective-permute-done.10.sums_recv
  38.4 0.1 shard_map.85
  38.4 0.3 collective-permute-start.11
  38.8 0.0 collective-permute-start.12
  38.8 2.0 %collective-permute-start.15 = (f32[16,128]{1,0:T(8,128)S(1)}, f32[16,128]{1,0:T(8,128)S(1)}, u32[]{:S(2)}, u32[]{:S(2)}) collective-permute-start(f32[16,128]{1,0:T(8,128)S(1)} %get-tuple-element.51), channel_id=1, source_target_pairs={{0,4},{1,5},{2,6},{3,7},{4,0},{5,1},{6,2},{7,3},{8,12},{9,13},{10,... | collective-permute-start | bytes 24584 | tf_op jit(solution)/shard_map/ppermute | solution.py:20
  40.8 12.2 %collective-permute-done.15 = f32[16,128]{1,0:T(8,128)S(1)} collective-permute-done((f32[16,128]{1,0:T(8,128)S(1)}, f32[16,128]{1,0:T(8,128)S(1)}, u32[]{:S(2)}, u32[]{:S(2)}) %collective-permute-start.15) | collective-permute-done | bytes 8224 | tf_op jit(solution)/shard_map/ppermute | solution.py:20
  53.0 2.2 %collective-permute-start.16 = (f32[16,128]{1,0:T(8,128)S(1)}, f32[16,128]{1,0:T(8,128)S(1)}, u32[]{:S(2)}, u32[]{:S(2)}) collective-permute-start(f32[16,128]{1,0:T(8,128)S(1)} %add.6), channel_id=1, source_target_pairs={{0,8},{1,9},{2,10},{3,11},{4,12},{5,13},{6,14},{7,15},{8,0},{9,1},... | collective-permute-start | bytes 24584 | tf_op jit(solution)/shard_map/ppermute | solution.py:20
  55.3 0.1 shard_map.87
  55.4 0.0 copy-start.4
  55.4 0.6 copy-done.4
  56.0 0.1 shard_map.83
  56.2 0.6 copy-done.2
  56.8 0.8 %collective-permute-done.16 = f32[16,128]{1,0:T(8,128)S(1)} collective-permute-done((f32[16,128]{1,0:T(8,128)S(1)}, f32[16,128]{1,0:T(8,128)S(1)}, u32[]{:S(2)}, u32[]{:S(2)}) %collective-permute-start.16) | collective-permute-done | bytes 8224 | tf_op jit(solution)/shard_map/ppermute | solution.py:20
  57.6 0.6 slice_reduce_fusion
  59.5 0.0 collective-permute-done.13.refs_4_
  59.5 0.0 copy-start.5
  59.5 0.8 %copy-done.5 = f32[128,128]{1,0:T(8,128)S(1)} copy-done((f32[128,128]{1,0:T(8,128)S(1)}, f32[128,128]{1,0:T(8,128)}, u32[]{:S(2)}) %copy-start.5) | copy-done | bytes 65560
  60.3 1.9 %shard_map.88 = (bf16[128,1152]{1,0:T(8,128)(2,1)}, f32[8,128]{1,0:T(8,128)S(1)}) custom-call(f32[128,1152]{1,0:T(8,128)S(1)} %get-tuple-element.44.refs_0_, f32[128,128]{1,0:T(8,128)S(1)} %copy-done.5, f32[1,1]{1,0:T(1,128)} %bitcast.5.refs_2_, f32[128,1152]{1,0:T(8,128)S(1)} %get-tuple-element.46.refs_3_, ...), custom_call_target="tpu_custom_call" | custom-call | flops 14745600 | tf_op jit(solution)/shard_map/pallas_call | solution.py:233
  62.3 0.0 collective-permute-done.11.refs_4_
  62.3 0.0 collective-permute-done.12.refs_5_
  62.3 2.0 %shard_map.89 = (bf16[128,1152]{1,0:T(8,128)(2,1)}, f32[8,128]{1,0:T(8,128)}) custom-call(f32[128,1152]{1,0:T(8,128)S(1)} %get-tuple-element.33.refs_0_, f32[128,128]{1,0:T(8,128)S(1)} %copy-done.3, f32[1,1]{1,0:T(1,128)} %bitcast.6.refs_2_, f32[128,1152]{1,0:T(8,128)S(1)} %get-tuple-element.35.refs_3_, bf16[128,1152]{1,0:T(8,128)(2,1)} %collective-permute-done.11.refs_4_, ...), custom_call_target="tpu_custom_call" | custom-call | flops 14745600 | tf_op jit(solution)/shard_map/pallas_call | solution.py:233
  (16 shorter events, 0.0 us)
Async XLA Ops:
  0.6 12.3 %copy-start.1 = (bf16[128,1152]{1,0:T(8,128)(2,1)S(1)}, bf16[128,1152]{1,0:T(8,128)(2,1)}, u32[]{:S(2)}) copy-start(bf16[128,1152]{1,0:T(8,128)(2,1)} %value.7) | copy-start | bytes 884740
  0.6 10.2 %collective-permute-start = (bf16[128,1152]{1,0:T(8,128)(2,1)}, bf16[128,1152]{1,0:T(8,128)(2,1)S(1)}, u32[]{:S(2)}, u32[]{:S(2)}) collective-permute-start(bf16[128,1152]{1,0:T(8,128)(2,1)} %value.6), channel_id=1, source_target_pairs={{0,2},{1,3},{2,0},{3,1},{4,6},{5,7},{6,4},{7,5},{8,10},{9,11},{10,... | collective-permute-start | bytes 884744 | tf_op jit(solution)/shard_map/ppermute | solution.py:20
  3.6 16.5 %collective-permute-start.1 = (bf16[128,1152]{1,0:T(8,128)(2,1)}, bf16[128,1152]{1,0:T(8,128)(2,1)S(1)}, u32[]{:S(2)}, u32[]{:S(2)}) collective-permute-start(bf16[128,1152]{1,0:T(8,128)(2,1)} %value.6), channel_id=1, source_target_pairs={{0,4},{1,5},{2,6},{3,7},{4,0},{5,1},{6,2},{7,3},{8,12},{9,13},{10,... | collective-permute-start | bytes 884744 | tf_op jit(solution)/shard_map/ppermute | solution.py:20
  5.2 16.6 %collective-permute-start.4 = (bf16[128,1152]{1,0:T(8,128)(2,1)}, bf16[128,1152]{1,0:T(8,128)(2,1)S(1)}, u32[]{:S(2)}, u32[]{:S(2)}) collective-permute-start(bf16[128,1152]{1,0:T(8,128)(2,1)} %value.7), channel_id=1, source_target_pairs={{0,8},{1,9},{2,10},{3,11},{4,12},{5,13},{6,14},{7,15},{8,0},{9,1},... | collective-permute-start | bytes 884744 | tf_op jit(solution)/shard_map/ppermute | solution.py:20
  11.0 11.5 %collective-permute-start.3 = (bf16[64,1152]{1,0:T(8,128)(2,1)S(1)}, bf16[64,1152]{1,0:T(8,128)(2,1)S(1)}, u32[]{:S(2)}, u32[]{:S(2)}) collective-permute-start(bf16[64,1152]{1,0:T(8,128)(2,1)S(1)} %get-tuple-element.31.refs_4_), channel_id=1, source_target_pairs={{0,4},{1,5},{2,6},{3,7},{4,0},{5,1},{6,2},{7,3},{8,12},{9,13},{10,... | collective-permute-start | bytes 442376 | tf_op jit(solution)/shard_map/ppermute | solution.py:20
  12.9 1.0 %copy-start = (bf16[128,1152]{1,0:T(8,128)(2,1)S(1)}, bf16[128,1152]{1,0:T(8,128)(2,1)}, u32[]{:S(2)}) copy-start(bf16[128,1152]{1,0:T(8,128)(2,1)} %value.6) | copy-start | bytes 884740
  20.3 5.2 %collective-permute-start.2 = (bf16[64,1152]{1,0:T(8,128)(2,1)S(1)}, bf16[64,1152]{1,0:T(8,128)(2,1)S(1)}, u32[]{:S(2)}, u32[]{:S(2)}) collective-permute-start(bf16[64,1152]{1,0:T(8,128)(2,1)S(1)} %get-tuple-element.29.refs_0_.refs_1_), channel_id=1, source_target_pairs={{0,2},{1,3},{2,0},{3,1},{4,6},{5,7},{6,4},{7,5},{8,10},{9,11},{10,... | collective-permute-start | bytes 442376 | tf_op jit(solution)/shard_map/ppermute | solution.py:20
  21.7 3.8 %collective-permute-start.5 = (bf16[128,1152]{1,0:T(8,128)(2,1)S(1)}, bf16[128,1152]{1,0:T(8,128)(2,1)S(1)}, u32[]{:S(2)}, u32[]{:S(2)}) collective-permute-start(bf16[128,1152]{1,0:T(8,128)(2,1)S(1)} %shard_map.76.refs_0_.refs_7_), channel_id=1, source_target_pairs={{0,1},{1,0},{2,3},{3,2},{4,5},{5,4},{6,7},{7,6},{8,9},{9,8},{10,11... | collective-permute-start | bytes 884744 | tf_op jit(solution)/shard_map/ppermute | solution.py:20
  21.9 3.5 %collective-permute-start.6 = (bf16[128,1152]{1,0:T(8,128)(2,1)S(1)}, bf16[128,1152]{1,0:T(8,128)(2,1)S(1)}, u32[]{:S(2)}, u32[]{:S(2)}) collective-permute-start(bf16[128,1152]{1,0:T(8,128)(2,1)S(1)} %shard_map.80.refs_8_), channel_id=1, source_target_pairs={{0,1},{1,0},{2,3},{3,2},{4,5},{5,4},{6,7},{7,6},{8,9},{9,8},{10,11... | collective-permute-start | bytes 884744 | tf_op jit(solution)/shard_map/ppermute | solution.py:20
  28.8 1.7 %collective-permute-start.8 = (bf16[128,1152]{1,0:T(8,128)(2,1)S(1)}, bf16[128,1152]{1,0:T(8,128)(2,1)S(1)}, u32[]{:S(2)}, u32[]{:S(2)}) collective-permute-start(bf16[128,1152]{1,0:T(8,128)(2,1)S(1)} %get-tuple-element.40), channel_id=1, source_target_pairs={{0,1},{1,0},{2,3},{3,2},{4,5},{5,4},{6,7},{7,6},{8,9},{9,8},{10,11... | collective-permute-start | bytes 884744 | tf_op jit(solution)/shard_map/ppermute | solution.py:20
  28.8 9.5 %collective-permute-start.7 = (bf16[128,1152]{1,0:T(8,128)(2,1)S(1)}, bf16[128,1152]{1,0:T(8,128)(2,1)S(1)}, u32[]{:S(2)}, u32[]{:S(2)}) collective-permute-start(bf16[128,1152]{1,0:T(8,128)(2,1)S(1)} %get-tuple-element.38), channel_id=1, source_target_pairs={{0,2},{1,3},{2,0},{3,1},{4,6},{5,7},{6,4},{7,5},{8,10},{9,11},{10,... | collective-permute-start | bytes 884744 | tf_op jit(solution)/shard_map/ppermute | solution.py:20
  29.3 1.2 %collective-permute-start.9 = (f32[16,128]{1,0:T(8,128)S(1)}, f32[16,128]{1,0:T(8,128)S(1)}, u32[]{:S(2)}, u32[]{:S(2)}) collective-permute-start(f32[16,128]{1,0:T(8,128)S(1)} %get-tuple-element.32.refs_0_.sums), channel_id=1, source_target_pairs={{0,1},{1,0},{2,3},{3,2},{4,5},{5,4},{6,7},{7,6},{8,9},{9,8},{10,11... | collective-permute-start | bytes 24584 | tf_op jit(solution)/shard_map/ppermute | solution.py:20
  30.5 7.8 %collective-permute-start.10 = (f32[16,128]{1,0:T(8,128)S(1)}, f32[16,128]{1,0:T(8,128)S(1)}, u32[]{:S(2)}, u32[]{:S(2)}) collective-permute-start(f32[16,128]{1,0:T(8,128)S(1)} %get-tuple-element.41.sums), channel_id=1, source_target_pairs={{0,2},{1,3},{2,0},{3,1},{4,6},{5,7},{6,4},{7,5},{8,10},{9,11},{10,... | collective-permute-start | bytes 24584 | tf_op jit(solution)/shard_map/ppermute | solution.py:20
  32.1 27.4 %collective-permute-start.13 = (bf16[128,1152]{1,0:T(8,128)(2,1)}, bf16[128,1152]{1,0:T(8,128)(2,1)S(1)}, u32[]{:S(2)}, u32[]{:S(2)}) collective-permute-start(bf16[128,1152]{1,0:T(8,128)(2,1)} %get-tuple-element.47), channel_id=1, source_target_pairs={{0,1},{1,0},{2,3},{3,2},{4,5},{5,4},{6,7},{7,6},{8,9},{9,8},{10,11... | collective-permute-start | bytes 884744 | tf_op jit(solution)/shard_map/ppermute | solution.py:20
  32.1 27.4 %collective-permute-start.14 = (bf16[128,1152]{1,0:T(8,128)(2,1)S(1)}, bf16[128,1152]{1,0:T(8,128)(2,1)}, u32[]{:S(2)}, u32[]{:S(2)}) collective-permute-start(bf16[128,1152]{1,0:T(8,128)(2,1)S(1)} %get-tuple-element.42.refs_0_), channel_id=1, source_target_pairs={{0,8},{1,9},{2,10},{3,11},{4,12},{5,13},{6,14},{7,15},{8,0},{9,1},... | collective-permute-start | bytes 884744 | tf_op jit(solution)/shard_map/ppermute | solution.py:20
  38.4 23.9 %collective-permute-start.11 = (bf16[128,1152]{1,0:T(8,128)(2,1)S(1)}, bf16[128,1152]{1,0:T(8,128)(2,1)}, u32[]{:S(2)}, u32[]{:S(2)}) collective-permute-start(bf16[128,1152]{1,0:T(8,128)(2,1)S(1)} %shard_map.86), channel_id=1, source_target_pairs={{0,2},{1,3},{2,0},{3,1},{4,6},{5,7},{6,4},{7,5},{8,10},{9,11},{10,... | collective-permute-start | bytes 884744 | tf_op jit(solution)/shard_map/ppermute | solution.py:20
  38.8 23.5 %collective-permute-start.12 = (bf16[128,1152]{1,0:T(8,128)(2,1)S(1)}, bf16[128,1152]{1,0:T(8,128)(2,1)}, u32[]{:S(2)}, u32[]{:S(2)}) collective-permute-start(bf16[128,1152]{1,0:T(8,128)(2,1)S(1)} %get-tuple-element.43.refs_1_), channel_id=1, source_target_pairs={{0,4},{1,5},{2,6},{3,7},{4,0},{5,1},{6,2},{7,3},{8,12},{9,13},{10,... | collective-permute-start | bytes 884744 | tf_op jit(solution)/shard_map/ppermute | solution.py:20
  38.8 14.2 %collective-permute-start.15 = (f32[16,128]{1,0:T(8,128)S(1)}, f32[16,128]{1,0:T(8,128)S(1)}, u32[]{:S(2)}, u32[]{:S(2)}) collective-permute-start(f32[16,128]{1,0:T(8,128)S(1)} %get-tuple-element.51), channel_id=1, source_target_pairs={{0,4},{1,5},{2,6},{3,7},{4,0},{5,1},{6,2},{7,3},{8,12},{9,13},{10,... | collective-permute-start | bytes 24584 | tf_op jit(solution)/shard_map/ppermute | solution.py:20
  53.0 4.5 %collective-permute-start.16 = (f32[16,128]{1,0:T(8,128)S(1)}, f32[16,128]{1,0:T(8,128)S(1)}, u32[]{:S(2)}, u32[]{:S(2)}) collective-permute-start(f32[16,128]{1,0:T(8,128)S(1)} %add.6), channel_id=1, source_target_pairs={{0,8},{1,9},{2,10},{3,11},{4,12},{5,13},{6,14},{7,15},{8,0},{9,1},... | collective-permute-start | bytes 24584 | tf_op jit(solution)/shard_map/ppermute | solution.py:20
  55.4 0.6 copy-start.4
  56.2 0.6 copy-start.2
  59.5 0.8 %copy-start.5 = (f32[128,128]{1,0:T(8,128)S(1)}, f32[128,128]{1,0:T(8,128)}, u32[]{:S(2)}) copy-start(f32[128,128]{1,0:T(8,128)} %copy-done.4) | copy-start | bytes 196612
  60.3 2.0 %copy-start.3 = (f32[128,128]{1,0:T(8,128)S(1)}, f32[128,128]{1,0:T(8,128)}, u32[]{:S(2)}) copy-start(f32[128,128]{1,0:T(8,128)} %copy-done.2) | copy-start | bytes 196612

commit v4 on v3

v4 whole, which is shorter than its diff:
```python
import functools

import jax
import jax.numpy as jnp
from jax import lax
from jax.experimental import pallas as pl
from jax.experimental.pallas import tpu as pltpu
from jax.sharding import PartitionSpec as P

TILE_VMEM = 32 * 1024 * 1024
SMALL_VMEM = 4 * 1024 * 1024
GATHER_COST = 4_000_000_000
RETURN_COST = 2_000_000_000
VMEM = pl.BlockSpec(memory_space=pltpu.VMEM)
ANY = pl.BlockSpec(memory_space=pl.ANY)


def swapped(x, bit):
    count = lax.axis_size("blk")
    return lax.ppermute(x, "blk", [(i, i ^ bit) for i in range(count)])


def after(value, *others, cost=0):
    return pl.pallas_call(
        lambda *refs: None,
        out_shape=jax.ShapeDtypeStruct(value.shape, value.dtype),
        in_specs=[ANY] * (1 + len(others)),
        out_specs=ANY,
        input_output_aliases={0: 0},
        cost_estimate=pl.CostEstimate(flops=cost, bytes_accessed=0, transcendentals=0),
        compiler_params=pltpu.CompilerParams(vmem_limit_bytes=SMALL_VMEM),
    )(value, *others)


def unit_rows(values):
    wide = values.astype(jnp.float32)
    inverse = lax.rsqrt(jnp.sum(wide * wide, axis=1, keepdims=True) + 1e-06)
    return (wide * inverse, inverse)


def lane_sums(values):
    rows = jnp.sum(values.reshape(values.shape[0] // 8, 8, values.shape[1]), axis=0)
    total = rows[:, :128]
    for start in range(128, values.shape[1], 128):
        total = total + rows[:, start : start + 128]
    return total


def piece_kernel(count, value, *refs):
    unit = unit_rows(value[...])[0].astype(jnp.bfloat16)
    size = value.shape[0] // count
    for place, piece in enumerate(refs[-count:]):
        piece[...] = unit[place * size : (place + 1) * size]


def unit_call(kernel, value, outs, others):
    return pl.pallas_call(
        kernel,
        out_shape=outs,
        in_specs=[VMEM] + [ANY] * len(others),
        out_specs=[VMEM] * len(outs),
        compiler_params=pltpu.CompilerParams(vmem_limit_bytes=SMALL_VMEM),
        cost_estimate=pl.CostEstimate(
            flops=4 * value.size, bytes_accessed=4 * value.size, transcendentals=value.shape[0]
        ),
    )(value, *others)


def unit_pieces(value, count, others):
    rows, width = value.shape
    outs = [jax.ShapeDtypeStruct((rows // count, width), jnp.bfloat16)] * count
    return unit_call(functools.partial(piece_kernel, count), value, outs, others)


def landed(arrays, costs):
    out = []
    for value, cost in zip(arrays, costs):
        out.append(after(value, *out[-1:], cost=cost))
    return out


def gathered(image, text, img_bits, txt_bits):
    half = image.shape[0] // 2
    raw = [swapped(image[:half], img_bits[0]), swapped(image[half:], img_bits[0])]
    img_raw = [swapped(image, bit) for bit in img_bits[1:]]
    txt_raw = swapped(text, txt_bits[0])
    imgs, txts = {}, {}
    imgs[1] = unit_pieces(raw[0], 1, [])
    others = imgs[1]
    for place, value in enumerate(img_raw):
        imgs[2 << place] = others = unit_pieces(value, 2, others[:1])
    txts[0] = unit_pieces(text, 1, others[:1])
    imgs[0] = unit_pieces(image, 1, txts[0])
    for place in range(1, len(txt_bits)):
        txts[1 << place] = [swapped(txts[0][0], txt_bits[place])]
    imgs[1] = imgs[1] + unit_pieces(raw[1], 1, imgs[0])
    txts[1] = unit_pieces(txt_raw, 1, imgs[1][1:])
    for blocks, bits in ((txts, txt_bits), (imgs, img_bits)):
        for offset in range(1 << len(bits)):
            if offset not in blocks:
                place = offset.bit_length() - 1
                blocks[offset] = [swapped(p, bits[place]) for p in blocks[offset ^ 1 << place]]
    imgs = [imgs[offset] for offset in range(1 << len(img_bits))]
    txts = [txts[offset] for offset in range(1 << len(txt_bits))]
    order = landed([txts[-2][0]] + imgs[-1] + [txts[-1][0]], [GATHER_COST] * 3 + [0])
    txts[-2], imgs[-1], txts[-1] = order[:1], order[1:-1], order[-1:]
    return imgs, txts


def store_part(part, start, outs, cuts, rows):
    for at in range(start // rows, (start + part.shape[0]) // rows):
        size = rows // cuts[at]
        for place in range(cuts[at]):
            out = outs[sum(cuts[:at]) + place]
            first = at * rows - start + place * size
            out[...] = part[first : first + size].astype(out.dtype)


def tile_kernel(img_places, txt_places, img_cuts, txt_cuts, rows, *refs):
    n_img, n_txt = len(img_places), len(txt_places)
    taken = 0
    sources = []
    for places in (img_places, txt_places):
        pieces = sum(places)
        sources.append(refs[taken : taken + pieces])
        taken += pieces
    log_temp, bias = refs[taken : taken + 2]
    taken += 2
    img_parts = refs[taken : taken + sum(img_cuts)]
    taken += sum(img_cuts)
    txt_parts = refs[taken : taken + sum(txt_cuts)]
    sums, img_b, txt_b, grad_b = refs[taken + sum(txt_cuts) :]
    for group, held in zip(sources, (img_b, txt_b)):
        start = 0
        for piece in group:
            end = start + piece.shape[0]
            held[start:end] = piece[...]
            start = end
    temp = jnp.exp(log_temp[...])
    shift_b = bias[...]
    sum_g = jnp.zeros((8, 128), jnp.float32)
    sum_gl = jnp.zeros((8, 128), jnp.float32)
    step = 2 * rows
    for start in range(0, n_img * rows, step):
        panel = img_b[start : start + step]
        cosine = lax.dot_general(
            panel, txt_b[...], (((1,), (1,)), ((), ())), preferred_element_type=jnp.float32
        )
        scaled = temp * cosine
        logits = scaled + shift_b
        if start == 0:
            at_row = lax.broadcasted_iota(jnp.int32, logits.shape, 0)
            at_col = lax.broadcasted_iota(jnp.int32, logits.shape, 1)
            own = jnp.logical_and(at_row == at_col, at_row < rows)
            sign = jnp.where(own, 1.0, -1.0)
            grads = -sign * jax.nn.sigmoid(-sign * logits)
        else:
            grads = jax.nn.sigmoid(logits)
        sum_g = sum_g + lane_sums(grads)
        sum_gl = sum_gl + lane_sums(grads * scaled)
        grads_b = grads.astype(jnp.bfloat16)
        grad_b[start : start + step] = grads_b
        part = jnp.dot(grads_b, txt_b[...], preferred_element_type=jnp.float32)
        store_part(temp * part, start, img_parts, img_cuts, rows)
    sums[0:8] = sum_g
    sums[8:16] = sum_gl
    for start in range(0, n_txt * rows, step):
        part = lax.dot_general(
            grad_b[:, start : start + step],
            img_b[...],
            (((0,), (0,)), ((), ())),
            preferred_element_type=jnp.float32,
        )
        store_part(temp * part, start, txt_parts, txt_cuts, rows)


def tile_call(imgs, txts, log_temp, bias):
    rows = sum(piece.shape[0] for piece in imgs[0])
    width = imgs[0][0].shape[1]
    n_img, n_txt = len(imgs), len(txts)
    flat = [piece for block in imgs + txts for piece in block]
    pairs = n_img * n_txt * rows * rows
    img_cuts = [2 if at > n_img // 2 else 1 for at in range(n_img)]
    txt_cuts = [1] * n_txt
    outs = []
    for cuts in (img_cuts, txt_cuts):
        for at, cut in enumerate(cuts):
            kind = jnp.float32 if at < len(cuts) // 2 else jnp.bfloat16
            outs += [jax.ShapeDtypeStruct((rows // cut, width), kind)] * cut
    results = pl.pallas_call(
        functools.partial(
            tile_kernel,
            [len(block) for block in imgs],
            [len(block) for block in txts],
            img_cuts,
            txt_cuts,
            rows,
        ),
        out_shape=outs + [jax.ShapeDtypeStruct((16, 128), jnp.float32)],
        in_specs=[VMEM] * (len(flat) + 2),
        out_specs=[VMEM] * (len(outs) + 1),
        scratch_shapes=[
            pltpu.VMEM((n_img * rows, width), jnp.bfloat16),
            pltpu.VMEM((n_txt * rows, width), jnp.bfloat16),
            pltpu.VMEM((n_img * rows, n_txt * rows), jnp.bfloat16),
        ],
        compiler_params=pltpu.CompilerParams(vmem_limit_bytes=TILE_VMEM),
        cost_estimate=pl.CostEstimate(
            flops=6 * pairs * width, bytes_accessed=0, transcendentals=2 * pairs
        ),
    )(*flat, log_temp, bias)
    results = list(results)
    sums = results.pop()
    parts = [[results.pop(0) for _ in range(cut)] for cut in img_cuts + txt_cuts]
    return parts[:n_img], parts[n_img:], sums


def finish_kernel(recv_counts, pairs, sums, sums_recv, *refs):
    total = sums[...] + sums_recv[...]
    for place in range(2):
        whole = jnp.sum(total[8 * place : 8 * place + 8], axis=0, keepdims=True)
        refs[place - 2][...] = jnp.sum(whole, axis=1, keepdims=True) / pairs
    outs = refs[-len(recv_counts) - 2 : -2]
    for out, count in zip(outs, recv_counts):
        value, keep = refs[:2]
        rows = value.shape[0]
        total = keep[...]
        start = 0
        pieces = []
        for recv in refs[2 : 2 + count]:
            pieces.append(recv[...].astype(jnp.float32))
            start += recv.shape[0]
            if start % rows == 0:
                total = total + jnp.concatenate(pieces, axis=0)
                pieces = []
        refs = refs[2 + count :]
        unit, inverse = unit_rows(value[...])
        along = jnp.sum(unit * total, axis=1, keepdims=True)
        out[...] = ((total - unit * along) * inverse).astype(jnp.bfloat16)


def finish_call(sums, sums_recv, pairs, sides):
    flat = [array for value, keep, recvs in sides for array in [value, keep] + recvs]
    return pl.pallas_call(
        functools.partial(finish_kernel, [len(recvs) for _, _, recvs in sides], pairs),
        out_shape=[jax.ShapeDtypeStruct(value.shape, jnp.bfloat16) for value, _, _ in sides]
        + [jax.ShapeDtypeStruct((1, 1), jnp.float32)] * 2,
        in_specs=[VMEM] * (2 + len(flat)),
        out_specs=[VMEM] * (2 + len(sides)),
        compiler_params=pltpu.CompilerParams(vmem_limit_bytes=2 * SMALL_VMEM),
    )(sums, sums_recv, *flat)


def add_kernel(count, at, *refs):
    keep, recv = refs[:2]
    out = refs[-count]
    kept = keep[...] if keep.shape == recv.shape else keep[pl.ds(at, recv.shape[0])]
    out[...] = (kept + recv[...].astype(jnp.float32)).astype(out.dtype)
    if count == 2:
        refs[-1][...] = refs[2][...] + refs[3][...]


def add_call(keep, recv, at, dtype, sums, bit, others):
    operands = [keep, recv]
    outs = [jax.ShapeDtypeStruct(recv.shape, dtype)]
    if bit is not None:
        operands += [sums, swapped(sums, bit)]
        outs.append(jax.ShapeDtypeStruct(sums.shape, sums.dtype))
    results = pl.pallas_call(
        functools.partial(add_kernel, len(outs), at),
        out_shape=outs,
        in_specs=[VMEM] * len(operands) + [ANY] * len(others),
        out_specs=[VMEM] * len(outs),
        compiler_params=pltpu.CompilerParams(vmem_limit_bytes=SMALL_VMEM),
        cost_estimate=pl.CostEstimate(
            flops=keep.size, bytes_accessed=keep.size, transcendentals=0
        ),
    )(*operands, *others)
    return results if bit is not None else [results[0], sums]


def returned(parts, bits, sums, sum_bits, others):
    parts = dict(enumerate(parts))
    recvs = []
    for place in reversed(range(len(bits))):
        arrived = []
        for offset in range(1, 1 << place):
            for at, piece in enumerate(parts.pop(offset | 1 << place)):
                arrived.append((offset, at, swapped(piece, bits[place])))
        new = {}
        for offset, at, recv in arrived:
            kept = parts[offset]
            kept = kept[at] if len(kept) > 1 else kept[0]
            kind = jnp.float32 if offset < 1 << (place - 1) else jnp.bfloat16
            bit = sum_bits.pop(0) if len(sum_bits) > 1 else None
            piece, sums = add_call(kept, recv, at * recv.shape[0], kind, sums, bit, others)
            others = [piece]
            new.setdefault(offset, []).append(piece)
        sends = parts.pop(1 << place)
        if len(sends) == 1 and len(arrived) > 1:
            sends = [after(sends[0], piece)]
        recvs.append([swapped(piece, bits[place]) for piece in sends])
        parts.update(new)
    return parts[0][0], recvs, sums, others


def shards(image_embeds, text_embeds, log_temp, bias):
    rows, width = image_embeds.shape
    count = lax.axis_size("blk")
    depth = count.bit_length() - 1
    all_bits = [1 << place for place in range(depth)]
    split = 1 + depth // 2
    img_bits = all_bits[1:split][::-1]
    txt_bits = (all_bits[:1] + all_bits[split:])[::-1]
    imgs, txts = gathered(image_embeds, text_embeds, img_bits, txt_bits)
    img_parts, txt_parts, sums = tile_call(imgs, txts, log_temp.reshape(1, 1), bias.reshape(1, 1))
    left = txt_bits[-1:] + txt_bits[:1] + [bit for bit in all_bits if bit not in (txt_bits[0], txt_bits[-1])]
    txt_keep, txt_recvs, sums, others = returned(txt_parts, txt_bits, sums, left, [])
    img_keep, img_recvs, sums, others = returned(img_parts, img_bits, sums, left, others)
    for bit in left[:-1]:
        sums = sums + swapped(sums, bit)
    sums_recv, txt_recvs, img_recvs = landed_sides(swapped(sums, left[-1]), txt_recvs, img_recvs)
    grad_text, grad_image, grad_bias, grad_temp = finish_call(
        sums,
        sums_recv,
        float(rows * count) * float(rows * count),
        [(text_embeds, txt_keep, txt_recvs), (image_embeds, img_keep, img_recvs)],
    )
    return (grad_image, grad_text, grad_temp.reshape(1), grad_bias.reshape(1))


def landed_sides(sums, txt_recvs, img_recvs):
    txts = [piece for recv in txt_recvs[::-1] for piece in recv]
    imgs = [piece for recv in img_recvs[::-1] for piece in recv]
    order = [sums] + txts + imgs[:1] + imgs[2:] + imgs[1:2]
    costs = [0] * (1 + len(txts)) + [RETURN_COST] + [0] * (len(imgs) - 1)
    sums, *order = landed(order, costs)
    txts, imgs = order[: len(txts)], order[len(txts) :]
    imgs = imgs[:1] + imgs[-1:] + imgs[1:-1]
    return sums, txts[::-1], imgs[2:] + imgs[:2]


def solution(mesh):
    in_specs = (P(("groups", "blk"), None), P(("groups", "blk"), None), P(), P())
    out_specs = (P(("groups", "blk"), None), P(("groups", "blk"), None), P("groups"), P("groups"))
    return jax.shard_map(shards, mesh=mesh, in_specs=in_specs, out_specs=out_specs, check_vma=False)
```

time: 66.8 us -> 64.5 us (0.966)
  waiting for transfers between devices: 31.2 us -> 37.3 us
  between operations: 5.62 us -> 2.11 us
  Pallas kernels: 8.36 us -> 4.85 us
  local copies, waits for them, and re-layouts: 2.89 us -> 1.02 us
  starting transfers between devices: 17.9 us -> 19.1 us
    ppermute x17 -> x20, waiting for transfers between devices: 31.2 us -> 37.3 us  [swapped(): return lax.ppermute(x, 'blk', [(i, i ^ bit) for i in range(count)])]
    unnamed x12 -> x4, local copies, waits for them, and re-layouts: 2.89 us -> 0.01 us
    pallas_call x4, Pallas kernels: 4.05 us -> 1.41 us  [the longest x1 1.3 us: finish_call(): pl.pallas_call(functools.partial(finish_kernel, [len(recvs) for _, _, rec...]
    ppermute x17 -> x20, starting transfers between devices: 17.9 us -> 19.1 us  [swapped(): return lax.ppermute(x, 'blk', [(i, i ^ bit) for i in range(count)])]
    slice x0 -> x1, local copies, waits for them, and re-layouts: none -> 1.01 us  [gathered(): image[half:]]
    pallas_call x1, Pallas kernels: 3.27 us -> 2.59 us  [tile_call(): pl.pallas_call(functools.partial(tile_kernel, [len(block) for block in im...]
  transfers between devices with their start and end apart: 17 -> 20, of which waited for: 8 -> 10; matrix products, arithmetic and copies ran while one was open for 1% -> 2% of each run, Pallas kernels for 5% -> 1%
where the time goes in v4:
time: 64.5 us; the launch traced here: 64.3 us
  waiting for transfers between devices  37.3 us (58%)
  starting transfers between devices  19.1 us (30%)
  Pallas kernels  4.85 us (8%)
  between operations  2.11 us (3%)
  local copies, waits for them, and re-layouts  1.02 us (2%)
    ppermute x20, waiting for transfers between devices, swapped(): return lax.ppermute(x, 'blk', [(i, i ^ bit) for i in range(count)])  37.3 us
    ppermute x20, starting transfers between devices, swapped(): return lax.ppermute(x, 'blk', [(i, i ^ bit) for i in range(count)])  19.1 us
    pallas_call x1, Pallas kernels, tile_call(): pl.pallas_call(functools.partial(tile_kernel, [len(block) for block in im...  2.59 us
    pallas_call x1, Pallas kernels, finish_call(): pl.pallas_call(functools.partial(finish_kernel, [len(recvs) for _, _, rec...  1.3 us
  transfers between devices with their start and end apart: 20, of which 10 were waited for; matrix products, arithmetic and copies ran while one was open for 2% of the time, Pallas kernels for 1%

profile of v4, /device:TPU:0, one launch (start us, length us, event | category | flops | bytes accessed | tf_op | source)
XLA Modules:
  0.0 64.3 jit_solution(7638569791859370420)
XLA Ops:
  0.6 3.0 %collective-permute-start = (bf16[128,1152]{1,0:T(8,128)(2,1)}, bf16[128,1152]{1,0:T(8,128)(2,1)S(1)}, u32[]{:S(2)}, u32[]{:S(2)}) collective-permute-start(bf16[128,1152]{1,0:T(8,128)(2,1)} %refs_4_.1), channel_id=1, source_target_pairs={{0,2},{1,3},{2,0},{3,1},{4,6},{5,7},{6,4},{7,5},{8,10},{9,11},{10,... | collective-permute-start | bytes 884744 | tf_op jit(solution)/shard_map/ppermute | solution.py:20
  3.6 1.0 %fusion = (bf16[64,1152]{1,0:T(8,128)(2,1)S(1)}, bf16[64,1152]{1,0:T(8,128)(2,1)S(1)}) fusion(bf16[128,1152]{1,0:T(8,128)(2,1)} %refs_4_.1), kind=kLoop, calls=%fused_computation | loop fusion | bytes 589824 | tf_op jit(solution)/shard_map/slice | solution.py:84
  4.7 1.6 %collective-permute-start.1 = (bf16[64,1152]{1,0:T(8,128)(2,1)S(1)}, bf16[64,1152]{1,0:T(8,128)(2,1)S(1)}, u32[]{:S(2)}, u32[]{:S(2)}) collective-permute-start(bf16[64,1152]{1,0:T(8,128)(2,1)S(1)} %get-tuple-element.49), channel_id=1, source_target_pairs={{0,4},{1,5},{2,6},{3,7},{4,0},{5,1},{6,2},{7,3},{8,12},{9,13},{10,... | collective-permute-start | bytes 442376 | tf_op jit(solution)/shard_map/ppermute | solution.py:20
  6.3 2.6 %collective-permute-start.6 = (bf16[128,1152]{1,0:T(8,128)(2,1)S(1)}, bf16[128,1152]{1,0:T(8,128)(2,1)S(1)}, u32[]{:S(2)}, u32[]{:S(2)}) collective-permute-start(bf16[128,1152]{1,0:T(8,128)(2,1)S(1)} %copy-done.1), channel_id=1, source_target_pairs={{0,8},{1,9},{2,10},{3,11},{4,12},{5,13},{6,14},{7,15},{8,0},{9,1},... | collective-permute-start | bytes 884744 | tf_op jit(solution)/shard_map/ppermute | solution.py:20
  8.9 3.5 %collective-permute-done.1.value = bf16[64,1152]{1,0:T(8,128)(2,1)S(1)} collective-permute-done((bf16[64,1152]{1,0:T(8,128)(2,1)S(1)}, bf16[64,1152]{1,0:T(8,128)(2,1)S(1)}, u32[]{:S(2)}, u32[]{:S(2)}) %collective-permute-start.1) | collective-permute-done | bytes 147488 | tf_op jit(solution)/shard_map/ppermute | solution.py:20
  12.4 0.1 shard_map.75.refs_0_.refs_1_
  12.5 0.0 collective-permute-done.value
  12.6 0.1 shard_map.76
  12.7 0.0 copy-start
  12.7 0.1 shard_map.77.refs_0_.refs_7_
  12.9 0.1 collective-permute-start.4
  12.9 0.2 collective-permute-start.2
  14.4 1.6 %collective-permute-start.3 = (bf16[64,1152]{1,0:T(8,128)(2,1)S(1)}, bf16[64,1152]{1,0:T(8,128)(2,1)S(1)}, u32[]{:S(2)}, u32[]{:S(2)}) collective-permute-start(bf16[64,1152]{1,0:T(8,128)(2,1)S(1)} %shard_map.75.refs_0_.refs_1_), channel_id=1, source_target_pairs={{0,2},{1,3},{2,0},{3,1},{4,6},{5,7},{6,4},{7,5},{8,10},{9,11},{10,... | collective-permute-start | bytes 442376 | tf_op jit(solution)/shard_map/ppermute | solution.py:20
  16.0 0.1 shard_map.78.refs_0_
  16.2 6.3 %collective-permute-done.2.value = bf16[64,1152]{1,0:T(8,128)(2,1)S(1)} collective-permute-done((bf16[64,1152]{1,0:T(8,128)(2,1)S(1)}, bf16[64,1152]{1,0:T(8,128)(2,1)S(1)}, u32[]{:S(2)}, u32[]{:S(2)}) %collective-permute-start.2) | collective-permute-done | bytes 147488 | tf_op jit(solution)/shard_map/ppermute | solution.py:20
  22.5 0.1 shard_map.79.refs_0_.refs_2_
  22.6 0.3 collective-permute-start.5
  22.9 0.1 shard_map.83.refs_8_
  23.0 0.1 collective-permute-start.7
  23.1 0.0 collective-permute-done.3.refs_0_
  23.2 4.9 %collective-permute-done.5.refs_0_ = bf16[64,1152]{1,0:T(8,128)(2,1)S(1)} collective-permute-done((bf16[64,1152]{1,0:T(8,128)(2,1)S(1)}, bf16[64,1152]{1,0:T(8,128)(2,1)S(1)}, u32[]{:S(2)}, u32[]{:S(2)}) %collective-permute-start.5) | collective-permute-done | bytes 147488 | tf_op jit(solution)/shard_map/ppermute | solution.py:20
  28.1 0.0 collective-permute-done.7.refs_0_
  28.1 2.6 %shard_map.85 = (f32[128,1152]{1,0:T(8,128)S(1)}, f32[128,1152]{1,0:T(8,128)S(1)}, bf16[128,1152]{1,0:T(8,128)(2,1)S(1)}, bf16[64,1152]{1,0:T(8,128)(2,1)S(1)}, ...) custom-call(bf16[128,1152]{1,0:T(8,128)(2,1)S(1)} %shard_map.78.refs, ...), custom_call_target="tpu_custom_call" | custom-call | flops 1811939328 | tf_op jit(solution)/shard_map/pallas_call | solution.py:190
  30.7 0.1 collective-permute-start.10
  30.8 0.5 collective-permute-start.11
  31.3 0.3 collective-permute-start.9
  31.6 0.8 %collective-permute-done.11.refs_3_ = f32[16,128]{1,0:T(8,128)S(1)} collective-permute-done((f32[16,128]{1,0:T(8,128)S(1)}, f32[16,128]{1,0:T(8,128)S(1)}, u32[]{:S(2)}, u32[]{:S(2)}) %collective-permute-start.11) | collective-permute-done | bytes 8224 | tf_op jit(solution)/shard_map/ppermute | solution.py:20
  32.4 0.0 collective-permute-done.10.refs_1_
  32.4 0.1 shard_map.86
  32.4 2.5 %collective-permute-start.16 = (bf16[128,1152]{1,0:T(8,128)(2,1)S(1)}, bf16[128,1152]{1,0:T(8,128)(2,1)S(1)}, u32[]{:S(2)}, u32[]{:S(2)}) collective-permute-start(bf16[128,1152]{1,0:T(8,128)(2,1)S(1)} %get-tuple-element.35.refs_4_), channel_id=1, source_target_pairs={{0,8},{1,9},{2,10},{3,11},{4,12},{5,13},{6,14},{7,15},{8,0},{9,1},... | collective-permute-start | bytes 884744 | tf_op jit(solution)/shard_map/ppermute | solution.py:20
  34.9 0.0 collective-permute-start.15
  34.9 0.9 %collective-permute-start.8 = (bf16[64,1152]{1,0:T(8,128)(2,1)S(1)}, bf16[64,1152]{1,0:T(8,128)(2,1)S(1)}, u32[]{:S(2)}, u32[]{:S(2)}) collective-permute-start(bf16[64,1152]{1,0:T(8,128)(2,1)S(1)} %get-tuple-element.29), channel_id=1, source_target_pairs={{0,2},{1,3},{2,0},{3,1},{4,6},{5,7},{6,4},{7,5},{8,10},{9,11},{10,... | collective-permute-start | bytes 442376 | tf_op jit(solution)/shard_map/ppermute | solution.py:20
  35.9 0.5 collective-permute-start.12
  36.4 0.7 %collective-permute-done.9.refs_1_ = bf16[64,1152]{1,0:T(8,128)(2,1)S(1)} collective-permute-done((bf16[64,1152]{1,0:T(8,128)(2,1)S(1)}, bf16[64,1152]{1,0:T(8,128)(2,1)S(1)}, u32[]{:S(2)}, u32[]{:S(2)}) %collective-permute-start.9) | collective-permute-done | bytes 147488 | tf_op jit(solution)/shard_map/ppermute | solution.py:20
  37.1 12.0 %collective-permute-done.12.refs_3_ = f32[16,128]{1,0:T(8,128)S(1)} collective-permute-done((f32[16,128]{1,0:T(8,128)S(1)}, f32[16,128]{1,0:T(8,128)S(1)}, u32[]{:S(2)}, u32[]{:S(2)}) %collective-permute-start.12) | collective-permute-done | bytes 8224 | tf_op jit(solution)/shard_map/ppermute | solution.py:20
  49.1 0.6 collective-permute-start.18
  49.7 0.7 %collective-permute-start.13 = (f32[16,128]{1,0:T(8,128)S(1)}, f32[16,128]{1,0:T(8,128)S(1)}, u32[]{:S(2)}, u32[]{:S(2)}) collective-permute-start(f32[16,128]{1,0:T(8,128)S(1)} %get-tuple-element.36.refs_2_), channel_id=1, source_target_pairs={{0,2},{1,3},{2,0},{3,1},{4,6},{5,7},{6,4},{7,5},{8,10},{9,11},{10,... | collective-permute-start | bytes 24584 | tf_op jit(solution)/shard_map/ppermute | solution.py:20
  50.4 0.0 collective-permute-done.8.refs_1_
  50.4 3.0 %collective-permute-done.13.refs_3_ = f32[16,128]{1,0:T(8,128)S(1)} collective-permute-done((f32[16,128]{1,0:T(8,128)S(1)}, f32[16,128]{1,0:T(8,128)S(1)}, u32[]{:S(2)}, u32[]{:S(2)}) %collective-permute-start.13) | collective-permute-done | bytes 8224 | tf_op jit(solution)/shard_map/ppermute | solution.py:20
  53.4 0.7 %collective-permute-start.17 = (bf16[128,1152]{1,0:T(8,128)(2,1)S(1)}, bf16[128,1152]{1,0:T(8,128)(2,1)S(1)}, u32[]{:S(2)}, u32[]{:S(2)}) collective-permute-start(bf16[128,1152]{1,0:T(8,128)(2,1)S(1)} %shard_map.92), channel_id=1, source_target_pairs={{0,2},{1,3},{2,0},{3,1},{4,6},{5,7},{6,4},{7,5},{8,10},{9,11},{10,... | collective-permute-start | bytes 884744 | tf_op jit(solution)/shard_map/ppermute | solution.py:20
  54.1 1.5 %collective-permute-start.14 = (f32[16,128]{1,0:T(8,128)S(1)}, f32[16,128]{1,0:T(8,128)S(1)}, u32[]{:S(2)}, u32[]{:S(2)}) collective-permute-start(f32[16,128]{1,0:T(8,128)S(1)} %get-tuple-element.38.sums), channel_id=1, source_target_pairs={{0,4},{1,5},{2,6},{3,7},{4,0},{5,1},{6,2},{7,3},{8,12},{9,13},{10,... | collective-permute-start | bytes 24584 | tf_op jit(solution)/shard_map/ppermute | solution.py:20
  55.6 2.3 %collective-permute-done.14.refs_0_ = f32[16,128]{1,0:T(8,128)S(1)} collective-permute-done((f32[16,128]{1,0:T(8,128)S(1)}, f32[16,128]{1,0:T(8,128)S(1)}, u32[]{:S(2)}, u32[]{:S(2)}) %collective-permute-start.14) | collective-permute-done | bytes 8224 | tf_op jit(solution)/shard_map/ppermute | solution.py:20
  57.9 1.5 %collective-permute-start.19 = (bf16[64,1152]{1,0:T(8,128)(2,1)S(1)}, bf16[64,1152]{1,0:T(8,128)(2,1)S(1)}, u32[]{:S(2)}, u32[]{:S(2)}) collective-permute-start(bf16[64,1152]{1,0:T(8,128)(2,1)S(1)} %get-tuple-element.43.refs_1_), channel_id=1, source_target_pairs={{0,4},{1,5},{2,6},{3,7},{4,0},{5,1},{6,2},{7,3},{8,12},{9,13},{10,... | collective-permute-start | bytes 442376 | tf_op jit(solution)/shard_map/ppermute | solution.py:20
  59.3 0.0 collective-permute-done.16.refs_0_
  59.3 0.0 collective-permute-done.18.refs_0_
  59.4 1.6 %collective-permute-done.17.refs_0_ = bf16[128,1152]{1,0:T(8,128)(2,1)S(1)} collective-permute-done((bf16[128,1152]{1,0:T(8,128)(2,1)S(1)}, bf16[128,1152]{1,0:T(8,128)(2,1)S(1)}, u32[]{:S(2)}, u32[]{:S(2)}) %collective-permute-start.17) | collective-permute-done | bytes 294944 | tf_op jit(solution)/shard_map/ppermute | solution.py:20
  61.0 2.0 %collective-permute-done.19.refs_0_ = bf16[64,1152]{1,0:T(8,128)(2,1)S(1)} collective-permute-done((bf16[64,1152]{1,0:T(8,128)(2,1)S(1)}, bf16[64,1152]{1,0:T(8,128)(2,1)S(1)}, u32[]{:S(2)}, u32[]{:S(2)}) %collective-permute-start.19) | collective-permute-done | bytes 147488 | tf_op jit(solution)/shard_map/ppermute | solution.py:20
  63.0 1.3 %shard_map.96 = (bf16[128,1152]{1,0:T(8,128)(2,1)}, bf16[128,1152]{1,0:T(8,128)(2,1)}, f32[1,1]{1,0:T(1,128)}, f32[1,1]{1,0:T(1,128)}) custom-call(f32[16,128]{1,0:T(8,128)S(1)} %get-tuple-element.38.sums, f32[16,128]{1,0:T(8,128)S(1)} %shard_map.89.refs_1_.sums_recv, bf16[128,1152]{1,0:T(8,128)(2,1)S(1)} %copy-done.1, ...), custom_call_target="tpu_custom_call" | custom-call | tf_op jit(solution)/shard_map/pallas_call | solution.py:244
  (19 shorter events, 0.1 us)
Async XLA Ops:
  0.6 5.7 %copy-start.1 = (bf16[128,1152]{1,0:T(8,128)(2,1)S(1)}, bf16[128,1152]{1,0:T(8,128)(2,1)}, u32[]{:S(2)}) copy-start(bf16[128,1152]{1,0:T(8,128)(2,1)} %refs_0_.1) | copy-start | bytes 884740
  0.6 11.9 %collective-permute-start = (bf16[128,1152]{1,0:T(8,128)(2,1)}, bf16[128,1152]{1,0:T(8,128)(2,1)S(1)}, u32[]{:S(2)}, u32[]{:S(2)}) collective-permute-start(bf16[128,1152]{1,0:T(8,128)(2,1)} %refs_4_.1), channel_id=1, source_target_pairs={{0,2},{1,3},{2,0},{3,1},{4,6},{5,7},{6,4},{7,5},{8,10},{9,11},{10,... | collective-permute-start | bytes 884744 | tf_op jit(solution)/shard_map/ppermute | solution.py:20
  4.7 7.8 %collective-permute-start.1 = (bf16[64,1152]{1,0:T(8,128)(2,1)S(1)}, bf16[64,1152]{1,0:T(8,128)(2,1)S(1)}, u32[]{:S(2)}, u32[]{:S(2)}) collective-permute-start(bf16[64,1152]{1,0:T(8,128)(2,1)S(1)} %get-tuple-element.49), channel_id=1, source_target_pairs={{0,4},{1,5},{2,6},{3,7},{4,0},{5,1},{6,2},{7,3},{8,12},{9,13},{10,... | collective-permute-start | bytes 442376 | tf_op jit(solution)/shard_map/ppermute | solution.py:20
  6.3 16.6 %collective-permute-start.6 = (bf16[128,1152]{1,0:T(8,128)(2,1)S(1)}, bf16[128,1152]{1,0:T(8,128)(2,1)S(1)}, u32[]{:S(2)}, u32[]{:S(2)}) collective-permute-start(bf16[128,1152]{1,0:T(8,128)(2,1)S(1)} %copy-done.1), channel_id=1, source_target_pairs={{0,8},{1,9},{2,10},{3,11},{4,12},{5,13},{6,14},{7,15},{8,0},{9,1},... | collective-permute-start | bytes 884744 | tf_op jit(solution)/shard_map/ppermute | solution.py:20
  12.7 3.3 %copy-start = (bf16[128,1152]{1,0:T(8,128)(2,1)S(1)}, bf16[128,1152]{1,0:T(8,128)(2,1)}, u32[]{:S(2)}) copy-start(bf16[128,1152]{1,0:T(8,128)(2,1)} %refs_4_.1) | copy-start | bytes 884740
  12.9 10.3 %collective-permute-start.4 = (bf16[128,1152]{1,0:T(8,128)(2,1)S(1)}, bf16[128,1152]{1,0:T(8,128)(2,1)S(1)}, u32[]{:S(2)}, u32[]{:S(2)}) collective-permute-start(bf16[128,1152]{1,0:T(8,128)(2,1)S(1)} %shard_map.77.refs_0_.refs_7_), channel_id=1, source_target_pairs={{0,1},{1,0},{2,3},{3,2},{4,5},{5,4},{6,7},{7,6},{8,9},{9,8},{10,11... | collective-permute-start | bytes 884744 | tf_op jit(solution)/shard_map/ppermute | solution.py:20
  12.9 9.5 %collective-permute-start.2 = (bf16[64,1152]{1,0:T(8,128)(2,1)S(1)}, bf16[64,1152]{1,0:T(8,128)(2,1)S(1)}, u32[]{:S(2)}, u32[]{:S(2)}) collective-permute-start(bf16[64,1152]{1,0:T(8,128)(2,1)S(1)} %get-tuple-element.48), channel_id=1, source_target_pairs={{0,4},{1,5},{2,6},{3,7},{4,0},{5,1},{6,2},{7,3},{8,12},{9,13},{10,... | collective-permute-start | bytes 442376 | tf_op jit(solution)/shard_map/ppermute | solution.py:20
  14.4 8.7 %collective-permute-start.3 = (bf16[64,1152]{1,0:T(8,128)(2,1)S(1)}, bf16[64,1152]{1,0:T(8,128)(2,1)S(1)}, u32[]{:S(2)}, u32[]{:S(2)}) collective-permute-start(bf16[64,1152]{1,0:T(8,128)(2,1)S(1)} %shard_map.75.refs_0_.refs_1_), channel_id=1, source_target_pairs={{0,2},{1,3},{2,0},{3,1},{4,6},{5,7},{6,4},{7,5},{8,10},{9,11},{10,... | collective-permute-start | bytes 442376 | tf_op jit(solution)/shard_map/ppermute | solution.py:20
  22.6 5.5 %collective-permute-start.5 = (bf16[64,1152]{1,0:T(8,128)(2,1)S(1)}, bf16[64,1152]{1,0:T(8,128)(2,1)S(1)}, u32[]{:S(2)}, u32[]{:S(2)}) collective-permute-start(bf16[64,1152]{1,0:T(8,128)(2,1)S(1)} %shard_map.79.refs_0_.refs_2_), channel_id=1, source_target_pairs={{0,2},{1,3},{2,0},{3,1},{4,6},{5,7},{6,4},{7,5},{8,10},{9,11},{10,... | collective-permute-start | bytes 442376 | tf_op jit(solution)/shard_map/ppermute | solution.py:20
  23.0 5.1 %collective-permute-start.7 = (bf16[128,1152]{1,0:T(8,128)(2,1)S(1)}, bf16[128,1152]{1,0:T(8,128)(2,1)S(1)}, u32[]{:S(2)}, u32[]{:S(2)}) collective-permute-start(bf16[128,1152]{1,0:T(8,128)(2,1)S(1)} %shard_map.83.refs_8_), channel_id=1, source_target_pairs={{0,1},{1,0},{2,3},{3,2},{4,5},{5,4},{6,7},{7,6},{8,9},{9,8},{10,11... | collective-permute-start | bytes 884744 | tf_op jit(solution)/shard_map/ppermute | solution.py:20
  30.7 1.7 %collective-permute-start.10 = (bf16[128,1152]{1,0:T(8,128)(2,1)S(1)}, bf16[128,1152]{1,0:T(8,128)(2,1)S(1)}, u32[]{:S(2)}, u32[]{:S(2)}) collective-permute-start(bf16[128,1152]{1,0:T(8,128)(2,1)S(1)} %get-tuple-element.32), channel_id=1, source_target_pairs={{0,1},{1,0},{2,3},{3,2},{4,5},{5,4},{6,7},{7,6},{8,9},{9,8},{10,11... | collective-permute-start | bytes 884744 | tf_op jit(solution)/shard_map/ppermute | solution.py:20
  30.8 1.6 %collective-permute-start.11 = (f32[16,128]{1,0:T(8,128)S(1)}, f32[16,128]{1,0:T(8,128)S(1)}, u32[]{:S(2)}, u32[]{:S(2)}) collective-permute-start(f32[16,128]{1,0:T(8,128)S(1)} %get-tuple-element.33.refs_2_), channel_id=1, source_target_pairs={{0,1},{1,0},{2,3},{3,2},{4,5},{5,4},{6,7},{7,6},{8,9},{9,8},{10,11... | collective-permute-start | bytes 24584 | tf_op jit(solution)/shard_map/ppermute | solution.py:20
  31.3 5.8 %collective-permute-start.9 = (bf16[64,1152]{1,0:T(8,128)(2,1)S(1)}, bf16[64,1152]{1,0:T(8,128)(2,1)S(1)}, u32[]{:S(2)}, u32[]{:S(2)}) collective-permute-start(bf16[64,1152]{1,0:T(8,128)(2,1)S(1)} %get-tuple-element.30), channel_id=1, source_target_pairs={{0,2},{1,3},{2,0},{3,1},{4,6},{5,7},{6,4},{7,5},{8,10},{9,11},{10,... | collective-permute-start | bytes 442376 | tf_op jit(solution)/shard_map/ppermute | solution.py:20
  32.4 26.9 %collective-permute-start.16 = (bf16[128,1152]{1,0:T(8,128)(2,1)S(1)}, bf16[128,1152]{1,0:T(8,128)(2,1)S(1)}, u32[]{:S(2)}, u32[]{:S(2)}) collective-permute-start(bf16[128,1152]{1,0:T(8,128)(2,1)S(1)} %get-tuple-element.35.refs_4_), channel_id=1, source_target_pairs={{0,8},{1,9},{2,10},{3,11},{4,12},{5,13},{6,14},{7,15},{8,0},{9,1},... | collective-permute-start | bytes 884744 | tf_op jit(solution)/shard_map/ppermute | solution.py:20
  34.9 24.4 %collective-permute-start.15 = (bf16[128,1152]{1,0:T(8,128)(2,1)S(1)}, bf16[128,1152]{1,0:T(8,128)(2,1)S(1)}, u32[]{:S(2)}, u32[]{:S(2)}) collective-permute-start(bf16[128,1152]{1,0:T(8,128)(2,1)S(1)} %get-tuple-element.40), channel_id=1, source_target_pairs={{0,1},{1,0},{2,3},{3,2},{4,5},{5,4},{6,7},{7,6},{8,9},{9,8},{10,11... | collective-permute-start | bytes 884744 | tf_op jit(solution)/shard_map/ppermute | solution.py:20
  34.9 15.5 %collective-permute-start.8 = (bf16[64,1152]{1,0:T(8,128)(2,1)S(1)}, bf16[64,1152]{1,0:T(8,128)(2,1)S(1)}, u32[]{:S(2)}, u32[]{:S(2)}) collective-permute-start(bf16[64,1152]{1,0:T(8,128)(2,1)S(1)} %get-tuple-element.29), channel_id=1, source_target_pairs={{0,2},{1,3},{2,0},{3,1},{4,6},{5,7},{6,4},{7,5},{8,10},{9,11},{10,... | collective-permute-start | bytes 442376 | tf_op jit(solution)/shard_map/ppermute | solution.py:20
  35.9 13.2 %collective-permute-start.12 = (f32[16,128]{1,0:T(8,128)S(1)}, f32[16,128]{1,0:T(8,128)S(1)}, u32[]{:S(2)}, u32[]{:S(2)}) collective-permute-start(f32[16,128]{1,0:T(8,128)S(1)} %get-tuple-element.34.refs_2_), channel_id=1, source_target_pairs={{0,8},{1,9},{2,10},{3,11},{4,12},{5,13},{6,14},{7,15},{8,0},{9,1},... | collective-permute-start | bytes 24584 | tf_op jit(solution)/shard_map/ppermute | solution.py:20
  49.1 10.2 %collective-permute-start.18 = (bf16[64,1152]{1,0:T(8,128)(2,1)S(1)}, bf16[64,1152]{1,0:T(8,128)(2,1)S(1)}, u32[]{:S(2)}, u32[]{:S(2)}) collective-permute-start(bf16[64,1152]{1,0:T(8,128)(2,1)S(1)} %get-tuple-element.37.refs_4_), channel_id=1, source_target_pairs={{0,4},{1,5},{2,6},{3,7},{4,0},{5,1},{6,2},{7,3},{8,12},{9,13},{10,... | collective-permute-start | bytes 442376 | tf_op jit(solution)/shard_map/ppermute | solution.py:20
  49.7 3.7 %collective-permute-start.13 = (f32[16,128]{1,0:T(8,128)S(1)}, f32[16,128]{1,0:T(8,128)S(1)}, u32[]{:S(2)}, u32[]{:S(2)}) collective-permute-start(f32[16,128]{1,0:T(8,128)S(1)} %get-tuple-element.36.refs_2_), channel_id=1, source_target_pairs={{0,2},{1,3},{2,0},{3,1},{4,6},{5,7},{6,4},{7,5},{8,10},{9,11},{10,... | collective-permute-start | bytes 24584 | tf_op jit(solution)/shard_map/ppermute | solution.py:20
  53.4 7.6 %collective-permute-start.17 = (bf16[128,1152]{1,0:T(8,128)(2,1)S(1)}, bf16[128,1152]{1,0:T(8,128)(2,1)S(1)}, u32[]{:S(2)}, u32[]{:S(2)}) collective-permute-start(bf16[128,1152]{1,0:T(8,128)(2,1)S(1)} %shard_map.92), channel_id=1, source_target_pairs={{0,2},{1,3},{2,0},{3,1},{4,6},{5,7},{6,4},{7,5},{8,10},{9,11},{10,... | collective-permute-start | bytes 884744 | tf_op jit(solution)/shard_map/ppermute | solution.py:20
  54.1 3.7 %collective-permute-start.14 = (f32[16,128]{1,0:T(8,128)S(1)}, f32[16,128]{1,0:T(8,128)S(1)}, u32[]{:S(2)}, u32[]{:S(2)}) collective-permute-start(f32[16,128]{1,0:T(8,128)S(1)} %get-tuple-element.38.sums), channel_id=1, source_target_pairs={{0,4},{1,5},{2,6},{3,7},{4,0},{5,1},{6,2},{7,3},{8,12},{9,13},{10,... | collective-permute-start | bytes 24584 | tf_op jit(solution)/shard_map/ppermute | solution.py:20
  57.9 5.1 %collective-permute-start.19 = (bf16[64,1152]{1,0:T(8,128)(2,1)S(1)}, bf16[64,1152]{1,0:T(8,128)(2,1)S(1)}, u32[]{:S(2)}, u32[]{:S(2)}) collective-permute-start(bf16[64,1152]{1,0:T(8,128)(2,1)S(1)} %get-tuple-element.43.refs_1_), channel_id=1, source_target_pairs={{0,4},{1,5},{2,6},{3,7},{4,0},{5,1},{6,2},{7,3},{8,12},{9,13},{10,... | collective-permute-start | bytes 442376 | tf_op jit(solution)/shard_map/ppermute | solution.py:20

commit v5 on v4

--- a/solution.py
+++ b/solution.py
@@ -10,7 +10,7 @@
 TILE_VMEM = 32 * 1024 * 1024
 SMALL_VMEM = 4 * 1024 * 1024
 GATHER_COST = 4_000_000_000
-RETURN_COST = 2_000_000_000
+RETURN_COST = 600_000_000
 VMEM = pl.BlockSpec(memory_space=pltpu.VMEM)
 ANY = pl.BlockSpec(memory_space=pl.ANY)
 
@@ -20,16 +20,18 @@
     return lax.ppermute(x, "blk", [(i, i ^ bit) for i in range(count)])
 
 
-def after(value, *others, cost=0):
-    return pl.pallas_call(
+def held(values, others, cost=0):
+    count = len(values)
+    results = pl.pallas_call(
         lambda *refs: None,
-        out_shape=jax.ShapeDtypeStruct(value.shape, value.dtype),
-        in_specs=[ANY] * (1 + len(others)),
-        out_specs=ANY,
-        input_output_aliases={0: 0},
+        out_shape=[jax.ShapeDtypeStruct(value.shape, value.dtype) for value in values],
+        in_specs=[ANY] * (count + len(others)),
+        out_specs=[ANY] * count,
+        input_output_aliases={place: place for place in range(count)},
         cost_estimate=pl.CostEstimate(flops=cost, bytes_accessed=0, transcendentals=0),
         compiler_params=pltpu.CompilerParams(vmem_limit_bytes=SMALL_VMEM),
-    )(value, *others)
+    )(*values, *others)
+    return list(results)
 
 
 def unit_rows(values):
@@ -75,7 +77,7 @@
 def landed(arrays, costs):
     out = []
     for value, cost in zip(arrays, costs):
-        out.append(after(value, *out[-1:], cost=cost))
+        out += held([value], out[-1:], cost)
     return out
 
 
@@ -83,7 +85,7 @@
     half = image.shape[0] // 2
     raw = [swapped(image[:half], img_bits[0]), swapped(image[half:], img_bits[0])]
     img_raw = [swapped(image, bit) for bit in img_bits[1:]]
-    txt_raw = swapped(text, txt_bits[0])
+    txt_raw = [swapped(text, bit) for bit in txt_bits]
     imgs, txts = {}, {}
     imgs[1] = unit_pieces(raw[0], 1, [])
     others = imgs[1]
@@ -91,10 +93,11 @@
         imgs[2 << place] = others = unit_pieces(value, 2, others[:1])
     txts[0] = unit_pieces(text, 1, others[:1])
     imgs[0] = unit_pieces(image, 1, txts[0])
+    others = imgs[0]
     for place in range(1, len(txt_bits)):
-        txts[1 << place] = [swapped(txts[0][0], txt_bits[place])]
-    imgs[1] = imgs[1] + unit_pieces(raw[1], 1, imgs[0])
-    txts[1] = unit_pieces(txt_raw, 1, imgs[1][1:])
+        txts[1 << place] = others = unit_pieces(txt_raw[place], 1, others)
+    imgs[1] = imgs[1] + unit_pieces(raw[1], 1, others)
+    txts[1] = unit_pieces(txt_raw[0], 1, imgs[1][1:])
     for blocks, bits in ((txts, txt_bits), (imgs, img_bits)):
         for offset in range(1 << len(bits)):
             if offset not in blocks:
@@ -102,8 +105,8 @@
                 blocks[offset] = [swapped(p, bits[place]) for p in blocks[offset ^ 1 << place]]
     imgs = [imgs[offset] for offset in range(1 << len(img_bits))]
     txts = [txts[offset] for offset in range(1 << len(txt_bits))]
-    order = landed([txts[-2][0]] + imgs[-1] + [txts[-1][0]], [GATHER_COST] * 3 + [0])
-    txts[-2], imgs[-1], txts[-1] = order[:1], order[1:-1], order[-1:]
+    order = landed(imgs[-1] + txts[-1], [GATHER_COST] * len(imgs[-1]) + [0])
+    imgs[-1], txts[-1] = order[:-1], order[-1:]
     return imgs, txts
 
 
@@ -180,7 +183,7 @@
     n_img, n_txt = len(imgs), len(txts)
     flat = [piece for block in imgs + txts for piece in block]
     pairs = n_img * n_txt * rows * rows
-    img_cuts = [2 if at > n_img // 2 else 1 for at in range(n_img)]
+    img_cuts = [2 if at >= n_img // 2 else 1 for at in range(n_img)]
     txt_cuts = [1] * n_txt
     outs = []
     for cuts in (img_cuts, txt_cuts):
@@ -297,8 +300,8 @@
             others = [piece]
             new.setdefault(offset, []).append(piece)
         sends = parts.pop(1 << place)
-        if len(sends) == 1 and len(arrived) > 1:
-            sends = [after(sends[0], piece)]
+        if len(sends) > 1 and arrived:
+            sends = held(sends, [piece])
         recvs.append([swapped(piece, bits[place]) for piece in sends])
         parts.update(new)
     return parts[0][0], recvs, sums, others
@@ -314,7 +317,7 @@
     txt_bits = (all_bits[:1] + all_bits[split:])[::-1]
     imgs, txts = gathered(image_embeds, text_embeds, img_bits, txt_bits)
     img_parts, txt_parts, sums = tile_call(imgs, txts, log_temp.reshape(1, 1), bias.reshape(1, 1))
-    left = txt_bits[-1:] + txt_bits[:1] + [bit for bit in all_bits if bit not in (txt_bits[0], txt_bits[-1])]
+    left = txt_bits[-1:] + img_bits + txt_bits[-2::-1]
     txt_keep, txt_recvs, sums, others = returned(txt_parts, txt_bits, sums, left, [])
     img_keep, img_recvs, sums, others = returned(img_parts, img_bits, sums, left, others)
     for bit in left[:-1]:
@@ -330,14 +333,11 @@
 
 
 def landed_sides(sums, txt_recvs, img_recvs):
-    txts = [piece for recv in txt_recvs[::-1] for piece in recv]
-    imgs = [piece for recv in img_recvs[::-1] for piece in recv]
-    order = [sums] + txts + imgs[:1] + imgs[2:] + imgs[1:2]
-    costs = [0] * (1 + len(txts)) + [RETURN_COST] + [0] * (len(imgs) - 1)
-    sums, *order = landed(order, costs)
-    txts, imgs = order[: len(txts)], order[len(txts) :]
-    imgs = imgs[:1] + imgs[-1:] + imgs[1:-1]
-    return sums, txts[::-1], imgs[2:] + imgs[:2]
+    txts = [piece for recv in txt_recvs for piece in recv]
+    imgs = [piece for recv in img_recvs for piece in recv]
+    at = len(imgs) - len(img_recvs[-1])
+    first = held(imgs[at : at + 1] + txts, [], RETURN_COST)
+    return sums, first[1:], imgs[:at] + first[:1] + imgs[at + 1 :]
 
 
 def solution(mesh):

time: 64.5 us -> 57.7 us (0.89)
  waiting for transfers between devices: 37.3 us -> 27.9 us
  starting transfers between devices: 19.1 us -> 20.7 us
  local copies, waits for them, and re-layouts: 1.02 us -> 1.82 us
    ppermute x20 -> x21, waiting for transfers between devices: 37.3 us -> 27.9 us  [swapped(): return lax.ppermute(x, 'blk', [(i, i ^ bit) for i in range(count)])]
    ppermute x20 -> x21, starting transfers between devices: 19.1 us -> 20.7 us  [swapped(): return lax.ppermute(x, 'blk', [(i, i ^ bit) for i in range(count)])]
    unnamed x4, local copies, waits for them, and re-layouts: 0.01 us -> 0.81 us
  transfers between devices with their start and end apart: 20 -> 21, of which waited for: 10 -> 8; matrix products, arithmetic and copies ran while one was open for 2% -> 2% of each run, Pallas kernels for 1% -> 2%
where the time goes in v5:
time: 57.7 us; the launch traced here: 57.5 us
  waiting for transfers between devices  27.9 us (48%)
  starting transfers between devices  20.7 us (36%)
  Pallas kernels  5.01 us (9%)
  between operations  2.11 us (4%)
  local copies, waits for them, and re-layouts  1.82 us (3%)
    ppermute x21, waiting for transfers between devices, swapped(): return lax.ppermute(x, 'blk', [(i, i ^ bit) for i in range(count)])  27.9 us
    ppermute x21, starting transfers between devices, swapped(): return lax.ppermute(x, 'blk', [(i, i ^ bit) for i in range(count)])  20.7 us
    pallas_call x1, Pallas kernels, tile_call(): pl.pallas_call(functools.partial(tile_kernel, [len(block) for block in im...  2.59 us
    pallas_call x1, Pallas kernels, finish_call(): pl.pallas_call(functools.partial(finish_kernel, [len(recvs) for _, _, rec...  1.32 us
  transfers between devices with their start and end apart: 21, of which 8 were waited for; matrix products, arithmetic and copies ran while one was open for 2% of the time, Pallas kernels for 2%

profile of v5, /device:TPU:0, one launch (start us, length us, event | category | flops | bytes accessed | tf_op | source)
XLA Modules:
  0.0 57.5 jit_solution(17894369086613234224)
XLA Ops:
  0.6 0.5 collective-permute-start.3
  1.1 3.7 %collective-permute-start.6 = (bf16[128,1152]{1,0:T(8,128)(2,1)}, bf16[128,1152]{1,0:T(8,128)(2,1)S(1)}, u32[]{:S(2)}, u32[]{:S(2)}) collective-permute-start(bf16[128,1152]{1,0:T(8,128)(2,1)} %refs_0_.1), channel_id=1, source_target_pairs={{0,8},{1,9},{2,10},{3,11},{4,12},{5,13},{6,14},{7,15},{8,0},{9,1},... | collective-permute-start | bytes 884744 | tf_op jit(solution)/shard_map/ppermute | solution.py:20
  4.8 1.5 %collective-permute-start = (bf16[128,1152]{1,0:T(8,128)(2,1)}, bf16[128,1152]{1,0:T(8,128)(2,1)S(1)}, u32[]{:S(2)}, u32[]{:S(2)}) collective-permute-start(bf16[128,1152]{1,0:T(8,128)(2,1)} %refs_4_.1), channel_id=1, source_target_pairs={{0,2},{1,3},{2,0},{3,1},{4,6},{5,7},{6,4},{7,5},{8,10},{9,11},{10,... | collective-permute-start | bytes 884744 | tf_op jit(solution)/shard_map/ppermute | solution.py:20
  6.3 1.0 %fusion = (bf16[64,1152]{1,0:T(8,128)(2,1)S(1)}, bf16[64,1152]{1,0:T(8,128)(2,1)S(1)}) fusion(bf16[128,1152]{1,0:T(8,128)(2,1)} %refs_4_.1), kind=kLoop, calls=%fused_computation | loop fusion | bytes 589824 | tf_op jit(solution)/shard_map/slice | solution.py:86
  7.3 1.6 %collective-permute-start.1 = (bf16[64,1152]{1,0:T(8,128)(2,1)S(1)}, bf16[64,1152]{1,0:T(8,128)(2,1)S(1)}, u32[]{:S(2)}, u32[]{:S(2)}) collective-permute-start(bf16[64,1152]{1,0:T(8,128)(2,1)S(1)} %get-tuple-element.61), channel_id=1, source_target_pairs={{0,4},{1,5},{2,6},{3,7},{4,0},{5,1},{6,2},{7,3},{8,12},{9,13},{10,... | collective-permute-start | bytes 442376 | tf_op jit(solution)/shard_map/ppermute | solution.py:20
  9.0 0.4 collective-permute-start.2
  9.4 9.8 %collective-permute-done.1.value = bf16[64,1152]{1,0:T(8,128)(2,1)S(1)} collective-permute-done((bf16[64,1152]{1,0:T(8,128)(2,1)S(1)}, bf16[64,1152]{1,0:T(8,128)(2,1)S(1)}, u32[]{:S(2)}, u32[]{:S(2)}) %collective-permute-start.1) | collective-permute-done | bytes 147488 | tf_op jit(solution)/shard_map/ppermute | solution.py:20
  19.3 0.1 shard_map.75.refs_0_.refs_1_
  19.4 0.0 copy-start.1
  19.4 0.1 collective-permute-start.4
  20.8 0.0 collective-permute-done.value
  20.8 0.1 shard_map.76
  21.0 0.0 copy-start
  21.0 0.1 shard_map.77.refs_0_.refs_7_
  21.1 0.8 %copy-done = bf16[128,1152]{1,0:T(8,128)(2,1)S(1)} copy-done((bf16[128,1152]{1,0:T(8,128)(2,1)S(1)}, bf16[128,1152]{1,0:T(8,128)(2,1)}, u32[]{:S(2)}) %copy-start) | copy-done | bytes 294936
  21.9 0.1 shard_map.78.refs_0_
  22.1 0.1 shard_map.79.refs_0_.refs_9_
  22.2 0.0 collective-permute-done.2.value
  22.3 0.1 shard_map.80.refs_0_.refs_2_
  22.4 2.1 %collective-permute-start.5 = (bf16[64,1152]{1,0:T(8,128)(2,1)S(1)}, bf16[64,1152]{1,0:T(8,128)(2,1)S(1)}, u32[]{:S(2)}, u32[]{:S(2)}) collective-permute-start(bf16[64,1152]{1,0:T(8,128)(2,1)S(1)} %shard_map.80.refs_0_.refs_2_), channel_id=1, source_target_pairs={{0,2},{1,3},{2,0},{3,1},{4,6},{5,7},{6,4},{7,5},{8,10},{9,11},{10,... | collective-permute-start | bytes 442376 | tf_op jit(solution)/shard_map/ppermute | solution.py:20
  24.4 0.1 shard_map.83.refs_8_
  24.6 0.1 collective-permute-start.7
  24.7 1.4 %collective-permute-done.4.refs_0_ = bf16[64,1152]{1,0:T(8,128)(2,1)S(1)} collective-permute-done((bf16[64,1152]{1,0:T(8,128)(2,1)S(1)}, bf16[64,1152]{1,0:T(8,128)(2,1)S(1)}, u32[]{:S(2)}, u32[]{:S(2)}) %collective-permute-start.4) | collective-permute-done | bytes 147488 | tf_op jit(solution)/shard_map/ppermute | solution.py:20
  26.1 1.7 %collective-permute-done.5.refs_0_ = bf16[64,1152]{1,0:T(8,128)(2,1)S(1)} collective-permute-done((bf16[64,1152]{1,0:T(8,128)(2,1)S(1)}, bf16[64,1152]{1,0:T(8,128)(2,1)S(1)}, u32[]{:S(2)}, u32[]{:S(2)}) %collective-permute-start.5) | collective-permute-done | bytes 147488 | tf_op jit(solution)/shard_map/ppermute | solution.py:20
  27.8 0.0 collective-permute-done.7.refs_0_
  27.8 2.6 %shard_map.85 = (f32[128,1152]{1,0:T(8,128)S(1)}, f32[128,1152]{1,0:T(8,128)S(1)}, bf16[64,1152]{1,0:T(8,128)(2,1)S(1)}, bf16[64,1152]{1,0:T(8,128)(2,1)S(1)}, b...) custom-call(bf16[128,1152]{1,0:T(8,128)(2,1)S(1)} %shard_map.78.refs, ...), custom_call_target="tpu_custom_call" | custom-call | flops 1811939328 | tf_op jit(solution)/shard_map/pallas_call | solution.py:193
  30.4 0.1 collective-permute-start.10
  30.4 0.5 collective-permute-start.16
  30.9 0.1 collective-permute-start.11
  31.0 1.8 %collective-permute-start.9 = (bf16[64,1152]{1,0:T(8,128)(2,1)S(1)}, bf16[64,1152]{1,0:T(8,128)(2,1)S(1)}, u32[]{:S(2)}, u32[]{:S(2)}) collective-permute-start(bf16[64,1152]{1,0:T(8,128)(2,1)S(1)} %get-tuple-element.36), channel_id=1, source_target_pairs={{0,2},{1,3},{2,0},{3,1},{4,6},{5,7},{6,4},{7,5},{8,10},{9,11},{10,... | collective-permute-start | bytes 442376 | tf_op jit(solution)/shard_map/ppermute | solution.py:20
  32.8 0.0 collective-permute-done.11.refs_3_
  32.8 0.0 collective-permute-done.10.refs_1_
  32.8 0.1 shard_map.86
  32.9 0.1 collective-permute-start.17
  33.0 1.5 %collective-permute-start.8 = (bf16[64,1152]{1,0:T(8,128)(2,1)S(1)}, bf16[64,1152]{1,0:T(8,128)(2,1)S(1)}, u32[]{:S(2)}, u32[]{:S(2)}) collective-permute-start(bf16[64,1152]{1,0:T(8,128)(2,1)S(1)} %get-tuple-element.35), channel_id=1, source_target_pairs={{0,2},{1,3},{2,0},{3,1},{4,6},{5,7},{6,4},{7,5},{8,10},{9,11},{10,... | collective-permute-start | bytes 442376 | tf_op jit(solution)/shard_map/ppermute | solution.py:20
  34.5 0.6 %collective-permute-start.12 = (f32[16,128]{1,0:T(8,128)S(1)}, f32[16,128]{1,0:T(8,128)S(1)}, u32[]{:S(2)}, u32[]{:S(2)}) collective-permute-start(f32[16,128]{1,0:T(8,128)S(1)} %get-tuple-element.40.refs_2_), channel_id=1, source_target_pairs={{0,4},{1,5},{2,6},{3,7},{4,0},{5,1},{6,2},{7,3},{8,12},{9,13},{10,... | collective-permute-start | bytes 24584 | tf_op jit(solution)/shard_map/ppermute | solution.py:20
  35.1 2.6 %collective-permute-done.9.refs_1_ = bf16[64,1152]{1,0:T(8,128)(2,1)S(1)} collective-permute-done((bf16[64,1152]{1,0:T(8,128)(2,1)S(1)}, bf16[64,1152]{1,0:T(8,128)(2,1)S(1)}, u32[]{:S(2)}, u32[]{:S(2)}) %collective-permute-start.9) | collective-permute-done | bytes 147488 | tf_op jit(solution)/shard_map/ppermute | solution.py:20
  37.7 2.4 %collective-permute-done.12.refs_3_ = f32[16,128]{1,0:T(8,128)S(1)} collective-permute-done((f32[16,128]{1,0:T(8,128)S(1)}, f32[16,128]{1,0:T(8,128)S(1)}, u32[]{:S(2)}, u32[]{:S(2)}) %collective-permute-start.12) | collective-permute-done | bytes 8224 | tf_op jit(solution)/shard_map/ppermute | solution.py:20
  40.1 2.5 %collective-permute-start.15 = (bf16[64,1152]{1,0:T(8,128)(2,1)S(1)}, bf16[64,1152]{1,0:T(8,128)(2,1)S(1)}, u32[]{:S(2)}, u32[]{:S(2)}) collective-permute-start(bf16[64,1152]{1,0:T(8,128)(2,1)S(1)} %get-tuple-element.43.refs_4_), channel_id=1, source_target_pairs={{0,4},{1,5},{2,6},{3,7},{4,0},{5,1},{6,2},{7,3},{8,12},{9,13},{10,... | collective-permute-start | bytes 442376 | tf_op jit(solution)/shard_map/ppermute | solution.py:20
  42.7 1.4 %collective-permute-start.13 = (f32[16,128]{1,0:T(8,128)S(1)}, f32[16,128]{1,0:T(8,128)S(1)}, u32[]{:S(2)}, u32[]{:S(2)}) collective-permute-start(f32[16,128]{1,0:T(8,128)S(1)} %get-tuple-element.42.refs_2_), channel_id=1, source_target_pairs={{0,2},{1,3},{2,0},{3,1},{4,6},{5,7},{6,4},{7,5},{8,10},{9,11},{10,... | collective-permute-start | bytes 24584 | tf_op jit(solution)/shard_map/ppermute | solution.py:20
  44.0 0.0 collective-permute-done.8.refs_1_
  44.0 2.3 %collective-permute-done.13.refs_3_ = f32[16,128]{1,0:T(8,128)S(1)} collective-permute-done((f32[16,128]{1,0:T(8,128)S(1)}, f32[16,128]{1,0:T(8,128)S(1)}, u32[]{:S(2)}, u32[]{:S(2)}) %collective-permute-start.13) | collective-permute-done | bytes 8224 | tf_op jit(solution)/shard_map/ppermute | solution.py:20
  46.3 1.5 %collective-permute-start.18 = (bf16[64,1152]{1,0:T(8,128)(2,1)S(1)}, bf16[64,1152]{1,0:T(8,128)(2,1)S(1)}, u32[]{:S(2)}, u32[]{:S(2)}) collective-permute-start(bf16[64,1152]{1,0:T(8,128)(2,1)S(1)} %get-tuple-element.53), channel_id=1, source_target_pairs={{0,2},{1,3},{2,0},{3,1},{4,6},{5,7},{6,4},{7,5},{8,10},{9,11},{10,... | collective-permute-start | bytes 442376 | tf_op jit(solution)/shard_map/ppermute | solution.py:20
  47.8 0.6 %collective-permute-start.19 = (bf16[64,1152]{1,0:T(8,128)(2,1)S(1)}, bf16[64,1152]{1,0:T(8,128)(2,1)S(1)}, u32[]{:S(2)}, u32[]{:S(2)}) collective-permute-start(bf16[64,1152]{1,0:T(8,128)(2,1)S(1)} %get-tuple-element.54), channel_id=1, source_target_pairs={{0,2},{1,3},{2,0},{3,1},{4,6},{5,7},{6,4},{7,5},{8,10},{9,11},{10,... | collective-permute-start | bytes 442376 | tf_op jit(solution)/shard_map/ppermute | solution.py:20
  48.4 0.1 collective-permute-start.20
  48.5 3.1 %collective-permute-done.15.refs_0_ = bf16[64,1152]{1,0:T(8,128)(2,1)S(1)} collective-permute-done((bf16[64,1152]{1,0:T(8,128)(2,1)S(1)}, bf16[64,1152]{1,0:T(8,128)(2,1)S(1)}, u32[]{:S(2)}, u32[]{:S(2)}) %collective-permute-start.15) | collective-permute-done | bytes 147488 | tf_op jit(solution)/shard_map/ppermute | solution.py:20
  51.6 4.5 %collective-permute-done.14.sums_recv = f32[16,128]{1,0:T(8,128)S(1)} collective-permute-done((f32[16,128]{1,0:T(8,128)S(1)}, f32[16,128]{1,0:T(8,128)S(1)}, u32[]{:S(2)}, u32[]{:S(2)}) %collective-permute-start.14) | collective-permute-done | bytes 8224 | tf_op jit(solution)/shard_map/ppermute | solution.py:20
  56.2 1.3 %shard_map.91 = (bf16[128,1152]{1,0:T(8,128)(2,1)}, bf16[128,1152]{1,0:T(8,128)(2,1)}, f32[1,1]{1,0:T(1,128)}, f32[1,1]{1,0:T(1,128)}) custom-call(f32[16,128]{1,0:T(8,128)S(1)} %get-tuple-element.44.sums, f32[16,128]{1,0:T(8,128)S(1)} %collective-permute-done.14.sums_recv, bf16[128,1152]{1,0:T(8,128)(2,1)S(1)} %copy-done.1, ...), custom_call_target="tpu_custom_call" | custom-call | tf_op jit(solution)/shard_map/pallas_call | solution.py:247
  (16 shorter events, 0.1 us)
Async XLA Ops:
  0.6 21.5 %collective-permute-start.3 = (bf16[128,1152]{1,0:T(8,128)(2,1)}, bf16[128,1152]{1,0:T(8,128)(2,1)S(1)}, u32[]{:S(2)}, u32[]{:S(2)}) collective-permute-start(bf16[128,1152]{1,0:T(8,128)(2,1)} %refs_0_.1), channel_id=1, source_target_pairs={{0,1},{1,0},{2,3},{3,2},{4,5},{5,4},{6,7},{7,6},{8,9},{9,8},{10,11... | collective-permute-start | bytes 884744 | tf_op jit(solution)/shard_map/ppermute | solution.py:20
  1.1 23.3 %collective-permute-start.6 = (bf16[128,1152]{1,0:T(8,128)(2,1)}, bf16[128,1152]{1,0:T(8,128)(2,1)S(1)}, u32[]{:S(2)}, u32[]{:S(2)}) collective-permute-start(bf16[128,1152]{1,0:T(8,128)(2,1)} %refs_0_.1), channel_id=1, source_target_pairs={{0,8},{1,9},{2,10},{3,11},{4,12},{5,13},{6,14},{7,15},{8,0},{9,1},... | collective-permute-start | bytes 884744 | tf_op jit(solution)/shard_map/ppermute | solution.py:20
  4.8 16.0 %collective-permute-start = (bf16[128,1152]{1,0:T(8,128)(2,1)}, bf16[128,1152]{1,0:T(8,128)(2,1)S(1)}, u32[]{:S(2)}, u32[]{:S(2)}) collective-permute-start(bf16[128,1152]{1,0:T(8,128)(2,1)} %refs_4_.1), channel_id=1, source_target_pairs={{0,2},{1,3},{2,0},{3,1},{4,6},{5,7},{6,4},{7,5},{8,10},{9,11},{10,... | collective-permute-start | bytes 884744 | tf_op jit(solution)/shard_map/ppermute | solution.py:20
  7.3 11.9 %collective-permute-start.1 = (bf16[64,1152]{1,0:T(8,128)(2,1)S(1)}, bf16[64,1152]{1,0:T(8,128)(2,1)S(1)}, u32[]{:S(2)}, u32[]{:S(2)}) collective-permute-start(bf16[64,1152]{1,0:T(8,128)(2,1)S(1)} %get-tuple-element.61), channel_id=1, source_target_pairs={{0,4},{1,5},{2,6},{3,7},{4,0},{5,1},{6,2},{7,3},{8,12},{9,13},{10,... | collective-permute-start | bytes 442376 | tf_op jit(solution)/shard_map/ppermute | solution.py:20
  9.0 13.3 %collective-permute-start.2 = (bf16[64,1152]{1,0:T(8,128)(2,1)S(1)}, bf16[64,1152]{1,0:T(8,128)(2,1)S(1)}, u32[]{:S(2)}, u32[]{:S(2)}) collective-permute-start(bf16[64,1152]{1,0:T(8,128)(2,1)S(1)} %get-tuple-element.60), channel_id=1, source_target_pairs={{0,4},{1,5},{2,6},{3,7},{4,0},{5,1},{6,2},{7,3},{8,12},{9,13},{10,... | collective-permute-start | bytes 442376 | tf_op jit(solution)/shard_map/ppermute | solution.py:20
  19.4 1.6 %copy-start.1 = (bf16[128,1152]{1,0:T(8,128)(2,1)S(1)}, bf16[128,1152]{1,0:T(8,128)(2,1)}, u32[]{:S(2)}) copy-start(bf16[128,1152]{1,0:T(8,128)(2,1)} %refs_0_.1) | copy-start | bytes 884740
  19.4 6.7 %collective-permute-start.4 = (bf16[64,1152]{1,0:T(8,128)(2,1)S(1)}, bf16[64,1152]{1,0:T(8,128)(2,1)S(1)}, u32[]{:S(2)}, u32[]{:S(2)}) collective-permute-start(bf16[64,1152]{1,0:T(8,128)(2,1)S(1)} %shard_map.75.refs_0_.refs_1_), channel_id=1, source_target_pairs={{0,2},{1,3},{2,0},{3,1},{4,6},{5,7},{6,4},{7,5},{8,10},{9,11},{10,... | collective-permute-start | bytes 442376 | tf_op jit(solution)/shard_map/ppermute | solution.py:20
  21.0 1.0 %copy-start = (bf16[128,1152]{1,0:T(8,128)(2,1)S(1)}, bf16[128,1152]{1,0:T(8,128)(2,1)}, u32[]{:S(2)}) copy-start(bf16[128,1152]{1,0:T(8,128)(2,1)} %refs_4_.1) | copy-start | bytes 884740
  22.4 5.4 %collective-permute-start.5 = (bf16[64,1152]{1,0:T(8,128)(2,1)S(1)}, bf16[64,1152]{1,0:T(8,128)(2,1)S(1)}, u32[]{:S(2)}, u32[]{:S(2)}) collective-permute-start(bf16[64,1152]{1,0:T(8,128)(2,1)S(1)} %shard_map.80.refs_0_.refs_2_), channel_id=1, source_target_pairs={{0,2},{1,3},{2,0},{3,1},{4,6},{5,7},{6,4},{7,5},{8,10},{9,11},{10,... | collective-permute-start | bytes 442376 | tf_op jit(solution)/shard_map/ppermute | solution.py:20
  24.6 3.2 %collective-permute-start.7 = (bf16[128,1152]{1,0:T(8,128)(2,1)S(1)}, bf16[128,1152]{1,0:T(8,128)(2,1)S(1)}, u32[]{:S(2)}, u32[]{:S(2)}) collective-permute-start(bf16[128,1152]{1,0:T(8,128)(2,1)S(1)} %shard_map.83.refs_8_), channel_id=1, source_target_pairs={{0,1},{1,0},{2,3},{3,2},{4,5},{5,4},{6,7},{7,6},{8,9},{9,8},{10,11... | collective-permute-start | bytes 884744 | tf_op jit(solution)/shard_map/ppermute | solution.py:20
  30.4 2.5 %collective-permute-start.10 = (bf16[128,1152]{1,0:T(8,128)(2,1)S(1)}, bf16[128,1152]{1,0:T(8,128)(2,1)S(1)}, u32[]{:S(2)}, u32[]{:S(2)}) collective-permute-start(bf16[128,1152]{1,0:T(8,128)(2,1)S(1)} %get-tuple-element.38), channel_id=1, source_target_pairs={{0,1},{1,0},{2,3},{3,2},{4,5},{5,4},{6,7},{7,6},{8,9},{9,8},{10,11... | collective-permute-start | bytes 884744 | tf_op jit(solution)/shard_map/ppermute | solution.py:20
  30.4 18.0 %collective-permute-start.16 = (bf16[128,1152]{1,0:T(8,128)(2,1)S(1)}, bf16[128,1152]{1,0:T(8,128)(2,1)S(1)}, u32[]{:S(2)}, u32[]{:S(2)}) collective-permute-start(bf16[128,1152]{1,0:T(8,128)(2,1)S(1)} %get-tuple-element.46), channel_id=1, source_target_pairs={{0,1},{1,0},{2,3},{3,2},{4,5},{5,4},{6,7},{7,6},{8,9},{9,8},{10,11... | collective-permute-start | bytes 884744 | tf_op jit(solution)/shard_map/ppermute | solution.py:20
  30.9 1.9 %collective-permute-start.11 = (f32[16,128]{1,0:T(8,128)S(1)}, f32[16,128]{1,0:T(8,128)S(1)}, u32[]{:S(2)}, u32[]{:S(2)}) collective-permute-start(f32[16,128]{1,0:T(8,128)S(1)} %get-tuple-element.39.refs_2_), channel_id=1, source_target_pairs={{0,1},{1,0},{2,3},{3,2},{4,5},{5,4},{6,7},{7,6},{8,9},{9,8},{10,11... | collective-permute-start | bytes 24584 | tf_op jit(solution)/shard_map/ppermute | solution.py:20
  31.0 6.6 %collective-permute-start.9 = (bf16[64,1152]{1,0:T(8,128)(2,1)S(1)}, bf16[64,1152]{1,0:T(8,128)(2,1)S(1)}, u32[]{:S(2)}, u32[]{:S(2)}) collective-permute-start(bf16[64,1152]{1,0:T(8,128)(2,1)S(1)} %get-tuple-element.36), channel_id=1, source_target_pairs={{0,2},{1,3},{2,0},{3,1},{4,6},{5,7},{6,4},{7,5},{8,10},{9,11},{10,... | collective-permute-start | bytes 442376 | tf_op jit(solution)/shard_map/ppermute | solution.py:20
  32.9 18.7 %collective-permute-start.17 = (bf16[128,1152]{1,0:T(8,128)(2,1)S(1)}, bf16[128,1152]{1,0:T(8,128)(2,1)S(1)}, u32[]{:S(2)}, u32[]{:S(2)}) collective-permute-start(bf16[128,1152]{1,0:T(8,128)(2,1)S(1)} %get-tuple-element.41.refs_4_), channel_id=1, source_target_pairs={{0,8},{1,9},{2,10},{3,11},{4,12},{5,13},{6,14},{7,15},{8,0},{9,1},... | collective-permute-start | bytes 884744 | tf_op jit(solution)/shard_map/ppermute | solution.py:20
  33.0 11.1 %collective-permute-start.8 = (bf16[64,1152]{1,0:T(8,128)(2,1)S(1)}, bf16[64,1152]{1,0:T(8,128)(2,1)S(1)}, u32[]{:S(2)}, u32[]{:S(2)}) collective-permute-start(bf16[64,1152]{1,0:T(8,128)(2,1)S(1)} %get-tuple-element.35), channel_id=1, source_target_pairs={{0,2},{1,3},{2,0},{3,1},{4,6},{5,7},{6,4},{7,5},{8,10},{9,11},{10,... | collective-permute-start | bytes 442376 | tf_op jit(solution)/shard_map/ppermute | solution.py:20
  34.5 5.6 %collective-permute-start.12 = (f32[16,128]{1,0:T(8,128)S(1)}, f32[16,128]{1,0:T(8,128)S(1)}, u32[]{:S(2)}, u32[]{:S(2)}) collective-permute-start(f32[16,128]{1,0:T(8,128)S(1)} %get-tuple-element.40.refs_2_), channel_id=1, source_target_pairs={{0,4},{1,5},{2,6},{3,7},{4,0},{5,1},{6,2},{7,3},{8,12},{9,13},{10,... | collective-permute-start | bytes 24584 | tf_op jit(solution)/shard_map/ppermute | solution.py:20
  40.1 11.5 %collective-permute-start.15 = (bf16[64,1152]{1,0:T(8,128)(2,1)S(1)}, bf16[64,1152]{1,0:T(8,128)(2,1)S(1)}, u32[]{:S(2)}, u32[]{:S(2)}) collective-permute-start(bf16[64,1152]{1,0:T(8,128)(2,1)S(1)} %get-tuple-element.43.refs_4_), channel_id=1, source_target_pairs={{0,4},{1,5},{2,6},{3,7},{4,0},{5,1},{6,2},{7,3},{8,12},{9,13},{10,... | collective-permute-start | bytes 442376 | tf_op jit(solution)/shard_map/ppermute | solution.py:20
  42.7 3.7 %collective-permute-start.13 = (f32[16,128]{1,0:T(8,128)S(1)}, f32[16,128]{1,0:T(8,128)S(1)}, u32[]{:S(2)}, u32[]{:S(2)}) collective-permute-start(f32[16,128]{1,0:T(8,128)S(1)} %get-tuple-element.42.refs_2_), channel_id=1, source_target_pairs={{0,2},{1,3},{2,0},{3,1},{4,6},{5,7},{6,4},{7,5},{8,10},{9,11},{10,... | collective-permute-start | bytes 24584 | tf_op jit(solution)/shard_map/ppermute | solution.py:20
  46.3 9.8 %collective-permute-start.18 = (bf16[64,1152]{1,0:T(8,128)(2,1)S(1)}, bf16[64,1152]{1,0:T(8,128)(2,1)S(1)}, u32[]{:S(2)}, u32[]{:S(2)}) collective-permute-start(bf16[64,1152]{1,0:T(8,128)(2,1)S(1)} %get-tuple-element.53), channel_id=1, source_target_pairs={{0,2},{1,3},{2,0},{3,1},{4,6},{5,7},{6,4},{7,5},{8,10},{9,11},{10,... | collective-permute-start | bytes 442376 | tf_op jit(solution)/shard_map/ppermute | solution.py:20
  47.8 8.3 %collective-permute-start.19 = (bf16[64,1152]{1,0:T(8,128)(2,1)S(1)}, bf16[64,1152]{1,0:T(8,128)(2,1)S(1)}, u32[]{:S(2)}, u32[]{:S(2)}) collective-permute-start(bf16[64,1152]{1,0:T(8,128)(2,1)S(1)} %get-tuple-element.54), channel_id=1, source_target_pairs={{0,2},{1,3},{2,0},{3,1},{4,6},{5,7},{6,4},{7,5},{8,10},{9,11},{10,... | collective-permute-start | bytes 442376 | tf_op jit(solution)/shard_map/ppermute | solution.py:20
  48.4 7.7 %collective-permute-start.20 = (bf16[64,1152]{1,0:T(8,128)(2,1)S(1)}, bf16[64,1152]{1,0:T(8,128)(2,1)S(1)}, u32[]{:S(2)}, u32[]{:S(2)}) collective-permute-start(bf16[64,1152]{1,0:T(8,128)(2,1)S(1)} %get-tuple-element.52.refs_2_), channel_id=1, source_target_pairs={{0,4},{1,5},{2,6},{3,7},{4,0},{5,1},{6,2},{7,3},{8,12},{9,13},{10,... | collective-permute-start | bytes 442376 | tf_op jit(solution)/shard_map/ppermute | solution.py:20
  51.6 4.5 %collective-permute-start.14 = (f32[16,128]{1,0:T(8,128)S(1)}, f32[16,128]{1,0:T(8,128)S(1)}, u32[]{:S(2)}, u32[]{:S(2)}) collective-permute-start(f32[16,128]{1,0:T(8,128)S(1)} %get-tuple-element.44.sums), channel_id=1, source_target_pairs={{0,8},{1,9},{2,10},{3,11},{4,12},{5,13},{6,14},{7,15},{8,0},{9,1},... | collective-permute-start | bytes 24584 | tf_op jit(solution)/shard_map/ppermute | solution.py:20

commit v6 on v5

--- a/solution.py
+++ b/solution.py
@@ -11,6 +11,7 @@
 SMALL_VMEM = 4 * 1024 * 1024
 GATHER_COST = 4_000_000_000
 RETURN_COST = 600_000_000
+SUMS_COST = 2_000_000_000
 VMEM = pl.BlockSpec(memory_space=pltpu.VMEM)
 ANY = pl.BlockSpec(memory_space=pl.ANY)
 
@@ -218,12 +219,26 @@
     return parts[:n_img], parts[n_img:], sums
 
 
-def finish_kernel(recv_counts, pairs, sums, sums_recv, *refs):
-    total = sums[...] + sums_recv[...]
-    for place in range(2):
+def total_kernel(pairs, sums, *outs):
+    total = jnp.sum(sums[...], axis=0)
+    for place, out in enumerate(outs):
         whole = jnp.sum(total[8 * place : 8 * place + 8], axis=0, keepdims=True)
-        refs[place - 2][...] = jnp.sum(whole, axis=1, keepdims=True) / pairs
-    outs = refs[-len(recv_counts) - 2 : -2]
+        out[...] = jnp.sum(whole, axis=1, keepdims=True) / pairs
+
+
+def total_call(sums, pairs):
+    return pl.pallas_call(
+        functools.partial(total_kernel, pairs),
+        out_shape=[jax.ShapeDtypeStruct((1, 1), jnp.float32)] * 2,
+        in_specs=[VMEM],
+        out_specs=[VMEM] * 2,
+        compiler_params=pltpu.CompilerParams(vmem_limit_bytes=SMALL_VMEM),
+        cost_estimate=pl.CostEstimate(flops=SUMS_COST, bytes_accessed=0, transcendentals=0),
+    )(sums)
+
+
+def finish_kernel(recv_counts, *refs):
+    outs = refs[-len(recv_counts) :]
     for out, count in zip(outs, recv_counts):
         value, keep = refs[:2]
         rows = value.shape[0]
@@ -242,47 +257,37 @@
         out[...] = ((total - unit * along) * inverse).astype(jnp.bfloat16)
 
 
-def finish_call(sums, sums_recv, pairs, sides):
+def finish_call(sides):
     flat = [array for value, keep, recvs in sides for array in [value, keep] + recvs]
     return pl.pallas_call(
-        functools.partial(finish_kernel, [len(recvs) for _, _, recvs in sides], pairs),
-        out_shape=[jax.ShapeDtypeStruct(value.shape, jnp.bfloat16) for value, _, _ in sides]
-        + [jax.ShapeDtypeStruct((1, 1), jnp.float32)] * 2,
-        in_specs=[VMEM] * (2 + len(flat)),
-        out_specs=[VMEM] * (2 + len(sides)),
+        functools.partial(finish_kernel, [len(recvs) for _, _, recvs in sides]),
+        out_shape=[jax.ShapeDtypeStruct(value.shape, jnp.bfloat16) for value, _, _ in sides],
+        in_specs=[VMEM] * len(flat),
+        out_specs=[VMEM] * len(sides),
         compiler_params=pltpu.CompilerParams(vmem_limit_bytes=2 * SMALL_VMEM),
-    )(sums, sums_recv, *flat)
-
-
-def add_kernel(count, at, *refs):
-    keep, recv = refs[:2]
-    out = refs[-count]
+    )(*flat)
+
+
+def add_kernel(at, keep, recv, *refs):
+    out = refs[-1]
     kept = keep[...] if keep.shape == recv.shape else keep[pl.ds(at, recv.shape[0])]
     out[...] = (kept + recv[...].astype(jnp.float32)).astype(out.dtype)
-    if count == 2:
-        refs[-1][...] = refs[2][...] + refs[3][...]
-
-
-def add_call(keep, recv, at, dtype, sums, bit, others):
-    operands = [keep, recv]
-    outs = [jax.ShapeDtypeStruct(recv.shape, dtype)]
-    if bit is not None:
-        operands += [sums, swapped(sums, bit)]
-        outs.append(jax.ShapeDtypeStruct(sums.shape, sums.dtype))
-    results = pl.pallas_call(
-        functools.partial(add_kernel, len(outs), at),
-        out_shape=outs,
-        in_specs=[VMEM] * len(operands) + [ANY] * len(others),
-        out_specs=[VMEM] * len(outs),
+
+
+def add_call(keep, recv, at, dtype, others):
+    return pl.pallas_call(
+        functools.partial(add_kernel, at),
+        out_shape=jax.ShapeDtypeStruct(recv.shape, dtype),
+        in_specs=[VMEM] * 2 + [ANY] * len(others),
+        out_specs=VMEM,
         compiler_params=pltpu.CompilerParams(vmem_limit_bytes=SMALL_VMEM),
         cost_estimate=pl.CostEstimate(
-            flops=keep.size, bytes_accessed=keep.size, transcendentals=0
+            flops=recv.size, bytes_accessed=recv.size, transcendentals=0
         ),
-    )(*operands, *others)
-    return results if bit is not None else [results[0], sums]
-
-
-def returned(parts, bits, sums, sum_bits, others):
+    )(keep, recv, *others)
+
+
+def returned(parts, bits, others):
     parts = dict(enumerate(parts))
     recvs = []
     for place in reversed(range(len(bits))):
@@ -295,8 +300,7 @@
             kept = parts[offset]
             kept = kept[at] if len(kept) > 1 else kept[0]
             kind = jnp.float32 if offset < 1 << (place - 1) else jnp.bfloat16
-            bit = sum_bits.pop(0) if len(sum_bits) > 1 else None
-            piece, sums = add_call(kept, recv, at * recv.shape[0], kind, sums, bit, others)
+            piece = add_call(kept, recv, at * recv.shape[0], kind, others)
             others = [piece]
             new.setdefault(offset, []).append(piece)
         sends = parts.pop(1 << place)
@@ -304,7 +308,7 @@
             sends = held(sends, [piece])
         recvs.append([swapped(piece, bits[place]) for piece in sends])
         parts.update(new)
-    return parts[0][0], recvs, sums, others
+    return parts[0][0], recvs, others
 
 
 def shards(image_embeds, text_embeds, log_temp, bias):
@@ -317,27 +321,23 @@
     txt_bits = (all_bits[:1] + all_bits[split:])[::-1]
     imgs, txts = gathered(image_embeds, text_embeds, img_bits, txt_bits)
     img_parts, txt_parts, sums = tile_call(imgs, txts, log_temp.reshape(1, 1), bias.reshape(1, 1))
-    left = txt_bits[-1:] + img_bits + txt_bits[-2::-1]
-    txt_keep, txt_recvs, sums, others = returned(txt_parts, txt_bits, sums, left, [])
-    img_keep, img_recvs, sums, others = returned(img_parts, img_bits, sums, left, others)
-    for bit in left[:-1]:
-        sums = sums + swapped(sums, bit)
-    sums_recv, txt_recvs, img_recvs = landed_sides(swapped(sums, left[-1]), txt_recvs, img_recvs)
-    grad_text, grad_image, grad_bias, grad_temp = finish_call(
-        sums,
-        sums_recv,
-        float(rows * count) * float(rows * count),
-        [(text_embeds, txt_keep, txt_recvs), (image_embeds, img_keep, img_recvs)],
+    pairs = float(rows * count) * float(rows * count)
+    grad_bias, grad_temp = total_call(lax.all_gather(sums, "blk"), pairs)
+    txt_keep, txt_recvs, others = returned(txt_parts, txt_bits, [])
+    img_keep, img_recvs, others = returned(img_parts, img_bits, others)
+    txt_recvs, img_recvs = landed_sides(txt_recvs, img_recvs, [grad_bias])
+    grad_text, grad_image = finish_call(
+        [(text_embeds, txt_keep, txt_recvs), (image_embeds, img_keep, img_recvs)]
     )
     return (grad_image, grad_text, grad_temp.reshape(1), grad_bias.reshape(1))
 
 
-def landed_sides(sums, txt_recvs, img_recvs):
+def landed_sides(txt_recvs, img_recvs, others):
     txts = [piece for recv in txt_recvs for piece in recv]
     imgs = [piece for recv in img_recvs for piece in recv]
     at = len(imgs) - len(img_recvs[-1])
-    first = held(imgs[at : at + 1] + txts, [], RETURN_COST)
-    return sums, first[1:], imgs[:at] + first[:1] + imgs[at + 1 :]
+    first = held(imgs[at : at + 1] + txts, others, RETURN_COST)
+    return first[1:], imgs[:at] + first[:1] + imgs[at + 1 :]
 
 
 def solution(mesh):

time: 57.7 us -> 69.9 us (1.21)
  blocking collectives: 0 us -> 22.3 us
  waiting for transfers between devices: 27.9 us -> 18.6 us
  starting transfers between devices: 20.7 us -> 18.6 us
  Pallas kernels: 5.01 us -> 6.23 us
    all_gather x0 -> x1, blocking collectives: none -> 22.3 us  [shards(): grad_bias, grad_temp = total_call(lax.all_gather(sums, 'blk'), pairs)]
    ppermute x21 -> x17, waiting for transfers between devices: 27.9 us -> 18.6 us  [swapped(): return lax.ppermute(x, 'blk', [(i, i ^ bit) for i in range(count)])]
    ppermute x21 -> x17, starting transfers between devices: 20.7 us -> 18.6 us  [swapped(): return lax.ppermute(x, 'blk', [(i, i ^ bit) for i in range(count)])]
  transfers between devices with their start and end apart: 21 -> 17, of which waited for: 8 -> 6; matrix products, arithmetic and copies ran while one was open for 2% -> 1% of each run, Pallas kernels for 2% -> 3%
where the time goes in v6:
time: 69.9 us; the launch traced here: 69.7 us
  blocking collectives  22.3 us (32%)
  starting transfers between devices  18.6 us (27%)
  waiting for transfers between devices  18.6 us (27%)
  Pallas kernels  6.23 us (9%)
  between operations  2.1 us (3%)
  local copies, waits for them, and re-layouts  1.82 us (3%)
    all_gather x1, blocking collectives, shards(): grad_bias, grad_temp = total_call(lax.all_gather(sums, 'blk'), pairs)  22.3 us
    ppermute x17, waiting for transfers between devices, swapped(): return lax.ppermute(x, 'blk', [(i, i ^ bit) for i in range(count)])  18.6 us
    ppermute x17, starting transfers between devices, swapped(): return lax.ppermute(x, 'blk', [(i, i ^ bit) for i in range(count)])  18.6 us
    pallas_call x1, Pallas kernels, tile_call(): pl.pallas_call(functools.partial(tile_kernel, [len(block) for block in im...  2.59 us
  transfers between devices with their start and end apart: 17, of which 6 were waited for; matrix products, arithmetic and copies ran while one was open for 1% of the time, Pallas kernels for 3%

profile of v6, /device:TPU:0, one launch (start us, length us, event | category | flops | bytes accessed | tf_op | source)
XLA Modules:
  0.0 69.7 jit_solution(14544971123719465941)
XLA Ops:
  0.6 0.5 collective-permute-start.3
  1.1 3.7 %collective-permute-start.6 = (bf16[128,1152]{1,0:T(8,128)(2,1)}, bf16[128,1152]{1,0:T(8,128)(2,1)S(1)}, u32[]{:S(2)}, u32[]{:S(2)}) collective-permute-start(bf16[128,1152]{1,0:T(8,128)(2,1)} %refs_0_.1), channel_id=1, source_target_pairs={{0,8},{1,9},{2,10},{3,11},{4,12},{5,13},{6,14},{7,15},{8,0},{9,1},... | collective-permute-start | bytes 884744 | tf_op jit(solution)/shard_map/ppermute | solution.py:21
  4.8 1.5 %collective-permute-start = (bf16[128,1152]{1,0:T(8,128)(2,1)}, bf16[128,1152]{1,0:T(8,128)(2,1)S(1)}, u32[]{:S(2)}, u32[]{:S(2)}) collective-permute-start(bf16[128,1152]{1,0:T(8,128)(2,1)} %refs_4_.1), channel_id=1, source_target_pairs={{0,2},{1,3},{2,0},{3,1},{4,6},{5,7},{6,4},{7,5},{8,10},{9,11},{10,... | collective-permute-start | bytes 884744 | tf_op jit(solution)/shard_map/ppermute | solution.py:21
  6.3 1.0 %fusion = (bf16[64,1152]{1,0:T(8,128)(2,1)S(1)}, bf16[64,1152]{1,0:T(8,128)(2,1)S(1)}) fusion(bf16[128,1152]{1,0:T(8,128)(2,1)} %refs_4_.1), kind=kLoop, calls=%fused_computation | loop fusion | bytes 589824 | tf_op jit(solution)/shard_map/slice | solution.py:87
  7.3 1.6 %collective-permute-start.1 = (bf16[64,1152]{1,0:T(8,128)(2,1)S(1)}, bf16[64,1152]{1,0:T(8,128)(2,1)S(1)}, u32[]{:S(2)}, u32[]{:S(2)}) collective-permute-start(bf16[64,1152]{1,0:T(8,128)(2,1)S(1)} %get-tuple-element.49), channel_id=1, source_target_pairs={{0,4},{1,5},{2,6},{3,7},{4,0},{5,1},{6,2},{7,3},{8,12},{9,13},{10,... | collective-permute-start | bytes 442376 | tf_op jit(solution)/shard_map/ppermute | solution.py:21
  9.0 0.4 collective-permute-start.2
  9.4 9.8 %collective-permute-done.1.value = bf16[64,1152]{1,0:T(8,128)(2,1)S(1)} collective-permute-done((bf16[64,1152]{1,0:T(8,128)(2,1)S(1)}, bf16[64,1152]{1,0:T(8,128)(2,1)S(1)}, u32[]{:S(2)}, u32[]{:S(2)}) %collective-permute-start.1) | collective-permute-done | bytes 147488 | tf_op jit(solution)/shard_map/ppermute | solution.py:21
  19.3 0.1 shard_map.75.refs_0_.refs_1_
  19.4 0.0 copy-start.1
  19.4 0.1 collective-permute-start.4
  20.8 0.0 collective-permute-done.value
  20.8 0.1 shard_map.76
  21.0 0.0 copy-start
  21.0 0.1 shard_map.77.refs_0_.refs_7_
  21.1 0.8 %copy-done = bf16[128,1152]{1,0:T(8,128)(2,1)S(1)} copy-done((bf16[128,1152]{1,0:T(8,128)(2,1)S(1)}, bf16[128,1152]{1,0:T(8,128)(2,1)}, u32[]{:S(2)}) %copy-start) | copy-done | bytes 294936
  21.9 0.1 shard_map.78.refs_0_
  22.1 0.0 collective-permute-done.3.value
  22.1 0.1 shard_map.79.refs_0_.refs_9_
  22.2 0.0 collective-permute-done.2.value
  22.3 0.1 shard_map.80.refs_0_.refs_2_
  22.4 2.1 %collective-permute-start.5 = (bf16[64,1152]{1,0:T(8,128)(2,1)S(1)}, bf16[64,1152]{1,0:T(8,128)(2,1)S(1)}, u32[]{:S(2)}, u32[]{:S(2)}) collective-permute-start(bf16[64,1152]{1,0:T(8,128)(2,1)S(1)} %shard_map.80.refs_0_.refs_2_), channel_id=1, source_target_pairs={{0,2},{1,3},{2,0},{3,1},{4,6},{5,7},{6,4},{7,5},{8,10},{9,11},{10,... | collective-permute-start | bytes 442376 | tf_op jit(solution)/shard_map/ppermute | solution.py:21
  24.4 0.0 collective-permute-done.6.value
  24.4 0.1 shard_map.83.refs_8_
  24.6 0.1 collective-permute-start.7
  24.7 1.4 %collective-permute-done.4.refs_0_ = bf16[64,1152]{1,0:T(8,128)(2,1)S(1)} collective-permute-done((bf16[64,1152]{1,0:T(8,128)(2,1)S(1)}, bf16[64,1152]{1,0:T(8,128)(2,1)S(1)}, u32[]{:S(2)}, u32[]{:S(2)}) %collective-permute-start.4) | collective-permute-done | bytes 147488 | tf_op jit(solution)/shard_map/ppermute | solution.py:21
  26.1 1.7 %collective-permute-done.5.refs_0_ = bf16[64,1152]{1,0:T(8,128)(2,1)S(1)} collective-permute-done((bf16[64,1152]{1,0:T(8,128)(2,1)S(1)}, bf16[64,1152]{1,0:T(8,128)(2,1)S(1)}, u32[]{:S(2)}, u32[]{:S(2)}) %collective-permute-start.5) | collective-permute-done | bytes 147488 | tf_op jit(solution)/shard_map/ppermute | solution.py:21
  27.8 0.0 collective-permute-done.7.refs_0_
  27.8 2.6 %shard_map.85 = (f32[128,1152]{1,0:T(8,128)S(1)}, f32[128,1152]{1,0:T(8,128)S(1)}, bf16[64,1152]{1,0:T(8,128)(2,1)S(1)}, bf16[64,1152]{1,0:T(8,128)(2,1)S(1)}, b...) custom-call(bf16[128,1152]{1,0:T(8,128)(2,1)S(1)} %shard_map.78.refs, ...), custom_call_target="tpu_custom_call" | custom-call | flops 1811939328 | tf_op jit(solution)/shard_map/pallas_call | solution.py:194
  30.4 0.1 collective-permute-start.9
  30.4 0.5 collective-permute-start.11
  30.9 1.8 %collective-permute-start.8 = (bf16[64,1152]{1,0:T(8,128)(2,1)S(1)}, bf16[64,1152]{1,0:T(8,128)(2,1)S(1)}, u32[]{:S(2)}, u32[]{:S(2)}) collective-permute-start(bf16[64,1152]{1,0:T(8,128)(2,1)S(1)} %get-tuple-element.30), channel_id=1, source_target_pairs={{0,2},{1,3},{2,0},{3,1},{4,6},{5,7},{6,4},{7,5},{8,10},{9,11},{10,... | collective-permute-start | bytes 442376 | tf_op jit(solution)/shard_map/ppermute | solution.py:21
  32.8 0.2 collective-permute-start.13
  33.0 0.0 collective-permute-done.9.recv
  33.0 0.1 shard_map.86.refs_0_
  33.0 0.1 collective-permute-start.12
  33.1 22.3 %all-gather = f32[256,128]{1,0:T(8,128)S(1)} all-gather(f32[16,128]{1,0:T(8,128)S(1)} %get-tuple-element.34), channel_id=2, replica_groups=mesh['groups'=2,'blk'=16] {'blk'}, dimensions={0}, use_global_device_ids=true | all-gather | bytes 139264 | tf_op jit(solution)/shard_map/all_gather | solution.py:325
  55.4 0.0 collective-permute-done.8.recv
  55.5 3.8 %collective-permute-start.10 = (bf16[64,1152]{1,0:T(8,128)(2,1)S(1)}, bf16[64,1152]{1,0:T(8,128)(2,1)S(1)}, u32[]{:S(2)}, u32[]{:S(2)}) collective-permute-start(bf16[64,1152]{1,0:T(8,128)(2,1)S(1)} %shard_map.87.refs_0_), channel_id=1, source_target_pairs={{0,4},{1,5},{2,6},{3,7},{4,0},{5,1},{6,2},{7,3},{8,12},{9,13},{10,... | collective-permute-start | bytes 442376 | tf_op jit(solution)/shard_map/ppermute | solution.py:21
  59.3 0.0 collective-permute-done.13.recv
  59.3 0.1 collective-permute-start.16
  59.4 0.1 collective-permute-start.14
  59.5 2.0 %collective-permute-start.15 = (bf16[64,1152]{1,0:T(8,128)(2,1)S(1)}, bf16[64,1152]{1,0:T(8,128)(2,1)S(1)}, u32[]{:S(2)}, u32[]{:S(2)}) collective-permute-start(bf16[64,1152]{1,0:T(8,128)(2,1)S(1)} %get-tuple-element.43), channel_id=1, source_target_pairs={{0,2},{1,3},{2,0},{3,1},{4,6},{5,7},{6,4},{7,5},{8,10},{9,11},{10,... | collective-permute-start | bytes 442376 | tf_op jit(solution)/shard_map/ppermute | solution.py:21
  61.5 0.6 shard_map.88
  62.1 1.8 %collective-permute-done.10.refs_0_ = bf16[64,1152]{1,0:T(8,128)(2,1)S(1)} collective-permute-done((bf16[64,1152]{1,0:T(8,128)(2,1)S(1)}, bf16[64,1152]{1,0:T(8,128)(2,1)S(1)}, u32[]{:S(2)}, u32[]{:S(2)}) %collective-permute-start.10) | collective-permute-done | bytes 147488 | tf_op jit(solution)/shard_map/ppermute | solution.py:21
  63.9 0.6 shard_map.89
  64.5 1.6 %collective-permute-done.14.refs_6_ = bf16[64,1152]{1,0:T(8,128)(2,1)S(1)} collective-permute-done((bf16[64,1152]{1,0:T(8,128)(2,1)S(1)}, bf16[64,1152]{1,0:T(8,128)(2,1)S(1)}, u32[]{:S(2)}, u32[]{:S(2)}) %collective-permute-start.14) | collective-permute-done | bytes 147488 | tf_op jit(solution)/shard_map/ppermute | solution.py:21
  66.2 2.3 %collective-permute-done.15.refs_7_ = bf16[64,1152]{1,0:T(8,128)(2,1)S(1)} collective-permute-done((bf16[64,1152]{1,0:T(8,128)(2,1)S(1)}, bf16[64,1152]{1,0:T(8,128)(2,1)S(1)}, u32[]{:S(2)}, u32[]{:S(2)}) %collective-permute-start.15) | collective-permute-done | bytes 147488 | tf_op jit(solution)/shard_map/ppermute | solution.py:21
  68.4 1.3 %shard_map.92 = (bf16[128,1152]{1,0:T(8,128)(2,1)}, bf16[128,1152]{1,0:T(8,128)(2,1)}) custom-call(bf16[128,1152]{1,0:T(8,128)(2,1)S(1)} %copy-done.1, f32[128,1152]{1,0:T(8,128)S(1)} %get-tuple-element.28.refs_1_, bf16[128,1152]{1,0:T(8,128)(2,1)S(1)} %get-tuple-element.36.refs_2_, bf16[128,1152]{1,0:T(8,128)(2,1)S(1)} %get-tuple-element.37.refs_3_, ...), custom_call_target="tpu_custom_call" | custom-call | tf_op jit(solution)/shard_map/pallas_call | solution.py:262
  (10 shorter events, 0.1 us)
Async XLA Ops:
  0.6 21.5 %collective-permute-start.3 = (bf16[128,1152]{1,0:T(8,128)(2,1)}, bf16[128,1152]{1,0:T(8,128)(2,1)S(1)}, u32[]{:S(2)}, u32[]{:S(2)}) collective-permute-start(bf16[128,1152]{1,0:T(8,128)(2,1)} %refs_0_.1), channel_id=1, source_target_pairs={{0,1},{1,0},{2,3},{3,2},{4,5},{5,4},{6,7},{7,6},{8,9},{9,8},{10,11... | collective-permute-start | bytes 884744 | tf_op jit(solution)/shard_map/ppermute | solution.py:21
  1.1 23.3 %collective-permute-start.6 = (bf16[128,1152]{1,0:T(8,128)(2,1)}, bf16[128,1152]{1,0:T(8,128)(2,1)S(1)}, u32[]{:S(2)}, u32[]{:S(2)}) collective-permute-start(bf16[128,1152]{1,0:T(8,128)(2,1)} %refs_0_.1), channel_id=1, source_target_pairs={{0,8},{1,9},{2,10},{3,11},{4,12},{5,13},{6,14},{7,15},{8,0},{9,1},... | collective-permute-start | bytes 884744 | tf_op jit(solution)/shard_map/ppermute | solution.py:21
  4.8 16.0 %collective-permute-start = (bf16[128,1152]{1,0:T(8,128)(2,1)}, bf16[128,1152]{1,0:T(8,128)(2,1)S(1)}, u32[]{:S(2)}, u32[]{:S(2)}) collective-permute-start(bf16[128,1152]{1,0:T(8,128)(2,1)} %refs_4_.1), channel_id=1, source_target_pairs={{0,2},{1,3},{2,0},{3,1},{4,6},{5,7},{6,4},{7,5},{8,10},{9,11},{10,... | collective-permute-start | bytes 884744 | tf_op jit(solution)/shard_map/ppermute | solution.py:21
  7.3 11.9 %collective-permute-start.1 = (bf16[64,1152]{1,0:T(8,128)(2,1)S(1)}, bf16[64,1152]{1,0:T(8,128)(2,1)S(1)}, u32[]{:S(2)}, u32[]{:S(2)}) collective-permute-start(bf16[64,1152]{1,0:T(8,128)(2,1)S(1)} %get-tuple-element.49), channel_id=1, source_target_pairs={{0,4},{1,5},{2,6},{3,7},{4,0},{5,1},{6,2},{7,3},{8,12},{9,13},{10,... | collective-permute-start | bytes 442376 | tf_op jit(solution)/shard_map/ppermute | solution.py:21
  9.0 13.3 %collective-permute-start.2 = (bf16[64,1152]{1,0:T(8,128)(2,1)S(1)}, bf16[64,1152]{1,0:T(8,128)(2,1)S(1)}, u32[]{:S(2)}, u32[]{:S(2)}) collective-permute-start(bf16[64,1152]{1,0:T(8,128)(2,1)S(1)} %get-tuple-element.48), channel_id=1, source_target_pairs={{0,4},{1,5},{2,6},{3,7},{4,0},{5,1},{6,2},{7,3},{8,12},{9,13},{10,... | collective-permute-start | bytes 442376 | tf_op jit(solution)/shard_map/ppermute | solution.py:21
  19.4 1.6 %copy-start.1 = (bf16[128,1152]{1,0:T(8,128)(2,1)S(1)}, bf16[128,1152]{1,0:T(8,128)(2,1)}, u32[]{:S(2)}) copy-start(bf16[128,1152]{1,0:T(8,128)(2,1)} %refs_0_.1) | copy-start | bytes 884740
  19.4 6.7 %collective-permute-start.4 = (bf16[64,1152]{1,0:T(8,128)(2,1)S(1)}, bf16[64,1152]{1,0:T(8,128)(2,1)S(1)}, u32[]{:S(2)}, u32[]{:S(2)}) collective-permute-start(bf16[64,1152]{1,0:T(8,128)(2,1)S(1)} %shard_map.75.refs_0_.refs_1_), channel_id=1, source_target_pairs={{0,2},{1,3},{2,0},{3,1},{4,6},{5,7},{6,4},{7,5},{8,10},{9,11},{10,... | collective-permute-start | bytes 442376 | tf_op jit(solution)/shard_map/ppermute | solution.py:21
  21.0 1.0 %copy-start = (bf16[128,1152]{1,0:T(8,128)(2,1)S(1)}, bf16[128,1152]{1,0:T(8,128)(2,1)}, u32[]{:S(2)}) copy-start(bf16[128,1152]{1,0:T(8,128)(2,1)} %refs_4_.1) | copy-start | bytes 884740
  22.4 5.4 %collective-permute-start.5 = (bf16[64,1152]{1,0:T(8,128)(2,1)S(1)}, bf16[64,1152]{1,0:T(8,128)(2,1)S(1)}, u32[]{:S(2)}, u32[]{:S(2)}) collective-permute-start(bf16[64,1152]{1,0:T(8,128)(2,1)S(1)} %shard_map.80.refs_0_.refs_2_), channel_id=1, source_target_pairs={{0,2},{1,3},{2,0},{3,1},{4,6},{5,7},{6,4},{7,5},{8,10},{9,11},{10,... | collective-permute-start | bytes 442376 | tf_op jit(solution)/shard_map/ppermute | solution.py:21
  24.6 3.2 %collective-permute-start.7 = (bf16[128,1152]{1,0:T(8,128)(2,1)S(1)}, bf16[128,1152]{1,0:T(8,128)(2,1)S(1)}, u32[]{:S(2)}, u32[]{:S(2)}) collective-permute-start(bf16[128,1152]{1,0:T(8,128)(2,1)S(1)} %shard_map.83.refs_8_), channel_id=1, source_target_pairs={{0,1},{1,0},{2,3},{3,2},{4,5},{5,4},{6,7},{7,6},{8,9},{9,8},{10,11... | collective-permute-start | bytes 884744 | tf_op jit(solution)/shard_map/ppermute | solution.py:21
  30.4 2.6 %collective-permute-start.9 = (bf16[128,1152]{1,0:T(8,128)(2,1)S(1)}, bf16[128,1152]{1,0:T(8,128)(2,1)S(1)}, u32[]{:S(2)}, u32[]{:S(2)}) collective-permute-start(bf16[128,1152]{1,0:T(8,128)(2,1)S(1)} %get-tuple-element.32), channel_id=1, source_target_pairs={{0,1},{1,0},{2,3},{3,2},{4,5},{5,4},{6,7},{7,6},{8,9},{9,8},{10,11... | collective-permute-start | bytes 884744 | tf_op jit(solution)/shard_map/ppermute | solution.py:21
  30.4 29.1 %collective-permute-start.11 = (bf16[128,1152]{1,0:T(8,128)(2,1)S(1)}, bf16[128,1152]{1,0:T(8,128)(2,1)S(1)}, u32[]{:S(2)}, u32[]{:S(2)}) collective-permute-start(bf16[128,1152]{1,0:T(8,128)(2,1)S(1)} %get-tuple-element.33), channel_id=1, source_target_pairs={{0,1},{1,0},{2,3},{3,2},{4,5},{5,4},{6,7},{7,6},{8,9},{9,8},{10,11... | collective-permute-start | bytes 884744 | tf_op jit(solution)/shard_map/ppermute | solution.py:21
  30.9 24.5 %collective-permute-start.8 = (bf16[64,1152]{1,0:T(8,128)(2,1)S(1)}, bf16[64,1152]{1,0:T(8,128)(2,1)S(1)}, u32[]{:S(2)}, u32[]{:S(2)}) collective-permute-start(bf16[64,1152]{1,0:T(8,128)(2,1)S(1)} %get-tuple-element.30), channel_id=1, source_target_pairs={{0,2},{1,3},{2,0},{3,1},{4,6},{5,7},{6,4},{7,5},{8,10},{9,11},{10,... | collective-permute-start | bytes 442376 | tf_op jit(solution)/shard_map/ppermute | solution.py:21
  32.8 26.5 %collective-permute-start.13 = (bf16[64,1152]{1,0:T(8,128)(2,1)S(1)}, bf16[64,1152]{1,0:T(8,128)(2,1)S(1)}, u32[]{:S(2)}, u32[]{:S(2)}) collective-permute-start(bf16[64,1152]{1,0:T(8,128)(2,1)S(1)} %get-tuple-element.41), channel_id=1, source_target_pairs={{0,2},{1,3},{2,0},{3,1},{4,6},{5,7},{6,4},{7,5},{8,10},{9,11},{10,... | collective-permute-start | bytes 442376 | tf_op jit(solution)/shard_map/ppermute | solution.py:21
  33.0 30.9 %collective-permute-start.12 = (bf16[128,1152]{1,0:T(8,128)(2,1)S(1)}, bf16[128,1152]{1,0:T(8,128)(2,1)S(1)}, u32[]{:S(2)}, u32[]{:S(2)}) collective-permute-start(bf16[128,1152]{1,0:T(8,128)(2,1)S(1)} %shard_map.86.refs_0_), channel_id=1, source_target_pairs={{0,8},{1,9},{2,10},{3,11},{4,12},{5,13},{6,14},{7,15},{8,0},{9,1},... | collective-permute-start | bytes 884744 | tf_op jit(solution)/shard_map/ppermute | solution.py:21
  55.5 8.4 %collective-permute-start.10 = (bf16[64,1152]{1,0:T(8,128)(2,1)S(1)}, bf16[64,1152]{1,0:T(8,128)(2,1)S(1)}, u32[]{:S(2)}, u32[]{:S(2)}) collective-permute-start(bf16[64,1152]{1,0:T(8,128)(2,1)S(1)} %shard_map.87.refs_0_), channel_id=1, source_target_pairs={{0,4},{1,5},{2,6},{3,7},{4,0},{5,1},{6,2},{7,3},{8,12},{9,13},{10,... | collective-permute-start | bytes 442376 | tf_op jit(solution)/shard_map/ppermute | solution.py:21
  59.3 9.1 %collective-permute-start.16 = (bf16[64,1152]{1,0:T(8,128)(2,1)S(1)}, bf16[64,1152]{1,0:T(8,128)(2,1)S(1)}, u32[]{:S(2)}, u32[]{:S(2)}) collective-permute-start(bf16[64,1152]{1,0:T(8,128)(2,1)S(1)} %shard_map.90.refs_2_), channel_id=1, source_target_pairs={{0,4},{1,5},{2,6},{3,7},{4,0},{5,1},{6,2},{7,3},{8,12},{9,13},{10,... | collective-permute-start | bytes 442376 | tf_op jit(solution)/shard_map/ppermute | solution.py:21
  59.4 6.8 %collective-permute-start.14 = (bf16[64,1152]{1,0:T(8,128)(2,1)S(1)}, bf16[64,1152]{1,0:T(8,128)(2,1)S(1)}, u32[]{:S(2)}, u32[]{:S(2)}) collective-permute-start(bf16[64,1152]{1,0:T(8,128)(2,1)S(1)} %get-tuple-element.42), channel_id=1, source_target_pairs={{0,2},{1,3},{2,0},{3,1},{4,6},{5,7},{6,4},{7,5},{8,10},{9,11},{10,... | collective-permute-start | bytes 442376 | tf_op jit(solution)/shard_map/ppermute | solution.py:21
  59.5 8.9 %collective-permute-start.15 = (bf16[64,1152]{1,0:T(8,128)(2,1)S(1)}, bf16[64,1152]{1,0:T(8,128)(2,1)S(1)}, u32[]{:S(2)}, u32[]{:S(2)}) collective-permute-start(bf16[64,1152]{1,0:T(8,128)(2,1)S(1)} %get-tuple-element.43), channel_id=1, source_target_pairs={{0,2},{1,3},{2,0},{3,1},{4,6},{5,7},{6,4},{7,5},{8,10},{9,11},{10,... | collective-permute-start | bytes 442376 | tf_op jit(solution)/shard_map/ppermute | solution.py:21

commit v7 on v5

--- a/solution.py
+++ b/solution.py
@@ -9,8 +9,9 @@
 
 TILE_VMEM = 32 * 1024 * 1024
 SMALL_VMEM = 4 * 1024 * 1024
-GATHER_COST = 4_000_000_000
-RETURN_COST = 600_000_000
+GATHER_COST = 20_000_000_000
+SUMS_COST = 300_000_000
+RETURN_COST = 1_500_000_000
 VMEM = pl.BlockSpec(memory_space=pltpu.VMEM)
 ANY = pl.BlockSpec(memory_space=pl.ANY)
 
@@ -48,65 +49,65 @@
     return total
 
 
-def piece_kernel(count, value, *refs):
+def piece_kernel(value, *refs):
     unit = unit_rows(value[...])[0].astype(jnp.bfloat16)
-    size = value.shape[0] // count
-    for place, piece in enumerate(refs[-count:]):
-        piece[...] = unit[place * size : (place + 1) * size]
-
-
-def unit_call(kernel, value, outs, others):
+    start = 0
+    for piece in refs:
+        piece[...] = unit[start : start + piece.shape[0]]
+        start += piece.shape[0]
+
+
+def piece_skip_kernel(count, value, *refs):
+    piece_kernel(value, *refs[-count:])
+
+
+def unit_pieces(value, cuts, others):
+    rows, width = value.shape
     return pl.pallas_call(
-        kernel,
-        out_shape=outs,
+        functools.partial(piece_skip_kernel, len(cuts)),
+        out_shape=[jax.ShapeDtypeStruct((cut, width), jnp.bfloat16) for cut in cuts],
         in_specs=[VMEM] + [ANY] * len(others),
-        out_specs=[VMEM] * len(outs),
+        out_specs=[VMEM] * len(cuts),
         compiler_params=pltpu.CompilerParams(vmem_limit_bytes=SMALL_VMEM),
         cost_estimate=pl.CostEstimate(
-            flops=4 * value.size, bytes_accessed=4 * value.size, transcendentals=value.shape[0]
+            flops=4 * value.size, bytes_accessed=4 * value.size, transcendentals=rows
         ),
     )(value, *others)
 
 
-def unit_pieces(value, count, others):
-    rows, width = value.shape
-    outs = [jax.ShapeDtypeStruct((rows // count, width), jnp.bfloat16)] * count
-    return unit_call(functools.partial(piece_kernel, count), value, outs, others)
-
-
-def landed(arrays, costs):
-    out = []
-    for value, cost in zip(arrays, costs):
-        out += held([value], out[-1:], cost)
-    return out
-
-
 def gathered(image, text, img_bits, txt_bits):
-    half = image.shape[0] // 2
-    raw = [swapped(image[:half], img_bits[0]), swapped(image[half:], img_bits[0])]
-    img_raw = [swapped(image, bit) for bit in img_bits[1:]]
-    txt_raw = [swapped(text, bit) for bit in txt_bits]
+    img_raw = [swapped(image, bit) for bit in img_bits]
+    txt_raw = swapped(text, txt_bits[0])
+    rows = image.shape[0]
+    cuts = [rows * 5 // 8, rows * 3 // 8]
     imgs, txts = {}, {}
-    imgs[1] = unit_pieces(raw[0], 1, [])
-    others = imgs[1]
-    for place, value in enumerate(img_raw):
-        imgs[2 << place] = others = unit_pieces(value, 2, others[:1])
-    txts[0] = unit_pieces(text, 1, others[:1])
-    imgs[0] = unit_pieces(image, 1, txts[0])
-    others = imgs[0]
+    others = []
+    for place in reversed(range(1, len(img_bits))):
+        imgs[1 << place] = unit_pieces(img_raw[place], cuts, others)
+        others = imgs[1 << place][:1]
+    txts[0] = unit_pieces(text, [rows], others)
+    imgs[0] = unit_pieces(image, [rows], txts[0])
     for place in range(1, len(txt_bits)):
-        txts[1 << place] = others = unit_pieces(txt_raw[place], 1, others)
-    imgs[1] = imgs[1] + unit_pieces(raw[1], 1, others)
-    txts[1] = unit_pieces(txt_raw[0], 1, imgs[1][1:])
-    for blocks, bits in ((txts, txt_bits), (imgs, img_bits)):
-        for offset in range(1 << len(bits)):
-            if offset not in blocks:
-                place = offset.bit_length() - 1
-                blocks[offset] = [swapped(p, bits[place]) for p in blocks[offset ^ 1 << place]]
+        txts[1 << place] = [swapped(txts[0][0], txt_bits[place])]
+    imgs[1] = unit_pieces(img_raw[0], cuts, imgs[0])
+    txts[1] = unit_pieces(txt_raw, [rows], imgs[1][:1])
+    for offset in range(1 << len(img_bits)):
+        if offset not in imgs:
+            high = offset.bit_length() - 1
+            low = (offset & -offset).bit_length() - 1
+            imgs[offset] = [
+                swapped(imgs[offset ^ 1 << high][0], img_bits[high]),
+                swapped(imgs[offset ^ 1 << low][1], img_bits[low]),
+            ]
+    for offset in range(1 << len(txt_bits)):
+        if offset not in txts:
+            high = offset.bit_length() - 1
+            txts[offset] = [swapped(txts[offset ^ 1 << high][0], txt_bits[high])]
     imgs = [imgs[offset] for offset in range(1 << len(img_bits))]
     txts = [txts[offset] for offset in range(1 << len(txt_bits))]
-    order = landed(imgs[-1] + txts[-1], [GATHER_COST] * len(imgs[-1]) + [0])
-    imgs[-1], txts[-1] = order[:-1], order[-1:]
+    last = held(imgs[-1][1:], [], GATHER_COST)
+    imgs[-1] = held(imgs[-1][:1], last, GATHER_COST) + last
+    txts[-1] = held(txts[-1], imgs[-1][:1])
     return imgs, txts
 
 
@@ -183,7 +184,7 @@
     n_img, n_txt = len(imgs), len(txts)
     flat = [piece for block in imgs + txts for piece in block]
     pairs = n_img * n_txt * rows * rows
-    img_cuts = [2 if at >= n_img // 2 else 1 for at in range(n_img)]
+    img_cuts = [1] * n_img
     txt_cuts = [1] * n_txt
     outs = []
     for cuts in (img_cuts, txt_cuts):
@@ -254,57 +255,75 @@
     )(sums, sums_recv, *flat)
 
 
-def add_kernel(count, at, *refs):
-    keep, recv = refs[:2]
-    out = refs[-count]
-    kept = keep[...] if keep.shape == recv.shape else keep[pl.ds(at, recv.shape[0])]
-    out[...] = (kept + recv[...].astype(jnp.float32)).astype(out.dtype)
-    if count == 2:
-        refs[-1][...] = refs[2][...] + refs[3][...]
-
-
-def add_call(keep, recv, at, dtype, sums, bit, others):
-    operands = [keep, recv]
-    outs = [jax.ShapeDtypeStruct(recv.shape, dtype)]
-    if bit is not None:
-        operands += [sums, swapped(sums, bit)]
-        outs.append(jax.ShapeDtypeStruct(sums.shape, sums.dtype))
-    results = pl.pallas_call(
-        functools.partial(add_kernel, len(outs), at),
+def add_kernel(keep, recv, *refs):
+    out = refs[-1]
+    out[...] = (keep[...] + recv[...].astype(jnp.float32)).astype(out.dtype)
+
+
+def sums_kernel(*refs):
+    total = refs[0][...]
+    for sums in refs[1:-1]:
+        total = total + sums[...]
+    refs[-1][...] = total
+
+
+def sums_call(sums):
+    return pl.pallas_call(
+        sums_kernel,
+        out_shape=jax.ShapeDtypeStruct(sums[0].shape, sums[0].dtype),
+        in_specs=[VMEM] * len(sums),
+        out_specs=VMEM,
+        compiler_params=pltpu.CompilerParams(vmem_limit_bytes=SMALL_VMEM),
+        cost_estimate=pl.CostEstimate(flops=SUMS_COST, bytes_accessed=0, transcendentals=0),
+    )(*sums)
+
+
+def add_sums_kernel(count, keep, recv, *refs):
+    total = refs[0][...]
+    for sums_recv in refs[1:count]:
+        total = total + sums_recv[...]
+    refs[-1][...] = total
+    add_kernel(keep, recv, refs[-2])
+
+
+def add_call(keep, recv, dtype, sums, others):
+    outs = [jax.ShapeDtypeStruct(keep.shape, dtype)]
+    kernel = add_kernel
+    if sums:
+        outs.append(jax.ShapeDtypeStruct(sums[0].shape, sums[0].dtype))
+        kernel = functools.partial(add_sums_kernel, len(sums))
+    return pl.pallas_call(
+        kernel,
         out_shape=outs,
-        in_specs=[VMEM] * len(operands) + [ANY] * len(others),
+        in_specs=[VMEM] * (2 + len(sums)) + [ANY] * len(others),
         out_specs=[VMEM] * len(outs),
         compiler_params=pltpu.CompilerParams(vmem_limit_bytes=SMALL_VMEM),
         cost_estimate=pl.CostEstimate(
             flops=keep.size, bytes_accessed=keep.size, transcendentals=0
         ),
-    )(*operands, *others)
-    return results if bit is not None else [results[0], sums]
-
-
-def returned(parts, bits, sums, sum_bits, others):
+    )(keep, recv, *sums, *others)
+
+
+def returned(parts, bits, sums, masks, others):
     parts = dict(enumerate(parts))
+    sums = [sums] + [swapped(sums, mask) for mask in masks]
     recvs = []
     for place in reversed(range(len(bits))):
-        arrived = []
+        arrived = {}
         for offset in range(1, 1 << place):
-            for at, piece in enumerate(parts.pop(offset | 1 << place)):
-                arrived.append((offset, at, swapped(piece, bits[place])))
-        new = {}
-        for offset, at, recv in arrived:
-            kept = parts[offset]
-            kept = kept[at] if len(kept) > 1 else kept[0]
+            arrived[offset] = swapped(parts.pop(offset | 1 << place), bits[place])
+        for offset, recv in arrived.items():
             kind = jnp.float32 if offset < 1 << (place - 1) else jnp.bfloat16
-            bit = sum_bits.pop(0) if len(sum_bits) > 1 else None
-            piece, sums = add_call(kept, recv, at * recv.shape[0], kind, sums, bit, others)
-            others = [piece]
-            new.setdefault(offset, []).append(piece)
-        sends = parts.pop(1 << place)
-        if len(sends) > 1 and arrived:
-            sends = held(sends, [piece])
-        recvs.append([swapped(piece, bits[place]) for piece in sends])
-        parts.update(new)
-    return parts[0][0], recvs, sums, others
+            parts[offset], *total = add_call(
+                parts[offset], recv, kind, sums if len(sums) > 1 else [], others
+            )
+            sums = total or sums
+            others = [parts[offset]]
+        send = parts.pop(1 << place)
+        if arrived and not masks:
+            send = held([send], others)[0]
+        recvs.append(swapped(send, bits[place]))
+    return parts[0], recvs, sums[0], others
 
 
 def shards(image_embeds, text_embeds, log_temp, bias):
@@ -317,12 +336,15 @@
     txt_bits = (all_bits[:1] + all_bits[split:])[::-1]
     imgs, txts = gathered(image_embeds, text_embeds, img_bits, txt_bits)
     img_parts, txt_parts, sums = tile_call(imgs, txts, log_temp.reshape(1, 1), bias.reshape(1, 1))
-    left = txt_bits[-1:] + img_bits + txt_bits[-2::-1]
-    txt_keep, txt_recvs, sums, others = returned(txt_parts, txt_bits, sums, left, [])
-    img_keep, img_recvs, sums, others = returned(img_parts, img_bits, sums, left, others)
-    for bit in left[:-1]:
+    img_parts, txt_parts = ([part[0] for part in parts] for parts in (img_parts, txt_parts))
+    masks = [sum(bit for at, bit in enumerate(img_bits) if 1 << at & pick) for pick in range(1, 1 << len(img_bits))]
+    txt_keep, txt_recvs, sums, others = returned(txt_parts, txt_bits, sums, txt_bits[-1:], [])
+    sums = sums_call([sums] + [swapped(sums, mask) for mask in masks])
+    img_keep, img_recvs, _, others = returned(img_parts, img_bits, sums, [], others + [sums])
+    for bit in txt_bits[1:-1]:
         sums = sums + swapped(sums, bit)
-    sums_recv, txt_recvs, img_recvs = landed_sides(swapped(sums, left[-1]), txt_recvs, img_recvs)
+    sums_recv = swapped(sums, txt_bits[0])
+    *txt_recvs, sums_recv = held(txt_recvs + [sums_recv], [], RETURN_COST)
     grad_text, grad_image, grad_bias, grad_temp = finish_call(
         sums,
         sums_recv,
@@ -332,14 +354,6 @@
     return (grad_image, grad_text, grad_temp.reshape(1), grad_bias.reshape(1))
 
 
-def landed_sides(sums, txt_recvs, img_recvs):
-    txts = [piece for recv in txt_recvs for piece in recv]
-    imgs = [piece for recv in img_recvs for piece in recv]
-    at = len(imgs) - len(img_recvs[-1])
-    first = held(imgs[at : at + 1] + txts, [], RETURN_COST)
-    return sums, first[1:], imgs[:at] + first[:1] + imgs[at + 1 :]
-
-
 def solution(mesh):
     in_specs = (P(("groups", "blk"), None), P(("groups", "blk"), None), P(), P())
     out_specs = (P(("groups", "blk"), None), P(("groups", "blk"), None), P("groups"), P("groups"))

time: 57.7 us -> 56.7 us (0.983)
  starting transfers between devices: 20.7 us -> 24.6 us
  waiting for transfers between devices: 27.9 us -> 24.4 us
  local copies, waits for them, and re-layouts: 1.82 us -> 0.73 us
    ppermute x21 -> x18, starting transfers between devices: 20.7 us -> 24.6 us  [swapped(): return lax.ppermute(x, 'blk', [(i, i ^ bit) for i in range(count)])]
    ppermute x21 -> x18, waiting for transfers between devices: 27.9 us -> 24.4 us  [swapped(): return lax.ppermute(x, 'blk', [(i, i ^ bit) for i in range(count)])]
    slice x1 -> x0, local copies, waits for them, and re-layouts: 1.01 us -> none  [gathered(): image[half:]]
  transfers between devices with their start and end apart: 21 -> 18, of which waited for: 8 -> 10; matrix products, arithmetic and copies ran while one was open for 2% -> 0% of each run, Pallas kernels for 2% -> 2%
where the time goes in v7:
time: 56.7 us; the launch traced here: 56.5 us
  starting transfers between devices  24.6 us (43%)
  waiting for transfers between devices  24.4 us (43%)
  Pallas kernels  4.77 us (8%)
  between operations  2.05 us (4%)
  local copies, waits for them, and re-layouts  0.73 us (1%)
    ppermute x18, starting transfers between devices, swapped(): return lax.ppermute(x, 'blk', [(i, i ^ bit) for i in range(count)])  24.6 us
    ppermute x18, waiting for transfers between devices, swapped(): return lax.ppermute(x, 'blk', [(i, i ^ bit) for i in range(count)])  24.4 us
    pallas_call x1, Pallas kernels, tile_call(): pl.pallas_call(functools.partial(tile_kernel, [len(block) for block in im...  2.6 us
    pallas_call x1, Pallas kernels, finish_call(): pl.pallas_call(functools.partial(finish_kernel, [len(recvs) for _, _, rec...  1.32 us
  transfers between devices with their start and end apart: 18, of which 10 were waited for; matrix products, arithmetic and copies ran while one was open for 0% of the time, Pallas kernels for 2%

profile of v7, /device:TPU:0, one launch (start us, length us, event | category | flops | bytes accessed | tf_op | source)
XLA Modules:
  0.0 56.5 jit_solution(138489169042559810)
XLA Ops:
  0.6 0.0 copy-start.1
  0.6 3.0 %collective-permute-start = (bf16[128,1152]{1,0:T(8,128)(2,1)}, bf16[128,1152]{1,0:T(8,128)(2,1)S(1)}, u32[]{:S(2)}, u32[]{:S(2)}) collective-permute-start(bf16[128,1152]{1,0:T(8,128)(2,1)} %refs_4_.1), channel_id=1, source_target_pairs={{0,2},{1,3},{2,0},{3,1},{4,6},{5,7},{6,4},{7,5},{8,10},{9,11},{10,... | collective-permute-start | bytes 884744 | tf_op jit(solution)/shard_map/ppermute | solution.py:21
  3.6 1.6 %collective-permute-start.1 = (bf16[128,1152]{1,0:T(8,128)(2,1)}, bf16[128,1152]{1,0:T(8,128)(2,1)S(1)}, u32[]{:S(2)}, u32[]{:S(2)}) collective-permute-start(bf16[128,1152]{1,0:T(8,128)(2,1)} %refs_4_.1), channel_id=1, source_target_pairs={{0,4},{1,5},{2,6},{3,7},{4,0},{5,1},{6,2},{7,3},{8,12},{9,13},{10,... | collective-permute-start | bytes 884744 | tf_op jit(solution)/shard_map/ppermute | solution.py:21
  5.2 2.6 %collective-permute-start.4 = (bf16[128,1152]{1,0:T(8,128)(2,1)}, bf16[128,1152]{1,0:T(8,128)(2,1)S(1)}, u32[]{:S(2)}, u32[]{:S(2)}) collective-permute-start(bf16[128,1152]{1,0:T(8,128)(2,1)} %refs_0_.1), channel_id=1, source_target_pairs={{0,8},{1,9},{2,10},{3,11},{4,12},{5,13},{6,14},{7,15},{8,0},{9,1},... | collective-permute-start | bytes 884744 | tf_op jit(solution)/shard_map/ppermute | solution.py:21
  7.8 3.1 %collective-permute-done.value = bf16[128,1152]{1,0:T(8,128)(2,1)S(1)} collective-permute-done((bf16[128,1152]{1,0:T(8,128)(2,1)}, bf16[128,1152]{1,0:T(8,128)(2,1)S(1)}, u32[]{:S(2)}, u32[]{:S(2)}) %collective-permute-start) | collective-permute-done | bytes 294944 | tf_op jit(solution)/shard_map/ppermute | solution.py:21
  10.9 0.1 shard_map.75
  11.0 1.9 %collective-permute-start.3 = (bf16[48,1152]{1,0:T(8,128)(2,1)S(1)}, bf16[48,1152]{1,0:T(8,128)(2,1)S(1)}, u32[]{:S(2)}, u32[]{:S(2)}) collective-permute-start(bf16[48,1152]{1,0:T(8,128)(2,1)S(1)} %get-tuple-element.29.refs_4_), channel_id=1, source_target_pairs={{0,4},{1,5},{2,6},{3,7},{4,0},{5,1},{6,2},{7,3},{8,12},{9,13},{10,... | collective-permute-start | bytes 331784 | tf_op jit(solution)/shard_map/ppermute | solution.py:21
  14.2 0.0 copy-start
  14.2 0.1 shard_map.76.refs_0_.refs_7_
  14.4 0.1 collective-permute-start.5
  14.5 0.7 %copy-done = bf16[128,1152]{1,0:T(8,128)(2,1)S(1)} copy-done((bf16[128,1152]{1,0:T(8,128)(2,1)S(1)}, bf16[128,1152]{1,0:T(8,128)(2,1)}, u32[]{:S(2)}) %copy-start) | copy-done | bytes 294936
  15.2 0.1 shard_map.77.refs_0_
  15.3 4.5 %collective-permute-done.1.value = bf16[128,1152]{1,0:T(8,128)(2,1)S(1)} collective-permute-done((bf16[128,1152]{1,0:T(8,128)(2,1)}, bf16[128,1152]{1,0:T(8,128)(2,1)S(1)}, u32[]{:S(2)}, u32[]{:S(2)}) %collective-permute-start.1) | collective-permute-done | bytes 294944 | tf_op jit(solution)/shard_map/ppermute | solution.py:21
  19.8 0.1 shard_map.78
  20.0 0.4 collective-permute-start.2
  20.4 0.0 collective-permute-done.4.value
  20.4 0.1 shard_map.81.refs_8_
  20.6 0.1 collective-permute-start.6
  20.6 0.4 collective-permute-done.3.refs_0_
  21.0 4.6 %collective-permute-done.2.refs_0_ = bf16[80,1152]{1,0:T(8,128)(2,1)S(1)} collective-permute-done((bf16[80,1152]{1,0:T(8,128)(2,1)S(1)}, bf16[80,1152]{1,0:T(8,128)(2,1)S(1)}, u32[]{:S(2)}, u32[]{:S(2)}) %collective-permute-start.2) | collective-permute-done | bytes 184352 | tf_op jit(solution)/shard_map/ppermute | solution.py:21
  25.6 0.0 collective-permute-done.6.refs_0_
  25.6 0.0 collective-permute-done.5.refs_9_
  25.6 2.6 %shard_map.83 = (f32[128,1152]{1,0:T(8,128)S(1)}, f32[128,1152]{1,0:T(8,128)S(1)}, bf16[128,1152]{1,0:T(8,128)(2,1)S(1)}, bf16[128,1152]{1,0:T(8,128)(2,1)S(1)},...) custom-call(bf16[128,1152]{1,0:T(8,128)(2,1)S(1)} %shard_map.77.refs, ...), custom_call_target="tpu_custom_call" | custom-call | flops 1811939328 | tf_op jit(solution)/shard_map/pallas_call | solution.py:194
  28.2 0.1 collective-permute-start.7
  28.3 0.4 collective-permute-start.15
  28.7 0.2 collective-permute-start.8
  28.9 0.3 collective-permute-start.12
  29.2 0.7 %collective-permute-done.8.refs_1_ = f32[16,128]{1,0:T(8,128)S(1)} collective-permute-done((f32[16,128]{1,0:T(8,128)S(1)}, f32[16,128]{1,0:T(8,128)S(1)}, u32[]{:S(2)}, u32[]{:S(2)}) %collective-permute-start.8) | collective-permute-done | bytes 8224 | tf_op jit(solution)/shard_map/ppermute | solution.py:21
  29.9 0.0 collective-permute-done.7.recv
  29.9 0.1 shard_map.84
  29.9 1.8 %collective-permute-start.13 = (bf16[128,1152]{1,0:T(8,128)(2,1)S(1)}, bf16[128,1152]{1,0:T(8,128)(2,1)S(1)}, u32[]{:S(2)}, u32[]{:S(2)}) collective-permute-start(bf16[128,1152]{1,0:T(8,128)(2,1)S(1)} %get-tuple-element.35.refs_0_), channel_id=1, source_target_pairs={{0,8},{1,9},{2,10},{3,11},{4,12},{5,13},{6,14},{7,15},{8,0},{9,1},... | collective-permute-start | bytes 884744 | tf_op jit(solution)/shard_map/ppermute | solution.py:21
  31.7 3.4 %collective-permute-start.11 = (f32[16,128]{1,0:T(8,128)S(1)}, f32[16,128]{1,0:T(8,128)S(1)}, u32[]{:S(2)}, u32[]{:S(2)}) collective-permute-start(f32[16,128]{1,0:T(8,128)S(1)} %get-tuple-element.33.refs_0_), channel_id=1, source_target_pairs={{0,6},{1,7},{2,4},{3,5},{4,2},{5,3},{6,0},{7,1},{8,14},{9,15},{10,... | collective-permute-start | bytes 24584 | tf_op jit(solution)/shard_map/ppermute | solution.py:21
  35.2 0.5 collective-permute-start.10
  35.7 2.9 %collective-permute-done.11.refs_3_ = f32[16,128]{1,0:T(8,128)S(1)} collective-permute-done((f32[16,128]{1,0:T(8,128)S(1)}, f32[16,128]{1,0:T(8,128)S(1)}, u32[]{:S(2)}, u32[]{:S(2)}) %collective-permute-start.11) | collective-permute-done | bytes 8224 | tf_op jit(solution)/shard_map/ppermute | solution.py:21
  38.6 3.4 %collective-permute-start.9 = (f32[16,128]{1,0:T(8,128)S(1)}, f32[16,128]{1,0:T(8,128)S(1)}, u32[]{:S(2)}, u32[]{:S(2)}) collective-permute-start(f32[16,128]{1,0:T(8,128)S(1)} %get-tuple-element.33.refs_0_), channel_id=1, source_target_pairs={{0,4},{1,5},{2,6},{3,7},{4,0},{5,1},{6,2},{7,3},{8,12},{9,13},{10,... | collective-permute-start | bytes 24584 | tf_op jit(solution)/shard_map/ppermute | solution.py:21
  42.0 0.0 collective-permute-done.10.refs_2_
  42.0 4.6 %collective-permute-done.9.refs_1_ = f32[16,128]{1,0:T(8,128)S(1)} collective-permute-done((f32[16,128]{1,0:T(8,128)S(1)}, f32[16,128]{1,0:T(8,128)S(1)}, u32[]{:S(2)}, u32[]{:S(2)}) %collective-permute-start.9) | collective-permute-done | bytes 8224 | tf_op jit(solution)/shard_map/ppermute | solution.py:21
  46.6 0.0 collective-permute-done.15.recv
  46.6 0.1 shard_map.87.refs_1_
  46.6 1.7 %collective-permute-start.16 = (bf16[128,1152]{1,0:T(8,128)(2,1)S(1)}, bf16[128,1152]{1,0:T(8,128)(2,1)S(1)}, u32[]{:S(2)}, u32[]{:S(2)}) collective-permute-start(bf16[128,1152]{1,0:T(8,128)(2,1)S(1)} %shard_map.88), channel_id=1, source_target_pairs={{0,2},{1,3},{2,0},{3,1},{4,6},{5,7},{6,4},{7,5},{8,10},{9,11},{10,... | collective-permute-start | bytes 884744 | tf_op jit(solution)/shard_map/ppermute | solution.py:21
  48.4 0.0 collective-permute-start.17
  48.4 3.0 %collective-permute-start.14 = (f32[16,128]{1,0:T(8,128)S(1)}, f32[16,128]{1,0:T(8,128)S(1)}, u32[]{:S(2)}, u32[]{:S(2)}) collective-permute-start(f32[16,128]{1,0:T(8,128)S(1)} %shard_map.85.refs_1_.sums), channel_id=1, source_target_pairs={{0,8},{1,9},{2,10},{3,11},{4,12},{5,13},{6,14},{7,15},{8,0},{9,1},... | collective-permute-start | bytes 24584 | tf_op jit(solution)/shard_map/ppermute | solution.py:21
  51.4 0.0 collective-permute-done.12.refs_0_
  51.4 1.7 %collective-permute-done.14.refs_2_ = f32[16,128]{1,0:T(8,128)S(1)} collective-permute-done((f32[16,128]{1,0:T(8,128)S(1)}, f32[16,128]{1,0:T(8,128)S(1)}, u32[]{:S(2)}, u32[]{:S(2)}) %collective-permute-start.14) | collective-permute-done | bytes 8224 | tf_op jit(solution)/shard_map/ppermute | solution.py:21
  53.1 0.0 collective-permute-done.13.refs_1_
  53.1 0.3 collective-permute-done.16.refs_6_
  53.4 1.8 %collective-permute-done.17.refs_7_ = bf16[128,1152]{1,0:T(8,128)(2,1)S(1)} collective-permute-done((bf16[128,1152]{1,0:T(8,128)(2,1)S(1)}, bf16[128,1152]{1,0:T(8,128)(2,1)S(1)}, u32[]{:S(2)}, u32[]{:S(2)}) %collective-permute-start.17) | collective-permute-done | bytes 294944 | tf_op jit(solution)/shard_map/ppermute | solution.py:21
  55.2 1.3 %shard_map.89 = (bf16[128,1152]{1,0:T(8,128)(2,1)}, bf16[128,1152]{1,0:T(8,128)(2,1)}, f32[1,1]{1,0:T(1,128)}, f32[1,1]{1,0:T(1,128)}) custom-call(f32[16,128]{1,0:T(8,128)S(1)} %shard_map.85.refs_1_.sums, f32[16,128]{1,0:T(8,128)S(1)} %get-tuple-element.36.sums_recv, bf16[128,1152]{1,0:T(8,128)(2,1)S(1)} %copy-done.1, ...), custom_call_target="tpu_custom_call" | custom-call | tf_op jit(solution)/shard_map/pallas_call | solution.py:248
  (7 shorter events, 0.0 us)
Async XLA Ops:
  0.6 13.6 %copy-start.1 = (bf16[128,1152]{1,0:T(8,128)(2,1)S(1)}, bf16[128,1152]{1,0:T(8,128)(2,1)}, u32[]{:S(2)}) copy-start(bf16[128,1152]{1,0:T(8,128)(2,1)} %refs_0_.1) | copy-start | bytes 884740
  0.6 10.2 %collective-permute-start = (bf16[128,1152]{1,0:T(8,128)(2,1)}, bf16[128,1152]{1,0:T(8,128)(2,1)S(1)}, u32[]{:S(2)}, u32[]{:S(2)}) collective-permute-start(bf16[128,1152]{1,0:T(8,128)(2,1)} %refs_4_.1), channel_id=1, source_target_pairs={{0,2},{1,3},{2,0},{3,1},{4,6},{5,7},{6,4},{7,5},{8,10},{9,11},{10,... | collective-permute-start | bytes 884744 | tf_op jit(solution)/shard_map/ppermute | solution.py:21
  3.6 16.2 %collective-permute-start.1 = (bf16[128,1152]{1,0:T(8,128)(2,1)}, bf16[128,1152]{1,0:T(8,128)(2,1)S(1)}, u32[]{:S(2)}, u32[]{:S(2)}) collective-permute-start(bf16[128,1152]{1,0:T(8,128)(2,1)} %refs_4_.1), channel_id=1, source_target_pairs={{0,4},{1,5},{2,6},{3,7},{4,0},{5,1},{6,2},{7,3},{8,12},{9,13},{10,... | collective-permute-start | bytes 884744 | tf_op jit(solution)/shard_map/ppermute | solution.py:21
  5.2 15.2 %collective-permute-start.4 = (bf16[128,1152]{1,0:T(8,128)(2,1)}, bf16[128,1152]{1,0:T(8,128)(2,1)S(1)}, u32[]{:S(2)}, u32[]{:S(2)}) collective-permute-start(bf16[128,1152]{1,0:T(8,128)(2,1)} %refs_0_.1), channel_id=1, source_target_pairs={{0,8},{1,9},{2,10},{3,11},{4,12},{5,13},{6,14},{7,15},{8,0},{9,1},... | collective-permute-start | bytes 884744 | tf_op jit(solution)/shard_map/ppermute | solution.py:21
  11.0 10.0 %collective-permute-start.3 = (bf16[48,1152]{1,0:T(8,128)(2,1)S(1)}, bf16[48,1152]{1,0:T(8,128)(2,1)S(1)}, u32[]{:S(2)}, u32[]{:S(2)}) collective-permute-start(bf16[48,1152]{1,0:T(8,128)(2,1)S(1)} %get-tuple-element.29.refs_4_), channel_id=1, source_target_pairs={{0,4},{1,5},{2,6},{3,7},{4,0},{5,1},{6,2},{7,3},{8,12},{9,13},{10,... | collective-permute-start | bytes 331784 | tf_op jit(solution)/shard_map/ppermute | solution.py:21
  14.2 1.0 %copy-start = (bf16[128,1152]{1,0:T(8,128)(2,1)S(1)}, bf16[128,1152]{1,0:T(8,128)(2,1)}, u32[]{:S(2)}) copy-start(bf16[128,1152]{1,0:T(8,128)(2,1)} %refs_4_.1) | copy-start | bytes 884740
  14.4 11.2 %collective-permute-start.5 = (bf16[128,1152]{1,0:T(8,128)(2,1)S(1)}, bf16[128,1152]{1,0:T(8,128)(2,1)S(1)}, u32[]{:S(2)}, u32[]{:S(2)}) collective-permute-start(bf16[128,1152]{1,0:T(8,128)(2,1)S(1)} %shard_map.76.refs_0_.refs_7_), channel_id=1, source_target_pairs={{0,1},{1,0},{2,3},{3,2},{4,5},{5,4},{6,7},{7,6},{8,9},{9,8},{10,11... | collective-permute-start | bytes 884744 | tf_op jit(solution)/shard_map/ppermute | solution.py:21
  20.0 5.6 %collective-permute-start.2 = (bf16[80,1152]{1,0:T(8,128)(2,1)S(1)}, bf16[80,1152]{1,0:T(8,128)(2,1)S(1)}, u32[]{:S(2)}, u32[]{:S(2)}) collective-permute-start(bf16[80,1152]{1,0:T(8,128)(2,1)S(1)} %get-tuple-element.27.refs_0_.refs_1_), channel_id=1, source_target_pairs={{0,2},{1,3},{2,0},{3,1},{4,6},{5,7},{6,4},{7,5},{8,10},{9,11},{10,... | collective-permute-start | bytes 552968 | tf_op jit(solution)/shard_map/ppermute | solution.py:21
  20.6 5.0 %collective-permute-start.6 = (bf16[128,1152]{1,0:T(8,128)(2,1)S(1)}, bf16[128,1152]{1,0:T(8,128)(2,1)S(1)}, u32[]{:S(2)}, u32[]{:S(2)}) collective-permute-start(bf16[128,1152]{1,0:T(8,128)(2,1)S(1)} %shard_map.81.refs_8_), channel_id=1, source_target_pairs={{0,1},{1,0},{2,3},{3,2},{4,5},{5,4},{6,7},{7,6},{8,9},{9,8},{10,11... | collective-permute-start | bytes 884744 | tf_op jit(solution)/shard_map/ppermute | solution.py:21
  28.2 1.7 %collective-permute-start.7 = (bf16[128,1152]{1,0:T(8,128)(2,1)S(1)}, bf16[128,1152]{1,0:T(8,128)(2,1)S(1)}, u32[]{:S(2)}, u32[]{:S(2)}) collective-permute-start(bf16[128,1152]{1,0:T(8,128)(2,1)S(1)} %get-tuple-element.31), channel_id=1, source_target_pairs={{0,1},{1,0},{2,3},{3,2},{4,5},{5,4},{6,7},{7,6},{8,9},{9,8},{10,11... | collective-permute-start | bytes 884744 | tf_op jit(solution)/shard_map/ppermute | solution.py:21
  28.3 18.3 %collective-permute-start.15 = (bf16[128,1152]{1,0:T(8,128)(2,1)S(1)}, bf16[128,1152]{1,0:T(8,128)(2,1)S(1)}, u32[]{:S(2)}, u32[]{:S(2)}) collective-permute-start(bf16[128,1152]{1,0:T(8,128)(2,1)S(1)} %get-tuple-element.43), channel_id=1, source_target_pairs={{0,2},{1,3},{2,0},{3,1},{4,6},{5,7},{6,4},{7,5},{8,10},{9,11},{10,... | collective-permute-start | bytes 884744 | tf_op jit(solution)/shard_map/ppermute | solution.py:21
  28.7 1.2 %collective-permute-start.8 = (f32[16,128]{1,0:T(8,128)S(1)}, f32[16,128]{1,0:T(8,128)S(1)}, u32[]{:S(2)}, u32[]{:S(2)}) collective-permute-start(f32[16,128]{1,0:T(8,128)S(1)} %get-tuple-element.32.refs_0_), channel_id=1, source_target_pairs={{0,1},{1,0},{2,3},{3,2},{4,5},{5,4},{6,7},{7,6},{8,9},{9,8},{10,11... | collective-permute-start | bytes 24584 | tf_op jit(solution)/shard_map/ppermute | solution.py:21
  28.9 22.5 %collective-permute-start.12 = (bf16[128,1152]{1,0:T(8,128)(2,1)S(1)}, bf16[128,1152]{1,0:T(8,128)(2,1)S(1)}, u32[]{:S(2)}, u32[]{:S(2)}) collective-permute-start(bf16[128,1152]{1,0:T(8,128)(2,1)S(1)} %get-tuple-element.34), channel_id=1, source_target_pairs={{0,1},{1,0},{2,3},{3,2},{4,5},{5,4},{6,7},{7,6},{8,9},{9,8},{10,11... | collective-permute-start | bytes 884744 | tf_op jit(solution)/shard_map/ppermute | solution.py:21
  29.9 23.2 %collective-permute-start.13 = (bf16[128,1152]{1,0:T(8,128)(2,1)S(1)}, bf16[128,1152]{1,0:T(8,128)(2,1)S(1)}, u32[]{:S(2)}, u32[]{:S(2)}) collective-permute-start(bf16[128,1152]{1,0:T(8,128)(2,1)S(1)} %get-tuple-element.35.refs_0_), channel_id=1, source_target_pairs={{0,8},{1,9},{2,10},{3,11},{4,12},{5,13},{6,14},{7,15},{8,0},{9,1},... | collective-permute-start | bytes 884744 | tf_op jit(solution)/shard_map/ppermute | solution.py:21
  31.7 6.8 %collective-permute-start.11 = (f32[16,128]{1,0:T(8,128)S(1)}, f32[16,128]{1,0:T(8,128)S(1)}, u32[]{:S(2)}, u32[]{:S(2)}) collective-permute-start(f32[16,128]{1,0:T(8,128)S(1)} %get-tuple-element.33.refs_0_), channel_id=1, source_target_pairs={{0,6},{1,7},{2,4},{3,5},{4,2},{5,3},{6,0},{7,1},{8,14},{9,15},{10,... | collective-permute-start | bytes 24584 | tf_op jit(solution)/shard_map/ppermute | solution.py:21
  35.2 6.8 %collective-permute-start.10 = (f32[16,128]{1,0:T(8,128)S(1)}, f32[16,128]{1,0:T(8,128)S(1)}, u32[]{:S(2)}, u32[]{:S(2)}) collective-permute-start(f32[16,128]{1,0:T(8,128)S(1)} %get-tuple-element.33.refs_0_), channel_id=1, source_target_pairs={{0,2},{1,3},{2,0},{3,1},{4,6},{5,7},{6,4},{7,5},{8,10},{9,11},{10,... | collective-permute-start | bytes 24584 | tf_op jit(solution)/shard_map/ppermute | solution.py:21
  38.6 8.0 %collective-permute-start.9 = (f32[16,128]{1,0:T(8,128)S(1)}, f32[16,128]{1,0:T(8,128)S(1)}, u32[]{:S(2)}, u32[]{:S(2)}) collective-permute-start(f32[16,128]{1,0:T(8,128)S(1)} %get-tuple-element.33.refs_0_), channel_id=1, source_target_pairs={{0,4},{1,5},{2,6},{3,7},{4,0},{5,1},{6,2},{7,3},{8,12},{9,13},{10,... | collective-permute-start | bytes 24584 | tf_op jit(solution)/shard_map/ppermute | solution.py:21
  46.6 6.8 %collective-permute-start.16 = (bf16[128,1152]{1,0:T(8,128)(2,1)S(1)}, bf16[128,1152]{1,0:T(8,128)(2,1)S(1)}, u32[]{:S(2)}, u32[]{:S(2)}) collective-permute-start(bf16[128,1152]{1,0:T(8,128)(2,1)S(1)} %shard_map.88), channel_id=1, source_target_pairs={{0,2},{1,3},{2,0},{3,1},{4,6},{5,7},{6,4},{7,5},{8,10},{9,11},{10,... | collective-permute-start | bytes 884744 | tf_op jit(solution)/shard_map/ppermute | solution.py:21
  48.4 6.8 %collective-permute-start.17 = (bf16[128,1152]{1,0:T(8,128)(2,1)S(1)}, bf16[128,1152]{1,0:T(8,128)(2,1)S(1)}, u32[]{:S(2)}, u32[]{:S(2)}) collective-permute-start(bf16[128,1152]{1,0:T(8,128)(2,1)S(1)} %shard_map.87.refs_1_), channel_id=1, source_target_pairs={{0,4},{1,5},{2,6},{3,7},{4,0},{5,1},{6,2},{7,3},{8,12},{9,13},{10,... | collective-permute-start | bytes 884744 | tf_op jit(solution)/shard_map/ppermute | solution.py:21
  48.4 4.8 %collective-permute-start.14 = (f32[16,128]{1,0:T(8,128)S(1)}, f32[16,128]{1,0:T(8,128)S(1)}, u32[]{:S(2)}, u32[]{:S(2)}) collective-permute-start(f32[16,128]{1,0:T(8,128)S(1)} %shard_map.85.refs_1_.sums), channel_id=1, source_target_pairs={{0,8},{1,9},{2,10},{3,11},{4,12},{5,13},{6,14},{7,15},{8,0},{9,1},... | collective-permute-start | bytes 24584 | tf_op jit(solution)/shard_map/ppermute | solution.py:21

commit v8 on v7

--- a/solution.py
+++ b/solution.py
@@ -11,7 +11,7 @@
 SMALL_VMEM = 4 * 1024 * 1024
 GATHER_COST = 20_000_000_000
 SUMS_COST = 300_000_000
-RETURN_COST = 1_500_000_000
+RETURN_COST = 1_000_000_000
 VMEM = pl.BlockSpec(memory_space=pltpu.VMEM)
 ANY = pl.BlockSpec(memory_space=pl.ANY)
 
@@ -260,53 +260,36 @@
     out[...] = (keep[...] + recv[...].astype(jnp.float32)).astype(out.dtype)
 
 
-def sums_kernel(*refs):
-    total = refs[0][...]
-    for sums in refs[1:-1]:
-        total = total + sums[...]
-    refs[-1][...] = total
-
-
-def sums_call(sums):
+def sums_kernel(first, second, *refs):
+    refs[-1][...] = first[...] + second[...]
+
+
+def sums_call(sums, others):
     return pl.pallas_call(
         sums_kernel,
         out_shape=jax.ShapeDtypeStruct(sums[0].shape, sums[0].dtype),
-        in_specs=[VMEM] * len(sums),
+        in_specs=[VMEM] * len(sums) + [ANY] * len(others),
         out_specs=VMEM,
         compiler_params=pltpu.CompilerParams(vmem_limit_bytes=SMALL_VMEM),
         cost_estimate=pl.CostEstimate(flops=SUMS_COST, bytes_accessed=0, transcendentals=0),
-    )(*sums)
-
-
-def add_sums_kernel(count, keep, recv, *refs):
-    total = refs[0][...]
-    for sums_recv in refs[1:count]:
-        total = total + sums_recv[...]
-    refs[-1][...] = total
-    add_kernel(keep, recv, refs[-2])
-
-
-def add_call(keep, recv, dtype, sums, others):
-    outs = [jax.ShapeDtypeStruct(keep.shape, dtype)]
-    kernel = add_kernel
-    if sums:
-        outs.append(jax.ShapeDtypeStruct(sums[0].shape, sums[0].dtype))
-        kernel = functools.partial(add_sums_kernel, len(sums))
+    )(*sums, *others)
+
+
+def add_call(keep, recv, dtype, others):
     return pl.pallas_call(
-        kernel,
-        out_shape=outs,
-        in_specs=[VMEM] * (2 + len(sums)) + [ANY] * len(others),
-        out_specs=[VMEM] * len(outs),
+        add_kernel,
+        out_shape=jax.ShapeDtypeStruct(keep.shape, dtype),
+        in_specs=[VMEM] * 2 + [ANY] * len(others),
+        out_specs=VMEM,
         compiler_params=pltpu.CompilerParams(vmem_limit_bytes=SMALL_VMEM),
         cost_estimate=pl.CostEstimate(
             flops=keep.size, bytes_accessed=keep.size, transcendentals=0
         ),
-    )(keep, recv, *sums, *others)
-
-
-def returned(parts, bits, sums, masks, others):
+    )(keep, recv, *others)
+
+
+def returned(parts, bits, others, wait):
     parts = dict(enumerate(parts))
-    sums = [sums] + [swapped(sums, mask) for mask in masks]
     recvs = []
     for place in reversed(range(len(bits))):
         arrived = {}
@@ -314,16 +297,13 @@
             arrived[offset] = swapped(parts.pop(offset | 1 << place), bits[place])
         for offset, recv in arrived.items():
             kind = jnp.float32 if offset < 1 << (place - 1) else jnp.bfloat16
-            parts[offset], *total = add_call(
-                parts[offset], recv, kind, sums if len(sums) > 1 else [], others
-            )
-            sums = total or sums
+            parts[offset] = add_call(parts[offset], recv, kind, others)
             others = [parts[offset]]
         send = parts.pop(1 << place)
-        if arrived and not masks:
+        if arrived and wait:
             send = held([send], others)[0]
         recvs.append(swapped(send, bits[place]))
-    return parts[0], recvs, sums[0], others
+    return parts[0], recvs, others
 
 
 def shards(image_embeds, text_embeds, log_temp, bias):
@@ -337,14 +317,12 @@
     imgs, txts = gathered(image_embeds, text_embeds, img_bits, txt_bits)
     img_parts, txt_parts, sums = tile_call(imgs, txts, log_temp.reshape(1, 1), bias.reshape(1, 1))
     img_parts, txt_parts = ([part[0] for part in parts] for parts in (img_parts, txt_parts))
-    masks = [sum(bit for at, bit in enumerate(img_bits) if 1 << at & pick) for pick in range(1, 1 << len(img_bits))]
-    txt_keep, txt_recvs, sums, others = returned(txt_parts, txt_bits, sums, txt_bits[-1:], [])
-    sums = sums_call([sums] + [swapped(sums, mask) for mask in masks])
-    img_keep, img_recvs, _, others = returned(img_parts, img_bits, sums, [], others + [sums])
-    for bit in txt_bits[1:-1]:
-        sums = sums + swapped(sums, bit)
-    sums_recv = swapped(sums, txt_bits[0])
-    *txt_recvs, sums_recv = held(txt_recvs + [sums_recv], [], RETURN_COST)
+    txt_keep, txt_recvs, others = returned(txt_parts, txt_bits, [], False)
+    for bit in txt_bits + img_bits[:0:-1]:
+        sums = sums_call([sums, swapped(sums, bit)], others)
+    img_keep, img_recvs, others = returned(img_parts, img_bits, others + [sums], True)
+    sums_recv = swapped(sums, img_bits[0])
+    txt_recvs = held(txt_recvs, [], RETURN_COST)
     grad_text, grad_image, grad_bias, grad_temp = finish_call(
         sums,
         sums_recv,

time: 56.7 us -> 54.4 us (0.959)
  starting transfers between devices: 24.6 us -> 18.6 us
  waiting for transfers between devices: 24.4 us -> 27.5 us
    ppermute x18 -> x17, starting transfers between devices: 24.6 us -> 18.6 us  [swapped(): return lax.ppermute(x, 'blk', [(i, i ^ bit) for i in range(count)])]
    ppermute x18 -> x17, waiting for transfers between devices: 24.4 us -> 27.5 us  [swapped(): return lax.ppermute(x, 'blk', [(i, i ^ bit) for i in range(count)])]
  transfers between devices with their start and end apart: 18 -> 17, of which waited for: 10 -> 9; matrix products, arithmetic and copies ran while one was open for 0% -> 0% of each run, Pallas kernels for 2% -> 2%
where the time goes in v8:
time: 54.4 us; the launch traced here: 53.6 us
  waiting for transfers between devices  27.5 us (51%)
  starting transfers between devices  18.6 us (34%)
  Pallas kernels  4.77 us (9%)
  between operations  2.04 us (4%)
  local copies, waits for them, and re-layouts  0.73 us (1%)
    ppermute x17, waiting for transfers between devices, swapped(): return lax.ppermute(x, 'blk', [(i, i ^ bit) for i in range(count)])  27.5 us
    ppermute x17, starting transfers between devices, swapped(): return lax.ppermute(x, 'blk', [(i, i ^ bit) for i in range(count)])  18.6 us
    pallas_call x1, Pallas kernels, tile_call(): pl.pallas_call(functools.partial(tile_kernel, [len(block) for block in im...  2.6 us
    pallas_call x1, Pallas kernels, finish_call(): pl.pallas_call(functools.partial(finish_kernel, [len(recvs) for _, _, rec...  1.32 us
  transfers between devices with their start and end apart: 17, of which 9 were waited for; matrix products, arithmetic and copies ran while one was open for 0% of the time, Pallas kernels for 2%

profile of v8, /device:TPU:0, one launch (start us, length us, event | category | flops | bytes accessed | tf_op | source)
XLA Modules:
  0.0 53.6 jit_solution(7956432031242716209)
XLA Ops:
  0.6 0.0 copy-start.1
  0.6 3.0 %collective-permute-start = (bf16[128,1152]{1,0:T(8,128)(2,1)}, bf16[128,1152]{1,0:T(8,128)(2,1)S(1)}, u32[]{:S(2)}, u32[]{:S(2)}) collective-permute-start(bf16[128,1152]{1,0:T(8,128)(2,1)} %refs_4_.1), channel_id=1, source_target_pairs={{0,2},{1,3},{2,0},{3,1},{4,6},{5,7},{6,4},{7,5},{8,10},{9,11},{10,... | collective-permute-start | bytes 884744 | tf_op jit(solution)/shard_map/ppermute | solution.py:21
  3.6 1.6 %collective-permute-start.1 = (bf16[128,1152]{1,0:T(8,128)(2,1)}, bf16[128,1152]{1,0:T(8,128)(2,1)S(1)}, u32[]{:S(2)}, u32[]{:S(2)}) collective-permute-start(bf16[128,1152]{1,0:T(8,128)(2,1)} %refs_4_.1), channel_id=1, source_target_pairs={{0,4},{1,5},{2,6},{3,7},{4,0},{5,1},{6,2},{7,3},{8,12},{9,13},{10,... | collective-permute-start | bytes 884744 | tf_op jit(solution)/shard_map/ppermute | solution.py:21
  5.2 2.6 %collective-permute-start.4 = (bf16[128,1152]{1,0:T(8,128)(2,1)}, bf16[128,1152]{1,0:T(8,128)(2,1)S(1)}, u32[]{:S(2)}, u32[]{:S(2)}) collective-permute-start(bf16[128,1152]{1,0:T(8,128)(2,1)} %refs_0_.1), channel_id=1, source_target_pairs={{0,8},{1,9},{2,10},{3,11},{4,12},{5,13},{6,14},{7,15},{8,0},{9,1},... | collective-permute-start | bytes 884744 | tf_op jit(solution)/shard_map/ppermute | solution.py:21
  7.8 3.1 %collective-permute-done.value = bf16[128,1152]{1,0:T(8,128)(2,1)S(1)} collective-permute-done((bf16[128,1152]{1,0:T(8,128)(2,1)}, bf16[128,1152]{1,0:T(8,128)(2,1)S(1)}, u32[]{:S(2)}, u32[]{:S(2)}) %collective-permute-start) | collective-permute-done | bytes 294944 | tf_op jit(solution)/shard_map/ppermute | solution.py:21
  10.9 0.1 shard_map.75
  11.0 1.9 %collective-permute-start.3 = (bf16[48,1152]{1,0:T(8,128)(2,1)S(1)}, bf16[48,1152]{1,0:T(8,128)(2,1)S(1)}, u32[]{:S(2)}, u32[]{:S(2)}) collective-permute-start(bf16[48,1152]{1,0:T(8,128)(2,1)S(1)} %get-tuple-element.26.refs_4_), channel_id=1, source_target_pairs={{0,4},{1,5},{2,6},{3,7},{4,0},{5,1},{6,2},{7,3},{8,12},{9,13},{10,... | collective-permute-start | bytes 331784 | tf_op jit(solution)/shard_map/ppermute | solution.py:21
  14.2 0.0 copy-done.1
  14.2 0.0 copy-start
  14.2 0.1 shard_map.76.refs_0_.refs_7_
  14.4 0.1 collective-permute-start.5
  14.5 0.7 %copy-done = bf16[128,1152]{1,0:T(8,128)(2,1)S(1)} copy-done((bf16[128,1152]{1,0:T(8,128)(2,1)S(1)}, bf16[128,1152]{1,0:T(8,128)(2,1)}, u32[]{:S(2)}) %copy-start) | copy-done | bytes 294936
  15.2 0.1 shard_map.77.refs_0_
  15.3 4.5 %collective-permute-done.1.value = bf16[128,1152]{1,0:T(8,128)(2,1)S(1)} collective-permute-done((bf16[128,1152]{1,0:T(8,128)(2,1)}, bf16[128,1152]{1,0:T(8,128)(2,1)S(1)}, u32[]{:S(2)}, u32[]{:S(2)}) %collective-permute-start.1) | collective-permute-done | bytes 294944 | tf_op jit(solution)/shard_map/ppermute | solution.py:21
  19.8 0.1 shard_map.78
  20.0 0.4 collective-permute-start.2
  20.4 0.0 collective-permute-done.4.value
  20.4 0.1 shard_map.81.refs_8_
  20.6 0.1 collective-permute-start.6
  20.6 0.4 collective-permute-done.3.refs_0_
  21.0 4.6 %collective-permute-done.2.refs_0_ = bf16[80,1152]{1,0:T(8,128)(2,1)S(1)} collective-permute-done((bf16[80,1152]{1,0:T(8,128)(2,1)S(1)}, bf16[80,1152]{1,0:T(8,128)(2,1)S(1)}, u32[]{:S(2)}, u32[]{:S(2)}) %collective-permute-start.2) | collective-permute-done | bytes 184352 | tf_op jit(solution)/shard_map/ppermute | solution.py:21
  25.6 0.0 collective-permute-done.6.refs_0_
  25.6 0.0 collective-permute-done.5.refs_9_
  25.6 2.6 %shard_map.83 = (f32[128,1152]{1,0:T(8,128)S(1)}, f32[128,1152]{1,0:T(8,128)S(1)}, bf16[128,1152]{1,0:T(8,128)(2,1)S(1)}, bf16[128,1152]{1,0:T(8,128)(2,1)S(1)},...) custom-call(bf16[128,1152]{1,0:T(8,128)(2,1)S(1)} %shard_map.77.refs, ...), custom_call_target="tpu_custom_call" | custom-call | flops 1811939328 | tf_op jit(solution)/shard_map/pallas_call | solution.py:194
  28.2 0.1 collective-permute-start.8
  28.3 0.4 collective-permute-start.14
  28.7 1.7 %collective-permute-start.7 = (f32[16,128]{1,0:T(8,128)S(1)}, f32[16,128]{1,0:T(8,128)S(1)}, u32[]{:S(2)}, u32[]{:S(2)}) collective-permute-start(f32[16,128]{1,0:T(8,128)S(1)} %get-tuple-element.27.first), channel_id=1, source_target_pairs={{0,8},{1,9},{2,10},{3,11},{4,12},{5,13},{6,14},{7,15},{8,0},{9,1},... | collective-permute-start | bytes 24584 | tf_op jit(solution)/shard_map/ppermute | solution.py:21
  30.4 0.0 collective-permute-start.12
  30.4 0.0 collective-permute-done.8.recv
  30.5 0.1 shard_map.84.refs_0_
  30.5 1.2 %collective-permute-start.13 = (bf16[128,1152]{1,0:T(8,128)(2,1)S(1)}, bf16[128,1152]{1,0:T(8,128)(2,1)S(1)}, u32[]{:S(2)}, u32[]{:S(2)}) collective-permute-start(bf16[128,1152]{1,0:T(8,128)(2,1)S(1)} %shard_map.84.refs_0_), channel_id=1, source_target_pairs={{0,8},{1,9},{2,10},{3,11},{4,12},{5,13},{6,14},{7,15},{8,0},{9,1},... | collective-permute-start | bytes 884744 | tf_op jit(solution)/shard_map/ppermute | solution.py:21
  31.8 1.5 %collective-permute-done.7.second = f32[16,128]{1,0:T(8,128)S(1)} collective-permute-done((f32[16,128]{1,0:T(8,128)S(1)}, f32[16,128]{1,0:T(8,128)S(1)}, u32[]{:S(2)}, u32[]{:S(2)}) %collective-permute-start.7) | collective-permute-done | bytes 8224 | tf_op jit(solution)/shard_map/ppermute | solution.py:21
  33.3 0.0 collective-permute-start.9
  33.3 1.2 %collective-permute-done.9.second = f32[16,128]{1,0:T(8,128)S(1)} collective-permute-done((f32[16,128]{1,0:T(8,128)S(1)}, f32[16,128]{1,0:T(8,128)S(1)}, u32[]{:S(2)}, u32[]{:S(2)}) %collective-permute-start.9) | collective-permute-done | bytes 8224 | tf_op jit(solution)/shard_map/ppermute | solution.py:21
  34.4 1.7 %collective-permute-start.10 = (f32[16,128]{1,0:T(8,128)S(1)}, f32[16,128]{1,0:T(8,128)S(1)}, u32[]{:S(2)}, u32[]{:S(2)}) collective-permute-start(f32[16,128]{1,0:T(8,128)S(1)} %shard_map.86.first), channel_id=1, source_target_pairs={{0,2},{1,3},{2,0},{3,1},{4,6},{5,7},{6,4},{7,5},{8,10},{9,11},{10,... | collective-permute-start | bytes 24584 | tf_op jit(solution)/shard_map/ppermute | solution.py:21
  36.1 2.0 %collective-permute-done.10.second = f32[16,128]{1,0:T(8,128)S(1)} collective-permute-done((f32[16,128]{1,0:T(8,128)S(1)}, f32[16,128]{1,0:T(8,128)S(1)}, u32[]{:S(2)}, u32[]{:S(2)}) %collective-permute-start.10) | collective-permute-done | bytes 8224 | tf_op jit(solution)/shard_map/ppermute | solution.py:21
  38.1 0.0 collective-permute-done.14.recv
  38.1 0.1 shard_map.89.refs_1_
  38.2 1.7 %collective-permute-start.15 = (bf16[128,1152]{1,0:T(8,128)(2,1)S(1)}, bf16[128,1152]{1,0:T(8,128)(2,1)S(1)}, u32[]{:S(2)}, u32[]{:S(2)}) collective-permute-start(bf16[128,1152]{1,0:T(8,128)(2,1)S(1)} %shard_map.90), channel_id=1, source_target_pairs={{0,2},{1,3},{2,0},{3,1},{4,6},{5,7},{6,4},{7,5},{8,10},{9,11},{10,... | collective-permute-start | bytes 884744 | tf_op jit(solution)/shard_map/ppermute | solution.py:21
  39.9 1.1 %collective-permute-start.16 = (bf16[128,1152]{1,0:T(8,128)(2,1)S(1)}, bf16[128,1152]{1,0:T(8,128)(2,1)S(1)}, u32[]{:S(2)}, u32[]{:S(2)}) collective-permute-start(bf16[128,1152]{1,0:T(8,128)(2,1)S(1)} %shard_map.89.refs_1_), channel_id=1, source_target_pairs={{0,4},{1,5},{2,6},{3,7},{4,0},{5,1},{6,2},{7,3},{8,12},{9,13},{10,... | collective-permute-start | bytes 884744 | tf_op jit(solution)/shard_map/ppermute | solution.py:21
  41.0 0.9 %collective-permute-start.11 = (f32[16,128]{1,0:T(8,128)S(1)}, f32[16,128]{1,0:T(8,128)S(1)}, u32[]{:S(2)}, u32[]{:S(2)}) collective-permute-start(f32[16,128]{1,0:T(8,128)S(1)} %shard_map.87.refs_1_.sums), channel_id=1, source_target_pairs={{0,4},{1,5},{2,6},{3,7},{4,0},{5,1},{6,2},{7,3},{8,12},{9,13},{10,... | collective-permute-start | bytes 24584 | tf_op jit(solution)/shard_map/ppermute | solution.py:21
  41.9 0.0 collective-permute-done.12.refs_0_
  41.9 5.4 %collective-permute-done.13.refs_1_ = bf16[128,1152]{1,0:T(8,128)(2,1)S(1)} collective-permute-done((bf16[128,1152]{1,0:T(8,128)(2,1)S(1)}, bf16[128,1152]{1,0:T(8,128)(2,1)S(1)}, u32[]{:S(2)}, u32[]{:S(2)}) %collective-permute-start.13) | collective-permute-done | bytes 294944 | tf_op jit(solution)/shard_map/ppermute | solution.py:21
  47.3 5.0 %collective-permute-done.11.sums_recv = f32[16,128]{1,0:T(8,128)S(1)} collective-permute-done((f32[16,128]{1,0:T(8,128)S(1)}, f32[16,128]{1,0:T(8,128)S(1)}, u32[]{:S(2)}, u32[]{:S(2)}) %collective-permute-start.11) | collective-permute-done | bytes 8224 | tf_op jit(solution)/shard_map/ppermute | solution.py:21
  52.3 0.0 collective-permute-done.15.refs_6_
  52.3 0.0 collective-permute-done.16.refs_7_
  52.3 1.3 %shard_map.91 = (bf16[128,1152]{1,0:T(8,128)(2,1)}, bf16[128,1152]{1,0:T(8,128)(2,1)}, f32[1,1]{1,0:T(1,128)}, f32[1,1]{1,0:T(1,128)}) custom-call(f32[16,128]{1,0:T(8,128)S(1)} %shard_map.87.refs_1_.sums, f32[16,128]{1,0:T(8,128)S(1)} %collective-permute-done.11.sums_recv, bf16[128,1152]{1,0:T(8,128)(2,1)S(1)} %copy-done.1, ...), custom_call_target="tpu_custom_call" | custom-call | tf_op jit(solution)/shard_map/pallas_call | solution.py:248
  (8 shorter events, 0.0 us)
Async XLA Ops:
  0.6 13.6 %copy-start.1 = (bf16[128,1152]{1,0:T(8,128)(2,1)S(1)}, bf16[128,1152]{1,0:T(8,128)(2,1)}, u32[]{:S(2)}) copy-start(bf16[128,1152]{1,0:T(8,128)(2,1)} %refs_0_.1) | copy-start | bytes 884740
  0.6 10.2 %collective-permute-start = (bf16[128,1152]{1,0:T(8,128)(2,1)}, bf16[128,1152]{1,0:T(8,128)(2,1)S(1)}, u32[]{:S(2)}, u32[]{:S(2)}) collective-permute-start(bf16[128,1152]{1,0:T(8,128)(2,1)} %refs_4_.1), channel_id=1, source_target_pairs={{0,2},{1,3},{2,0},{3,1},{4,6},{5,7},{6,4},{7,5},{8,10},{9,11},{10,... | collective-permute-start | bytes 884744 | tf_op jit(solution)/shard_map/ppermute | solution.py:21
  3.6 16.2 %collective-permute-start.1 = (bf16[128,1152]{1,0:T(8,128)(2,1)}, bf16[128,1152]{1,0:T(8,128)(2,1)S(1)}, u32[]{:S(2)}, u32[]{:S(2)}) collective-permute-start(bf16[128,1152]{1,0:T(8,128)(2,1)} %refs_4_.1), channel_id=1, source_target_pairs={{0,4},{1,5},{2,6},{3,7},{4,0},{5,1},{6,2},{7,3},{8,12},{9,13},{10,... | collective-permute-start | bytes 884744 | tf_op jit(solution)/shard_map/ppermute | solution.py:21
  5.2 15.2 %collective-permute-start.4 = (bf16[128,1152]{1,0:T(8,128)(2,1)}, bf16[128,1152]{1,0:T(8,128)(2,1)S(1)}, u32[]{:S(2)}, u32[]{:S(2)}) collective-permute-start(bf16[128,1152]{1,0:T(8,128)(2,1)} %refs_0_.1), channel_id=1, source_target_pairs={{0,8},{1,9},{2,10},{3,11},{4,12},{5,13},{6,14},{7,15},{8,0},{9,1},... | collective-permute-start | bytes 884744 | tf_op jit(solution)/shard_map/ppermute | solution.py:21
  11.0 10.0 %collective-permute-start.3 = (bf16[48,1152]{1,0:T(8,128)(2,1)S(1)}, bf16[48,1152]{1,0:T(8,128)(2,1)S(1)}, u32[]{:S(2)}, u32[]{:S(2)}) collective-permute-start(bf16[48,1152]{1,0:T(8,128)(2,1)S(1)} %get-tuple-element.26.refs_4_), channel_id=1, source_target_pairs={{0,4},{1,5},{2,6},{3,7},{4,0},{5,1},{6,2},{7,3},{8,12},{9,13},{10,... | collective-permute-start | bytes 331784 | tf_op jit(solution)/shard_map/ppermute | solution.py:21
  14.2 1.0 %copy-start = (bf16[128,1152]{1,0:T(8,128)(2,1)S(1)}, bf16[128,1152]{1,0:T(8,128)(2,1)}, u32[]{:S(2)}) copy-start(bf16[128,1152]{1,0:T(8,128)(2,1)} %refs_4_.1) | copy-start | bytes 884740
  14.4 11.2 %collective-permute-start.5 = (bf16[128,1152]{1,0:T(8,128)(2,1)S(1)}, bf16[128,1152]{1,0:T(8,128)(2,1)S(1)}, u32[]{:S(2)}, u32[]{:S(2)}) collective-permute-start(bf16[128,1152]{1,0:T(8,128)(2,1)S(1)} %shard_map.76.refs_0_.refs_7_), channel_id=1, source_target_pairs={{0,1},{1,0},{2,3},{3,2},{4,5},{5,4},{6,7},{7,6},{8,9},{9,8},{10,11... | collective-permute-start | bytes 884744 | tf_op jit(solution)/shard_map/ppermute | solution.py:21
  20.0 5.6 %collective-permute-start.2 = (bf16[80,1152]{1,0:T(8,128)(2,1)S(1)}, bf16[80,1152]{1,0:T(8,128)(2,1)S(1)}, u32[]{:S(2)}, u32[]{:S(2)}) collective-permute-start(bf16[80,1152]{1,0:T(8,128)(2,1)S(1)} %get-tuple-element.24.refs_0_.refs_1_), channel_id=1, source_target_pairs={{0,2},{1,3},{2,0},{3,1},{4,6},{5,7},{6,4},{7,5},{8,10},{9,11},{10,... | collective-permute-start | bytes 552968 | tf_op jit(solution)/shard_map/ppermute | solution.py:21
  20.6 5.0 %collective-permute-start.6 = (bf16[128,1152]{1,0:T(8,128)(2,1)S(1)}, bf16[128,1152]{1,0:T(8,128)(2,1)S(1)}, u32[]{:S(2)}, u32[]{:S(2)}) collective-permute-start(bf16[128,1152]{1,0:T(8,128)(2,1)S(1)} %shard_map.81.refs_8_), channel_id=1, source_target_pairs={{0,1},{1,0},{2,3},{3,2},{4,5},{5,4},{6,7},{7,6},{8,9},{9,8},{10,11... | collective-permute-start | bytes 884744 | tf_op jit(solution)/shard_map/ppermute | solution.py:21
  28.2 2.3 %collective-permute-start.8 = (bf16[128,1152]{1,0:T(8,128)(2,1)S(1)}, bf16[128,1152]{1,0:T(8,128)(2,1)S(1)}, u32[]{:S(2)}, u32[]{:S(2)}) collective-permute-start(bf16[128,1152]{1,0:T(8,128)(2,1)S(1)} %get-tuple-element.29), channel_id=1, source_target_pairs={{0,1},{1,0},{2,3},{3,2},{4,5},{5,4},{6,7},{7,6},{8,9},{9,8},{10,11... | collective-permute-start | bytes 884744 | tf_op jit(solution)/shard_map/ppermute | solution.py:21
  28.3 9.8 %collective-permute-start.14 = (bf16[128,1152]{1,0:T(8,128)(2,1)S(1)}, bf16[128,1152]{1,0:T(8,128)(2,1)S(1)}, u32[]{:S(2)}, u32[]{:S(2)}) collective-permute-start(bf16[128,1152]{1,0:T(8,128)(2,1)S(1)} %get-tuple-element.37), channel_id=1, source_target_pairs={{0,2},{1,3},{2,0},{3,1},{4,6},{5,7},{6,4},{7,5},{8,10},{9,11},{10,... | collective-permute-start | bytes 884744 | tf_op jit(solution)/shard_map/ppermute | solution.py:21
  28.7 4.5 %collective-permute-start.7 = (f32[16,128]{1,0:T(8,128)S(1)}, f32[16,128]{1,0:T(8,128)S(1)}, u32[]{:S(2)}, u32[]{:S(2)}) collective-permute-start(f32[16,128]{1,0:T(8,128)S(1)} %get-tuple-element.27.first), channel_id=1, source_target_pairs={{0,8},{1,9},{2,10},{3,11},{4,12},{5,13},{6,14},{7,15},{8,0},{9,1},... | collective-permute-start | bytes 24584 | tf_op jit(solution)/shard_map/ppermute | solution.py:21
  30.4 11.5 %collective-permute-start.12 = (bf16[128,1152]{1,0:T(8,128)(2,1)S(1)}, bf16[128,1152]{1,0:T(8,128)(2,1)S(1)}, u32[]{:S(2)}, u32[]{:S(2)}) collective-permute-start(bf16[128,1152]{1,0:T(8,128)(2,1)S(1)} %get-tuple-element.31), channel_id=1, source_target_pairs={{0,1},{1,0},{2,3},{3,2},{4,5},{5,4},{6,7},{7,6},{8,9},{9,8},{10,11... | collective-permute-start | bytes 884744 | tf_op jit(solution)/shard_map/ppermute | solution.py:21
  30.5 16.8 %collective-permute-start.13 = (bf16[128,1152]{1,0:T(8,128)(2,1)S(1)}, bf16[128,1152]{1,0:T(8,128)(2,1)S(1)}, u32[]{:S(2)}, u32[]{:S(2)}) collective-permute-start(bf16[128,1152]{1,0:T(8,128)(2,1)S(1)} %shard_map.84.refs_0_), channel_id=1, source_target_pairs={{0,8},{1,9},{2,10},{3,11},{4,12},{5,13},{6,14},{7,15},{8,0},{9,1},... | collective-permute-start | bytes 884744 | tf_op jit(solution)/shard_map/ppermute | solution.py:21
  33.3 1.2 %collective-permute-start.9 = (f32[16,128]{1,0:T(8,128)S(1)}, f32[16,128]{1,0:T(8,128)S(1)}, u32[]{:S(2)}, u32[]{:S(2)}) collective-permute-start(f32[16,128]{1,0:T(8,128)S(1)} %shard_map.85.first), channel_id=1, source_target_pairs={{0,1},{1,0},{2,3},{3,2},{4,5},{5,4},{6,7},{7,6},{8,9},{9,8},{10,11... | collective-permute-start | bytes 24584 | tf_op jit(solution)/shard_map/ppermute | solution.py:21
  34.4 3.7 %collective-permute-start.10 = (f32[16,128]{1,0:T(8,128)S(1)}, f32[16,128]{1,0:T(8,128)S(1)}, u32[]{:S(2)}, u32[]{:S(2)}) collective-permute-start(f32[16,128]{1,0:T(8,128)S(1)} %shard_map.86.first), channel_id=1, source_target_pairs={{0,2},{1,3},{2,0},{3,1},{4,6},{5,7},{6,4},{7,5},{8,10},{9,11},{10,... | collective-permute-start | bytes 24584 | tf_op jit(solution)/shard_map/ppermute | solution.py:21
  38.2 14.2 %collective-permute-start.15 = (bf16[128,1152]{1,0:T(8,128)(2,1)S(1)}, bf16[128,1152]{1,0:T(8,128)(2,1)S(1)}, u32[]{:S(2)}, u32[]{:S(2)}) collective-permute-start(bf16[128,1152]{1,0:T(8,128)(2,1)S(1)} %shard_map.90), channel_id=1, source_target_pairs={{0,2},{1,3},{2,0},{3,1},{4,6},{5,7},{6,4},{7,5},{8,10},{9,11},{10,... | collective-permute-start | bytes 884744 | tf_op jit(solution)/shard_map/ppermute | solution.py:21
  39.9 12.4 %collective-permute-start.16 = (bf16[128,1152]{1,0:T(8,128)(2,1)S(1)}, bf16[128,1152]{1,0:T(8,128)(2,1)S(1)}, u32[]{:S(2)}, u32[]{:S(2)}) collective-permute-start(bf16[128,1152]{1,0:T(8,128)(2,1)S(1)} %shard_map.89.refs_1_), channel_id=1, source_target_pairs={{0,4},{1,5},{2,6},{3,7},{4,0},{5,1},{6,2},{7,3},{8,12},{9,13},{10,... | collective-permute-start | bytes 884744 | tf_op jit(solution)/shard_map/ppermute | solution.py:21
  41.0 11.3 %collective-permute-start.11 = (f32[16,128]{1,0:T(8,128)S(1)}, f32[16,128]{1,0:T(8,128)S(1)}, u32[]{:S(2)}, u32[]{:S(2)}) collective-permute-start(f32[16,128]{1,0:T(8,128)S(1)} %shard_map.87.refs_1_.sums), channel_id=1, source_target_pairs={{0,4},{1,5},{2,6},{3,7},{4,0},{5,1},{6,2},{7,3},{8,12},{9,13},{10,... | collective-permute-start | bytes 24584 | tf_op jit(solution)/shard_map/ppermute | solution.py:21

commit v9 on v8

--- a/solution.py
+++ b/solution.py
@@ -318,10 +318,10 @@
     img_parts, txt_parts, sums = tile_call(imgs, txts, log_temp.reshape(1, 1), bias.reshape(1, 1))
     img_parts, txt_parts = ([part[0] for part in parts] for parts in (img_parts, txt_parts))
     txt_keep, txt_recvs, others = returned(txt_parts, txt_bits, [], False)
-    for bit in txt_bits + img_bits[:0:-1]:
+    for bit in img_bits[:1] + txt_bits[1:] + img_bits[:0:-1]:
         sums = sums_call([sums, swapped(sums, bit)], others)
     img_keep, img_recvs, others = returned(img_parts, img_bits, others + [sums], True)
-    sums_recv = swapped(sums, img_bits[0])
+    sums_recv = swapped(sums, txt_bits[0])
     txt_recvs = held(txt_recvs, [], RETURN_COST)
     grad_text, grad_image, grad_bias, grad_temp = finish_call(
         sums,

time: 54.4 us -> 55.1 us (1.013); the launches traced: 53.6 us -> 54.9 us
  starting transfers between devices: 18.6 us -> 20.3 us
    ppermute x17, starting transfers between devices: 18.6 us -> 20.3 us  [swapped(): return lax.ppermute(x, 'blk', [(i, i ^ bit) for i in range(count)])]
  transfers between devices with their start and end apart: 17 -> 17, of which waited for: 9 -> 10; matrix products, arithmetic and copies ran while one was open for 0% -> 0% of each run, Pallas kernels for 2% -> 2%
where the time goes in v9:
time: 55.1 us; the launch traced here: 54.9 us
  waiting for transfers between devices  27.1 us (49%)
  starting transfers between devices  20.3 us (37%)
  Pallas kernels  4.77 us (9%)
  between operations  2.04 us (4%)
  local copies, waits for them, and re-layouts  0.73 us (1%)
    ppermute x17, waiting for transfers between devices, swapped(): return lax.ppermute(x, 'blk', [(i, i ^ bit) for i in range(count)])  27.1 us
    ppermute x17, starting transfers between devices, swapped(): return lax.ppermute(x, 'blk', [(i, i ^ bit) for i in range(count)])  20.3 us
    pallas_call x1, Pallas kernels, tile_call(): pl.pallas_call(functools.partial(tile_kernel, [len(block) for block in im...  2.6 us
    pallas_call x1, Pallas kernels, finish_call(): pl.pallas_call(functools.partial(finish_kernel, [len(recvs) for _, _, rec...  1.32 us
  transfers between devices with their start and end apart: 17, of which 10 were waited for; matrix products, arithmetic and copies ran while one was open for 0% of the time, Pallas kernels for 2%

profile of v9, /device:TPU:0, one launch (start us, length us, event | category | flops | bytes accessed | tf_op | source)
XLA Modules:
  0.0 54.9 jit_solution(3066277972998650247)
XLA Ops:
  0.6 0.0 copy-start.1
  0.6 3.0 %collective-permute-start = (bf16[128,1152]{1,0:T(8,128)(2,1)}, bf16[128,1152]{1,0:T(8,128)(2,1)S(1)}, u32[]{:S(2)}, u32[]{:S(2)}) collective-permute-start(bf16[128,1152]{1,0:T(8,128)(2,1)} %refs_4_.1), channel_id=1, source_target_pairs={{0,2},{1,3},{2,0},{3,1},{4,6},{5,7},{6,4},{7,5},{8,10},{9,11},{10,... | collective-permute-start | bytes 884744 | tf_op jit(solution)/shard_map/ppermute | solution.py:21
  3.6 1.6 %collective-permute-start.1 = (bf16[128,1152]{1,0:T(8,128)(2,1)}, bf16[128,1152]{1,0:T(8,128)(2,1)S(1)}, u32[]{:S(2)}, u32[]{:S(2)}) collective-permute-start(bf16[128,1152]{1,0:T(8,128)(2,1)} %refs_4_.1), channel_id=1, source_target_pairs={{0,4},{1,5},{2,6},{3,7},{4,0},{5,1},{6,2},{7,3},{8,12},{9,13},{10,... | collective-permute-start | bytes 884744 | tf_op jit(solution)/shard_map/ppermute | solution.py:21
  5.2 2.6 %collective-permute-start.4 = (bf16[128,1152]{1,0:T(8,128)(2,1)}, bf16[128,1152]{1,0:T(8,128)(2,1)S(1)}, u32[]{:S(2)}, u32[]{:S(2)}) collective-permute-start(bf16[128,1152]{1,0:T(8,128)(2,1)} %refs_0_.1), channel_id=1, source_target_pairs={{0,8},{1,9},{2,10},{3,11},{4,12},{5,13},{6,14},{7,15},{8,0},{9,1},... | collective-permute-start | bytes 884744 | tf_op jit(solution)/shard_map/ppermute | solution.py:21
  7.8 3.1 %collective-permute-done.value = bf16[128,1152]{1,0:T(8,128)(2,1)S(1)} collective-permute-done((bf16[128,1152]{1,0:T(8,128)(2,1)}, bf16[128,1152]{1,0:T(8,128)(2,1)S(1)}, u32[]{:S(2)}, u32[]{:S(2)}) %collective-permute-start) | collective-permute-done | bytes 294944 | tf_op jit(solution)/shard_map/ppermute | solution.py:21
  10.9 0.1 shard_map.75
  11.0 1.9 %collective-permute-start.3 = (bf16[48,1152]{1,0:T(8,128)(2,1)S(1)}, bf16[48,1152]{1,0:T(8,128)(2,1)S(1)}, u32[]{:S(2)}, u32[]{:S(2)}) collective-permute-start(bf16[48,1152]{1,0:T(8,128)(2,1)S(1)} %get-tuple-element.26.refs_4_), channel_id=1, source_target_pairs={{0,4},{1,5},{2,6},{3,7},{4,0},{5,1},{6,2},{7,3},{8,12},{9,13},{10,... | collective-permute-start | bytes 331784 | tf_op jit(solution)/shard_map/ppermute | solution.py:21
  14.2 0.0 copy-done.1
  14.2 0.0 copy-start
  14.2 0.1 shard_map.76.refs_0_.refs_7_
  14.4 0.1 collective-permute-start.5
  14.5 0.7 %copy-done = bf16[128,1152]{1,0:T(8,128)(2,1)S(1)} copy-done((bf16[128,1152]{1,0:T(8,128)(2,1)S(1)}, bf16[128,1152]{1,0:T(8,128)(2,1)}, u32[]{:S(2)}) %copy-start) | copy-done | bytes 294936
  15.2 0.1 shard_map.77.refs_0_
  15.3 4.5 %collective-permute-done.1.value = bf16[128,1152]{1,0:T(8,128)(2,1)S(1)} collective-permute-done((bf16[128,1152]{1,0:T(8,128)(2,1)}, bf16[128,1152]{1,0:T(8,128)(2,1)S(1)}, u32[]{:S(2)}, u32[]{:S(2)}) %collective-permute-start.1) | collective-permute-done | bytes 294944 | tf_op jit(solution)/shard_map/ppermute | solution.py:21
  19.8 0.1 shard_map.78
  20.0 0.4 collective-permute-start.2
  20.4 0.0 collective-permute-done.4.value
  20.4 0.1 shard_map.81.refs_8_
  20.6 0.1 collective-permute-start.6
  20.6 0.4 collective-permute-done.3.refs_0_
  21.0 4.6 %collective-permute-done.2.refs_0_ = bf16[80,1152]{1,0:T(8,128)(2,1)S(1)} collective-permute-done((bf16[80,1152]{1,0:T(8,128)(2,1)S(1)}, bf16[80,1152]{1,0:T(8,128)(2,1)S(1)}, u32[]{:S(2)}, u32[]{:S(2)}) %collective-permute-start.2) | collective-permute-done | bytes 184352 | tf_op jit(solution)/shard_map/ppermute | solution.py:21
  25.6 0.0 collective-permute-done.6.refs_0_
  25.6 0.0 collective-permute-done.5.refs_9_
  25.6 2.6 %shard_map.83 = (f32[128,1152]{1,0:T(8,128)S(1)}, f32[128,1152]{1,0:T(8,128)S(1)}, bf16[128,1152]{1,0:T(8,128)(2,1)S(1)}, bf16[128,1152]{1,0:T(8,128)(2,1)S(1)},...) custom-call(bf16[128,1152]{1,0:T(8,128)(2,1)S(1)} %shard_map.77.refs, ...), custom_call_target="tpu_custom_call" | custom-call | flops 1811939328 | tf_op jit(solution)/shard_map/pallas_call | solution.py:194
  28.2 0.1 collective-permute-start.8
  28.3 0.4 collective-permute-start.14
  28.7 0.0 collective-permute-start.7
  28.7 0.2 collective-permute-start.12
  28.9 1.0 %collective-permute-done.8.recv = bf16[128,1152]{1,0:T(8,128)(2,1)S(1)} collective-permute-done((bf16[128,1152]{1,0:T(8,128)(2,1)S(1)}, bf16[128,1152]{1,0:T(8,128)(2,1)S(1)}, u32[]{:S(2)}, u32[]{:S(2)}) %collective-permute-start.8) | collective-permute-done | bytes 294944 | tf_op jit(solution)/shard_map/ppermute | solution.py:21
  29.8 0.1 shard_map.84.refs_0_
  29.9 3.2 %collective-permute-start.13 = (bf16[128,1152]{1,0:T(8,128)(2,1)S(1)}, bf16[128,1152]{1,0:T(8,128)(2,1)S(1)}, u32[]{:S(2)}, u32[]{:S(2)}) collective-permute-start(bf16[128,1152]{1,0:T(8,128)(2,1)S(1)} %shard_map.84.refs_0_), channel_id=1, source_target_pairs={{0,8},{1,9},{2,10},{3,11},{4,12},{5,13},{6,14},{7,15},{8,0},{9,1},... | collective-permute-start | bytes 884744 | tf_op jit(solution)/shard_map/ppermute | solution.py:21
  33.1 0.0 collective-permute-done.7.second
  33.1 0.2 collective-permute-start.9
  33.3 0.9 %collective-permute-done.9.second = f32[16,128]{1,0:T(8,128)S(1)} collective-permute-done((f32[16,128]{1,0:T(8,128)S(1)}, f32[16,128]{1,0:T(8,128)S(1)}, u32[]{:S(2)}, u32[]{:S(2)}) %collective-permute-start.9) | collective-permute-done | bytes 8224 | tf_op jit(solution)/shard_map/ppermute | solution.py:21
  34.3 1.5 %collective-permute-start.10 = (f32[16,128]{1,0:T(8,128)S(1)}, f32[16,128]{1,0:T(8,128)S(1)}, u32[]{:S(2)}, u32[]{:S(2)}) collective-permute-start(f32[16,128]{1,0:T(8,128)S(1)} %shard_map.86.first), channel_id=1, source_target_pairs={{0,2},{1,3},{2,0},{3,1},{4,6},{5,7},{6,4},{7,5},{8,10},{9,11},{10,... | collective-permute-start | bytes 24584 | tf_op jit(solution)/shard_map/ppermute | solution.py:21
  35.7 2.2 %collective-permute-done.10.second = f32[16,128]{1,0:T(8,128)S(1)} collective-permute-done((f32[16,128]{1,0:T(8,128)S(1)}, f32[16,128]{1,0:T(8,128)S(1)}, u32[]{:S(2)}, u32[]{:S(2)}) %collective-permute-start.10) | collective-permute-done | bytes 8224 | tf_op jit(solution)/shard_map/ppermute | solution.py:21
  37.9 0.0 collective-permute-done.14.recv
  37.9 0.1 shard_map.89.refs_1_
  38.0 1.6 %collective-permute-start.15 = (bf16[128,1152]{1,0:T(8,128)(2,1)S(1)}, bf16[128,1152]{1,0:T(8,128)(2,1)S(1)}, u32[]{:S(2)}, u32[]{:S(2)}) collective-permute-start(bf16[128,1152]{1,0:T(8,128)(2,1)S(1)} %shard_map.90), channel_id=1, source_target_pairs={{0,2},{1,3},{2,0},{3,1},{4,6},{5,7},{6,4},{7,5},{8,10},{9,11},{10,... | collective-permute-start | bytes 884744 | tf_op jit(solution)/shard_map/ppermute | solution.py:21
  39.5 0.2 collective-permute-start.16
  39.7 3.4 %collective-permute-start.11 = (f32[16,128]{1,0:T(8,128)S(1)}, f32[16,128]{1,0:T(8,128)S(1)}, u32[]{:S(2)}, u32[]{:S(2)}) collective-permute-start(f32[16,128]{1,0:T(8,128)S(1)} %shard_map.87.refs_1_.sums), channel_id=1, source_target_pairs={{0,8},{1,9},{2,10},{3,11},{4,12},{5,13},{6,14},{7,15},{8,0},{9,1},... | collective-permute-start | bytes 24584 | tf_op jit(solution)/shard_map/ppermute | solution.py:21
  43.1 0.0 collective-permute-done.12.refs_0_
  43.1 4.2 %collective-permute-done.13.refs_1_ = bf16[128,1152]{1,0:T(8,128)(2,1)S(1)} collective-permute-done((bf16[128,1152]{1,0:T(8,128)(2,1)S(1)}, bf16[128,1152]{1,0:T(8,128)(2,1)S(1)}, u32[]{:S(2)}, u32[]{:S(2)}) %collective-permute-start.13) | collective-permute-done | bytes 294944 | tf_op jit(solution)/shard_map/ppermute | solution.py:21
  47.3 0.1 collective-permute-done.11.sums_recv
  47.4 0.0 collective-permute-done.15.refs_6_
  47.4 6.2 %collective-permute-done.16.refs_7_ = bf16[128,1152]{1,0:T(8,128)(2,1)S(1)} collective-permute-done((bf16[128,1152]{1,0:T(8,128)(2,1)S(1)}, bf16[128,1152]{1,0:T(8,128)(2,1)S(1)}, u32[]{:S(2)}, u32[]{:S(2)}) %collective-permute-start.16) | collective-permute-done | bytes 294944 | tf_op jit(solution)/shard_map/ppermute | solution.py:21
  53.6 1.3 %shard_map.91 = (bf16[128,1152]{1,0:T(8,128)(2,1)}, bf16[128,1152]{1,0:T(8,128)(2,1)}, f32[1,1]{1,0:T(1,128)}, f32[1,1]{1,0:T(1,128)}) custom-call(f32[16,128]{1,0:T(8,128)S(1)} %shard_map.87.refs_1_.sums, f32[16,128]{1,0:T(8,128)S(1)} %collective-permute-done.11.sums_recv, bf16[128,1152]{1,0:T(8,128)(2,1)S(1)} %copy-done.1, ...), custom_call_target="tpu_custom_call" | custom-call | tf_op jit(solution)/shard_map/pallas_call | solution.py:248
  (8 shorter events, 0.0 us)
Async XLA Ops:
  0.6 13.6 %copy-start.1 = (bf16[128,1152]{1,0:T(8,128)(2,1)S(1)}, bf16[128,1152]{1,0:T(8,128)(2,1)}, u32[]{:S(2)}) copy-start(bf16[128,1152]{1,0:T(8,128)(2,1)} %refs_0_.1) | copy-start | bytes 884740
  0.6 10.2 %collective-permute-start = (bf16[128,1152]{1,0:T(8,128)(2,1)}, bf16[128,1152]{1,0:T(8,128)(2,1)S(1)}, u32[]{:S(2)}, u32[]{:S(2)}) collective-permute-start(bf16[128,1152]{1,0:T(8,128)(2,1)} %refs_4_.1), channel_id=1, source_target_pairs={{0,2},{1,3},{2,0},{3,1},{4,6},{5,7},{6,4},{7,5},{8,10},{9,11},{10,... | collective-permute-start | bytes 884744 | tf_op jit(solution)/shard_map/ppermute | solution.py:21
  3.6 16.2 %collective-permute-start.1 = (bf16[128,1152]{1,0:T(8,128)(2,1)}, bf16[128,1152]{1,0:T(8,128)(2,1)S(1)}, u32[]{:S(2)}, u32[]{:S(2)}) collective-permute-start(bf16[128,1152]{1,0:T(8,128)(2,1)} %refs_4_.1), channel_id=1, source_target_pairs={{0,4},{1,5},{2,6},{3,7},{4,0},{5,1},{6,2},{7,3},{8,12},{9,13},{10,... | collective-permute-start | bytes 884744 | tf_op jit(solution)/shard_map/ppermute | solution.py:21
  5.2 15.2 %collective-permute-start.4 = (bf16[128,1152]{1,0:T(8,128)(2,1)}, bf16[128,1152]{1,0:T(8,128)(2,1)S(1)}, u32[]{:S(2)}, u32[]{:S(2)}) collective-permute-start(bf16[128,1152]{1,0:T(8,128)(2,1)} %refs_0_.1), channel_id=1, source_target_pairs={{0,8},{1,9},{2,10},{3,11},{4,12},{5,13},{6,14},{7,15},{8,0},{9,1},... | collective-permute-start | bytes 884744 | tf_op jit(solution)/shard_map/ppermute | solution.py:21
  11.0 10.0 %collective-permute-start.3 = (bf16[48,1152]{1,0:T(8,128)(2,1)S(1)}, bf16[48,1152]{1,0:T(8,128)(2,1)S(1)}, u32[]{:S(2)}, u32[]{:S(2)}) collective-permute-start(bf16[48,1152]{1,0:T(8,128)(2,1)S(1)} %get-tuple-element.26.refs_4_), channel_id=1, source_target_pairs={{0,4},{1,5},{2,6},{3,7},{4,0},{5,1},{6,2},{7,3},{8,12},{9,13},{10,... | collective-permute-start | bytes 331784 | tf_op jit(solution)/shard_map/ppermute | solution.py:21
  14.2 1.0 %copy-start = (bf16[128,1152]{1,0:T(8,128)(2,1)S(1)}, bf16[128,1152]{1,0:T(8,128)(2,1)}, u32[]{:S(2)}) copy-start(bf16[128,1152]{1,0:T(8,128)(2,1)} %refs_4_.1) | copy-start | bytes 884740
  14.4 11.2 %collective-permute-start.5 = (bf16[128,1152]{1,0:T(8,128)(2,1)S(1)}, bf16[128,1152]{1,0:T(8,128)(2,1)S(1)}, u32[]{:S(2)}, u32[]{:S(2)}) collective-permute-start(bf16[128,1152]{1,0:T(8,128)(2,1)S(1)} %shard_map.76.refs_0_.refs_7_), channel_id=1, source_target_pairs={{0,1},{1,0},{2,3},{3,2},{4,5},{5,4},{6,7},{7,6},{8,9},{9,8},{10,11... | collective-permute-start | bytes 884744 | tf_op jit(solution)/shard_map/ppermute | solution.py:21
  20.0 5.6 %collective-permute-start.2 = (bf16[80,1152]{1,0:T(8,128)(2,1)S(1)}, bf16[80,1152]{1,0:T(8,128)(2,1)S(1)}, u32[]{:S(2)}, u32[]{:S(2)}) collective-permute-start(bf16[80,1152]{1,0:T(8,128)(2,1)S(1)} %get-tuple-element.24.refs_0_.refs_1_), channel_id=1, source_target_pairs={{0,2},{1,3},{2,0},{3,1},{4,6},{5,7},{6,4},{7,5},{8,10},{9,11},{10,... | collective-permute-start | bytes 552968 | tf_op jit(solution)/shard_map/ppermute | solution.py:21
  20.6 5.0 %collective-permute-start.6 = (bf16[128,1152]{1,0:T(8,128)(2,1)S(1)}, bf16[128,1152]{1,0:T(8,128)(2,1)S(1)}, u32[]{:S(2)}, u32[]{:S(2)}) collective-permute-start(bf16[128,1152]{1,0:T(8,128)(2,1)S(1)} %shard_map.81.refs_8_), channel_id=1, source_target_pairs={{0,1},{1,0},{2,3},{3,2},{4,5},{5,4},{6,7},{7,6},{8,9},{9,8},{10,11... | collective-permute-start | bytes 884744 | tf_op jit(solution)/shard_map/ppermute | solution.py:21
  28.2 1.6 %collective-permute-start.8 = (bf16[128,1152]{1,0:T(8,128)(2,1)S(1)}, bf16[128,1152]{1,0:T(8,128)(2,1)S(1)}, u32[]{:S(2)}, u32[]{:S(2)}) collective-permute-start(bf16[128,1152]{1,0:T(8,128)(2,1)S(1)} %get-tuple-element.29), channel_id=1, source_target_pairs={{0,1},{1,0},{2,3},{3,2},{4,5},{5,4},{6,7},{7,6},{8,9},{9,8},{10,11... | collective-permute-start | bytes 884744 | tf_op jit(solution)/shard_map/ppermute | solution.py:21
  28.3 9.6 %collective-permute-start.14 = (bf16[128,1152]{1,0:T(8,128)(2,1)S(1)}, bf16[128,1152]{1,0:T(8,128)(2,1)S(1)}, u32[]{:S(2)}, u32[]{:S(2)}) collective-permute-start(bf16[128,1152]{1,0:T(8,128)(2,1)S(1)} %get-tuple-element.37), channel_id=1, source_target_pairs={{0,2},{1,3},{2,0},{3,1},{4,6},{5,7},{6,4},{7,5},{8,10},{9,11},{10,... | collective-permute-start | bytes 884744 | tf_op jit(solution)/shard_map/ppermute | solution.py:21
  28.7 4.4 %collective-permute-start.7 = (f32[16,128]{1,0:T(8,128)S(1)}, f32[16,128]{1,0:T(8,128)S(1)}, u32[]{:S(2)}, u32[]{:S(2)}) collective-permute-start(f32[16,128]{1,0:T(8,128)S(1)} %get-tuple-element.27.first), channel_id=1, source_target_pairs={{0,4},{1,5},{2,6},{3,7},{4,0},{5,1},{6,2},{7,3},{8,12},{9,13},{10,... | collective-permute-start | bytes 24584 | tf_op jit(solution)/shard_map/ppermute | solution.py:21
  28.7 14.4 %collective-permute-start.12 = (bf16[128,1152]{1,0:T(8,128)(2,1)S(1)}, bf16[128,1152]{1,0:T(8,128)(2,1)S(1)}, u32[]{:S(2)}, u32[]{:S(2)}) collective-permute-start(bf16[128,1152]{1,0:T(8,128)(2,1)S(1)} %get-tuple-element.31), channel_id=1, source_target_pairs={{0,1},{1,0},{2,3},{3,2},{4,5},{5,4},{6,7},{7,6},{8,9},{9,8},{10,11... | collective-permute-start | bytes 884744 | tf_op jit(solution)/shard_map/ppermute | solution.py:21
  29.9 17.4 %collective-permute-start.13 = (bf16[128,1152]{1,0:T(8,128)(2,1)S(1)}, bf16[128,1152]{1,0:T(8,128)(2,1)S(1)}, u32[]{:S(2)}, u32[]{:S(2)}) collective-permute-start(bf16[128,1152]{1,0:T(8,128)(2,1)S(1)} %shard_map.84.refs_0_), channel_id=1, source_target_pairs={{0,8},{1,9},{2,10},{3,11},{4,12},{5,13},{6,14},{7,15},{8,0},{9,1},... | collective-permute-start | bytes 884744 | tf_op jit(solution)/shard_map/ppermute | solution.py:21
  33.1 1.2 %collective-permute-start.9 = (f32[16,128]{1,0:T(8,128)S(1)}, f32[16,128]{1,0:T(8,128)S(1)}, u32[]{:S(2)}, u32[]{:S(2)}) collective-permute-start(f32[16,128]{1,0:T(8,128)S(1)} %shard_map.85.first), channel_id=1, source_target_pairs={{0,1},{1,0},{2,3},{3,2},{4,5},{5,4},{6,7},{7,6},{8,9},{9,8},{10,11... | collective-permute-start | bytes 24584 | tf_op jit(solution)/shard_map/ppermute | solution.py:21
  34.3 3.7 %collective-permute-start.10 = (f32[16,128]{1,0:T(8,128)S(1)}, f32[16,128]{1,0:T(8,128)S(1)}, u32[]{:S(2)}, u32[]{:S(2)}) collective-permute-start(f32[16,128]{1,0:T(8,128)S(1)} %shard_map.86.first), channel_id=1, source_target_pairs={{0,2},{1,3},{2,0},{3,1},{4,6},{5,7},{6,4},{7,5},{8,10},{9,11},{10,... | collective-permute-start | bytes 24584 | tf_op jit(solution)/shard_map/ppermute | solution.py:21
  38.0 9.4 %collective-permute-start.15 = (bf16[128,1152]{1,0:T(8,128)(2,1)S(1)}, bf16[128,1152]{1,0:T(8,128)(2,1)S(1)}, u32[]{:S(2)}, u32[]{:S(2)}) collective-permute-start(bf16[128,1152]{1,0:T(8,128)(2,1)S(1)} %shard_map.90), channel_id=1, source_target_pairs={{0,2},{1,3},{2,0},{3,1},{4,6},{5,7},{6,4},{7,5},{8,10},{9,11},{10,... | collective-permute-start | bytes 884744 | tf_op jit(solution)/shard_map/ppermute | solution.py:21
  39.5 14.0 %collective-permute-start.16 = (bf16[128,1152]{1,0:T(8,128)(2,1)S(1)}, bf16[128,1152]{1,0:T(8,128)(2,1)S(1)}, u32[]{:S(2)}, u32[]{:S(2)}) collective-permute-start(bf16[128,1152]{1,0:T(8,128)(2,1)S(1)} %shard_map.89.refs_1_), channel_id=1, source_target_pairs={{0,4},{1,5},{2,6},{3,7},{4,0},{5,1},{6,2},{7,3},{8,12},{9,13},{10,... | collective-permute-start | bytes 884744 | tf_op jit(solution)/shard_map/ppermute | solution.py:21
  39.7 7.6 %collective-permute-start.11 = (f32[16,128]{1,0:T(8,128)S(1)}, f32[16,128]{1,0:T(8,128)S(1)}, u32[]{:S(2)}, u32[]{:S(2)}) collective-permute-start(f32[16,128]{1,0:T(8,128)S(1)} %shard_map.87.refs_1_.sums), channel_id=1, source_target_pairs={{0,8},{1,9},{2,10},{3,11},{4,12},{5,13},{6,14},{7,15},{8,0},{9,1},... | collective-permute-start | bytes 24584 | tf_op jit(solution)/shard_map/ppermute | solution.py:21

commit v10 on v9

--- a/solution.py
+++ b/solution.py
@@ -314,6 +314,7 @@
     split = 1 + depth // 2
     img_bits = all_bits[1:split][::-1]
     txt_bits = (all_bits[:1] + all_bits[split:])[::-1]
+    txt_bits[0] |= img_bits[0]
     imgs, txts = gathered(image_embeds, text_embeds, img_bits, txt_bits)
     img_parts, txt_parts, sums = tile_call(imgs, txts, log_temp.reshape(1, 1), bias.reshape(1, 1))
     img_parts, txt_parts = ([part[0] for part in parts] for parts in (img_parts, txt_parts))

time: 55.1 us -> 49 us (0.89)
  waiting for transfers between devices: 27.1 us -> 20.8 us
    ppermute x17, waiting for transfers between devices: 27.1 us -> 20.8 us  [swapped(): return lax.ppermute(x, 'blk', [(i, i ^ bit) for i in range(count)])]
  transfers between devices with their start and end apart: 17 -> 17, of which waited for: 10 -> 7; matrix products, arithmetic and copies ran while one was open for 0% -> 0% of each run, Pallas kernels for 2% -> 2%
where the time goes in v10:
time: 49 us; the launch traced here: 48.8 us
  waiting for transfers between devices  20.8 us (42%)
  starting transfers between devices  20.5 us (42%)
  Pallas kernels  4.76 us (10%)
  between operations  2.07 us (4%)
  local copies, waits for them, and re-layouts  0.73 us (1%)
    ppermute x17, waiting for transfers between devices, swapped(): return lax.ppermute(x, 'blk', [(i, i ^ bit) for i in range(count)])  20.8 us
    ppermute x17, starting transfers between devices, swapped(): return lax.ppermute(x, 'blk', [(i, i ^ bit) for i in range(count)])  20.5 us
    pallas_call x1, Pallas kernels, tile_call(): pl.pallas_call(functools.partial(tile_kernel, [len(block) for block in im...  2.58 us
    pallas_call x1, Pallas kernels, finish_call(): pl.pallas_call(functools.partial(finish_kernel, [len(recvs) for _, _, rec...  1.32 us
  transfers between devices with their start and end apart: 17, of which 7 were waited for; matrix products, arithmetic and copies ran while one was open for 0% of the time, Pallas kernels for 2%

profile of v10, /device:TPU:0, one launch (start us, length us, event | category | flops | bytes accessed | tf_op | source)
XLA Modules:
  0.0 48.8 jit_solution(5394953295299883419)
XLA Ops:
  0.6 0.0 copy-start.1
  0.6 3.0 %collective-permute-start = (bf16[128,1152]{1,0:T(8,128)(2,1)}, bf16[128,1152]{1,0:T(8,128)(2,1)S(1)}, u32[]{:S(2)}, u32[]{:S(2)}) collective-permute-start(bf16[128,1152]{1,0:T(8,128)(2,1)} %refs_4_.1), channel_id=1, source_target_pairs={{0,2},{1,3},{2,0},{3,1},{4,6},{5,7},{6,4},{7,5},{8,10},{9,11},{10,... | collective-permute-start | bytes 884744 | tf_op jit(solution)/shard_map/ppermute | solution.py:21
  3.6 1.6 %collective-permute-start.1 = (bf16[128,1152]{1,0:T(8,128)(2,1)}, bf16[128,1152]{1,0:T(8,128)(2,1)S(1)}, u32[]{:S(2)}, u32[]{:S(2)}) collective-permute-start(bf16[128,1152]{1,0:T(8,128)(2,1)} %refs_4_.1), channel_id=1, source_target_pairs={{0,4},{1,5},{2,6},{3,7},{4,0},{5,1},{6,2},{7,3},{8,12},{9,13},{10,... | collective-permute-start | bytes 884744 | tf_op jit(solution)/shard_map/ppermute | solution.py:21
  5.2 2.5 %collective-permute-start.4 = (bf16[128,1152]{1,0:T(8,128)(2,1)}, bf16[128,1152]{1,0:T(8,128)(2,1)S(1)}, u32[]{:S(2)}, u32[]{:S(2)}) collective-permute-start(bf16[128,1152]{1,0:T(8,128)(2,1)} %refs_0_.1), channel_id=1, source_target_pairs={{0,12},{1,13},{2,14},{3,15},{4,8},{5,9},{6,10},{7,11},{8,4},{9,5},... | collective-permute-start | bytes 884744 | tf_op jit(solution)/shard_map/ppermute | solution.py:21
  7.7 3.2 %collective-permute-done.value = bf16[128,1152]{1,0:T(8,128)(2,1)S(1)} collective-permute-done((bf16[128,1152]{1,0:T(8,128)(2,1)}, bf16[128,1152]{1,0:T(8,128)(2,1)S(1)}, u32[]{:S(2)}, u32[]{:S(2)}) %collective-permute-start) | collective-permute-done | bytes 294944 | tf_op jit(solution)/shard_map/ppermute | solution.py:21
  10.9 0.1 shard_map.75
  11.0 1.9 %collective-permute-start.3 = (bf16[48,1152]{1,0:T(8,128)(2,1)S(1)}, bf16[48,1152]{1,0:T(8,128)(2,1)S(1)}, u32[]{:S(2)}, u32[]{:S(2)}) collective-permute-start(bf16[48,1152]{1,0:T(8,128)(2,1)S(1)} %get-tuple-element.26.refs_4_), channel_id=1, source_target_pairs={{0,4},{1,5},{2,6},{3,7},{4,0},{5,1},{6,2},{7,3},{8,12},{9,13},{10,... | collective-permute-start | bytes 331784 | tf_op jit(solution)/shard_map/ppermute | solution.py:21
  14.2 0.0 copy-done.1
  14.2 0.0 copy-start
  14.2 0.1 shard_map.76.refs_0_.refs_7_
  14.4 0.1 collective-permute-start.5
  14.5 0.7 %copy-done = bf16[128,1152]{1,0:T(8,128)(2,1)S(1)} copy-done((bf16[128,1152]{1,0:T(8,128)(2,1)S(1)}, bf16[128,1152]{1,0:T(8,128)(2,1)}, u32[]{:S(2)}) %copy-start) | copy-done | bytes 294936
  15.2 0.1 shard_map.77.refs_0_
  15.3 0.0 collective-permute-done.1.value
  15.3 0.1 shard_map.78
  15.5 1.6 %collective-permute-start.2 = (bf16[80,1152]{1,0:T(8,128)(2,1)S(1)}, bf16[80,1152]{1,0:T(8,128)(2,1)S(1)}, u32[]{:S(2)}, u32[]{:S(2)}) collective-permute-start(bf16[80,1152]{1,0:T(8,128)(2,1)S(1)} %get-tuple-element.24.refs_0_.refs_1_), channel_id=1, source_target_pairs={{0,2},{1,3},{2,0},{3,1},{4,6},{5,7},{6,4},{7,5},{8,10},{9,11},{10,... | collective-permute-start | bytes 552968 | tf_op jit(solution)/shard_map/ppermute | solution.py:21
  17.0 4.8 %collective-permute-done.4.value = bf16[128,1152]{1,0:T(8,128)(2,1)S(1)} collective-permute-done((bf16[128,1152]{1,0:T(8,128)(2,1)}, bf16[128,1152]{1,0:T(8,128)(2,1)S(1)}, u32[]{:S(2)}, u32[]{:S(2)}) %collective-permute-start.4) | collective-permute-done | bytes 294944 | tf_op jit(solution)/shard_map/ppermute | solution.py:21
  21.9 0.1 shard_map.81.refs_8_
  22.1 0.1 collective-permute-start.6
  22.1 0.0 collective-permute-done.3.refs_0_
  22.1 0.0 collective-permute-done.2.refs_0_
  22.2 1.5 %collective-permute-done.6.refs_0_ = bf16[128,1152]{1,0:T(8,128)(2,1)S(1)} collective-permute-done((bf16[128,1152]{1,0:T(8,128)(2,1)S(1)}, bf16[128,1152]{1,0:T(8,128)(2,1)S(1)}, u32[]{:S(2)}, u32[]{:S(2)}) %collective-permute-start.6) | collective-permute-done | bytes 294944 | tf_op jit(solution)/shard_map/ppermute | solution.py:21
  23.7 0.0 collective-permute-done.5.refs_9_
  23.7 2.6 %shard_map.83 = (f32[128,1152]{1,0:T(8,128)S(1)}, f32[128,1152]{1,0:T(8,128)S(1)}, bf16[128,1152]{1,0:T(8,128)(2,1)S(1)}, bf16[128,1152]{1,0:T(8,128)(2,1)S(1)},...) custom-call(bf16[128,1152]{1,0:T(8,128)(2,1)S(1)} %shard_map.77.refs, ...), custom_call_target="tpu_custom_call" | custom-call | flops 1811939328 | tf_op jit(solution)/shard_map/pallas_call | solution.py:194
  26.3 0.2 collective-permute-start.8
  26.5 0.6 %collective-permute-start.14 = (bf16[128,1152]{1,0:T(8,128)(2,1)S(1)}, bf16[128,1152]{1,0:T(8,128)(2,1)S(1)}, u32[]{:S(2)}, u32[]{:S(2)}) collective-permute-start(bf16[128,1152]{1,0:T(8,128)(2,1)S(1)} %get-tuple-element.37), channel_id=1, source_target_pairs={{0,2},{1,3},{2,0},{3,1},{4,6},{5,7},{6,4},{7,5},{8,10},{9,11},{10,... | collective-permute-start | bytes 884744 | tf_op jit(solution)/shard_map/ppermute | solution.py:21
  27.1 0.0 collective-permute-start.7
  27.1 0.1 collective-permute-start.12
  27.2 0.8 %collective-permute-done.8.recv = bf16[128,1152]{1,0:T(8,128)(2,1)S(1)} collective-permute-done((bf16[128,1152]{1,0:T(8,128)(2,1)S(1)}, bf16[128,1152]{1,0:T(8,128)(2,1)S(1)}, u32[]{:S(2)}, u32[]{:S(2)}) %collective-permute-start.8) | collective-permute-done | bytes 294944 | tf_op jit(solution)/shard_map/ppermute | solution.py:21
  27.9 0.1 shard_map.84.refs_0_
  28.0 4.1 %collective-permute-start.13 = (bf16[128,1152]{1,0:T(8,128)(2,1)S(1)}, bf16[128,1152]{1,0:T(8,128)(2,1)S(1)}, u32[]{:S(2)}, u32[]{:S(2)}) collective-permute-start(bf16[128,1152]{1,0:T(8,128)(2,1)S(1)} %shard_map.84.refs_0_), channel_id=1, source_target_pairs={{0,12},{1,13},{2,14},{3,15},{4,8},{5,9},{6,10},{7,11},{8,4},{9,5},... | collective-permute-start | bytes 884744 | tf_op jit(solution)/shard_map/ppermute | solution.py:21
  32.1 0.0 collective-permute-done.7.second
  32.1 0.0 collective-permute-start.9
  32.1 1.2 %collective-permute-done.9.second = f32[16,128]{1,0:T(8,128)S(1)} collective-permute-done((f32[16,128]{1,0:T(8,128)S(1)}, f32[16,128]{1,0:T(8,128)S(1)}, u32[]{:S(2)}, u32[]{:S(2)}) %collective-permute-start.9) | collective-permute-done | bytes 8224 | tf_op jit(solution)/shard_map/ppermute | solution.py:21
  33.3 0.7 %collective-permute-start.10 = (f32[16,128]{1,0:T(8,128)S(1)}, f32[16,128]{1,0:T(8,128)S(1)}, u32[]{:S(2)}, u32[]{:S(2)}) collective-permute-start(f32[16,128]{1,0:T(8,128)S(1)} %shard_map.86.first), channel_id=1, source_target_pairs={{0,2},{1,3},{2,0},{3,1},{4,6},{5,7},{6,4},{7,5},{8,10},{9,11},{10,... | collective-permute-start | bytes 24584 | tf_op jit(solution)/shard_map/ppermute | solution.py:21
  34.0 3.0 %collective-permute-done.10.second = f32[16,128]{1,0:T(8,128)S(1)} collective-permute-done((f32[16,128]{1,0:T(8,128)S(1)}, f32[16,128]{1,0:T(8,128)S(1)}, u32[]{:S(2)}, u32[]{:S(2)}) %collective-permute-start.10) | collective-permute-done | bytes 8224 | tf_op jit(solution)/shard_map/ppermute | solution.py:21
  36.9 0.0 collective-permute-done.14.recv
  36.9 0.1 shard_map.89.refs_1_
  37.0 0.8 %collective-permute-start.15 = (bf16[128,1152]{1,0:T(8,128)(2,1)S(1)}, bf16[128,1152]{1,0:T(8,128)(2,1)S(1)}, u32[]{:S(2)}, u32[]{:S(2)}) collective-permute-start(bf16[128,1152]{1,0:T(8,128)(2,1)S(1)} %shard_map.90), channel_id=1, source_target_pairs={{0,2},{1,3},{2,0},{3,1},{4,6},{5,7},{6,4},{7,5},{8,10},{9,11},{10,... | collective-permute-start | bytes 884744 | tf_op jit(solution)/shard_map/ppermute | solution.py:21
  37.8 1.0 %collective-permute-start.16 = (bf16[128,1152]{1,0:T(8,128)(2,1)S(1)}, bf16[128,1152]{1,0:T(8,128)(2,1)S(1)}, u32[]{:S(2)}, u32[]{:S(2)}) collective-permute-start(bf16[128,1152]{1,0:T(8,128)(2,1)S(1)} %shard_map.89.refs_1_), channel_id=1, source_target_pairs={{0,4},{1,5},{2,6},{3,7},{4,0},{5,1},{6,2},{7,3},{8,12},{9,13},{10,... | collective-permute-start | bytes 884744 | tf_op jit(solution)/shard_map/ppermute | solution.py:21
  38.7 2.5 %collective-permute-start.11 = (f32[16,128]{1,0:T(8,128)S(1)}, f32[16,128]{1,0:T(8,128)S(1)}, u32[]{:S(2)}, u32[]{:S(2)}) collective-permute-start(f32[16,128]{1,0:T(8,128)S(1)} %shard_map.87.refs_1_.sums), channel_id=1, source_target_pairs={{0,12},{1,13},{2,14},{3,15},{4,8},{5,9},{6,10},{7,11},{8,4},{9,5},... | collective-permute-start | bytes 24584 | tf_op jit(solution)/shard_map/ppermute | solution.py:21
  41.2 0.0 collective-permute-done.12.refs_0_
  41.2 0.0 collective-permute-done.13.refs_1_
  41.2 6.3 %collective-permute-done.11.sums_recv = f32[16,128]{1,0:T(8,128)S(1)} collective-permute-done((f32[16,128]{1,0:T(8,128)S(1)}, f32[16,128]{1,0:T(8,128)S(1)}, u32[]{:S(2)}, u32[]{:S(2)}) %collective-permute-start.11) | collective-permute-done | bytes 8224 | tf_op jit(solution)/shard_map/ppermute | solution.py:21
  47.5 0.0 collective-permute-done.15.refs_6_
  47.5 0.0 collective-permute-done.16.refs_7_
  47.5 1.3 %shard_map.91 = (bf16[128,1152]{1,0:T(8,128)(2,1)}, bf16[128,1152]{1,0:T(8,128)(2,1)}, f32[1,1]{1,0:T(1,128)}, f32[1,1]{1,0:T(1,128)}) custom-call(f32[16,128]{1,0:T(8,128)S(1)} %shard_map.87.refs_1_.sums, f32[16,128]{1,0:T(8,128)S(1)} %collective-permute-done.11.sums_recv, bf16[128,1152]{1,0:T(8,128)(2,1)S(1)} %copy-done.1, ...), custom_call_target="tpu_custom_call" | custom-call | tf_op jit(solution)/shard_map/pallas_call | solution.py:248
  (8 shorter events, 0.0 us)
Async XLA Ops:
  0.6 13.6 %copy-start.1 = (bf16[128,1152]{1,0:T(8,128)(2,1)S(1)}, bf16[128,1152]{1,0:T(8,128)(2,1)}, u32[]{:S(2)}) copy-start(bf16[128,1152]{1,0:T(8,128)(2,1)} %refs_0_.1) | copy-start | bytes 884740
  0.6 10.2 %collective-permute-start = (bf16[128,1152]{1,0:T(8,128)(2,1)}, bf16[128,1152]{1,0:T(8,128)(2,1)S(1)}, u32[]{:S(2)}, u32[]{:S(2)}) collective-permute-start(bf16[128,1152]{1,0:T(8,128)(2,1)} %refs_4_.1), channel_id=1, source_target_pairs={{0,2},{1,3},{2,0},{3,1},{4,6},{5,7},{6,4},{7,5},{8,10},{9,11},{10,... | collective-permute-start | bytes 884744 | tf_op jit(solution)/shard_map/ppermute | solution.py:21
  3.6 11.7 %collective-permute-start.1 = (bf16[128,1152]{1,0:T(8,128)(2,1)}, bf16[128,1152]{1,0:T(8,128)(2,1)S(1)}, u32[]{:S(2)}, u32[]{:S(2)}) collective-permute-start(bf16[128,1152]{1,0:T(8,128)(2,1)} %refs_4_.1), channel_id=1, source_target_pairs={{0,4},{1,5},{2,6},{3,7},{4,0},{5,1},{6,2},{7,3},{8,12},{9,13},{10,... | collective-permute-start | bytes 884744 | tf_op jit(solution)/shard_map/ppermute | solution.py:21
  5.2 16.7 %collective-permute-start.4 = (bf16[128,1152]{1,0:T(8,128)(2,1)}, bf16[128,1152]{1,0:T(8,128)(2,1)S(1)}, u32[]{:S(2)}, u32[]{:S(2)}) collective-permute-start(bf16[128,1152]{1,0:T(8,128)(2,1)} %refs_0_.1), channel_id=1, source_target_pairs={{0,12},{1,13},{2,14},{3,15},{4,8},{5,9},{6,10},{7,11},{8,4},{9,5},... | collective-permute-start | bytes 884744 | tf_op jit(solution)/shard_map/ppermute | solution.py:21
  11.0 11.1 %collective-permute-start.3 = (bf16[48,1152]{1,0:T(8,128)(2,1)S(1)}, bf16[48,1152]{1,0:T(8,128)(2,1)S(1)}, u32[]{:S(2)}, u32[]{:S(2)}) collective-permute-start(bf16[48,1152]{1,0:T(8,128)(2,1)S(1)} %get-tuple-element.26.refs_4_), channel_id=1, source_target_pairs={{0,4},{1,5},{2,6},{3,7},{4,0},{5,1},{6,2},{7,3},{8,12},{9,13},{10,... | collective-permute-start | bytes 331784 | tf_op jit(solution)/shard_map/ppermute | solution.py:21
  14.2 1.0 %copy-start = (bf16[128,1152]{1,0:T(8,128)(2,1)S(1)}, bf16[128,1152]{1,0:T(8,128)(2,1)}, u32[]{:S(2)}) copy-start(bf16[128,1152]{1,0:T(8,128)(2,1)} %refs_4_.1) | copy-start | bytes 884740
  14.4 9.3 %collective-permute-start.5 = (bf16[128,1152]{1,0:T(8,128)(2,1)S(1)}, bf16[128,1152]{1,0:T(8,128)(2,1)S(1)}, u32[]{:S(2)}, u32[]{:S(2)}) collective-permute-start(bf16[128,1152]{1,0:T(8,128)(2,1)S(1)} %shard_map.76.refs_0_.refs_7_), channel_id=1, source_target_pairs={{0,1},{1,0},{2,3},{3,2},{4,5},{5,4},{6,7},{7,6},{8,9},{9,8},{10,11... | collective-permute-start | bytes 884744 | tf_op jit(solution)/shard_map/ppermute | solution.py:21
  15.5 6.7 %collective-permute-start.2 = (bf16[80,1152]{1,0:T(8,128)(2,1)S(1)}, bf16[80,1152]{1,0:T(8,128)(2,1)S(1)}, u32[]{:S(2)}, u32[]{:S(2)}) collective-permute-start(bf16[80,1152]{1,0:T(8,128)(2,1)S(1)} %get-tuple-element.24.refs_0_.refs_1_), channel_id=1, source_target_pairs={{0,2},{1,3},{2,0},{3,1},{4,6},{5,7},{6,4},{7,5},{8,10},{9,11},{10,... | collective-permute-start | bytes 552968 | tf_op jit(solution)/shard_map/ppermute | solution.py:21
  22.1 1.6 %collective-permute-start.6 = (bf16[128,1152]{1,0:T(8,128)(2,1)S(1)}, bf16[128,1152]{1,0:T(8,128)(2,1)S(1)}, u32[]{:S(2)}, u32[]{:S(2)}) collective-permute-start(bf16[128,1152]{1,0:T(8,128)(2,1)S(1)} %shard_map.81.refs_8_), channel_id=1, source_target_pairs={{0,1},{1,0},{2,3},{3,2},{4,5},{5,4},{6,7},{7,6},{8,9},{9,8},{10,11... | collective-permute-start | bytes 884744 | tf_op jit(solution)/shard_map/ppermute | solution.py:21
  26.3 1.6 %collective-permute-start.8 = (bf16[128,1152]{1,0:T(8,128)(2,1)S(1)}, bf16[128,1152]{1,0:T(8,128)(2,1)S(1)}, u32[]{:S(2)}, u32[]{:S(2)}) collective-permute-start(bf16[128,1152]{1,0:T(8,128)(2,1)S(1)} %get-tuple-element.29), channel_id=1, source_target_pairs={{0,1},{1,0},{2,3},{3,2},{4,5},{5,4},{6,7},{7,6},{8,9},{9,8},{10,11... | collective-permute-start | bytes 884744 | tf_op jit(solution)/shard_map/ppermute | solution.py:21
  26.5 10.4 %collective-permute-start.14 = (bf16[128,1152]{1,0:T(8,128)(2,1)S(1)}, bf16[128,1152]{1,0:T(8,128)(2,1)S(1)}, u32[]{:S(2)}, u32[]{:S(2)}) collective-permute-start(bf16[128,1152]{1,0:T(8,128)(2,1)S(1)} %get-tuple-element.37), channel_id=1, source_target_pairs={{0,2},{1,3},{2,0},{3,1},{4,6},{5,7},{6,4},{7,5},{8,10},{9,11},{10,... | collective-permute-start | bytes 884744 | tf_op jit(solution)/shard_map/ppermute | solution.py:21
  27.1 5.0 %collective-permute-start.7 = (f32[16,128]{1,0:T(8,128)S(1)}, f32[16,128]{1,0:T(8,128)S(1)}, u32[]{:S(2)}, u32[]{:S(2)}) collective-permute-start(f32[16,128]{1,0:T(8,128)S(1)} %get-tuple-element.27.first), channel_id=1, source_target_pairs={{0,4},{1,5},{2,6},{3,7},{4,0},{5,1},{6,2},{7,3},{8,12},{9,13},{10,... | collective-permute-start | bytes 24584 | tf_op jit(solution)/shard_map/ppermute | solution.py:21
  27.1 14.1 %collective-permute-start.12 = (bf16[128,1152]{1,0:T(8,128)(2,1)S(1)}, bf16[128,1152]{1,0:T(8,128)(2,1)S(1)}, u32[]{:S(2)}, u32[]{:S(2)}) collective-permute-start(bf16[128,1152]{1,0:T(8,128)(2,1)S(1)} %get-tuple-element.31), channel_id=1, source_target_pairs={{0,1},{1,0},{2,3},{3,2},{4,5},{5,4},{6,7},{7,6},{8,9},{9,8},{10,11... | collective-permute-start | bytes 884744 | tf_op jit(solution)/shard_map/ppermute | solution.py:21
  28.0 13.2 %collective-permute-start.13 = (bf16[128,1152]{1,0:T(8,128)(2,1)S(1)}, bf16[128,1152]{1,0:T(8,128)(2,1)S(1)}, u32[]{:S(2)}, u32[]{:S(2)}) collective-permute-start(bf16[128,1152]{1,0:T(8,128)(2,1)S(1)} %shard_map.84.refs_0_), channel_id=1, source_target_pairs={{0,12},{1,13},{2,14},{3,15},{4,8},{5,9},{6,10},{7,11},{8,4},{9,5},... | collective-permute-start | bytes 884744 | tf_op jit(solution)/shard_map/ppermute | solution.py:21
  32.1 1.2 %collective-permute-start.9 = (f32[16,128]{1,0:T(8,128)S(1)}, f32[16,128]{1,0:T(8,128)S(1)}, u32[]{:S(2)}, u32[]{:S(2)}) collective-permute-start(f32[16,128]{1,0:T(8,128)S(1)} %shard_map.85.first), channel_id=1, source_target_pairs={{0,1},{1,0},{2,3},{3,2},{4,5},{5,4},{6,7},{7,6},{8,9},{9,8},{10,11... | collective-permute-start | bytes 24584 | tf_op jit(solution)/shard_map/ppermute | solution.py:21
  33.3 3.7 %collective-permute-start.10 = (f32[16,128]{1,0:T(8,128)S(1)}, f32[16,128]{1,0:T(8,128)S(1)}, u32[]{:S(2)}, u32[]{:S(2)}) collective-permute-start(f32[16,128]{1,0:T(8,128)S(1)} %shard_map.86.first), channel_id=1, source_target_pairs={{0,2},{1,3},{2,0},{3,1},{4,6},{5,7},{6,4},{7,5},{8,10},{9,11},{10,... | collective-permute-start | bytes 24584 | tf_op jit(solution)/shard_map/ppermute | solution.py:21
  37.0 10.5 %collective-permute-start.15 = (bf16[128,1152]{1,0:T(8,128)(2,1)S(1)}, bf16[128,1152]{1,0:T(8,128)(2,1)S(1)}, u32[]{:S(2)}, u32[]{:S(2)}) collective-permute-start(bf16[128,1152]{1,0:T(8,128)(2,1)S(1)} %shard_map.90), channel_id=1, source_target_pairs={{0,2},{1,3},{2,0},{3,1},{4,6},{5,7},{6,4},{7,5},{8,10},{9,11},{10,... | collective-permute-start | bytes 884744 | tf_op jit(solution)/shard_map/ppermute | solution.py:21
  37.8 9.7 %collective-permute-start.16 = (bf16[128,1152]{1,0:T(8,128)(2,1)S(1)}, bf16[128,1152]{1,0:T(8,128)(2,1)S(1)}, u32[]{:S(2)}, u32[]{:S(2)}) collective-permute-start(bf16[128,1152]{1,0:T(8,128)(2,1)S(1)} %shard_map.89.refs_1_), channel_id=1, source_target_pairs={{0,4},{1,5},{2,6},{3,7},{4,0},{5,1},{6,2},{7,3},{8,12},{9,13},{10,... | collective-permute-start | bytes 884744 | tf_op jit(solution)/shard_map/ppermute | solution.py:21
  38.7 8.8 %collective-permute-start.11 = (f32[16,128]{1,0:T(8,128)S(1)}, f32[16,128]{1,0:T(8,128)S(1)}, u32[]{:S(2)}, u32[]{:S(2)}) collective-permute-start(f32[16,128]{1,0:T(8,128)S(1)} %shard_map.87.refs_1_.sums), channel_id=1, source_target_pairs={{0,12},{1,13},{2,14},{3,15},{4,8},{5,9},{6,10},{7,11},{8,4},{9,5},... | collective-permute-start | bytes 24584 | tf_op jit(solution)/shard_map/ppermute | solution.py:21

commit v11 on v10

--- a/solution.py
+++ b/solution.py
@@ -49,65 +49,46 @@
     return total
 
 
-def piece_kernel(value, *refs):
-    unit = unit_rows(value[...])[0].astype(jnp.bfloat16)
-    start = 0
-    for piece in refs:
-        piece[...] = unit[start : start + piece.shape[0]]
-        start += piece.shape[0]
-
-
-def piece_skip_kernel(count, value, *refs):
-    piece_kernel(value, *refs[-count:])
-
-
-def unit_pieces(value, cuts, others):
-    rows, width = value.shape
-    return pl.pallas_call(
-        functools.partial(piece_skip_kernel, len(cuts)),
-        out_shape=[jax.ShapeDtypeStruct((cut, width), jnp.bfloat16) for cut in cuts],
-        in_specs=[VMEM] + [ANY] * len(others),
-        out_specs=[VMEM] * len(cuts),
-        compiler_params=pltpu.CompilerParams(vmem_limit_bytes=SMALL_VMEM),
-        cost_estimate=pl.CostEstimate(
-            flops=4 * value.size, bytes_accessed=4 * value.size, transcendentals=rows
-        ),
-    )(value, *others)
+def unit_kernel(value, *refs):
+    refs[-1][...] = unit_rows(value[...])[0].astype(jnp.bfloat16)
+
+
+def unit_block(value, others):
+    return [
+        pl.pallas_call(
+            unit_kernel,
+            out_shape=jax.ShapeDtypeStruct(value.shape, jnp.bfloat16),
+            in_specs=[VMEM] + [ANY] * len(others),
+            out_specs=VMEM,
+            compiler_params=pltpu.CompilerParams(vmem_limit_bytes=SMALL_VMEM),
+            cost_estimate=pl.CostEstimate(
+                flops=4 * value.size, bytes_accessed=4 * value.size, transcendentals=0
+            ),
+        )(value, *others)
+    ]
 
 
 def gathered(image, text, img_bits, txt_bits):
     img_raw = [swapped(image, bit) for bit in img_bits]
     txt_raw = swapped(text, txt_bits[0])
-    rows = image.shape[0]
-    cuts = [rows * 5 // 8, rows * 3 // 8]
     imgs, txts = {}, {}
-    others = []
-    for place in reversed(range(1, len(img_bits))):
-        imgs[1 << place] = unit_pieces(img_raw[place], cuts, others)
-        others = imgs[1 << place][:1]
-    txts[0] = unit_pieces(text, [rows], others)
-    imgs[0] = unit_pieces(image, [rows], txts[0])
+    imgs[1] = unit_block(img_raw[0], [])
+    txts[0] = unit_block(text, imgs[1])
+    imgs[0] = unit_block(image, txts[0])
     for place in range(1, len(txt_bits)):
         txts[1 << place] = [swapped(txts[0][0], txt_bits[place])]
-    imgs[1] = unit_pieces(img_raw[0], cuts, imgs[0])
-    txts[1] = unit_pieces(txt_raw, [rows], imgs[1][:1])
-    for offset in range(1 << len(img_bits)):
-        if offset not in imgs:
-            high = offset.bit_length() - 1
-            low = (offset & -offset).bit_length() - 1
-            imgs[offset] = [
-                swapped(imgs[offset ^ 1 << high][0], img_bits[high]),
-                swapped(imgs[offset ^ 1 << low][1], img_bits[low]),
-            ]
-    for offset in range(1 << len(txt_bits)):
-        if offset not in txts:
-            high = offset.bit_length() - 1
-            txts[offset] = [swapped(txts[offset ^ 1 << high][0], txt_bits[high])]
+    txts[1] = others = unit_block(txt_raw, imgs[0])
+    for place in range(1, len(img_bits)):
+        imgs[1 << place] = others = unit_block(img_raw[place], others)
+    for blocks, bits in ((imgs, img_bits), (txts, txt_bits)):
+        for offset in range(1 << len(bits)):
+            if offset not in blocks:
+                high = offset.bit_length() - 1
+                blocks[offset] = [swapped(blocks[offset ^ 1 << high][0], bits[high])]
     imgs = [imgs[offset] for offset in range(1 << len(img_bits))]
     txts = [txts[offset] for offset in range(1 << len(txt_bits))]
-    last = held(imgs[-1][1:], [], GATHER_COST)
-    imgs[-1] = held(imgs[-1][:1], last, GATHER_COST) + last
-    txts[-1] = held(txts[-1], imgs[-1][:1])
+    imgs[-1] = held(imgs[-1], [], GATHER_COST)
+    txts[-1] = held(txts[-1], imgs[-1])
     return imgs, txts
 
 

time: 49 us -> 50.1 us (1.022)
  starting transfers between devices: 20.5 us -> 23.1 us
  waiting for transfers between devices: 20.8 us -> 19.3 us
    ppermute x17 -> x16, starting transfers between devices: 20.5 us -> 23.1 us  [swapped(): return lax.ppermute(x, 'blk', [(i, i ^ bit) for i in range(count)])]
    ppermute x17 -> x16, waiting for transfers between devices: 20.8 us -> 19.3 us  [swapped(): return lax.ppermute(x, 'blk', [(i, i ^ bit) for i in range(count)])]
  transfers between devices with their start and end apart: 17 -> 16, of which waited for: 7 -> 7; matrix products, arithmetic and copies ran while one was open for 0% -> 0% of each run, Pallas kernels for 2% -> 2%
where the time goes in v11:
time: 50.1 us; the launch traced here: 49.9 us
  starting transfers between devices  23.1 us (46%)
  waiting for transfers between devices  19.3 us (39%)
  Pallas kernels  4.76 us (10%)
  between operations  2.03 us (4%)
  local copies, waits for them, and re-layouts  0.73 us (1%)
    ppermute x16, starting transfers between devices, swapped(): return lax.ppermute(x, 'blk', [(i, i ^ bit) for i in range(count)])  23.1 us
    ppermute x16, waiting for transfers between devices, swapped(): return lax.ppermute(x, 'blk', [(i, i ^ bit) for i in range(count)])  19.3 us
    pallas_call x1, Pallas kernels, tile_call(): pl.pallas_call(functools.partial(tile_kernel, [len(block) for block in im...  2.59 us
    pallas_call x1, Pallas kernels, finish_call(): pl.pallas_call(functools.partial(finish_kernel, [len(recvs) for _, _, rec...  1.32 us
  transfers between devices with their start and end apart: 16, of which 7 were waited for; matrix products, arithmetic and copies ran while one was open for 0% of the time, Pallas kernels for 2%

profile of v11, /device:TPU:0, one launch (start us, length us, event | category | flops | bytes accessed | tf_op | source)
XLA Modules:
  0.0 49.9 jit_solution(6513156108295365756)
XLA Ops:
  0.6 0.0 copy-start.1
  0.6 3.1 %collective-permute-start = (bf16[128,1152]{1,0:T(8,128)(2,1)}, bf16[128,1152]{1,0:T(8,128)(2,1)S(1)}, u32[]{:S(2)}, u32[]{:S(2)}) collective-permute-start(bf16[128,1152]{1,0:T(8,128)(2,1)} %refs_4_.1), channel_id=1, source_target_pairs={{0,4},{1,5},{2,6},{3,7},{4,0},{5,1},{6,2},{7,3},{8,12},{9,13},{10,... | collective-permute-start | bytes 884744 | tf_op jit(solution)/shard_map/ppermute | solution.py:21
  3.7 2.5 %collective-permute-start.2 = (bf16[128,1152]{1,0:T(8,128)(2,1)}, bf16[128,1152]{1,0:T(8,128)(2,1)S(1)}, u32[]{:S(2)}, u32[]{:S(2)}) collective-permute-start(bf16[128,1152]{1,0:T(8,128)(2,1)} %refs_0_.1), channel_id=1, source_target_pairs={{0,12},{1,13},{2,14},{3,15},{4,8},{5,9},{6,10},{7,11},{8,4},{9,5},... | collective-permute-start | bytes 884744 | tf_op jit(solution)/shard_map/ppermute | solution.py:21
  6.2 1.5 %collective-permute-start.1 = (bf16[128,1152]{1,0:T(8,128)(2,1)}, bf16[128,1152]{1,0:T(8,128)(2,1)S(1)}, u32[]{:S(2)}, u32[]{:S(2)}) collective-permute-start(bf16[128,1152]{1,0:T(8,128)(2,1)} %refs_4_.1), channel_id=1, source_target_pairs={{0,2},{1,3},{2,0},{3,1},{4,6},{5,7},{6,4},{7,5},{8,10},{9,11},{10,... | collective-permute-start | bytes 884744 | tf_op jit(solution)/shard_map/ppermute | solution.py:21
  7.7 3.8 %collective-permute-done.value = bf16[128,1152]{1,0:T(8,128)(2,1)S(1)} collective-permute-done((bf16[128,1152]{1,0:T(8,128)(2,1)}, bf16[128,1152]{1,0:T(8,128)(2,1)S(1)}, u32[]{:S(2)}, u32[]{:S(2)}) %collective-permute-start) | collective-permute-done | bytes 294944 | tf_op jit(solution)/shard_map/ppermute | solution.py:21
  11.5 0.1 shard_map.75.refs_0_.refs_1_
  11.6 1.6 %collective-permute-start.3 = (bf16[128,1152]{1,0:T(8,128)(2,1)S(1)}, bf16[128,1152]{1,0:T(8,128)(2,1)S(1)}, u32[]{:S(2)}, u32[]{:S(2)}) collective-permute-start(bf16[128,1152]{1,0:T(8,128)(2,1)S(1)} %shard_map.75.refs_0_.refs_1_), channel_id=1, source_target_pairs={{0,2},{1,3},{2,0},{3,1},{4,6},{5,7},{6,4},{7,5},{8,10},{9,11},{10,... | collective-permute-start | bytes 884744 | tf_op jit(solution)/shard_map/ppermute | solution.py:21
  14.5 0.0 copy-done.1
  14.5 0.0 copy-start
  14.5 0.1 shard_map.76.refs_0_.refs_4_
  14.6 0.1 collective-permute-start.4
  14.7 0.7 %copy-done = bf16[128,1152]{1,0:T(8,128)(2,1)S(1)} copy-done((bf16[128,1152]{1,0:T(8,128)(2,1)S(1)}, bf16[128,1152]{1,0:T(8,128)(2,1)}, u32[]{:S(2)}) %copy-start) | copy-done | bytes 294936
  15.4 0.1 shard_map.77.refs_0_
  15.6 4.0 %collective-permute-done.2.value = bf16[128,1152]{1,0:T(8,128)(2,1)S(1)} collective-permute-done((bf16[128,1152]{1,0:T(8,128)(2,1)}, bf16[128,1152]{1,0:T(8,128)(2,1)S(1)}, u32[]{:S(2)}, u32[]{:S(2)}) %collective-permute-start.2) | collective-permute-done | bytes 294944 | tf_op jit(solution)/shard_map/ppermute | solution.py:21
  19.6 0.1 shard_map.78.refs_0_.refs_5_
  19.7 0.1 collective-permute-start.5
  19.8 0.0 collective-permute-done.1.value
  19.8 0.1 shard_map.79.refs_2_
  20.0 1.0 %collective-permute-done.3.refs_0_ = bf16[128,1152]{1,0:T(8,128)(2,1)S(1)} collective-permute-done((bf16[128,1152]{1,0:T(8,128)(2,1)S(1)}, bf16[128,1152]{1,0:T(8,128)(2,1)S(1)}, u32[]{:S(2)}, u32[]{:S(2)}) %collective-permute-start.3) | collective-permute-done | bytes 294944 | tf_op jit(solution)/shard_map/ppermute | solution.py:21
  20.9 0.4 collective-permute-done.5.refs_0_
  21.4 0.0 collective-permute-done.4.refs_6_
  21.4 2.6 %shard_map.82 = (f32[128,1152]{1,0:T(8,128)S(1)}, f32[128,1152]{1,0:T(8,128)S(1)}, bf16[128,1152]{1,0:T(8,128)(2,1)S(1)}, bf16[128,1152]{1,0:T(8,128)(2,1)S(1)},...) custom-call(bf16[128,1152]{1,0:T(8,128)(2,1)S(1)} %shard_map.77.refs, ...), custom_call_target="tpu_custom_call" | custom-call | flops 1811939328 | tf_op jit(solution)/shard_map/pallas_call | solution.py:175
  24.0 0.2 collective-permute-start.7
  24.2 1.5 %collective-permute-start.13 = (bf16[128,1152]{1,0:T(8,128)(2,1)S(1)}, bf16[128,1152]{1,0:T(8,128)(2,1)S(1)}, u32[]{:S(2)}, u32[]{:S(2)}) collective-permute-start(bf16[128,1152]{1,0:T(8,128)(2,1)S(1)} %get-tuple-element.29), channel_id=1, source_target_pairs={{0,2},{1,3},{2,0},{3,1},{4,6},{5,7},{6,4},{7,5},{8,10},{9,11},{10,... | collective-permute-start | bytes 884744 | tf_op jit(solution)/shard_map/ppermute | solution.py:21
  25.7 0.6 %collective-permute-start.6 = (f32[16,128]{1,0:T(8,128)S(1)}, f32[16,128]{1,0:T(8,128)S(1)}, u32[]{:S(2)}, u32[]{:S(2)}) collective-permute-start(f32[16,128]{1,0:T(8,128)S(1)} %get-tuple-element.19.first), channel_id=1, source_target_pairs={{0,4},{1,5},{2,6},{3,7},{4,0},{5,1},{6,2},{7,3},{8,12},{9,13},{10,... | collective-permute-start | bytes 24584 | tf_op jit(solution)/shard_map/ppermute | solution.py:21
  26.2 0.0 collective-permute-start.11
  26.2 0.0 collective-permute-done.7.recv
  26.2 0.1 shard_map.83.refs_0_
  26.3 6.2 %collective-permute-start.12 = (bf16[128,1152]{1,0:T(8,128)(2,1)S(1)}, bf16[128,1152]{1,0:T(8,128)(2,1)S(1)}, u32[]{:S(2)}, u32[]{:S(2)}) collective-permute-start(bf16[128,1152]{1,0:T(8,128)(2,1)S(1)} %shard_map.83.refs_0_), channel_id=1, source_target_pairs={{0,12},{1,13},{2,14},{3,15},{4,8},{5,9},{6,10},{7,11},{8,4},{9,5},... | collective-permute-start | bytes 884744 | tf_op jit(solution)/shard_map/ppermute | solution.py:21
  32.5 0.0 collective-permute-done.6.second
  32.5 0.1 collective-permute-start.8
  32.6 1.1 %collective-permute-done.8.second = f32[16,128]{1,0:T(8,128)S(1)} collective-permute-done((f32[16,128]{1,0:T(8,128)S(1)}, f32[16,128]{1,0:T(8,128)S(1)}, u32[]{:S(2)}, u32[]{:S(2)}) %collective-permute-start.8) | collective-permute-done | bytes 8224 | tf_op jit(solution)/shard_map/ppermute | solution.py:21
  33.7 1.3 %collective-permute-start.9 = (f32[16,128]{1,0:T(8,128)S(1)}, f32[16,128]{1,0:T(8,128)S(1)}, u32[]{:S(2)}, u32[]{:S(2)}) collective-permute-start(f32[16,128]{1,0:T(8,128)S(1)} %shard_map.85.first), channel_id=1, source_target_pairs={{0,2},{1,3},{2,0},{3,1},{4,6},{5,7},{6,4},{7,5},{8,10},{9,11},{10,... | collective-permute-start | bytes 24584 | tf_op jit(solution)/shard_map/ppermute | solution.py:21
  35.0 2.3 %collective-permute-done.9.second = f32[16,128]{1,0:T(8,128)S(1)} collective-permute-done((f32[16,128]{1,0:T(8,128)S(1)}, f32[16,128]{1,0:T(8,128)S(1)}, u32[]{:S(2)}, u32[]{:S(2)}) %collective-permute-start.9) | collective-permute-done | bytes 8224 | tf_op jit(solution)/shard_map/ppermute | solution.py:21
  37.4 0.0 collective-permute-done.13.recv
  37.4 0.1 shard_map.88.refs_1_
  37.4 1.4 %collective-permute-start.14 = (bf16[128,1152]{1,0:T(8,128)(2,1)S(1)}, bf16[128,1152]{1,0:T(8,128)(2,1)S(1)}, u32[]{:S(2)}, u32[]{:S(2)}) collective-permute-start(bf16[128,1152]{1,0:T(8,128)(2,1)S(1)} %shard_map.89), channel_id=1, source_target_pairs={{0,2},{1,3},{2,0},{3,1},{4,6},{5,7},{6,4},{7,5},{8,10},{9,11},{10,... | collective-permute-start | bytes 884744 | tf_op jit(solution)/shard_map/ppermute | solution.py:21
  38.8 0.2 collective-permute-start.15
  39.0 2.9 %collective-permute-start.10 = (f32[16,128]{1,0:T(8,128)S(1)}, f32[16,128]{1,0:T(8,128)S(1)}, u32[]{:S(2)}, u32[]{:S(2)}) collective-permute-start(f32[16,128]{1,0:T(8,128)S(1)} %shard_map.86.refs_1_.sums), channel_id=1, source_target_pairs={{0,12},{1,13},{2,14},{3,15},{4,8},{5,9},{6,10},{7,11},{8,4},{9,5},... | collective-permute-start | bytes 24584 | tf_op jit(solution)/shard_map/ppermute | solution.py:21
  41.9 0.0 collective-permute-done.11.refs_0_
  41.9 0.0 collective-permute-done.12.refs_1_
  41.9 6.7 %collective-permute-done.10.sums_recv = f32[16,128]{1,0:T(8,128)S(1)} collective-permute-done((f32[16,128]{1,0:T(8,128)S(1)}, f32[16,128]{1,0:T(8,128)S(1)}, u32[]{:S(2)}, u32[]{:S(2)}) %collective-permute-start.10) | collective-permute-done | bytes 8224 | tf_op jit(solution)/shard_map/ppermute | solution.py:21
  48.6 0.0 collective-permute-done.14.refs_6_
  48.6 0.0 collective-permute-done.15.refs_7_
  48.6 1.3 %shard_map.90 = (bf16[128,1152]{1,0:T(8,128)(2,1)}, bf16[128,1152]{1,0:T(8,128)(2,1)}, f32[1,1]{1,0:T(1,128)}, f32[1,1]{1,0:T(1,128)}) custom-call(f32[16,128]{1,0:T(8,128)S(1)} %shard_map.86.refs_1_.sums, f32[16,128]{1,0:T(8,128)S(1)} %collective-permute-done.10.sums_recv, bf16[128,1152]{1,0:T(8,128)(2,1)S(1)} %copy-done.1, ...), custom_call_target="tpu_custom_call" | custom-call | tf_op jit(solution)/shard_map/pallas_call | solution.py:229
  (7 shorter events, 0.0 us)
Async XLA Ops:
  0.6 13.8 %copy-start.1 = (bf16[128,1152]{1,0:T(8,128)(2,1)S(1)}, bf16[128,1152]{1,0:T(8,128)(2,1)}, u32[]{:S(2)}) copy-start(bf16[128,1152]{1,0:T(8,128)(2,1)} %refs_0_.1) | copy-start | bytes 884740
  0.6 10.8 %collective-permute-start = (bf16[128,1152]{1,0:T(8,128)(2,1)}, bf16[128,1152]{1,0:T(8,128)(2,1)S(1)}, u32[]{:S(2)}, u32[]{:S(2)}) collective-permute-start(bf16[128,1152]{1,0:T(8,128)(2,1)} %refs_4_.1), channel_id=1, source_target_pairs={{0,4},{1,5},{2,6},{3,7},{4,0},{5,1},{6,2},{7,3},{8,12},{9,13},{10,... | collective-permute-start | bytes 884744 | tf_op jit(solution)/shard_map/ppermute | solution.py:21
  3.7 15.8 %collective-permute-start.2 = (bf16[128,1152]{1,0:T(8,128)(2,1)}, bf16[128,1152]{1,0:T(8,128)(2,1)S(1)}, u32[]{:S(2)}, u32[]{:S(2)}) collective-permute-start(bf16[128,1152]{1,0:T(8,128)(2,1)} %refs_0_.1), channel_id=1, source_target_pairs={{0,12},{1,13},{2,14},{3,15},{4,8},{5,9},{6,10},{7,11},{8,4},{9,5},... | collective-permute-start | bytes 884744 | tf_op jit(solution)/shard_map/ppermute | solution.py:21
  6.2 13.6 %collective-permute-start.1 = (bf16[128,1152]{1,0:T(8,128)(2,1)}, bf16[128,1152]{1,0:T(8,128)(2,1)S(1)}, u32[]{:S(2)}, u32[]{:S(2)}) collective-permute-start(bf16[128,1152]{1,0:T(8,128)(2,1)} %refs_4_.1), channel_id=1, source_target_pairs={{0,2},{1,3},{2,0},{3,1},{4,6},{5,7},{6,4},{7,5},{8,10},{9,11},{10,... | collective-permute-start | bytes 884744 | tf_op jit(solution)/shard_map/ppermute | solution.py:21
  11.6 9.3 %collective-permute-start.3 = (bf16[128,1152]{1,0:T(8,128)(2,1)S(1)}, bf16[128,1152]{1,0:T(8,128)(2,1)S(1)}, u32[]{:S(2)}, u32[]{:S(2)}) collective-permute-start(bf16[128,1152]{1,0:T(8,128)(2,1)S(1)} %shard_map.75.refs_0_.refs_1_), channel_id=1, source_target_pairs={{0,2},{1,3},{2,0},{3,1},{4,6},{5,7},{6,4},{7,5},{8,10},{9,11},{10,... | collective-permute-start | bytes 884744 | tf_op jit(solution)/shard_map/ppermute | solution.py:21
  14.5 1.0 %copy-start = (bf16[128,1152]{1,0:T(8,128)(2,1)S(1)}, bf16[128,1152]{1,0:T(8,128)(2,1)}, u32[]{:S(2)}) copy-start(bf16[128,1152]{1,0:T(8,128)(2,1)} %refs_4_.1) | copy-start | bytes 884740
  14.6 6.7 %collective-permute-start.4 = (bf16[128,1152]{1,0:T(8,128)(2,1)S(1)}, bf16[128,1152]{1,0:T(8,128)(2,1)S(1)}, u32[]{:S(2)}, u32[]{:S(2)}) collective-permute-start(bf16[128,1152]{1,0:T(8,128)(2,1)S(1)} %shard_map.76.refs_0_.refs_4_), channel_id=1, source_target_pairs={{0,1},{1,0},{2,3},{3,2},{4,5},{5,4},{6,7},{7,6},{8,9},{9,8},{10,11... | collective-permute-start | bytes 884744 | tf_op jit(solution)/shard_map/ppermute | solution.py:21
  19.7 1.6 %collective-permute-start.5 = (bf16[128,1152]{1,0:T(8,128)(2,1)S(1)}, bf16[128,1152]{1,0:T(8,128)(2,1)S(1)}, u32[]{:S(2)}, u32[]{:S(2)}) collective-permute-start(bf16[128,1152]{1,0:T(8,128)(2,1)S(1)} %shard_map.78.refs_0_.refs_5_), channel_id=1, source_target_pairs={{0,1},{1,0},{2,3},{3,2},{4,5},{5,4},{6,7},{7,6},{8,9},{9,8},{10,11... | collective-permute-start | bytes 884744 | tf_op jit(solution)/shard_map/ppermute | solution.py:21
  24.0 2.3 %collective-permute-start.7 = (bf16[128,1152]{1,0:T(8,128)(2,1)S(1)}, bf16[128,1152]{1,0:T(8,128)(2,1)S(1)}, u32[]{:S(2)}, u32[]{:S(2)}) collective-permute-start(bf16[128,1152]{1,0:T(8,128)(2,1)S(1)} %get-tuple-element.21), channel_id=1, source_target_pairs={{0,1},{1,0},{2,3},{3,2},{4,5},{5,4},{6,7},{7,6},{8,9},{9,8},{10,11... | collective-permute-start | bytes 884744 | tf_op jit(solution)/shard_map/ppermute | solution.py:21
  24.2 13.2 %collective-permute-start.13 = (bf16[128,1152]{1,0:T(8,128)(2,1)S(1)}, bf16[128,1152]{1,0:T(8,128)(2,1)S(1)}, u32[]{:S(2)}, u32[]{:S(2)}) collective-permute-start(bf16[128,1152]{1,0:T(8,128)(2,1)S(1)} %get-tuple-element.29), channel_id=1, source_target_pairs={{0,2},{1,3},{2,0},{3,1},{4,6},{5,7},{6,4},{7,5},{8,10},{9,11},{10,... | collective-permute-start | bytes 884744 | tf_op jit(solution)/shard_map/ppermute | solution.py:21
  25.7 6.8 %collective-permute-start.6 = (f32[16,128]{1,0:T(8,128)S(1)}, f32[16,128]{1,0:T(8,128)S(1)}, u32[]{:S(2)}, u32[]{:S(2)}) collective-permute-start(f32[16,128]{1,0:T(8,128)S(1)} %get-tuple-element.19.first), channel_id=1, source_target_pairs={{0,4},{1,5},{2,6},{3,7},{4,0},{5,1},{6,2},{7,3},{8,12},{9,13},{10,... | collective-permute-start | bytes 24584 | tf_op jit(solution)/shard_map/ppermute | solution.py:21
  26.2 15.7 %collective-permute-start.11 = (bf16[128,1152]{1,0:T(8,128)(2,1)S(1)}, bf16[128,1152]{1,0:T(8,128)(2,1)S(1)}, u32[]{:S(2)}, u32[]{:S(2)}) collective-permute-start(bf16[128,1152]{1,0:T(8,128)(2,1)S(1)} %get-tuple-element.23), channel_id=1, source_target_pairs={{0,1},{1,0},{2,3},{3,2},{4,5},{5,4},{6,7},{7,6},{8,9},{9,8},{10,11... | collective-permute-start | bytes 884744 | tf_op jit(solution)/shard_map/ppermute | solution.py:21
  26.3 15.6 %collective-permute-start.12 = (bf16[128,1152]{1,0:T(8,128)(2,1)S(1)}, bf16[128,1152]{1,0:T(8,128)(2,1)S(1)}, u32[]{:S(2)}, u32[]{:S(2)}) collective-permute-start(bf16[128,1152]{1,0:T(8,128)(2,1)S(1)} %shard_map.83.refs_0_), channel_id=1, source_target_pairs={{0,12},{1,13},{2,14},{3,15},{4,8},{5,9},{6,10},{7,11},{8,4},{9,5},... | collective-permute-start | bytes 884744 | tf_op jit(solution)/shard_map/ppermute | solution.py:21
  32.5 1.2 %collective-permute-start.8 = (f32[16,128]{1,0:T(8,128)S(1)}, f32[16,128]{1,0:T(8,128)S(1)}, u32[]{:S(2)}, u32[]{:S(2)}) collective-permute-start(f32[16,128]{1,0:T(8,128)S(1)} %shard_map.84.first), channel_id=1, source_target_pairs={{0,1},{1,0},{2,3},{3,2},{4,5},{5,4},{6,7},{7,6},{8,9},{9,8},{10,11... | collective-permute-start | bytes 24584 | tf_op jit(solution)/shard_map/ppermute | solution.py:21
  33.7 3.7 %collective-permute-start.9 = (f32[16,128]{1,0:T(8,128)S(1)}, f32[16,128]{1,0:T(8,128)S(1)}, u32[]{:S(2)}, u32[]{:S(2)}) collective-permute-start(f32[16,128]{1,0:T(8,128)S(1)} %shard_map.85.first), channel_id=1, source_target_pairs={{0,2},{1,3},{2,0},{3,1},{4,6},{5,7},{6,4},{7,5},{8,10},{9,11},{10,... | collective-permute-start | bytes 24584 | tf_op jit(solution)/shard_map/ppermute | solution.py:21
  37.4 11.2 %collective-permute-start.14 = (bf16[128,1152]{1,0:T(8,128)(2,1)S(1)}, bf16[128,1152]{1,0:T(8,128)(2,1)S(1)}, u32[]{:S(2)}, u32[]{:S(2)}) collective-permute-start(bf16[128,1152]{1,0:T(8,128)(2,1)S(1)} %shard_map.89), channel_id=1, source_target_pairs={{0,2},{1,3},{2,0},{3,1},{4,6},{5,7},{6,4},{7,5},{8,10},{9,11},{10,... | collective-permute-start | bytes 884744 | tf_op jit(solution)/shard_map/ppermute | solution.py:21
  38.8 9.8 %collective-permute-start.15 = (bf16[128,1152]{1,0:T(8,128)(2,1)S(1)}, bf16[128,1152]{1,0:T(8,128)(2,1)S(1)}, u32[]{:S(2)}, u32[]{:S(2)}) collective-permute-start(bf16[128,1152]{1,0:T(8,128)(2,1)S(1)} %shard_map.88.refs_1_), channel_id=1, source_target_pairs={{0,4},{1,5},{2,6},{3,7},{4,0},{5,1},{6,2},{7,3},{8,12},{9,13},{10,... | collective-permute-start | bytes 884744 | tf_op jit(solution)/shard_map/ppermute | solution.py:21
  39.0 9.6 %collective-permute-start.10 = (f32[16,128]{1,0:T(8,128)S(1)}, f32[16,128]{1,0:T(8,128)S(1)}, u32[]{:S(2)}, u32[]{:S(2)}) collective-permute-start(f32[16,128]{1,0:T(8,128)S(1)} %shard_map.86.refs_1_.sums), channel_id=1, source_target_pairs={{0,12},{1,13},{2,14},{3,15},{4,8},{5,9},{6,10},{7,11},{8,4},{9,5},... | collective-permute-start | bytes 24584 | tf_op jit(solution)/shard_map/ppermute | solution.py:21

commit v12 on v11

--- a/solution.py
+++ b/solution.py
@@ -77,9 +77,10 @@
     imgs[0] = unit_block(image, txts[0])
     for place in range(1, len(txt_bits)):
         txts[1 << place] = [swapped(txts[0][0], txt_bits[place])]
-    txts[1] = others = unit_block(txt_raw, imgs[0])
+    others = imgs[0]
     for place in range(1, len(img_bits)):
         imgs[1 << place] = others = unit_block(img_raw[place], others)
+    txts[1] = unit_block(txt_raw, others)
     for blocks, bits in ((imgs, img_bits), (txts, txt_bits)):
         for offset in range(1 << len(bits)):
             if offset not in blocks:

time: 50.1 us -> 50.1 us (level)
  transfers between devices with their start and end apart: 16 -> 16, of which waited for: 7 -> 6; matrix products, arithmetic and copies ran while one was open for 0% -> 0% of each run, Pallas kernels for 2% -> 2%
where the time goes in v12:
time: 50.1 us; the launch traced here: 49.9 us
  starting transfers between devices  23.1 us (46%)
  waiting for transfers between devices  19.3 us (39%)
  Pallas kernels  4.77 us (10%)
  between operations  2.05 us (4%)
  local copies, waits for them, and re-layouts  0.73 us (1%)
    ppermute x16, starting transfers between devices, swapped(): return lax.ppermute(x, 'blk', [(i, i ^ bit) for i in range(count)])  23.1 us
    ppermute x16, waiting for transfers between devices, swapped(): return lax.ppermute(x, 'blk', [(i, i ^ bit) for i in range(count)])  19.3 us
    pallas_call x1, Pallas kernels, tile_call(): pl.pallas_call(functools.partial(tile_kernel, [len(block) for block in im...  2.6 us
    pallas_call x1, Pallas kernels, finish_call(): pl.pallas_call(functools.partial(finish_kernel, [len(recvs) for _, _, rec...  1.32 us
  transfers between devices with their start and end apart: 16, of which 6 were waited for; matrix products, arithmetic and copies ran while one was open for 0% of the time, Pallas kernels for 2%

profile of v12, /device:TPU:0, one launch (start us, length us, event | category | flops | bytes accessed | tf_op | source)
XLA Modules:
  0.0 49.9 jit_solution(4537615671008281548)
XLA Ops:
  0.6 0.0 copy-start.1
  0.6 3.1 %collective-permute-start = (bf16[128,1152]{1,0:T(8,128)(2,1)}, bf16[128,1152]{1,0:T(8,128)(2,1)S(1)}, u32[]{:S(2)}, u32[]{:S(2)}) collective-permute-start(bf16[128,1152]{1,0:T(8,128)(2,1)} %refs_4_.1), channel_id=1, source_target_pairs={{0,4},{1,5},{2,6},{3,7},{4,0},{5,1},{6,2},{7,3},{8,12},{9,13},{10,... | collective-permute-start | bytes 884744 | tf_op jit(solution)/shard_map/ppermute | solution.py:21
  3.7 1.5 %collective-permute-start.1 = (bf16[128,1152]{1,0:T(8,128)(2,1)}, bf16[128,1152]{1,0:T(8,128)(2,1)S(1)}, u32[]{:S(2)}, u32[]{:S(2)}) collective-permute-start(bf16[128,1152]{1,0:T(8,128)(2,1)} %refs_4_.1), channel_id=1, source_target_pairs={{0,2},{1,3},{2,0},{3,1},{4,6},{5,7},{6,4},{7,5},{8,10},{9,11},{10,... | collective-permute-start | bytes 884744 | tf_op jit(solution)/shard_map/ppermute | solution.py:21
  5.2 2.5 %collective-permute-start.3 = (bf16[128,1152]{1,0:T(8,128)(2,1)}, bf16[128,1152]{1,0:T(8,128)(2,1)S(1)}, u32[]{:S(2)}, u32[]{:S(2)}) collective-permute-start(bf16[128,1152]{1,0:T(8,128)(2,1)} %refs_0_.1), channel_id=1, source_target_pairs={{0,12},{1,13},{2,14},{3,15},{4,8},{5,9},{6,10},{7,11},{8,4},{9,5},... | collective-permute-start | bytes 884744 | tf_op jit(solution)/shard_map/ppermute | solution.py:21
  7.7 3.8 %collective-permute-done.value = bf16[128,1152]{1,0:T(8,128)(2,1)S(1)} collective-permute-done((bf16[128,1152]{1,0:T(8,128)(2,1)}, bf16[128,1152]{1,0:T(8,128)(2,1)S(1)}, u32[]{:S(2)}, u32[]{:S(2)}) %collective-permute-start) | collective-permute-done | bytes 294944 | tf_op jit(solution)/shard_map/ppermute | solution.py:21
  11.5 0.1 shard_map.75.refs_0_.refs_1_
  11.6 1.6 %collective-permute-start.2 = (bf16[128,1152]{1,0:T(8,128)(2,1)S(1)}, bf16[128,1152]{1,0:T(8,128)(2,1)S(1)}, u32[]{:S(2)}, u32[]{:S(2)}) collective-permute-start(bf16[128,1152]{1,0:T(8,128)(2,1)S(1)} %shard_map.75.refs_0_.refs_1_), channel_id=1, source_target_pairs={{0,2},{1,3},{2,0},{3,1},{4,6},{5,7},{6,4},{7,5},{8,10},{9,11},{10,... | collective-permute-start | bytes 884744 | tf_op jit(solution)/shard_map/ppermute | solution.py:21
  14.5 0.0 copy-done.1
  14.5 0.0 copy-start
  14.5 0.1 shard_map.76.refs_0_.refs_4_
  14.6 0.1 collective-permute-start.4
  14.7 0.7 %copy-done = bf16[128,1152]{1,0:T(8,128)(2,1)S(1)} copy-done((bf16[128,1152]{1,0:T(8,128)(2,1)S(1)}, bf16[128,1152]{1,0:T(8,128)(2,1)}, u32[]{:S(2)}) %copy-start) | copy-done | bytes 294936
  15.4 0.1 shard_map.77.refs_0_
  15.6 0.0 collective-permute-done.1.value
  15.6 0.1 shard_map.78.refs_0_.refs_2_
  15.8 3.8 %collective-permute-done.3.value = bf16[128,1152]{1,0:T(8,128)(2,1)S(1)} collective-permute-done((bf16[128,1152]{1,0:T(8,128)(2,1)}, bf16[128,1152]{1,0:T(8,128)(2,1)S(1)}, u32[]{:S(2)}, u32[]{:S(2)}) %collective-permute-start.3) | collective-permute-done | bytes 294944 | tf_op jit(solution)/shard_map/ppermute | solution.py:21
  19.6 0.1 shard_map.80.refs_5_
  19.7 0.1 collective-permute-start.5
  19.8 0.0 collective-permute-done.2.refs_0_
  19.8 1.5 %collective-permute-done.5.refs_0_ = bf16[128,1152]{1,0:T(8,128)(2,1)S(1)} collective-permute-done((bf16[128,1152]{1,0:T(8,128)(2,1)S(1)}, bf16[128,1152]{1,0:T(8,128)(2,1)S(1)}, u32[]{:S(2)}, u32[]{:S(2)}) %collective-permute-start.5) | collective-permute-done | bytes 294944 | tf_op jit(solution)/shard_map/ppermute | solution.py:21
  21.4 0.0 collective-permute-done.4.refs_6_
  21.4 2.6 %shard_map.82 = (f32[128,1152]{1,0:T(8,128)S(1)}, f32[128,1152]{1,0:T(8,128)S(1)}, bf16[128,1152]{1,0:T(8,128)(2,1)S(1)}, bf16[128,1152]{1,0:T(8,128)(2,1)S(1)},...) custom-call(bf16[128,1152]{1,0:T(8,128)(2,1)S(1)} %shard_map.77.refs, ...), custom_call_target="tpu_custom_call" | custom-call | flops 1811939328 | tf_op jit(solution)/shard_map/pallas_call | solution.py:176
  24.0 0.2 collective-permute-start.7
  24.2 1.5 %collective-permute-start.13 = (bf16[128,1152]{1,0:T(8,128)(2,1)S(1)}, bf16[128,1152]{1,0:T(8,128)(2,1)S(1)}, u32[]{:S(2)}, u32[]{:S(2)}) collective-permute-start(bf16[128,1152]{1,0:T(8,128)(2,1)S(1)} %get-tuple-element.29), channel_id=1, source_target_pairs={{0,2},{1,3},{2,0},{3,1},{4,6},{5,7},{6,4},{7,5},{8,10},{9,11},{10,... | collective-permute-start | bytes 884744 | tf_op jit(solution)/shard_map/ppermute | solution.py:21
  25.7 0.8 %collective-permute-start.6 = (f32[16,128]{1,0:T(8,128)S(1)}, f32[16,128]{1,0:T(8,128)S(1)}, u32[]{:S(2)}, u32[]{:S(2)}) collective-permute-start(f32[16,128]{1,0:T(8,128)S(1)} %get-tuple-element.19.first), channel_id=1, source_target_pairs={{0,4},{1,5},{2,6},{3,7},{4,0},{5,1},{6,2},{7,3},{8,12},{9,13},{10,... | collective-permute-start | bytes 24584 | tf_op jit(solution)/shard_map/ppermute | solution.py:21
  26.5 0.0 collective-permute-start.11
  26.5 0.0 collective-permute-done.7.recv
  26.5 0.1 shard_map.83.refs_0_
  26.6 5.9 %collective-permute-start.12 = (bf16[128,1152]{1,0:T(8,128)(2,1)S(1)}, bf16[128,1152]{1,0:T(8,128)(2,1)S(1)}, u32[]{:S(2)}, u32[]{:S(2)}) collective-permute-start(bf16[128,1152]{1,0:T(8,128)(2,1)S(1)} %shard_map.83.refs_0_), channel_id=1, source_target_pairs={{0,12},{1,13},{2,14},{3,15},{4,8},{5,9},{6,10},{7,11},{8,4},{9,5},... | collective-permute-start | bytes 884744 | tf_op jit(solution)/shard_map/ppermute | solution.py:21
  32.5 0.0 collective-permute-done.6.second
  32.5 0.1 collective-permute-start.8
  32.6 1.1 %collective-permute-done.8.second = f32[16,128]{1,0:T(8,128)S(1)} collective-permute-done((f32[16,128]{1,0:T(8,128)S(1)}, f32[16,128]{1,0:T(8,128)S(1)}, u32[]{:S(2)}, u32[]{:S(2)}) %collective-permute-start.8) | collective-permute-done | bytes 8224 | tf_op jit(solution)/shard_map/ppermute | solution.py:21
  33.7 1.3 %collective-permute-start.9 = (f32[16,128]{1,0:T(8,128)S(1)}, f32[16,128]{1,0:T(8,128)S(1)}, u32[]{:S(2)}, u32[]{:S(2)}) collective-permute-start(f32[16,128]{1,0:T(8,128)S(1)} %shard_map.85.first), channel_id=1, source_target_pairs={{0,2},{1,3},{2,0},{3,1},{4,6},{5,7},{6,4},{7,5},{8,10},{9,11},{10,... | collective-permute-start | bytes 24584 | tf_op jit(solution)/shard_map/ppermute | solution.py:21
  35.0 2.3 %collective-permute-done.9.second = f32[16,128]{1,0:T(8,128)S(1)} collective-permute-done((f32[16,128]{1,0:T(8,128)S(1)}, f32[16,128]{1,0:T(8,128)S(1)}, u32[]{:S(2)}, u32[]{:S(2)}) %collective-permute-start.9) | collective-permute-done | bytes 8224 | tf_op jit(solution)/shard_map/ppermute | solution.py:21
  37.4 0.0 collective-permute-done.13.recv
  37.4 0.1 shard_map.88.refs_1_
  37.4 1.4 %collective-permute-start.14 = (bf16[128,1152]{1,0:T(8,128)(2,1)S(1)}, bf16[128,1152]{1,0:T(8,128)(2,1)S(1)}, u32[]{:S(2)}, u32[]{:S(2)}) collective-permute-start(bf16[128,1152]{1,0:T(8,128)(2,1)S(1)} %shard_map.89), channel_id=1, source_target_pairs={{0,2},{1,3},{2,0},{3,1},{4,6},{5,7},{6,4},{7,5},{8,10},{9,11},{10,... | collective-permute-start | bytes 884744 | tf_op jit(solution)/shard_map/ppermute | solution.py:21
  38.8 0.2 collective-permute-start.15
  39.0 2.9 %collective-permute-start.10 = (f32[16,128]{1,0:T(8,128)S(1)}, f32[16,128]{1,0:T(8,128)S(1)}, u32[]{:S(2)}, u32[]{:S(2)}) collective-permute-start(f32[16,128]{1,0:T(8,128)S(1)} %shard_map.86.refs_1_.sums), channel_id=1, source_target_pairs={{0,12},{1,13},{2,14},{3,15},{4,8},{5,9},{6,10},{7,11},{8,4},{9,5},... | collective-permute-start | bytes 24584 | tf_op jit(solution)/shard_map/ppermute | solution.py:21
  41.9 0.0 collective-permute-done.11.refs_0_
  41.9 0.0 collective-permute-done.12.refs_1_
  41.9 6.7 %collective-permute-done.10.sums_recv = f32[16,128]{1,0:T(8,128)S(1)} collective-permute-done((f32[16,128]{1,0:T(8,128)S(1)}, f32[16,128]{1,0:T(8,128)S(1)}, u32[]{:S(2)}, u32[]{:S(2)}) %collective-permute-start.10) | collective-permute-done | bytes 8224 | tf_op jit(solution)/shard_map/ppermute | solution.py:21
  48.6 0.0 collective-permute-done.14.refs_6_
  48.6 0.0 collective-permute-done.15.refs_7_
  48.6 1.3 %shard_map.90 = (bf16[128,1152]{1,0:T(8,128)(2,1)}, bf16[128,1152]{1,0:T(8,128)(2,1)}, f32[1,1]{1,0:T(1,128)}, f32[1,1]{1,0:T(1,128)}) custom-call(f32[16,128]{1,0:T(8,128)S(1)} %shard_map.86.refs_1_.sums, f32[16,128]{1,0:T(8,128)S(1)} %collective-permute-done.10.sums_recv, bf16[128,1152]{1,0:T(8,128)(2,1)S(1)} %copy-done.1, ...), custom_call_target="tpu_custom_call" | custom-call | tf_op jit(solution)/shard_map/pallas_call | solution.py:230
  (7 shorter events, 0.0 us)
Async XLA Ops:
  0.6 13.8 %copy-start.1 = (bf16[128,1152]{1,0:T(8,128)(2,1)S(1)}, bf16[128,1152]{1,0:T(8,128)(2,1)}, u32[]{:S(2)}) copy-start(bf16[128,1152]{1,0:T(8,128)(2,1)} %refs_0_.1) | copy-start | bytes 884740
  0.6 10.8 %collective-permute-start = (bf16[128,1152]{1,0:T(8,128)(2,1)}, bf16[128,1152]{1,0:T(8,128)(2,1)S(1)}, u32[]{:S(2)}, u32[]{:S(2)}) collective-permute-start(bf16[128,1152]{1,0:T(8,128)(2,1)} %refs_4_.1), channel_id=1, source_target_pairs={{0,4},{1,5},{2,6},{3,7},{4,0},{5,1},{6,2},{7,3},{8,12},{9,13},{10,... | collective-permute-start | bytes 884744 | tf_op jit(solution)/shard_map/ppermute | solution.py:21
  3.7 11.9 %collective-permute-start.1 = (bf16[128,1152]{1,0:T(8,128)(2,1)}, bf16[128,1152]{1,0:T(8,128)(2,1)S(1)}, u32[]{:S(2)}, u32[]{:S(2)}) collective-permute-start(bf16[128,1152]{1,0:T(8,128)(2,1)} %refs_4_.1), channel_id=1, source_target_pairs={{0,2},{1,3},{2,0},{3,1},{4,6},{5,7},{6,4},{7,5},{8,10},{9,11},{10,... | collective-permute-start | bytes 884744 | tf_op jit(solution)/shard_map/ppermute | solution.py:21
  5.2 14.3 %collective-permute-start.3 = (bf16[128,1152]{1,0:T(8,128)(2,1)}, bf16[128,1152]{1,0:T(8,128)(2,1)S(1)}, u32[]{:S(2)}, u32[]{:S(2)}) collective-permute-start(bf16[128,1152]{1,0:T(8,128)(2,1)} %refs_0_.1), channel_id=1, source_target_pairs={{0,12},{1,13},{2,14},{3,15},{4,8},{5,9},{6,10},{7,11},{8,4},{9,5},... | collective-permute-start | bytes 884744 | tf_op jit(solution)/shard_map/ppermute | solution.py:21
  11.6 8.2 %collective-permute-start.2 = (bf16[128,1152]{1,0:T(8,128)(2,1)S(1)}, bf16[128,1152]{1,0:T(8,128)(2,1)S(1)}, u32[]{:S(2)}, u32[]{:S(2)}) collective-permute-start(bf16[128,1152]{1,0:T(8,128)(2,1)S(1)} %shard_map.75.refs_0_.refs_1_), channel_id=1, source_target_pairs={{0,2},{1,3},{2,0},{3,1},{4,6},{5,7},{6,4},{7,5},{8,10},{9,11},{10,... | collective-permute-start | bytes 884744 | tf_op jit(solution)/shard_map/ppermute | solution.py:21
  14.5 1.0 %copy-start = (bf16[128,1152]{1,0:T(8,128)(2,1)S(1)}, bf16[128,1152]{1,0:T(8,128)(2,1)}, u32[]{:S(2)}) copy-start(bf16[128,1152]{1,0:T(8,128)(2,1)} %refs_4_.1) | copy-start | bytes 884740
  14.6 6.7 %collective-permute-start.4 = (bf16[128,1152]{1,0:T(8,128)(2,1)S(1)}, bf16[128,1152]{1,0:T(8,128)(2,1)S(1)}, u32[]{:S(2)}, u32[]{:S(2)}) collective-permute-start(bf16[128,1152]{1,0:T(8,128)(2,1)S(1)} %shard_map.76.refs_0_.refs_4_), channel_id=1, source_target_pairs={{0,1},{1,0},{2,3},{3,2},{4,5},{5,4},{6,7},{7,6},{8,9},{9,8},{10,11... | collective-permute-start | bytes 884744 | tf_op jit(solution)/shard_map/ppermute | solution.py:21
  19.7 1.6 %collective-permute-start.5 = (bf16[128,1152]{1,0:T(8,128)(2,1)S(1)}, bf16[128,1152]{1,0:T(8,128)(2,1)S(1)}, u32[]{:S(2)}, u32[]{:S(2)}) collective-permute-start(bf16[128,1152]{1,0:T(8,128)(2,1)S(1)} %shard_map.80.refs_5_), channel_id=1, source_target_pairs={{0,1},{1,0},{2,3},{3,2},{4,5},{5,4},{6,7},{7,6},{8,9},{9,8},{10,11... | collective-permute-start | bytes 884744 | tf_op jit(solution)/shard_map/ppermute | solution.py:21
  24.0 2.5 %collective-permute-start.7 = (bf16[128,1152]{1,0:T(8,128)(2,1)S(1)}, bf16[128,1152]{1,0:T(8,128)(2,1)S(1)}, u32[]{:S(2)}, u32[]{:S(2)}) collective-permute-start(bf16[128,1152]{1,0:T(8,128)(2,1)S(1)} %get-tuple-element.21), channel_id=1, source_target_pairs={{0,1},{1,0},{2,3},{3,2},{4,5},{5,4},{6,7},{7,6},{8,9},{9,8},{10,11... | collective-permute-start | bytes 884744 | tf_op jit(solution)/shard_map/ppermute | solution.py:21
  24.2 13.2 %collective-permute-start.13 = (bf16[128,1152]{1,0:T(8,128)(2,1)S(1)}, bf16[128,1152]{1,0:T(8,128)(2,1)S(1)}, u32[]{:S(2)}, u32[]{:S(2)}) collective-permute-start(bf16[128,1152]{1,0:T(8,128)(2,1)S(1)} %get-tuple-element.29), channel_id=1, source_target_pairs={{0,2},{1,3},{2,0},{3,1},{4,6},{5,7},{6,4},{7,5},{8,10},{9,11},{10,... | collective-permute-start | bytes 884744 | tf_op jit(solution)/shard_map/ppermute | solution.py:21
  25.7 6.8 %collective-permute-start.6 = (f32[16,128]{1,0:T(8,128)S(1)}, f32[16,128]{1,0:T(8,128)S(1)}, u32[]{:S(2)}, u32[]{:S(2)}) collective-permute-start(f32[16,128]{1,0:T(8,128)S(1)} %get-tuple-element.19.first), channel_id=1, source_target_pairs={{0,4},{1,5},{2,6},{3,7},{4,0},{5,1},{6,2},{7,3},{8,12},{9,13},{10,... | collective-permute-start | bytes 24584 | tf_op jit(solution)/shard_map/ppermute | solution.py:21
  26.5 15.4 %collective-permute-start.11 = (bf16[128,1152]{1,0:T(8,128)(2,1)S(1)}, bf16[128,1152]{1,0:T(8,128)(2,1)S(1)}, u32[]{:S(2)}, u32[]{:S(2)}) collective-permute-start(bf16[128,1152]{1,0:T(8,128)(2,1)S(1)} %get-tuple-element.23), channel_id=1, source_target_pairs={{0,1},{1,0},{2,3},{3,2},{4,5},{5,4},{6,7},{7,6},{8,9},{9,8},{10,11... | collective-permute-start | bytes 884744 | tf_op jit(solution)/shard_map/ppermute | solution.py:21
  26.6 15.3 %collective-permute-start.12 = (bf16[128,1152]{1,0:T(8,128)(2,1)S(1)}, bf16[128,1152]{1,0:T(8,128)(2,1)S(1)}, u32[]{:S(2)}, u32[]{:S(2)}) collective-permute-start(bf16[128,1152]{1,0:T(8,128)(2,1)S(1)} %shard_map.83.refs_0_), channel_id=1, source_target_pairs={{0,12},{1,13},{2,14},{3,15},{4,8},{5,9},{6,10},{7,11},{8,4},{9,5},... | collective-permute-start | bytes 884744 | tf_op jit(solution)/shard_map/ppermute | solution.py:21
  32.5 1.2 %collective-permute-start.8 = (f32[16,128]{1,0:T(8,128)S(1)}, f32[16,128]{1,0:T(8,128)S(1)}, u32[]{:S(2)}, u32[]{:S(2)}) collective-permute-start(f32[16,128]{1,0:T(8,128)S(1)} %shard_map.84.first), channel_id=1, source_target_pairs={{0,1},{1,0},{2,3},{3,2},{4,5},{5,4},{6,7},{7,6},{8,9},{9,8},{10,11... | collective-permute-start | bytes 24584 | tf_op jit(solution)/shard_map/ppermute | solution.py:21
  33.7 3.7 %collective-permute-start.9 = (f32[16,128]{1,0:T(8,128)S(1)}, f32[16,128]{1,0:T(8,128)S(1)}, u32[]{:S(2)}, u32[]{:S(2)}) collective-permute-start(f32[16,128]{1,0:T(8,128)S(1)} %shard_map.85.first), channel_id=1, source_target_pairs={{0,2},{1,3},{2,0},{3,1},{4,6},{5,7},{6,4},{7,5},{8,10},{9,11},{10,... | collective-permute-start | bytes 24584 | tf_op jit(solution)/shard_map/ppermute | solution.py:21
  37.4 11.2 %collective-permute-start.14 = (bf16[128,1152]{1,0:T(8,128)(2,1)S(1)}, bf16[128,1152]{1,0:T(8,128)(2,1)S(1)}, u32[]{:S(2)}, u32[]{:S(2)}) collective-permute-start(bf16[128,1152]{1,0:T(8,128)(2,1)S(1)} %shard_map.89), channel_id=1, source_target_pairs={{0,2},{1,3},{2,0},{3,1},{4,6},{5,7},{6,4},{7,5},{8,10},{9,11},{10,... | collective-permute-start | bytes 884744 | tf_op jit(solution)/shard_map/ppermute | solution.py:21
  38.8 9.8 %collective-permute-start.15 = (bf16[128,1152]{1,0:T(8,128)(2,1)S(1)}, bf16[128,1152]{1,0:T(8,128)(2,1)S(1)}, u32[]{:S(2)}, u32[]{:S(2)}) collective-permute-start(bf16[128,1152]{1,0:T(8,128)(2,1)S(1)} %shard_map.88.refs_1_), channel_id=1, source_target_pairs={{0,4},{1,5},{2,6},{3,7},{4,0},{5,1},{6,2},{7,3},{8,12},{9,13},{10,... | collective-permute-start | bytes 884744 | tf_op jit(solution)/shard_map/ppermute | solution.py:21
  39.0 9.6 %collective-permute-start.10 = (f32[16,128]{1,0:T(8,128)S(1)}, f32[16,128]{1,0:T(8,128)S(1)}, u32[]{:S(2)}, u32[]{:S(2)}) collective-permute-start(f32[16,128]{1,0:T(8,128)S(1)} %shard_map.86.refs_1_.sums), channel_id=1, source_target_pairs={{0,12},{1,13},{2,14},{3,15},{4,8},{5,9},{6,10},{7,11},{8,4},{9,5},... | collective-permute-start | bytes 24584 | tf_op jit(solution)/shard_map/ppermute | solution.py:21

commit v13 on v10

--- a/solution.py
+++ b/solution.py
@@ -219,40 +219,51 @@
     return parts[:n_img], parts[n_img:], sums
 
 
-def finish_kernel(recv_counts, pairs, sums, sums_recv, *refs):
+def finish_rows(value, keep, recvs, out):
+    total = keep[...]
+    for recv in recvs:
+        total = total + recv[...].astype(jnp.float32)
+    unit, inverse = unit_rows(value[...])
+    along = jnp.sum(unit * total, axis=1, keepdims=True)
+    out[...] = ((total - unit * along) * inverse).astype(jnp.bfloat16)
+
+
+def finish_first_kernel(value, keep, *refs):
+    finish_rows(value, keep, refs[:-2], refs[-2])
+    refs[-1][...] = jnp.zeros(refs[-1].shape, jnp.float32)
+
+
+def finish_first(value, keep, recvs):
+    return pl.pallas_call(
+        finish_first_kernel,
+        out_shape=(
+            jax.ShapeDtypeStruct(value.shape, jnp.bfloat16),
+            jax.ShapeDtypeStruct((8, 128), jnp.float32),
+        ),
+        in_specs=[VMEM] * (2 + len(recvs)),
+        out_specs=[VMEM] * 2,
+        compiler_params=pltpu.CompilerParams(vmem_limit_bytes=SMALL_VMEM),
+        cost_estimate=pl.CostEstimate(flops=RETURN_COST, bytes_accessed=0, transcendentals=0),
+    )(value, keep, *recvs)
+
+
+def finish_last_kernel(pairs, token, sums, sums_recv, value, keep, *refs):
     total = sums[...] + sums_recv[...]
     for place in range(2):
         whole = jnp.sum(total[8 * place : 8 * place + 8], axis=0, keepdims=True)
         refs[place - 2][...] = jnp.sum(whole, axis=1, keepdims=True) / pairs
-    outs = refs[-len(recv_counts) - 2 : -2]
-    for out, count in zip(outs, recv_counts):
-        value, keep = refs[:2]
-        rows = value.shape[0]
-        total = keep[...]
-        start = 0
-        pieces = []
-        for recv in refs[2 : 2 + count]:
-            pieces.append(recv[...].astype(jnp.float32))
-            start += recv.shape[0]
-            if start % rows == 0:
-                total = total + jnp.concatenate(pieces, axis=0)
-                pieces = []
-        refs = refs[2 + count :]
-        unit, inverse = unit_rows(value[...])
-        along = jnp.sum(unit * total, axis=1, keepdims=True)
-        out[...] = ((total - unit * along) * inverse).astype(jnp.bfloat16)
-
-
-def finish_call(sums, sums_recv, pairs, sides):
-    flat = [array for value, keep, recvs in sides for array in [value, keep] + recvs]
-    return pl.pallas_call(
-        functools.partial(finish_kernel, [len(recvs) for _, _, recvs in sides], pairs),
-        out_shape=[jax.ShapeDtypeStruct(value.shape, jnp.bfloat16) for value, _, _ in sides]
+    finish_rows(value, keep, refs[:-3], refs[-3])
+
+
+def finish_last(token, sums, sums_recv, pairs, value, keep, recvs):
+    return pl.pallas_call(
+        functools.partial(finish_last_kernel, pairs),
+        out_shape=[jax.ShapeDtypeStruct(value.shape, jnp.bfloat16)]
         + [jax.ShapeDtypeStruct((1, 1), jnp.float32)] * 2,
-        in_specs=[VMEM] * (2 + len(flat)),
-        out_specs=[VMEM] * (2 + len(sides)),
-        compiler_params=pltpu.CompilerParams(vmem_limit_bytes=2 * SMALL_VMEM),
-    )(sums, sums_recv, *flat)
+        in_specs=[ANY] + [VMEM] * (4 + len(recvs)),
+        out_specs=[VMEM] * 3,
+        compiler_params=pltpu.CompilerParams(vmem_limit_bytes=SMALL_VMEM),
+    )(token, sums, sums_recv, value, keep, *recvs)
 
 
 def add_kernel(keep, recv, *refs):
@@ -323,12 +334,10 @@
         sums = sums_call([sums, swapped(sums, bit)], others)
     img_keep, img_recvs, others = returned(img_parts, img_bits, others + [sums], True)
     sums_recv = swapped(sums, txt_bits[0])
-    txt_recvs = held(txt_recvs, [], RETURN_COST)
-    grad_text, grad_image, grad_bias, grad_temp = finish_call(
-        sums,
-        sums_recv,
-        float(rows * count) * float(rows * count),
-        [(text_embeds, txt_keep, txt_recvs), (image_embeds, img_keep, img_recvs)],
+    grad_text, token = finish_first(text_embeds, txt_keep, txt_recvs)
+    pairs = float(rows * count) * float(rows * count)
+    grad_image, grad_bias, grad_temp = finish_last(
+        token, sums, sums_recv, pairs, image_embeds, img_keep, img_recvs
     )
     return (grad_image, grad_text, grad_temp.reshape(1), grad_bias.reshape(1))
 

time: 49 us -> 48.7 us (level)
  waiting for transfers between devices: 20.8 us -> 19.8 us
  Pallas kernels: 4.76 us -> 5.48 us
    ppermute x17, waiting for transfers between devices: 20.8 us -> 19.8 us  [swapped(): return lax.ppermute(x, 'blk', [(i, i ^ bit) for i in range(count)])]
    pallas_call x1 -> x2, Pallas kernels: 1.32 us -> 2.03 us  [the longest x1 1.02 us: finish_first(): pl.pallas_call(finish_first_kernel, out_shape=(jax.ShapeDtypeStruct(value...]
  transfers between devices with their start and end apart: 17 -> 17, of which waited for: 7 -> 7; matrix products, arithmetic and copies ran while one was open for 0% -> 0% of each run, Pallas kernels for 2% -> 4%
where the time goes in v13:
time: 48.7 us; the launch traced here: 48.5 us
  starting transfers between devices  20.5 us (42%)
  waiting for transfers between devices  19.8 us (41%)
  Pallas kernels  5.48 us (11%)
  between operations  2.07 us (4%)
  local copies, waits for them, and re-layouts  0.73 us (1%)
    ppermute x17, starting transfers between devices, swapped(): return lax.ppermute(x, 'blk', [(i, i ^ bit) for i in range(count)])  20.5 us
    ppermute x17, waiting for transfers between devices, swapped(): return lax.ppermute(x, 'blk', [(i, i ^ bit) for i in range(count)])  19.8 us
    pallas_call x1, Pallas kernels, tile_call(): pl.pallas_call(functools.partial(tile_kernel, [len(block) for block in im...  2.59 us
    pallas_call x1, Pallas kernels, finish_first(): pl.pallas_call(finish_first_kernel, out_shape=(jax.ShapeDtypeStruct(value...  1.02 us
    pallas_call x1, Pallas kernels, finish_last(): pl.pallas_call(functools.partial(finish_last_kernel, pairs), out_shape=[j...  1.01 us
  transfers between devices with their start and end apart: 17, of which 7 were waited for; matrix products, arithmetic and copies ran while one was open for 0% of the time, Pallas kernels for 4%

profile of v13, /device:TPU:0, one launch (start us, length us, event | category | flops | bytes accessed | tf_op | source)
XLA Modules:
  0.0 48.5 jit_solution(17969370083620197808)
XLA Ops:
  0.6 0.0 copy-start.1
  0.6 3.0 %collective-permute-start = (bf16[128,1152]{1,0:T(8,128)(2,1)}, bf16[128,1152]{1,0:T(8,128)(2,1)S(1)}, u32[]{:S(2)}, u32[]{:S(2)}) collective-permute-start(bf16[128,1152]{1,0:T(8,128)(2,1)} %value.7), channel_id=1, source_target_pairs={{0,2},{1,3},{2,0},{3,1},{4,6},{5,7},{6,4},{7,5},{8,10},{9,11},{10,... | collective-permute-start | bytes 884744 | tf_op jit(solution)/shard_map/ppermute | solution.py:21
  3.6 1.6 %collective-permute-start.1 = (bf16[128,1152]{1,0:T(8,128)(2,1)}, bf16[128,1152]{1,0:T(8,128)(2,1)S(1)}, u32[]{:S(2)}, u32[]{:S(2)}) collective-permute-start(bf16[128,1152]{1,0:T(8,128)(2,1)} %value.7), channel_id=1, source_target_pairs={{0,4},{1,5},{2,6},{3,7},{4,0},{5,1},{6,2},{7,3},{8,12},{9,13},{10,... | collective-permute-start | bytes 884744 | tf_op jit(solution)/shard_map/ppermute | solution.py:21
  5.2 2.5 %collective-permute-start.4 = (bf16[128,1152]{1,0:T(8,128)(2,1)}, bf16[128,1152]{1,0:T(8,128)(2,1)S(1)}, u32[]{:S(2)}, u32[]{:S(2)}) collective-permute-start(bf16[128,1152]{1,0:T(8,128)(2,1)} %value.6), channel_id=1, source_target_pairs={{0,12},{1,13},{2,14},{3,15},{4,8},{5,9},{6,10},{7,11},{8,4},{9,5},... | collective-permute-start | bytes 884744 | tf_op jit(solution)/shard_map/ppermute | solution.py:21
  7.7 3.2 %collective-permute-done.value = bf16[128,1152]{1,0:T(8,128)(2,1)S(1)} collective-permute-done((bf16[128,1152]{1,0:T(8,128)(2,1)}, bf16[128,1152]{1,0:T(8,128)(2,1)S(1)}, u32[]{:S(2)}, u32[]{:S(2)}) %collective-permute-start) | collective-permute-done | bytes 294944 | tf_op jit(solution)/shard_map/ppermute | solution.py:21
  10.9 0.1 shard_map.75
  11.0 1.9 %collective-permute-start.3 = (bf16[48,1152]{1,0:T(8,128)(2,1)S(1)}, bf16[48,1152]{1,0:T(8,128)(2,1)S(1)}, u32[]{:S(2)}, u32[]{:S(2)}) collective-permute-start(bf16[48,1152]{1,0:T(8,128)(2,1)S(1)} %get-tuple-element.25.refs_4_), channel_id=1, source_target_pairs={{0,4},{1,5},{2,6},{3,7},{4,0},{5,1},{6,2},{7,3},{8,12},{9,13},{10,... | collective-permute-start | bytes 331784 | tf_op jit(solution)/shard_map/ppermute | solution.py:21
  14.2 0.0 copy-done.1
  14.2 0.0 copy-start
  14.2 0.1 shard_map.76.refs_0_.refs_7_
  14.4 0.1 collective-permute-start.5
  14.5 0.7 %copy-done = bf16[128,1152]{1,0:T(8,128)(2,1)S(1)} copy-done((bf16[128,1152]{1,0:T(8,128)(2,1)S(1)}, bf16[128,1152]{1,0:T(8,128)(2,1)}, u32[]{:S(2)}) %copy-start) | copy-done | bytes 294936
  15.2 0.1 shard_map.77.refs_0_
  15.3 0.0 collective-permute-done.1.value
  15.3 0.1 shard_map.78
  15.5 1.6 %collective-permute-start.2 = (bf16[80,1152]{1,0:T(8,128)(2,1)S(1)}, bf16[80,1152]{1,0:T(8,128)(2,1)S(1)}, u32[]{:S(2)}, u32[]{:S(2)}) collective-permute-start(bf16[80,1152]{1,0:T(8,128)(2,1)S(1)} %get-tuple-element.23.refs_0_.refs_1_), channel_id=1, source_target_pairs={{0,2},{1,3},{2,0},{3,1},{4,6},{5,7},{6,4},{7,5},{8,10},{9,11},{10,... | collective-permute-start | bytes 552968 | tf_op jit(solution)/shard_map/ppermute | solution.py:21
  17.0 4.8 %collective-permute-done.4.value = bf16[128,1152]{1,0:T(8,128)(2,1)S(1)} collective-permute-done((bf16[128,1152]{1,0:T(8,128)(2,1)}, bf16[128,1152]{1,0:T(8,128)(2,1)S(1)}, u32[]{:S(2)}, u32[]{:S(2)}) %collective-permute-start.4) | collective-permute-done | bytes 294944 | tf_op jit(solution)/shard_map/ppermute | solution.py:21
  21.9 0.1 shard_map.81.refs_8_
  22.1 0.1 collective-permute-start.6
  22.1 0.0 collective-permute-done.3.refs_0_
  22.1 0.0 collective-permute-done.2.refs_0_
  22.2 1.5 %collective-permute-done.6.refs_0_ = bf16[128,1152]{1,0:T(8,128)(2,1)S(1)} collective-permute-done((bf16[128,1152]{1,0:T(8,128)(2,1)S(1)}, bf16[128,1152]{1,0:T(8,128)(2,1)S(1)}, u32[]{:S(2)}, u32[]{:S(2)}) %collective-permute-start.6) | collective-permute-done | bytes 294944 | tf_op jit(solution)/shard_map/ppermute | solution.py:21
  23.7 0.0 collective-permute-done.5.refs_9_
  23.7 2.6 %shard_map.83 = (f32[128,1152]{1,0:T(8,128)S(1)}, f32[128,1152]{1,0:T(8,128)S(1)}, bf16[128,1152]{1,0:T(8,128)(2,1)S(1)}, bf16[128,1152]{1,0:T(8,128)(2,1)S(1)},...) custom-call(bf16[128,1152]{1,0:T(8,128)(2,1)S(1)} %shard_map.77.refs, ...), custom_call_target="tpu_custom_call" | custom-call | flops 1811939328 | tf_op jit(solution)/shard_map/pallas_call | solution.py:194
  26.3 0.2 collective-permute-start.8
  26.5 0.6 %collective-permute-start.14 = (bf16[128,1152]{1,0:T(8,128)(2,1)S(1)}, bf16[128,1152]{1,0:T(8,128)(2,1)S(1)}, u32[]{:S(2)}, u32[]{:S(2)}) collective-permute-start(bf16[128,1152]{1,0:T(8,128)(2,1)S(1)} %get-tuple-element.35), channel_id=1, source_target_pairs={{0,2},{1,3},{2,0},{3,1},{4,6},{5,7},{6,4},{7,5},{8,10},{9,11},{10,... | collective-permute-start | bytes 884744 | tf_op jit(solution)/shard_map/ppermute | solution.py:21
  27.1 0.0 collective-permute-start.10
  27.1 0.1 collective-permute-start.7
  27.2 0.8 %collective-permute-done.8.recv = bf16[128,1152]{1,0:T(8,128)(2,1)S(1)} collective-permute-done((bf16[128,1152]{1,0:T(8,128)(2,1)S(1)}, bf16[128,1152]{1,0:T(8,128)(2,1)S(1)}, u32[]{:S(2)}, u32[]{:S(2)}) %collective-permute-start.8) | collective-permute-done | bytes 294944 | tf_op jit(solution)/shard_map/ppermute | solution.py:21
  27.9 0.1 shard_map.84.refs_0_
  28.0 4.1 %collective-permute-start.9 = (bf16[128,1152]{1,0:T(8,128)(2,1)S(1)}, bf16[128,1152]{1,0:T(8,128)(2,1)S(1)}, u32[]{:S(2)}, u32[]{:S(2)}) collective-permute-start(bf16[128,1152]{1,0:T(8,128)(2,1)S(1)} %shard_map.84.refs_0_), channel_id=1, source_target_pairs={{0,12},{1,13},{2,14},{3,15},{4,8},{5,9},{6,10},{7,11},{8,4},{9,5},... | collective-permute-start | bytes 884744 | tf_op jit(solution)/shard_map/ppermute | solution.py:21
  32.1 0.0 collective-permute-done.10.second
  32.1 0.0 collective-permute-start.11
  32.1 1.2 %collective-permute-done.11.second = f32[16,128]{1,0:T(8,128)S(1)} collective-permute-done((f32[16,128]{1,0:T(8,128)S(1)}, f32[16,128]{1,0:T(8,128)S(1)}, u32[]{:S(2)}, u32[]{:S(2)}) %collective-permute-start.11) | collective-permute-done | bytes 8224 | tf_op jit(solution)/shard_map/ppermute | solution.py:21
  33.3 0.7 %collective-permute-start.12 = (f32[16,128]{1,0:T(8,128)S(1)}, f32[16,128]{1,0:T(8,128)S(1)}, u32[]{:S(2)}, u32[]{:S(2)}) collective-permute-start(f32[16,128]{1,0:T(8,128)S(1)} %shard_map.87.first), channel_id=1, source_target_pairs={{0,2},{1,3},{2,0},{3,1},{4,6},{5,7},{6,4},{7,5},{8,10},{9,11},{10,... | collective-permute-start | bytes 24584 | tf_op jit(solution)/shard_map/ppermute | solution.py:21
  34.0 3.0 %collective-permute-done.12.second = f32[16,128]{1,0:T(8,128)S(1)} collective-permute-done((f32[16,128]{1,0:T(8,128)S(1)}, f32[16,128]{1,0:T(8,128)S(1)}, u32[]{:S(2)}, u32[]{:S(2)}) %collective-permute-start.12) | collective-permute-done | bytes 8224 | tf_op jit(solution)/shard_map/ppermute | solution.py:21
  36.9 0.0 collective-permute-done.14.recv
  36.9 0.1 shard_map.89.refs_1_
  37.0 0.8 %collective-permute-start.15 = (bf16[128,1152]{1,0:T(8,128)(2,1)S(1)}, bf16[128,1152]{1,0:T(8,128)(2,1)S(1)}, u32[]{:S(2)}, u32[]{:S(2)}) collective-permute-start(bf16[128,1152]{1,0:T(8,128)(2,1)S(1)} %shard_map.90), channel_id=1, source_target_pairs={{0,2},{1,3},{2,0},{3,1},{4,6},{5,7},{6,4},{7,5},{8,10},{9,11},{10,... | collective-permute-start | bytes 884744 | tf_op jit(solution)/shard_map/ppermute | solution.py:21
  37.8 1.0 %collective-permute-start.16 = (bf16[128,1152]{1,0:T(8,128)(2,1)S(1)}, bf16[128,1152]{1,0:T(8,128)(2,1)S(1)}, u32[]{:S(2)}, u32[]{:S(2)}) collective-permute-start(bf16[128,1152]{1,0:T(8,128)(2,1)S(1)} %shard_map.89.refs_1_), channel_id=1, source_target_pairs={{0,4},{1,5},{2,6},{3,7},{4,0},{5,1},{6,2},{7,3},{8,12},{9,13},{10,... | collective-permute-start | bytes 884744 | tf_op jit(solution)/shard_map/ppermute | solution.py:21
  38.7 2.5 %collective-permute-start.13 = (f32[16,128]{1,0:T(8,128)S(1)}, f32[16,128]{1,0:T(8,128)S(1)}, u32[]{:S(2)}, u32[]{:S(2)}) collective-permute-start(f32[16,128]{1,0:T(8,128)S(1)} %shard_map.88.refs_1_.sums), channel_id=1, source_target_pairs={{0,12},{1,13},{2,14},{3,15},{4,8},{5,9},{6,10},{7,11},{8,4},{9,5},... | collective-permute-start | bytes 24584 | tf_op jit(solution)/shard_map/ppermute | solution.py:21
  41.2 0.0 collective-permute-done.7.refs_0_
  41.2 0.0 collective-permute-done.9.refs_1_
  41.2 1.0 %shard_map.85 = (bf16[128,1152]{1,0:T(8,128)(2,1)}, f32[8,128]{1,0:T(8,128)S(1)}) custom-call(bf16[128,1152]{1,0:T(8,128)(2,1)S(1)} %copy-done.1, f32[128,1152]{1,0:T(8,128)S(1)} %get-tuple-element.26.keep, bf16[128,1152]{1,0:T(8,128)(2,1)S(1)} %collective-permute-done.7.refs_0_, bf16[128,1152]{1,0:T(8,128)(2,1)S(1)} %collective-permute-done.9.refs_1_), custom_call_target="tpu_custom_call" | custom-call | flops 1000000000 | tf_op jit(solution)/shard_map/pallas_call | solution.py:237
  42.2 5.3 %collective-permute-done.13.sums_recv = f32[16,128]{1,0:T(8,128)S(1)} collective-permute-done((f32[16,128]{1,0:T(8,128)S(1)}, f32[16,128]{1,0:T(8,128)S(1)}, u32[]{:S(2)}, u32[]{:S(2)}) %collective-permute-start.13) | collective-permute-done | bytes 8224 | tf_op jit(solution)/shard_map/ppermute | solution.py:21
  47.5 0.0 collective-permute-done.15.refs_0_
  47.5 0.0 collective-permute-done.16.refs_1_
  47.5 1.0 %shard_map.91 = (bf16[128,1152]{1,0:T(8,128)(2,1)}, f32[1,1]{1,0:T(1,128)}, f32[1,1]{1,0:T(1,128)}) custom-call(f32[8,128]{1,0:T(8,128)S(1)} %get-tuple-element.30.token, f32[16,128]{1,0:T(8,128)S(1)} %shard_map.88.refs_1_.sums, f32[16,128]{1,0:T(8,128)S(1)} %collective-permute-done.13.sums_recv, bf16[128,1152]{1,0:T(8,128)(2,1)S(1)} %copy-done, ...), custom_call_target="tpu_custom_call" | custom-call | tf_op jit(solution)/shard_map/pallas_call | solution.py:259
  (7 shorter events, 0.0 us)
Async XLA Ops:
  0.6 13.6 %copy-start.1 = (bf16[128,1152]{1,0:T(8,128)(2,1)S(1)}, bf16[128,1152]{1,0:T(8,128)(2,1)}, u32[]{:S(2)}) copy-start(bf16[128,1152]{1,0:T(8,128)(2,1)} %value.6) | copy-start | bytes 884740
  0.6 10.2 %collective-permute-start = (bf16[128,1152]{1,0:T(8,128)(2,1)}, bf16[128,1152]{1,0:T(8,128)(2,1)S(1)}, u32[]{:S(2)}, u32[]{:S(2)}) collective-permute-start(bf16[128,1152]{1,0:T(8,128)(2,1)} %value.7), channel_id=1, source_target_pairs={{0,2},{1,3},{2,0},{3,1},{4,6},{5,7},{6,4},{7,5},{8,10},{9,11},{10,... | collective-permute-start | bytes 884744 | tf_op jit(solution)/shard_map/ppermute | solution.py:21
  3.6 11.7 %collective-permute-start.1 = (bf16[128,1152]{1,0:T(8,128)(2,1)}, bf16[128,1152]{1,0:T(8,128)(2,1)S(1)}, u32[]{:S(2)}, u32[]{:S(2)}) collective-permute-start(bf16[128,1152]{1,0:T(8,128)(2,1)} %value.7), channel_id=1, source_target_pairs={{0,4},{1,5},{2,6},{3,7},{4,0},{5,1},{6,2},{7,3},{8,12},{9,13},{10,... | collective-permute-start | bytes 884744 | tf_op jit(solution)/shard_map/ppermute | solution.py:21
  5.2 16.7 %collective-permute-start.4 = (bf16[128,1152]{1,0:T(8,128)(2,1)}, bf16[128,1152]{1,0:T(8,128)(2,1)S(1)}, u32[]{:S(2)}, u32[]{:S(2)}) collective-permute-start(bf16[128,1152]{1,0:T(8,128)(2,1)} %value.6), channel_id=1, source_target_pairs={{0,12},{1,13},{2,14},{3,15},{4,8},{5,9},{6,10},{7,11},{8,4},{9,5},... | collective-permute-start | bytes 884744 | tf_op jit(solution)/shard_map/ppermute | solution.py:21
  11.0 11.1 %collective-permute-start.3 = (bf16[48,1152]{1,0:T(8,128)(2,1)S(1)}, bf16[48,1152]{1,0:T(8,128)(2,1)S(1)}, u32[]{:S(2)}, u32[]{:S(2)}) collective-permute-start(bf16[48,1152]{1,0:T(8,128)(2,1)S(1)} %get-tuple-element.25.refs_4_), channel_id=1, source_target_pairs={{0,4},{1,5},{2,6},{3,7},{4,0},{5,1},{6,2},{7,3},{8,12},{9,13},{10,... | collective-permute-start | bytes 331784 | tf_op jit(solution)/shard_map/ppermute | solution.py:21
  14.2 1.0 %copy-start = (bf16[128,1152]{1,0:T(8,128)(2,1)S(1)}, bf16[128,1152]{1,0:T(8,128)(2,1)}, u32[]{:S(2)}) copy-start(bf16[128,1152]{1,0:T(8,128)(2,1)} %value.7) | copy-start | bytes 884740
  14.4 9.3 %collective-permute-start.5 = (bf16[128,1152]{1,0:T(8,128)(2,1)S(1)}, bf16[128,1152]{1,0:T(8,128)(2,1)S(1)}, u32[]{:S(2)}, u32[]{:S(2)}) collective-permute-start(bf16[128,1152]{1,0:T(8,128)(2,1)S(1)} %shard_map.76.refs_0_.refs_7_), channel_id=1, source_target_pairs={{0,1},{1,0},{2,3},{3,2},{4,5},{5,4},{6,7},{7,6},{8,9},{9,8},{10,11... | collective-permute-start | bytes 884744 | tf_op jit(solution)/shard_map/ppermute | solution.py:21
  15.5 6.7 %collective-permute-start.2 = (bf16[80,1152]{1,0:T(8,128)(2,1)S(1)}, bf16[80,1152]{1,0:T(8,128)(2,1)S(1)}, u32[]{:S(2)}, u32[]{:S(2)}) collective-permute-start(bf16[80,1152]{1,0:T(8,128)(2,1)S(1)} %get-tuple-element.23.refs_0_.refs_1_), channel_id=1, source_target_pairs={{0,2},{1,3},{2,0},{3,1},{4,6},{5,7},{6,4},{7,5},{8,10},{9,11},{10,... | collective-permute-start | bytes 552968 | tf_op jit(solution)/shard_map/ppermute | solution.py:21
  22.1 1.6 %collective-permute-start.6 = (bf16[128,1152]{1,0:T(8,128)(2,1)S(1)}, bf16[128,1152]{1,0:T(8,128)(2,1)S(1)}, u32[]{:S(2)}, u32[]{:S(2)}) collective-permute-start(bf16[128,1152]{1,0:T(8,128)(2,1)S(1)} %shard_map.81.refs_8_), channel_id=1, source_target_pairs={{0,1},{1,0},{2,3},{3,2},{4,5},{5,4},{6,7},{7,6},{8,9},{9,8},{10,11... | collective-permute-start | bytes 884744 | tf_op jit(solution)/shard_map/ppermute | solution.py:21
  26.3 1.6 %collective-permute-start.8 = (bf16[128,1152]{1,0:T(8,128)(2,1)S(1)}, bf16[128,1152]{1,0:T(8,128)(2,1)S(1)}, u32[]{:S(2)}, u32[]{:S(2)}) collective-permute-start(bf16[128,1152]{1,0:T(8,128)(2,1)S(1)} %get-tuple-element.29), channel_id=1, source_target_pairs={{0,1},{1,0},{2,3},{3,2},{4,5},{5,4},{6,7},{7,6},{8,9},{9,8},{10,11... | collective-permute-start | bytes 884744 | tf_op jit(solution)/shard_map/ppermute | solution.py:21
  26.5 10.4 %collective-permute-start.14 = (bf16[128,1152]{1,0:T(8,128)(2,1)S(1)}, bf16[128,1152]{1,0:T(8,128)(2,1)S(1)}, u32[]{:S(2)}, u32[]{:S(2)}) collective-permute-start(bf16[128,1152]{1,0:T(8,128)(2,1)S(1)} %get-tuple-element.35), channel_id=1, source_target_pairs={{0,2},{1,3},{2,0},{3,1},{4,6},{5,7},{6,4},{7,5},{8,10},{9,11},{10,... | collective-permute-start | bytes 884744 | tf_op jit(solution)/shard_map/ppermute | solution.py:21
  27.1 5.0 %collective-permute-start.10 = (f32[16,128]{1,0:T(8,128)S(1)}, f32[16,128]{1,0:T(8,128)S(1)}, u32[]{:S(2)}, u32[]{:S(2)}) collective-permute-start(f32[16,128]{1,0:T(8,128)S(1)} %get-tuple-element.31.first), channel_id=1, source_target_pairs={{0,4},{1,5},{2,6},{3,7},{4,0},{5,1},{6,2},{7,3},{8,12},{9,13},{10,... | collective-permute-start | bytes 24584 | tf_op jit(solution)/shard_map/ppermute | solution.py:21
  27.1 14.1 %collective-permute-start.7 = (bf16[128,1152]{1,0:T(8,128)(2,1)S(1)}, bf16[128,1152]{1,0:T(8,128)(2,1)S(1)}, u32[]{:S(2)}, u32[]{:S(2)}) collective-permute-start(bf16[128,1152]{1,0:T(8,128)(2,1)S(1)} %get-tuple-element.27), channel_id=1, source_target_pairs={{0,1},{1,0},{2,3},{3,2},{4,5},{5,4},{6,7},{7,6},{8,9},{9,8},{10,11... | collective-permute-start | bytes 884744 | tf_op jit(solution)/shard_map/ppermute | solution.py:21
  28.0 13.2 %collective-permute-start.9 = (bf16[128,1152]{1,0:T(8,128)(2,1)S(1)}, bf16[128,1152]{1,0:T(8,128)(2,1)S(1)}, u32[]{:S(2)}, u32[]{:S(2)}) collective-permute-start(bf16[128,1152]{1,0:T(8,128)(2,1)S(1)} %shard_map.84.refs_0_), channel_id=1, source_target_pairs={{0,12},{1,13},{2,14},{3,15},{4,8},{5,9},{6,10},{7,11},{8,4},{9,5},... | collective-permute-start | bytes 884744 | tf_op jit(solution)/shard_map/ppermute | solution.py:21
  32.1 1.2 %collective-permute-start.11 = (f32[16,128]{1,0:T(8,128)S(1)}, f32[16,128]{1,0:T(8,128)S(1)}, u32[]{:S(2)}, u32[]{:S(2)}) collective-permute-start(f32[16,128]{1,0:T(8,128)S(1)} %shard_map.86.first), channel_id=1, source_target_pairs={{0,1},{1,0},{2,3},{3,2},{4,5},{5,4},{6,7},{7,6},{8,9},{9,8},{10,11... | collective-permute-start | bytes 24584 | tf_op jit(solution)/shard_map/ppermute | solution.py:21
  33.3 3.7 %collective-permute-start.12 = (f32[16,128]{1,0:T(8,128)S(1)}, f32[16,128]{1,0:T(8,128)S(1)}, u32[]{:S(2)}, u32[]{:S(2)}) collective-permute-start(f32[16,128]{1,0:T(8,128)S(1)} %shard_map.87.first), channel_id=1, source_target_pairs={{0,2},{1,3},{2,0},{3,1},{4,6},{5,7},{6,4},{7,5},{8,10},{9,11},{10,... | collective-permute-start | bytes 24584 | tf_op jit(solution)/shard_map/ppermute | solution.py:21
  37.0 10.5 %collective-permute-start.15 = (bf16[128,1152]{1,0:T(8,128)(2,1)S(1)}, bf16[128,1152]{1,0:T(8,128)(2,1)S(1)}, u32[]{:S(2)}, u32[]{:S(2)}) collective-permute-start(bf16[128,1152]{1,0:T(8,128)(2,1)S(1)} %shard_map.90), channel_id=1, source_target_pairs={{0,2},{1,3},{2,0},{3,1},{4,6},{5,7},{6,4},{7,5},{8,10},{9,11},{10,... | collective-permute-start | bytes 884744 | tf_op jit(solution)/shard_map/ppermute | solution.py:21
  37.8 9.7 %collective-permute-start.16 = (bf16[128,1152]{1,0:T(8,128)(2,1)S(1)}, bf16[128,1152]{1,0:T(8,128)(2,1)S(1)}, u32[]{:S(2)}, u32[]{:S(2)}) collective-permute-start(bf16[128,1152]{1,0:T(8,128)(2,1)S(1)} %shard_map.89.refs_1_), channel_id=1, source_target_pairs={{0,4},{1,5},{2,6},{3,7},{4,0},{5,1},{6,2},{7,3},{8,12},{9,13},{10,... | collective-permute-start | bytes 884744 | tf_op jit(solution)/shard_map/ppermute | solution.py:21
  38.7 8.8 %collective-permute-start.13 = (f32[16,128]{1,0:T(8,128)S(1)}, f32[16,128]{1,0:T(8,128)S(1)}, u32[]{:S(2)}, u32[]{:S(2)}) collective-permute-start(f32[16,128]{1,0:T(8,128)S(1)} %shard_map.88.refs_1_.sums), channel_id=1, source_target_pairs={{0,12},{1,13},{2,14},{3,15},{4,8},{5,9},{6,10},{7,11},{8,4},{9,5},... | collective-permute-start | bytes 24584 | tf_op jit(solution)/shard_map/ppermute | solution.py:21

commit v14 on v13

--- a/solution.py
+++ b/solution.py
@@ -133,7 +133,7 @@
     img_parts = refs[taken : taken + sum(img_cuts)]
     taken += sum(img_cuts)
     txt_parts = refs[taken : taken + sum(txt_cuts)]
-    sums, img_b, txt_b, grad_b = refs[taken + sum(txt_cuts) :]
+    sums, scale, img_b, txt_b, grad_b = refs[taken + sum(txt_cuts) :]
     for group, held in zip(sources, (img_b, txt_b)):
         start = 0
         for piece in group:
@@ -152,22 +152,25 @@
         )
         scaled = temp * cosine
         logits = scaled + shift_b
+        grads = jax.nn.sigmoid(logits)
         if start == 0:
-            at_row = lax.broadcasted_iota(jnp.int32, logits.shape, 0)
-            at_col = lax.broadcasted_iota(jnp.int32, logits.shape, 1)
-            own = jnp.logical_and(at_row == at_col, at_row < rows)
-            sign = jnp.where(own, 1.0, -1.0)
-            grads = -sign * jax.nn.sigmoid(-sign * logits)
-        else:
-            grads = jax.nn.sigmoid(logits)
+            corner = (rows, rows)
+            at_row = lax.broadcasted_iota(jnp.int32, corner, 0)
+            at_col = lax.broadcasted_iota(jnp.int32, corner, 1)
+            own = jnp.where(
+                at_row == at_col, -jax.nn.sigmoid(-logits[:rows, :rows]), grads[:rows, :rows]
+            )
+            top = jnp.concatenate([own, grads[:rows, rows:]], axis=1)
+            grads = jnp.concatenate([top, grads[rows:]], axis=0)
         sum_g = sum_g + lane_sums(grads)
         sum_gl = sum_gl + lane_sums(grads * scaled)
         grads_b = grads.astype(jnp.bfloat16)
         grad_b[start : start + step] = grads_b
         part = jnp.dot(grads_b, txt_b[...], preferred_element_type=jnp.float32)
-        store_part(temp * part, start, img_parts, img_cuts, rows)
+        store_part(part, start, img_parts, img_cuts, rows)
     sums[0:8] = sum_g
     sums[8:16] = sum_gl
+    scale[...] = jnp.broadcast_to(temp, scale.shape)
     for start in range(0, n_txt * rows, step):
         part = lax.dot_general(
             grad_b[:, start : start + step],
@@ -175,7 +178,7 @@
             (((0,), (0,)), ((), ())),
             preferred_element_type=jnp.float32,
         )
-        store_part(temp * part, start, txt_parts, txt_cuts, rows)
+        store_part(part, start, txt_parts, txt_cuts, rows)
 
 
 def tile_call(imgs, txts, log_temp, bias):
@@ -200,9 +203,13 @@
             txt_cuts,
             rows,
         ),
-        out_shape=outs + [jax.ShapeDtypeStruct((16, 128), jnp.float32)],
+        out_shape=outs
+        + [
+            jax.ShapeDtypeStruct((16, 128), jnp.float32),
+            jax.ShapeDtypeStruct((8, 128), jnp.float32),
+        ],
         in_specs=[VMEM] * (len(flat) + 2),
-        out_specs=[VMEM] * (len(outs) + 1),
+        out_specs=[VMEM] * (len(outs) + 2),
         scratch_shapes=[
             pltpu.VMEM((n_img * rows, width), jnp.bfloat16),
             pltpu.VMEM((n_txt * rows, width), jnp.bfloat16),
@@ -214,56 +221,58 @@
         ),
     )(*flat, log_temp, bias)
     results = list(results)
+    scale = results.pop()
     sums = results.pop()
     parts = [[results.pop(0) for _ in range(cut)] for cut in img_cuts + txt_cuts]
-    return parts[:n_img], parts[n_img:], sums
-
-
-def finish_rows(value, keep, recvs, out):
+    return parts[:n_img], parts[n_img:], sums, scale
+
+
+def finish_rows(scale, value, keep, recvs, out):
     total = keep[...]
     for recv in recvs:
         total = total + recv[...].astype(jnp.float32)
     unit, inverse = unit_rows(value[...])
+    inverse = inverse * scale[:1, :1]
     along = jnp.sum(unit * total, axis=1, keepdims=True)
     out[...] = ((total - unit * along) * inverse).astype(jnp.bfloat16)
 
 
-def finish_first_kernel(value, keep, *refs):
-    finish_rows(value, keep, refs[:-2], refs[-2])
+def finish_first_kernel(scale, value, keep, *refs):
+    finish_rows(scale, value, keep, refs[:-2], refs[-2])
     refs[-1][...] = jnp.zeros(refs[-1].shape, jnp.float32)
 
 
-def finish_first(value, keep, recvs):
+def finish_first(scale, value, keep, recvs):
     return pl.pallas_call(
         finish_first_kernel,
         out_shape=(
             jax.ShapeDtypeStruct(value.shape, jnp.bfloat16),
             jax.ShapeDtypeStruct((8, 128), jnp.float32),
         ),
-        in_specs=[VMEM] * (2 + len(recvs)),
+        in_specs=[VMEM] * (3 + len(recvs)),
         out_specs=[VMEM] * 2,
         compiler_params=pltpu.CompilerParams(vmem_limit_bytes=SMALL_VMEM),
         cost_estimate=pl.CostEstimate(flops=RETURN_COST, bytes_accessed=0, transcendentals=0),
-    )(value, keep, *recvs)
-
-
-def finish_last_kernel(pairs, token, sums, sums_recv, value, keep, *refs):
+    )(scale, value, keep, *recvs)
+
+
+def finish_last_kernel(pairs, token, sums, sums_recv, scale, value, keep, *refs):
     total = sums[...] + sums_recv[...]
     for place in range(2):
         whole = jnp.sum(total[8 * place : 8 * place + 8], axis=0, keepdims=True)
         refs[place - 2][...] = jnp.sum(whole, axis=1, keepdims=True) / pairs
-    finish_rows(value, keep, refs[:-3], refs[-3])
-
-
-def finish_last(token, sums, sums_recv, pairs, value, keep, recvs):
+    finish_rows(scale, value, keep, refs[:-3], refs[-3])
+
+
+def finish_last(token, sums, sums_recv, pairs, scale, value, keep, recvs):
     return pl.pallas_call(
         functools.partial(finish_last_kernel, pairs),
         out_shape=[jax.ShapeDtypeStruct(value.shape, jnp.bfloat16)]
         + [jax.ShapeDtypeStruct((1, 1), jnp.float32)] * 2,
-        in_specs=[ANY] + [VMEM] * (4 + len(recvs)),
+        in_specs=[ANY] + [VMEM] * (5 + len(recvs)),
         out_specs=[VMEM] * 3,
         compiler_params=pltpu.CompilerParams(vmem_limit_bytes=SMALL_VMEM),
-    )(token, sums, sums_recv, value, keep, *recvs)
+    )(token, sums, sums_recv, scale, value, keep, *recvs)
 
 
 def add_kernel(keep, recv, *refs):
@@ -327,17 +336,19 @@
     txt_bits = (all_bits[:1] + all_bits[split:])[::-1]
     txt_bits[0] |= img_bits[0]
     imgs, txts = gathered(image_embeds, text_embeds, img_bits, txt_bits)
-    img_parts, txt_parts, sums = tile_call(imgs, txts, log_temp.reshape(1, 1), bias.reshape(1, 1))
+    img_parts, txt_parts, sums, scale = tile_call(
+        imgs, txts, log_temp.reshape(1, 1), bias.reshape(1, 1)
+    )
     img_parts, txt_parts = ([part[0] for part in parts] for parts in (img_parts, txt_parts))
     txt_keep, txt_recvs, others = returned(txt_parts, txt_bits, [], False)
     for bit in img_bits[:1] + txt_bits[1:] + img_bits[:0:-1]:
         sums = sums_call([sums, swapped(sums, bit)], others)
     img_keep, img_recvs, others = returned(img_parts, img_bits, others + [sums], True)
     sums_recv = swapped(sums, txt_bits[0])
-    grad_text, token = finish_first(text_embeds, txt_keep, txt_recvs)
+    grad_text, token = finish_first(scale, text_embeds, txt_keep, txt_recvs)
     pairs = float(rows * count) * float(rows * count)
     grad_image, grad_bias, grad_temp = finish_last(
-        token, sums, sums_recv, pairs, image_embeds, img_keep, img_recvs
+        token, sums, sums_recv, pairs, scale, image_embeds, img_keep, img_recvs
     )
     return (grad_image, grad_text, grad_temp.reshape(1), grad_bias.reshape(1))
 

time: 48.7 us -> 48.7 us (level)
  no operation moved by 1% of the time
where the time goes in v14:
time: 48.7 us; the launch traced here: 48.6 us
  starting transfers between devices  20.5 us (42%)
  waiting for transfers between devices  19.7 us (40%)
  Pallas kernels  5.55 us (11%)
  between operations  2.07 us (4%)
  local copies, waits for them, and re-layouts  0.73 us (1%)
    ppermute x17, starting transfers between devices, swapped(): return lax.ppermute(x, 'blk', [(i, i ^ bit) for i in range(count)])  20.5 us
    ppermute x17, waiting for transfers between devices, swapped(): return lax.ppermute(x, 'blk', [(i, i ^ bit) for i in range(count)])  19.7 us
    pallas_call x1, Pallas kernels, tile_call(): pl.pallas_call(functools.partial(tile_kernel, [len(block) for block in im...  2.59 us
    pallas_call x1, Pallas kernels, finish_first(): pl.pallas_call(finish_first_kernel, out_shape=(jax.ShapeDtypeStruct(value...  1.05 us
    pallas_call x1, Pallas kernels, finish_last(): pl.pallas_call(functools.partial(finish_last_kernel, pairs), out_shape=[j...  1.04 us
  transfers between devices with their start and end apart: 17, of which 7 were waited for; matrix products, arithmetic and copies ran while one was open for 0% of the time, Pallas kernels for 4%

profile of v14, /device:TPU:0, one launch (start us, length us, event | category | flops | bytes accessed | tf_op | source)
XLA Modules:
  0.0 48.6 jit_solution(15180567955017801439)
XLA Ops:
  0.6 0.0 copy-start.1
  0.6 3.0 %collective-permute-start = (bf16[128,1152]{1,0:T(8,128)(2,1)}, bf16[128,1152]{1,0:T(8,128)(2,1)S(1)}, u32[]{:S(2)}, u32[]{:S(2)}) collective-permute-start(bf16[128,1152]{1,0:T(8,128)(2,1)} %value.7), channel_id=1, source_target_pairs={{0,2},{1,3},{2,0},{3,1},{4,6},{5,7},{6,4},{7,5},{8,10},{9,11},{10,... | collective-permute-start | bytes 884744 | tf_op jit(solution)/shard_map/ppermute | solution.py:21
  3.6 1.6 %collective-permute-start.1 = (bf16[128,1152]{1,0:T(8,128)(2,1)}, bf16[128,1152]{1,0:T(8,128)(2,1)S(1)}, u32[]{:S(2)}, u32[]{:S(2)}) collective-permute-start(bf16[128,1152]{1,0:T(8,128)(2,1)} %value.7), channel_id=1, source_target_pairs={{0,4},{1,5},{2,6},{3,7},{4,0},{5,1},{6,2},{7,3},{8,12},{9,13},{10,... | collective-permute-start | bytes 884744 | tf_op jit(solution)/shard_map/ppermute | solution.py:21
  5.2 2.5 %collective-permute-start.4 = (bf16[128,1152]{1,0:T(8,128)(2,1)}, bf16[128,1152]{1,0:T(8,128)(2,1)S(1)}, u32[]{:S(2)}, u32[]{:S(2)}) collective-permute-start(bf16[128,1152]{1,0:T(8,128)(2,1)} %value.6), channel_id=1, source_target_pairs={{0,12},{1,13},{2,14},{3,15},{4,8},{5,9},{6,10},{7,11},{8,4},{9,5},... | collective-permute-start | bytes 884744 | tf_op jit(solution)/shard_map/ppermute | solution.py:21
  7.7 3.2 %collective-permute-done.value = bf16[128,1152]{1,0:T(8,128)(2,1)S(1)} collective-permute-done((bf16[128,1152]{1,0:T(8,128)(2,1)}, bf16[128,1152]{1,0:T(8,128)(2,1)S(1)}, u32[]{:S(2)}, u32[]{:S(2)}) %collective-permute-start) | collective-permute-done | bytes 294944 | tf_op jit(solution)/shard_map/ppermute | solution.py:21
  10.9 0.1 shard_map.75
  11.0 1.9 %collective-permute-start.3 = (bf16[48,1152]{1,0:T(8,128)(2,1)S(1)}, bf16[48,1152]{1,0:T(8,128)(2,1)S(1)}, u32[]{:S(2)}, u32[]{:S(2)}) collective-permute-start(bf16[48,1152]{1,0:T(8,128)(2,1)S(1)} %get-tuple-element.26.refs_4_), channel_id=1, source_target_pairs={{0,4},{1,5},{2,6},{3,7},{4,0},{5,1},{6,2},{7,3},{8,12},{9,13},{10,... | collective-permute-start | bytes 331784 | tf_op jit(solution)/shard_map/ppermute | solution.py:21
  14.2 0.0 copy-done.1
  14.2 0.0 copy-start
  14.2 0.1 shard_map.76.refs_0_.refs_7_
  14.4 0.1 collective-permute-start.5
  14.5 0.7 %copy-done = bf16[128,1152]{1,0:T(8,128)(2,1)S(1)} copy-done((bf16[128,1152]{1,0:T(8,128)(2,1)S(1)}, bf16[128,1152]{1,0:T(8,128)(2,1)}, u32[]{:S(2)}) %copy-start) | copy-done | bytes 294936
  15.2 0.1 shard_map.77.refs_0_
  15.3 0.0 collective-permute-done.1.value
  15.3 0.1 shard_map.78
  15.5 1.6 %collective-permute-start.2 = (bf16[80,1152]{1,0:T(8,128)(2,1)S(1)}, bf16[80,1152]{1,0:T(8,128)(2,1)S(1)}, u32[]{:S(2)}, u32[]{:S(2)}) collective-permute-start(bf16[80,1152]{1,0:T(8,128)(2,1)S(1)} %get-tuple-element.24.refs_0_.refs_1_), channel_id=1, source_target_pairs={{0,2},{1,3},{2,0},{3,1},{4,6},{5,7},{6,4},{7,5},{8,10},{9,11},{10,... | collective-permute-start | bytes 552968 | tf_op jit(solution)/shard_map/ppermute | solution.py:21
  17.0 4.8 %collective-permute-done.4.value = bf16[128,1152]{1,0:T(8,128)(2,1)S(1)} collective-permute-done((bf16[128,1152]{1,0:T(8,128)(2,1)}, bf16[128,1152]{1,0:T(8,128)(2,1)S(1)}, u32[]{:S(2)}, u32[]{:S(2)}) %collective-permute-start.4) | collective-permute-done | bytes 294944 | tf_op jit(solution)/shard_map/ppermute | solution.py:21
  21.9 0.1 shard_map.81.refs_8_
  22.1 0.1 collective-permute-start.6
  22.1 0.0 collective-permute-done.3.refs_0_
  22.1 0.0 collective-permute-done.2.refs_0_
  22.2 1.5 %collective-permute-done.6.refs_0_ = bf16[128,1152]{1,0:T(8,128)(2,1)S(1)} collective-permute-done((bf16[128,1152]{1,0:T(8,128)(2,1)S(1)}, bf16[128,1152]{1,0:T(8,128)(2,1)S(1)}, u32[]{:S(2)}, u32[]{:S(2)}) %collective-permute-start.6) | collective-permute-done | bytes 294944 | tf_op jit(solution)/shard_map/ppermute | solution.py:21
  23.7 0.0 collective-permute-done.5.refs_9_
  23.7 2.6 %shard_map.83 = (f32[128,1152]{1,0:T(8,128)S(1)}, f32[128,1152]{1,0:T(8,128)S(1)}, bf16[128,1152]{1,0:T(8,128)(2,1)S(1)}, bf16[128,1152]{1,0:T(8,128)(2,1)S(1)},...) custom-call(bf16[128,1152]{1,0:T(8,128)(2,1)S(1)} %shard_map.77.refs, ...), custom_call_target="tpu_custom_call" | custom-call | flops 1811939328 | tf_op jit(solution)/shard_map/pallas_call | solution.py:197
  26.3 0.2 collective-permute-start.8
  26.5 0.6 %collective-permute-start.14 = (bf16[128,1152]{1,0:T(8,128)(2,1)S(1)}, bf16[128,1152]{1,0:T(8,128)(2,1)S(1)}, u32[]{:S(2)}, u32[]{:S(2)}) collective-permute-start(bf16[128,1152]{1,0:T(8,128)(2,1)S(1)} %get-tuple-element.37), channel_id=1, source_target_pairs={{0,2},{1,3},{2,0},{3,1},{4,6},{5,7},{6,4},{7,5},{8,10},{9,11},{10,... | collective-permute-start | bytes 884744 | tf_op jit(solution)/shard_map/ppermute | solution.py:21
  27.1 0.0 collective-permute-start.10
  27.1 0.1 collective-permute-start.7
  27.2 0.8 %collective-permute-done.8.recv = bf16[128,1152]{1,0:T(8,128)(2,1)S(1)} collective-permute-done((bf16[128,1152]{1,0:T(8,128)(2,1)S(1)}, bf16[128,1152]{1,0:T(8,128)(2,1)S(1)}, u32[]{:S(2)}, u32[]{:S(2)}) %collective-permute-start.8) | collective-permute-done | bytes 294944 | tf_op jit(solution)/shard_map/ppermute | solution.py:21
  27.9 0.1 shard_map.84.refs_0_
  28.0 4.1 %collective-permute-start.9 = (bf16[128,1152]{1,0:T(8,128)(2,1)S(1)}, bf16[128,1152]{1,0:T(8,128)(2,1)S(1)}, u32[]{:S(2)}, u32[]{:S(2)}) collective-permute-start(bf16[128,1152]{1,0:T(8,128)(2,1)S(1)} %shard_map.84.refs_0_), channel_id=1, source_target_pairs={{0,12},{1,13},{2,14},{3,15},{4,8},{5,9},{6,10},{7,11},{8,4},{9,5},... | collective-permute-start | bytes 884744 | tf_op jit(solution)/shard_map/ppermute | solution.py:21
  32.1 0.0 collective-permute-done.10.second
  32.1 0.0 collective-permute-start.11
  32.1 1.2 %collective-permute-done.11.second = f32[16,128]{1,0:T(8,128)S(1)} collective-permute-done((f32[16,128]{1,0:T(8,128)S(1)}, f32[16,128]{1,0:T(8,128)S(1)}, u32[]{:S(2)}, u32[]{:S(2)}) %collective-permute-start.11) | collective-permute-done | bytes 8224 | tf_op jit(solution)/shard_map/ppermute | solution.py:21
  33.3 0.7 %collective-permute-start.12 = (f32[16,128]{1,0:T(8,128)S(1)}, f32[16,128]{1,0:T(8,128)S(1)}, u32[]{:S(2)}, u32[]{:S(2)}) collective-permute-start(f32[16,128]{1,0:T(8,128)S(1)} %shard_map.87.first), channel_id=1, source_target_pairs={{0,2},{1,3},{2,0},{3,1},{4,6},{5,7},{6,4},{7,5},{8,10},{9,11},{10,... | collective-permute-start | bytes 24584 | tf_op jit(solution)/shard_map/ppermute | solution.py:21
  34.0 3.0 %collective-permute-done.12.second = f32[16,128]{1,0:T(8,128)S(1)} collective-permute-done((f32[16,128]{1,0:T(8,128)S(1)}, f32[16,128]{1,0:T(8,128)S(1)}, u32[]{:S(2)}, u32[]{:S(2)}) %collective-permute-start.12) | collective-permute-done | bytes 8224 | tf_op jit(solution)/shard_map/ppermute | solution.py:21
  36.9 0.0 collective-permute-done.14.recv
  36.9 0.1 shard_map.89.refs_1_
  37.0 0.8 %collective-permute-start.15 = (bf16[128,1152]{1,0:T(8,128)(2,1)S(1)}, bf16[128,1152]{1,0:T(8,128)(2,1)S(1)}, u32[]{:S(2)}, u32[]{:S(2)}) collective-permute-start(bf16[128,1152]{1,0:T(8,128)(2,1)S(1)} %shard_map.90), channel_id=1, source_target_pairs={{0,2},{1,3},{2,0},{3,1},{4,6},{5,7},{6,4},{7,5},{8,10},{9,11},{10,... | collective-permute-start | bytes 884744 | tf_op jit(solution)/shard_map/ppermute | solution.py:21
  37.8 1.0 %collective-permute-start.16 = (bf16[128,1152]{1,0:T(8,128)(2,1)S(1)}, bf16[128,1152]{1,0:T(8,128)(2,1)S(1)}, u32[]{:S(2)}, u32[]{:S(2)}) collective-permute-start(bf16[128,1152]{1,0:T(8,128)(2,1)S(1)} %shard_map.89.refs_1_), channel_id=1, source_target_pairs={{0,4},{1,5},{2,6},{3,7},{4,0},{5,1},{6,2},{7,3},{8,12},{9,13},{10,... | collective-permute-start | bytes 884744 | tf_op jit(solution)/shard_map/ppermute | solution.py:21
  38.7 2.5 %collective-permute-start.13 = (f32[16,128]{1,0:T(8,128)S(1)}, f32[16,128]{1,0:T(8,128)S(1)}, u32[]{:S(2)}, u32[]{:S(2)}) collective-permute-start(f32[16,128]{1,0:T(8,128)S(1)} %shard_map.88.refs_1_.sums), channel_id=1, source_target_pairs={{0,12},{1,13},{2,14},{3,15},{4,8},{5,9},{6,10},{7,11},{8,4},{9,5},... | collective-permute-start | bytes 24584 | tf_op jit(solution)/shard_map/ppermute | solution.py:21
  41.2 0.0 collective-permute-done.7.refs_0_
  41.2 0.0 collective-permute-done.9.refs_1_
  41.2 1.0 %shard_map.85 = (bf16[128,1152]{1,0:T(8,128)(2,1)}, f32[8,128]{1,0:T(8,128)S(1)}) custom-call(f32[8,128]{1,0:T(8,128)S(1)} %get-tuple-element.27.scale, bf16[128,1152]{1,0:T(8,128)(2,1)S(1)} %copy-done.1, f32[128,1152]{1,0:T(8,128)S(1)} %get-tuple-element.28.keep, bf16[128,1152]{1,0:T(8,128)(2,1)S(1)} %collective-permute-done.7.refs_0_, ...), custom_call_target="tpu_custom_call" | custom-call | flops 1000000000 | tf_op jit(solution)/shard_map/pallas_call | solution.py:246
  42.3 5.2 %collective-permute-done.13.sums_recv = f32[16,128]{1,0:T(8,128)S(1)} collective-permute-done((f32[16,128]{1,0:T(8,128)S(1)}, f32[16,128]{1,0:T(8,128)S(1)}, u32[]{:S(2)}, u32[]{:S(2)}) %collective-permute-start.13) | collective-permute-done | bytes 8224 | tf_op jit(solution)/shard_map/ppermute | solution.py:21
  47.5 0.0 collective-permute-done.15.refs_0_
  47.5 0.0 collective-permute-done.16.refs_1_
  47.5 1.0 %shard_map.91 = (bf16[128,1152]{1,0:T(8,128)(2,1)}, f32[1,1]{1,0:T(1,128)}, f32[1,1]{1,0:T(1,128)}) custom-call(f32[8,128]{1,0:T(8,128)S(1)} %get-tuple-element.32.token, f32[16,128]{1,0:T(8,128)S(1)} %shard_map.88.refs_1_.sums, f32[16,128]{1,0:T(8,128)S(1)} %collective-permute-done.13.sums_recv, f32[8,128]{1,0:T(8,128)S(1)} %get-tuple-element.27.scale, ...), custom_call_target="tpu_custom_call" | custom-call | tf_op jit(solution)/shard_map/pallas_call | solution.py:268
  (7 shorter events, 0.0 us)
Async XLA Ops:
  0.6 13.6 %copy-start.1 = (bf16[128,1152]{1,0:T(8,128)(2,1)S(1)}, bf16[128,1152]{1,0:T(8,128)(2,1)}, u32[]{:S(2)}) copy-start(bf16[128,1152]{1,0:T(8,128)(2,1)} %value.6) | copy-start | bytes 884740
  0.6 10.2 %collective-permute-start = (bf16[128,1152]{1,0:T(8,128)(2,1)}, bf16[128,1152]{1,0:T(8,128)(2,1)S(1)}, u32[]{:S(2)}, u32[]{:S(2)}) collective-permute-start(bf16[128,1152]{1,0:T(8,128)(2,1)} %value.7), channel_id=1, source_target_pairs={{0,2},{1,3},{2,0},{3,1},{4,6},{5,7},{6,4},{7,5},{8,10},{9,11},{10,... | collective-permute-start | bytes 884744 | tf_op jit(solution)/shard_map/ppermute | solution.py:21
  3.6 11.7 %collective-permute-start.1 = (bf16[128,1152]{1,0:T(8,128)(2,1)}, bf16[128,1152]{1,0:T(8,128)(2,1)S(1)}, u32[]{:S(2)}, u32[]{:S(2)}) collective-permute-start(bf16[128,1152]{1,0:T(8,128)(2,1)} %value.7), channel_id=1, source_target_pairs={{0,4},{1,5},{2,6},{3,7},{4,0},{5,1},{6,2},{7,3},{8,12},{9,13},{10,... | collective-permute-start | bytes 884744 | tf_op jit(solution)/shard_map/ppermute | solution.py:21
  5.2 16.7 %collective-permute-start.4 = (bf16[128,1152]{1,0:T(8,128)(2,1)}, bf16[128,1152]{1,0:T(8,128)(2,1)S(1)}, u32[]{:S(2)}, u32[]{:S(2)}) collective-permute-start(bf16[128,1152]{1,0:T(8,128)(2,1)} %value.6), channel_id=1, source_target_pairs={{0,12},{1,13},{2,14},{3,15},{4,8},{5,9},{6,10},{7,11},{8,4},{9,5},... | collective-permute-start | bytes 884744 | tf_op jit(solution)/shard_map/ppermute | solution.py:21
  11.0 11.1 %collective-permute-start.3 = (bf16[48,1152]{1,0:T(8,128)(2,1)S(1)}, bf16[48,1152]{1,0:T(8,128)(2,1)S(1)}, u32[]{:S(2)}, u32[]{:S(2)}) collective-permute-start(bf16[48,1152]{1,0:T(8,128)(2,1)S(1)} %get-tuple-element.26.refs_4_), channel_id=1, source_target_pairs={{0,4},{1,5},{2,6},{3,7},{4,0},{5,1},{6,2},{7,3},{8,12},{9,13},{10,... | collective-permute-start | bytes 331784 | tf_op jit(solution)/shard_map/ppermute | solution.py:21
  14.2 1.0 %copy-start = (bf16[128,1152]{1,0:T(8,128)(2,1)S(1)}, bf16[128,1152]{1,0:T(8,128)(2,1)}, u32[]{:S(2)}) copy-start(bf16[128,1152]{1,0:T(8,128)(2,1)} %value.7) | copy-start | bytes 884740
  14.4 9.3 %collective-permute-start.5 = (bf16[128,1152]{1,0:T(8,128)(2,1)S(1)}, bf16[128,1152]{1,0:T(8,128)(2,1)S(1)}, u32[]{:S(2)}, u32[]{:S(2)}) collective-permute-start(bf16[128,1152]{1,0:T(8,128)(2,1)S(1)} %shard_map.76.refs_0_.refs_7_), channel_id=1, source_target_pairs={{0,1},{1,0},{2,3},{3,2},{4,5},{5,4},{6,7},{7,6},{8,9},{9,8},{10,11... | collective-permute-start | bytes 884744 | tf_op jit(solution)/shard_map/ppermute | solution.py:21
  15.5 6.7 %collective-permute-start.2 = (bf16[80,1152]{1,0:T(8,128)(2,1)S(1)}, bf16[80,1152]{1,0:T(8,128)(2,1)S(1)}, u32[]{:S(2)}, u32[]{:S(2)}) collective-permute-start(bf16[80,1152]{1,0:T(8,128)(2,1)S(1)} %get-tuple-element.24.refs_0_.refs_1_), channel_id=1, source_target_pairs={{0,2},{1,3},{2,0},{3,1},{4,6},{5,7},{6,4},{7,5},{8,10},{9,11},{10,... | collective-permute-start | bytes 552968 | tf_op jit(solution)/shard_map/ppermute | solution.py:21
  22.1 1.6 %collective-permute-start.6 = (bf16[128,1152]{1,0:T(8,128)(2,1)S(1)}, bf16[128,1152]{1,0:T(8,128)(2,1)S(1)}, u32[]{:S(2)}, u32[]{:S(2)}) collective-permute-start(bf16[128,1152]{1,0:T(8,128)(2,1)S(1)} %shard_map.81.refs_8_), channel_id=1, source_target_pairs={{0,1},{1,0},{2,3},{3,2},{4,5},{5,4},{6,7},{7,6},{8,9},{9,8},{10,11... | collective-permute-start | bytes 884744 | tf_op jit(solution)/shard_map/ppermute | solution.py:21
  26.3 1.6 %collective-permute-start.8 = (bf16[128,1152]{1,0:T(8,128)(2,1)S(1)}, bf16[128,1152]{1,0:T(8,128)(2,1)S(1)}, u32[]{:S(2)}, u32[]{:S(2)}) collective-permute-start(bf16[128,1152]{1,0:T(8,128)(2,1)S(1)} %get-tuple-element.31), channel_id=1, source_target_pairs={{0,1},{1,0},{2,3},{3,2},{4,5},{5,4},{6,7},{7,6},{8,9},{9,8},{10,11... | collective-permute-start | bytes 884744 | tf_op jit(solution)/shard_map/ppermute | solution.py:21
  26.5 10.4 %collective-permute-start.14 = (bf16[128,1152]{1,0:T(8,128)(2,1)S(1)}, bf16[128,1152]{1,0:T(8,128)(2,1)S(1)}, u32[]{:S(2)}, u32[]{:S(2)}) collective-permute-start(bf16[128,1152]{1,0:T(8,128)(2,1)S(1)} %get-tuple-element.37), channel_id=1, source_target_pairs={{0,2},{1,3},{2,0},{3,1},{4,6},{5,7},{6,4},{7,5},{8,10},{9,11},{10,... | collective-permute-start | bytes 884744 | tf_op jit(solution)/shard_map/ppermute | solution.py:21
  27.1 5.0 %collective-permute-start.10 = (f32[16,128]{1,0:T(8,128)S(1)}, f32[16,128]{1,0:T(8,128)S(1)}, u32[]{:S(2)}, u32[]{:S(2)}) collective-permute-start(f32[16,128]{1,0:T(8,128)S(1)} %get-tuple-element.33.first), channel_id=1, source_target_pairs={{0,4},{1,5},{2,6},{3,7},{4,0},{5,1},{6,2},{7,3},{8,12},{9,13},{10,... | collective-permute-start | bytes 24584 | tf_op jit(solution)/shard_map/ppermute | solution.py:21
  27.1 14.1 %collective-permute-start.7 = (bf16[128,1152]{1,0:T(8,128)(2,1)S(1)}, bf16[128,1152]{1,0:T(8,128)(2,1)S(1)}, u32[]{:S(2)}, u32[]{:S(2)}) collective-permute-start(bf16[128,1152]{1,0:T(8,128)(2,1)S(1)} %get-tuple-element.29), channel_id=1, source_target_pairs={{0,1},{1,0},{2,3},{3,2},{4,5},{5,4},{6,7},{7,6},{8,9},{9,8},{10,11... | collective-permute-start | bytes 884744 | tf_op jit(solution)/shard_map/ppermute | solution.py:21
  28.0 13.2 %collective-permute-start.9 = (bf16[128,1152]{1,0:T(8,128)(2,1)S(1)}, bf16[128,1152]{1,0:T(8,128)(2,1)S(1)}, u32[]{:S(2)}, u32[]{:S(2)}) collective-permute-start(bf16[128,1152]{1,0:T(8,128)(2,1)S(1)} %shard_map.84.refs_0_), channel_id=1, source_target_pairs={{0,12},{1,13},{2,14},{3,15},{4,8},{5,9},{6,10},{7,11},{8,4},{9,5},... | collective-permute-start | bytes 884744 | tf_op jit(solution)/shard_map/ppermute | solution.py:21
  32.1 1.2 %collective-permute-start.11 = (f32[16,128]{1,0:T(8,128)S(1)}, f32[16,128]{1,0:T(8,128)S(1)}, u32[]{:S(2)}, u32[]{:S(2)}) collective-permute-start(f32[16,128]{1,0:T(8,128)S(1)} %shard_map.86.first), channel_id=1, source_target_pairs={{0,1},{1,0},{2,3},{3,2},{4,5},{5,4},{6,7},{7,6},{8,9},{9,8},{10,11... | collective-permute-start | bytes 24584 | tf_op jit(solution)/shard_map/ppermute | solution.py:21
  33.3 3.7 %collective-permute-start.12 = (f32[16,128]{1,0:T(8,128)S(1)}, f32[16,128]{1,0:T(8,128)S(1)}, u32[]{:S(2)}, u32[]{:S(2)}) collective-permute-start(f32[16,128]{1,0:T(8,128)S(1)} %shard_map.87.first), channel_id=1, source_target_pairs={{0,2},{1,3},{2,0},{3,1},{4,6},{5,7},{6,4},{7,5},{8,10},{9,11},{10,... | collective-permute-start | bytes 24584 | tf_op jit(solution)/shard_map/ppermute | solution.py:21
  37.0 10.5 %collective-permute-start.15 = (bf16[128,1152]{1,0:T(8,128)(2,1)S(1)}, bf16[128,1152]{1,0:T(8,128)(2,1)S(1)}, u32[]{:S(2)}, u32[]{:S(2)}) collective-permute-start(bf16[128,1152]{1,0:T(8,128)(2,1)S(1)} %shard_map.90), channel_id=1, source_target_pairs={{0,2},{1,3},{2,0},{3,1},{4,6},{5,7},{6,4},{7,5},{8,10},{9,11},{10,... | collective-permute-start | bytes 884744 | tf_op jit(solution)/shard_map/ppermute | solution.py:21
  37.8 9.7 %collective-permute-start.16 = (bf16[128,1152]{1,0:T(8,128)(2,1)S(1)}, bf16[128,1152]{1,0:T(8,128)(2,1)S(1)}, u32[]{:S(2)}, u32[]{:S(2)}) collective-permute-start(bf16[128,1152]{1,0:T(8,128)(2,1)S(1)} %shard_map.89.refs_1_), channel_id=1, source_target_pairs={{0,4},{1,5},{2,6},{3,7},{4,0},{5,1},{6,2},{7,3},{8,12},{9,13},{10,... | collective-permute-start | bytes 884744 | tf_op jit(solution)/shard_map/ppermute | solution.py:21
  38.7 8.8 %collective-permute-start.13 = (f32[16,128]{1,0:T(8,128)S(1)}, f32[16,128]{1,0:T(8,128)S(1)}, u32[]{:S(2)}, u32[]{:S(2)}) collective-permute-start(f32[16,128]{1,0:T(8,128)S(1)} %shard_map.88.refs_1_.sums), channel_id=1, source_target_pairs={{0,12},{1,13},{2,14},{3,15},{4,8},{5,9},{6,10},{7,11},{8,4},{9,5},... | collective-permute-start | bytes 24584 | tf_op jit(solution)/shard_map/ppermute | solution.py:21

commit v15 on v13

--- a/solution.py
+++ b/solution.py
@@ -79,7 +79,7 @@
     img_raw = [swapped(image, bit) for bit in img_bits]
     txt_raw = swapped(text, txt_bits[0])
     rows = image.shape[0]
-    cuts = [rows * 5 // 8, rows * 3 // 8]
+    cuts = [rows * 3 // 4, rows // 4]
     imgs, txts = {}, {}
     others = []
     for place in reversed(range(1, len(img_bits))):

time: 48.7 us -> 49.1 us (level)
  starting transfers between devices: 20.5 us -> 21.9 us
  waiting for transfers between devices: 19.8 us -> 18.8 us
    ppermute x17, starting transfers between devices: 20.5 us -> 21.9 us  [swapped(): return lax.ppermute(x, 'blk', [(i, i ^ bit) for i in range(count)])]
    ppermute x17, waiting for transfers between devices: 19.8 us -> 18.8 us  [swapped(): return lax.ppermute(x, 'blk', [(i, i ^ bit) for i in range(count)])]
  transfers between devices with their start and end apart: 17 -> 17, of which waited for: 7 -> 8; matrix products, arithmetic and copies ran while one was open for 0% -> 0% of each run, Pallas kernels for 4% -> 4%
where the time goes in v15:
time: 49.1 us; the launch traced here: 48.9 us
  starting transfers between devices  21.9 us (45%)
  waiting for transfers between devices  18.8 us (38%)
  Pallas kernels  5.48 us (11%)
  between operations  2.06 us (4%)
  local copies, waits for them, and re-layouts  0.73 us (1%)
    ppermute x17, starting transfers between devices, swapped(): return lax.ppermute(x, 'blk', [(i, i ^ bit) for i in range(count)])  21.9 us
    ppermute x17, waiting for transfers between devices, swapped(): return lax.ppermute(x, 'blk', [(i, i ^ bit) for i in range(count)])  18.8 us
    pallas_call x1, Pallas kernels, tile_call(): pl.pallas_call(functools.partial(tile_kernel, [len(block) for block in im...  2.59 us
    pallas_call x1, Pallas kernels, finish_first(): pl.pallas_call(finish_first_kernel, out_shape=(jax.ShapeDtypeStruct(value...  1.02 us
    pallas_call x1, Pallas kernels, finish_last(): pl.pallas_call(functools.partial(finish_last_kernel, pairs), out_shape=[j...  1.01 us
  transfers between devices with their start and end apart: 17, of which 8 were waited for; matrix products, arithmetic and copies ran while one was open for 0% of the time, Pallas kernels for 4%

profile of v15, /device:TPU:0, one launch (start us, length us, event | category | flops | bytes accessed | tf_op | source)
XLA Modules:
  0.0 48.9 jit_solution(16727288187116987)
XLA Ops:
  0.6 0.0 copy-start.1
  0.6 3.0 %collective-permute-start = (bf16[128,1152]{1,0:T(8,128)(2,1)}, bf16[128,1152]{1,0:T(8,128)(2,1)S(1)}, u32[]{:S(2)}, u32[]{:S(2)}) collective-permute-start(bf16[128,1152]{1,0:T(8,128)(2,1)} %value.7), channel_id=1, source_target_pairs={{0,2},{1,3},{2,0},{3,1},{4,6},{5,7},{6,4},{7,5},{8,10},{9,11},{10,... | collective-permute-start | bytes 884744 | tf_op jit(solution)/shard_map/ppermute | solution.py:21
  3.6 1.6 %collective-permute-start.1 = (bf16[128,1152]{1,0:T(8,128)(2,1)}, bf16[128,1152]{1,0:T(8,128)(2,1)S(1)}, u32[]{:S(2)}, u32[]{:S(2)}) collective-permute-start(bf16[128,1152]{1,0:T(8,128)(2,1)} %value.7), channel_id=1, source_target_pairs={{0,4},{1,5},{2,6},{3,7},{4,0},{5,1},{6,2},{7,3},{8,12},{9,13},{10,... | collective-permute-start | bytes 884744 | tf_op jit(solution)/shard_map/ppermute | solution.py:21
  5.2 2.5 %collective-permute-start.4 = (bf16[128,1152]{1,0:T(8,128)(2,1)}, bf16[128,1152]{1,0:T(8,128)(2,1)S(1)}, u32[]{:S(2)}, u32[]{:S(2)}) collective-permute-start(bf16[128,1152]{1,0:T(8,128)(2,1)} %value.6), channel_id=1, source_target_pairs={{0,12},{1,13},{2,14},{3,15},{4,8},{5,9},{6,10},{7,11},{8,4},{9,5},... | collective-permute-start | bytes 884744 | tf_op jit(solution)/shard_map/ppermute | solution.py:21
  7.7 3.2 %collective-permute-done.value = bf16[128,1152]{1,0:T(8,128)(2,1)S(1)} collective-permute-done((bf16[128,1152]{1,0:T(8,128)(2,1)}, bf16[128,1152]{1,0:T(8,128)(2,1)S(1)}, u32[]{:S(2)}, u32[]{:S(2)}) %collective-permute-start) | collective-permute-done | bytes 294944 | tf_op jit(solution)/shard_map/ppermute | solution.py:21
  10.9 0.1 shard_map.75
  11.0 1.9 %collective-permute-start.3 = (bf16[32,1152]{1,0:T(8,128)(2,1)S(1)}, bf16[32,1152]{1,0:T(8,128)(2,1)S(1)}, u32[]{:S(2)}, u32[]{:S(2)}) collective-permute-start(bf16[32,1152]{1,0:T(8,128)(2,1)S(1)} %get-tuple-element.25.refs_4_), channel_id=1, source_target_pairs={{0,4},{1,5},{2,6},{3,7},{4,0},{5,1},{6,2},{7,3},{8,12},{9,13},{10,... | collective-permute-start | bytes 221192 | tf_op jit(solution)/shard_map/ppermute | solution.py:21
  14.2 0.0 copy-done.1
  14.2 0.0 copy-start
  14.2 0.1 shard_map.76.refs_0_.refs_7_
  14.4 0.1 collective-permute-start.5
  14.5 0.7 %copy-done = bf16[128,1152]{1,0:T(8,128)(2,1)S(1)} copy-done((bf16[128,1152]{1,0:T(8,128)(2,1)S(1)}, bf16[128,1152]{1,0:T(8,128)(2,1)}, u32[]{:S(2)}) %copy-start) | copy-done | bytes 294936
  15.2 0.1 shard_map.77.refs_0_
  15.3 0.0 collective-permute-done.1.value
  15.3 0.1 shard_map.78
  15.5 1.6 %collective-permute-start.2 = (bf16[96,1152]{1,0:T(8,128)(2,1)S(1)}, bf16[96,1152]{1,0:T(8,128)(2,1)S(1)}, u32[]{:S(2)}, u32[]{:S(2)}) collective-permute-start(bf16[96,1152]{1,0:T(8,128)(2,1)S(1)} %get-tuple-element.23.refs_0_.refs_1_), channel_id=1, source_target_pairs={{0,2},{1,3},{2,0},{3,1},{4,6},{5,7},{6,4},{7,5},{8,10},{9,11},{10,... | collective-permute-start | bytes 663560 | tf_op jit(solution)/shard_map/ppermute | solution.py:21
  17.0 4.5 %collective-permute-done.4.value = bf16[128,1152]{1,0:T(8,128)(2,1)S(1)} collective-permute-done((bf16[128,1152]{1,0:T(8,128)(2,1)}, bf16[128,1152]{1,0:T(8,128)(2,1)S(1)}, u32[]{:S(2)}, u32[]{:S(2)}) %collective-permute-start.4) | collective-permute-done | bytes 294944 | tf_op jit(solution)/shard_map/ppermute | solution.py:21
  21.5 0.1 shard_map.81.refs_8_
  21.7 0.1 collective-permute-start.6
  21.7 0.0 collective-permute-done.3.refs_0_
  21.8 0.9 %collective-permute-done.2.refs_0_ = bf16[96,1152]{1,0:T(8,128)(2,1)S(1)} collective-permute-done((bf16[96,1152]{1,0:T(8,128)(2,1)S(1)}, bf16[96,1152]{1,0:T(8,128)(2,1)S(1)}, u32[]{:S(2)}, u32[]{:S(2)}) %collective-permute-start.2) | collective-permute-done | bytes 221216 | tf_op jit(solution)/shard_map/ppermute | solution.py:21
  22.7 0.6 %collective-permute-done.6.refs_0_ = bf16[128,1152]{1,0:T(8,128)(2,1)S(1)} collective-permute-done((bf16[128,1152]{1,0:T(8,128)(2,1)S(1)}, bf16[128,1152]{1,0:T(8,128)(2,1)S(1)}, u32[]{:S(2)}, u32[]{:S(2)}) %collective-permute-start.6) | collective-permute-done | bytes 294944 | tf_op jit(solution)/shard_map/ppermute | solution.py:21
  23.3 0.0 collective-permute-done.5.refs_9_
  23.3 2.6 %shard_map.83 = (f32[128,1152]{1,0:T(8,128)S(1)}, f32[128,1152]{1,0:T(8,128)S(1)}, bf16[128,1152]{1,0:T(8,128)(2,1)S(1)}, bf16[128,1152]{1,0:T(8,128)(2,1)S(1)},...) custom-call(bf16[128,1152]{1,0:T(8,128)(2,1)S(1)} %shard_map.77.refs, ...), custom_call_target="tpu_custom_call" | custom-call | flops 1811939328 | tf_op jit(solution)/shard_map/pallas_call | solution.py:194
  25.9 0.2 collective-permute-start.8
  26.1 0.8 %collective-permute-start.14 = (bf16[128,1152]{1,0:T(8,128)(2,1)S(1)}, bf16[128,1152]{1,0:T(8,128)(2,1)S(1)}, u32[]{:S(2)}, u32[]{:S(2)}) collective-permute-start(bf16[128,1152]{1,0:T(8,128)(2,1)S(1)} %get-tuple-element.35), channel_id=1, source_target_pairs={{0,2},{1,3},{2,0},{3,1},{4,6},{5,7},{6,4},{7,5},{8,10},{9,11},{10,... | collective-permute-start | bytes 884744 | tf_op jit(solution)/shard_map/ppermute | solution.py:21
  26.9 0.5 collective-permute-start.10
  27.4 0.0 collective-permute-start.7
  27.4 0.2 collective-permute-done.8.recv
  27.6 0.1 shard_map.84.refs_0_
  27.6 4.9 %collective-permute-start.9 = (bf16[128,1152]{1,0:T(8,128)(2,1)S(1)}, bf16[128,1152]{1,0:T(8,128)(2,1)S(1)}, u32[]{:S(2)}, u32[]{:S(2)}) collective-permute-start(bf16[128,1152]{1,0:T(8,128)(2,1)S(1)} %shard_map.84.refs_0_), channel_id=1, source_target_pairs={{0,12},{1,13},{2,14},{3,15},{4,8},{5,9},{6,10},{7,11},{8,4},{9,5},... | collective-permute-start | bytes 884744 | tf_op jit(solution)/shard_map/ppermute | solution.py:21
  32.5 0.0 collective-permute-done.10.second
  32.5 0.0 collective-permute-start.11
  32.5 1.2 %collective-permute-done.11.second = f32[16,128]{1,0:T(8,128)S(1)} collective-permute-done((f32[16,128]{1,0:T(8,128)S(1)}, f32[16,128]{1,0:T(8,128)S(1)}, u32[]{:S(2)}, u32[]{:S(2)}) %collective-permute-start.11) | collective-permute-done | bytes 8224 | tf_op jit(solution)/shard_map/ppermute | solution.py:21
  33.7 0.7 %collective-permute-start.12 = (f32[16,128]{1,0:T(8,128)S(1)}, f32[16,128]{1,0:T(8,128)S(1)}, u32[]{:S(2)}, u32[]{:S(2)}) collective-permute-start(f32[16,128]{1,0:T(8,128)S(1)} %shard_map.87.first), channel_id=1, source_target_pairs={{0,2},{1,3},{2,0},{3,1},{4,6},{5,7},{6,4},{7,5},{8,10},{9,11},{10,... | collective-permute-start | bytes 24584 | tf_op jit(solution)/shard_map/ppermute | solution.py:21
  34.4 3.0 %collective-permute-done.12.second = f32[16,128]{1,0:T(8,128)S(1)} collective-permute-done((f32[16,128]{1,0:T(8,128)S(1)}, f32[16,128]{1,0:T(8,128)S(1)}, u32[]{:S(2)}, u32[]{:S(2)}) %collective-permute-start.12) | collective-permute-done | bytes 8224 | tf_op jit(solution)/shard_map/ppermute | solution.py:21
  37.3 0.0 collective-permute-done.14.recv
  37.3 0.1 shard_map.89.refs_1_
  37.4 0.8 %collective-permute-start.15 = (bf16[128,1152]{1,0:T(8,128)(2,1)S(1)}, bf16[128,1152]{1,0:T(8,128)(2,1)S(1)}, u32[]{:S(2)}, u32[]{:S(2)}) collective-permute-start(bf16[128,1152]{1,0:T(8,128)(2,1)S(1)} %shard_map.90), channel_id=1, source_target_pairs={{0,2},{1,3},{2,0},{3,1},{4,6},{5,7},{6,4},{7,5},{8,10},{9,11},{10,... | collective-permute-start | bytes 884744 | tf_op jit(solution)/shard_map/ppermute | solution.py:21
  38.2 1.0 %collective-permute-start.16 = (bf16[128,1152]{1,0:T(8,128)(2,1)S(1)}, bf16[128,1152]{1,0:T(8,128)(2,1)S(1)}, u32[]{:S(2)}, u32[]{:S(2)}) collective-permute-start(bf16[128,1152]{1,0:T(8,128)(2,1)S(1)} %shard_map.89.refs_1_), channel_id=1, source_target_pairs={{0,4},{1,5},{2,6},{3,7},{4,0},{5,1},{6,2},{7,3},{8,12},{9,13},{10,... | collective-permute-start | bytes 884744 | tf_op jit(solution)/shard_map/ppermute | solution.py:21
  39.1 2.5 %collective-permute-start.13 = (f32[16,128]{1,0:T(8,128)S(1)}, f32[16,128]{1,0:T(8,128)S(1)}, u32[]{:S(2)}, u32[]{:S(2)}) collective-permute-start(f32[16,128]{1,0:T(8,128)S(1)} %shard_map.88.refs_1_.sums), channel_id=1, source_target_pairs={{0,12},{1,13},{2,14},{3,15},{4,8},{5,9},{6,10},{7,11},{8,4},{9,5},... | collective-permute-start | bytes 24584 | tf_op jit(solution)/shard_map/ppermute | solution.py:21
  41.6 0.0 collective-permute-done.7.refs_0_
  41.6 0.0 collective-permute-done.9.refs_1_
  41.6 1.0 %shard_map.85 = (bf16[128,1152]{1,0:T(8,128)(2,1)}, f32[8,128]{1,0:T(8,128)S(1)}) custom-call(bf16[128,1152]{1,0:T(8,128)(2,1)S(1)} %copy-done.1, f32[128,1152]{1,0:T(8,128)S(1)} %get-tuple-element.26.keep, bf16[128,1152]{1,0:T(8,128)(2,1)S(1)} %collective-permute-done.7.refs_0_, bf16[128,1152]{1,0:T(8,128)(2,1)S(1)} %collective-permute-done.9.refs_1_), custom_call_target="tpu_custom_call" | custom-call | flops 1000000000 | tf_op jit(solution)/shard_map/pallas_call | solution.py:237
  42.6 5.3 %collective-permute-done.13.sums_recv = f32[16,128]{1,0:T(8,128)S(1)} collective-permute-done((f32[16,128]{1,0:T(8,128)S(1)}, f32[16,128]{1,0:T(8,128)S(1)}, u32[]{:S(2)}, u32[]{:S(2)}) %collective-permute-start.13) | collective-permute-done | bytes 8224 | tf_op jit(solution)/shard_map/ppermute | solution.py:21
  47.9 0.0 collective-permute-done.15.refs_0_
  47.9 0.0 collective-permute-done.16.refs_1_
  47.9 1.0 %shard_map.91 = (bf16[128,1152]{1,0:T(8,128)(2,1)}, f32[1,1]{1,0:T(1,128)}, f32[1,1]{1,0:T(1,128)}) custom-call(f32[8,128]{1,0:T(8,128)S(1)} %get-tuple-element.30.token, f32[16,128]{1,0:T(8,128)S(1)} %shard_map.88.refs_1_.sums, f32[16,128]{1,0:T(8,128)S(1)} %collective-permute-done.13.sums_recv, bf16[128,1152]{1,0:T(8,128)(2,1)S(1)} %copy-done, ...), custom_call_target="tpu_custom_call" | custom-call | tf_op jit(solution)/shard_map/pallas_call | solution.py:259
  (7 shorter events, 0.0 us)
Async XLA Ops:
  0.6 13.6 %copy-start.1 = (bf16[128,1152]{1,0:T(8,128)(2,1)S(1)}, bf16[128,1152]{1,0:T(8,128)(2,1)}, u32[]{:S(2)}) copy-start(bf16[128,1152]{1,0:T(8,128)(2,1)} %value.6) | copy-start | bytes 884740
  0.6 10.2 %collective-permute-start = (bf16[128,1152]{1,0:T(8,128)(2,1)}, bf16[128,1152]{1,0:T(8,128)(2,1)S(1)}, u32[]{:S(2)}, u32[]{:S(2)}) collective-permute-start(bf16[128,1152]{1,0:T(8,128)(2,1)} %value.7), channel_id=1, source_target_pairs={{0,2},{1,3},{2,0},{3,1},{4,6},{5,7},{6,4},{7,5},{8,10},{9,11},{10,... | collective-permute-start | bytes 884744 | tf_op jit(solution)/shard_map/ppermute | solution.py:21
  3.6 11.7 %collective-permute-start.1 = (bf16[128,1152]{1,0:T(8,128)(2,1)}, bf16[128,1152]{1,0:T(8,128)(2,1)S(1)}, u32[]{:S(2)}, u32[]{:S(2)}) collective-permute-start(bf16[128,1152]{1,0:T(8,128)(2,1)} %value.7), channel_id=1, source_target_pairs={{0,4},{1,5},{2,6},{3,7},{4,0},{5,1},{6,2},{7,3},{8,12},{9,13},{10,... | collective-permute-start | bytes 884744 | tf_op jit(solution)/shard_map/ppermute | solution.py:21
  5.2 16.3 %collective-permute-start.4 = (bf16[128,1152]{1,0:T(8,128)(2,1)}, bf16[128,1152]{1,0:T(8,128)(2,1)S(1)}, u32[]{:S(2)}, u32[]{:S(2)}) collective-permute-start(bf16[128,1152]{1,0:T(8,128)(2,1)} %value.6), channel_id=1, source_target_pairs={{0,12},{1,13},{2,14},{3,15},{4,8},{5,9},{6,10},{7,11},{8,4},{9,5},... | collective-permute-start | bytes 884744 | tf_op jit(solution)/shard_map/ppermute | solution.py:21
  11.0 10.7 %collective-permute-start.3 = (bf16[32,1152]{1,0:T(8,128)(2,1)S(1)}, bf16[32,1152]{1,0:T(8,128)(2,1)S(1)}, u32[]{:S(2)}, u32[]{:S(2)}) collective-permute-start(bf16[32,1152]{1,0:T(8,128)(2,1)S(1)} %get-tuple-element.25.refs_4_), channel_id=1, source_target_pairs={{0,4},{1,5},{2,6},{3,7},{4,0},{5,1},{6,2},{7,3},{8,12},{9,13},{10,... | collective-permute-start | bytes 221192 | tf_op jit(solution)/shard_map/ppermute | solution.py:21
  14.2 1.0 %copy-start = (bf16[128,1152]{1,0:T(8,128)(2,1)S(1)}, bf16[128,1152]{1,0:T(8,128)(2,1)}, u32[]{:S(2)}) copy-start(bf16[128,1152]{1,0:T(8,128)(2,1)} %value.7) | copy-start | bytes 884740
  14.4 8.9 %collective-permute-start.5 = (bf16[128,1152]{1,0:T(8,128)(2,1)S(1)}, bf16[128,1152]{1,0:T(8,128)(2,1)S(1)}, u32[]{:S(2)}, u32[]{:S(2)}) collective-permute-start(bf16[128,1152]{1,0:T(8,128)(2,1)S(1)} %shard_map.76.refs_0_.refs_7_), channel_id=1, source_target_pairs={{0,1},{1,0},{2,3},{3,2},{4,5},{5,4},{6,7},{7,6},{8,9},{9,8},{10,11... | collective-permute-start | bytes 884744 | tf_op jit(solution)/shard_map/ppermute | solution.py:21
  15.5 7.2 %collective-permute-start.2 = (bf16[96,1152]{1,0:T(8,128)(2,1)S(1)}, bf16[96,1152]{1,0:T(8,128)(2,1)S(1)}, u32[]{:S(2)}, u32[]{:S(2)}) collective-permute-start(bf16[96,1152]{1,0:T(8,128)(2,1)S(1)} %get-tuple-element.23.refs_0_.refs_1_), channel_id=1, source_target_pairs={{0,2},{1,3},{2,0},{3,1},{4,6},{5,7},{6,4},{7,5},{8,10},{9,11},{10,... | collective-permute-start | bytes 663560 | tf_op jit(solution)/shard_map/ppermute | solution.py:21
  21.7 1.6 %collective-permute-start.6 = (bf16[128,1152]{1,0:T(8,128)(2,1)S(1)}, bf16[128,1152]{1,0:T(8,128)(2,1)S(1)}, u32[]{:S(2)}, u32[]{:S(2)}) collective-permute-start(bf16[128,1152]{1,0:T(8,128)(2,1)S(1)} %shard_map.81.refs_8_), channel_id=1, source_target_pairs={{0,1},{1,0},{2,3},{3,2},{4,5},{5,4},{6,7},{7,6},{8,9},{9,8},{10,11... | collective-permute-start | bytes 884744 | tf_op jit(solution)/shard_map/ppermute | solution.py:21
  25.9 1.6 %collective-permute-start.8 = (bf16[128,1152]{1,0:T(8,128)(2,1)S(1)}, bf16[128,1152]{1,0:T(8,128)(2,1)S(1)}, u32[]{:S(2)}, u32[]{:S(2)}) collective-permute-start(bf16[128,1152]{1,0:T(8,128)(2,1)S(1)} %get-tuple-element.29), channel_id=1, source_target_pairs={{0,1},{1,0},{2,3},{3,2},{4,5},{5,4},{6,7},{7,6},{8,9},{9,8},{10,11... | collective-permute-start | bytes 884744 | tf_op jit(solution)/shard_map/ppermute | solution.py:21
  26.1 11.2 %collective-permute-start.14 = (bf16[128,1152]{1,0:T(8,128)(2,1)S(1)}, bf16[128,1152]{1,0:T(8,128)(2,1)S(1)}, u32[]{:S(2)}, u32[]{:S(2)}) collective-permute-start(bf16[128,1152]{1,0:T(8,128)(2,1)S(1)} %get-tuple-element.35), channel_id=1, source_target_pairs={{0,2},{1,3},{2,0},{3,1},{4,6},{5,7},{6,4},{7,5},{8,10},{9,11},{10,... | collective-permute-start | bytes 884744 | tf_op jit(solution)/shard_map/ppermute | solution.py:21
  26.9 5.6 %collective-permute-start.10 = (f32[16,128]{1,0:T(8,128)S(1)}, f32[16,128]{1,0:T(8,128)S(1)}, u32[]{:S(2)}, u32[]{:S(2)}) collective-permute-start(f32[16,128]{1,0:T(8,128)S(1)} %get-tuple-element.31.first), channel_id=1, source_target_pairs={{0,4},{1,5},{2,6},{3,7},{4,0},{5,1},{6,2},{7,3},{8,12},{9,13},{10,... | collective-permute-start | bytes 24584 | tf_op jit(solution)/shard_map/ppermute | solution.py:21
  27.4 14.2 %collective-permute-start.7 = (bf16[128,1152]{1,0:T(8,128)(2,1)S(1)}, bf16[128,1152]{1,0:T(8,128)(2,1)S(1)}, u32[]{:S(2)}, u32[]{:S(2)}) collective-permute-start(bf16[128,1152]{1,0:T(8,128)(2,1)S(1)} %get-tuple-element.27), channel_id=1, source_target_pairs={{0,1},{1,0},{2,3},{3,2},{4,5},{5,4},{6,7},{7,6},{8,9},{9,8},{10,11... | collective-permute-start | bytes 884744 | tf_op jit(solution)/shard_map/ppermute | solution.py:21
  27.6 14.0 %collective-permute-start.9 = (bf16[128,1152]{1,0:T(8,128)(2,1)S(1)}, bf16[128,1152]{1,0:T(8,128)(2,1)S(1)}, u32[]{:S(2)}, u32[]{:S(2)}) collective-permute-start(bf16[128,1152]{1,0:T(8,128)(2,1)S(1)} %shard_map.84.refs_0_), channel_id=1, source_target_pairs={{0,12},{1,13},{2,14},{3,15},{4,8},{5,9},{6,10},{7,11},{8,4},{9,5},... | collective-permute-start | bytes 884744 | tf_op jit(solution)/shard_map/ppermute | solution.py:21
  32.5 1.2 %collective-permute-start.11 = (f32[16,128]{1,0:T(8,128)S(1)}, f32[16,128]{1,0:T(8,128)S(1)}, u32[]{:S(2)}, u32[]{:S(2)}) collective-permute-start(f32[16,128]{1,0:T(8,128)S(1)} %shard_map.86.first), channel_id=1, source_target_pairs={{0,1},{1,0},{2,3},{3,2},{4,5},{5,4},{6,7},{7,6},{8,9},{9,8},{10,11... | collective-permute-start | bytes 24584 | tf_op jit(solution)/shard_map/ppermute | solution.py:21
  33.7 3.7 %collective-permute-start.12 = (f32[16,128]{1,0:T(8,128)S(1)}, f32[16,128]{1,0:T(8,128)S(1)}, u32[]{:S(2)}, u32[]{:S(2)}) collective-permute-start(f32[16,128]{1,0:T(8,128)S(1)} %shard_map.87.first), channel_id=1, source_target_pairs={{0,2},{1,3},{2,0},{3,1},{4,6},{5,7},{6,4},{7,5},{8,10},{9,11},{10,... | collective-permute-start | bytes 24584 | tf_op jit(solution)/shard_map/ppermute | solution.py:21
  37.4 10.5 %collective-permute-start.15 = (bf16[128,1152]{1,0:T(8,128)(2,1)S(1)}, bf16[128,1152]{1,0:T(8,128)(2,1)S(1)}, u32[]{:S(2)}, u32[]{:S(2)}) collective-permute-start(bf16[128,1152]{1,0:T(8,128)(2,1)S(1)} %shard_map.90), channel_id=1, source_target_pairs={{0,2},{1,3},{2,0},{3,1},{4,6},{5,7},{6,4},{7,5},{8,10},{9,11},{10,... | collective-permute-start | bytes 884744 | tf_op jit(solution)/shard_map/ppermute | solution.py:21
  38.2 9.7 %collective-permute-start.16 = (bf16[128,1152]{1,0:T(8,128)(2,1)S(1)}, bf16[128,1152]{1,0:T(8,128)(2,1)S(1)}, u32[]{:S(2)}, u32[]{:S(2)}) collective-permute-start(bf16[128,1152]{1,0:T(8,128)(2,1)S(1)} %shard_map.89.refs_1_), channel_id=1, source_target_pairs={{0,4},{1,5},{2,6},{3,7},{4,0},{5,1},{6,2},{7,3},{8,12},{9,13},{10,... | collective-permute-start | bytes 884744 | tf_op jit(solution)/shard_map/ppermute | solution.py:21
  39.1 8.8 %collective-permute-start.13 = (f32[16,128]{1,0:T(8,128)S(1)}, f32[16,128]{1,0:T(8,128)S(1)}, u32[]{:S(2)}, u32[]{:S(2)}) collective-permute-start(f32[16,128]{1,0:T(8,128)S(1)} %shard_map.88.refs_1_.sums), channel_id=1, source_target_pairs={{0,12},{1,13},{2,14},{3,15},{4,8},{5,9},{6,10},{7,11},{8,4},{9,5},... | collective-permute-start | bytes 24584 | tf_op jit(solution)/shard_map/ppermute | solution.py:21

commit v16 on v15

--- a/solution.py
+++ b/solution.py
@@ -79,7 +79,7 @@
     img_raw = [swapped(image, bit) for bit in img_bits]
     txt_raw = swapped(text, txt_bits[0])
     rows = image.shape[0]
-    cuts = [rows * 3 // 4, rows // 4]
+    cuts = [rows // 2, rows // 2]
     imgs, txts = {}, {}
     others = []
     for place in reversed(range(1, len(img_bits))):

time: 49.1 us -> 48.3 us (0.984)
  starting transfers between devices: 21.9 us -> 19.8 us
  waiting for transfers between devices: 18.8 us -> 20.1 us
    ppermute x17, starting transfers between devices: 21.9 us -> 19.8 us  [swapped(): return lax.ppermute(x, 'blk', [(i, i ^ bit) for i in range(count)])]
    ppermute x17, waiting for transfers between devices: 18.8 us -> 20.1 us  [swapped(): return lax.ppermute(x, 'blk', [(i, i ^ bit) for i in range(count)])]
  transfers between devices with their start and end apart: 17 -> 17, of which waited for: 8 -> 7; matrix products, arithmetic and copies ran while one was open for 0% -> 0% of each run, Pallas kernels for 4% -> 4%
where the time goes in v16:
time: 48.3 us; the launch traced here: 48.1 us
  waiting for transfers between devices  20.1 us (42%)
  starting transfers between devices  19.8 us (41%)
  Pallas kernels  5.48 us (11%)
  between operations  2.07 us (4%)
  local copies, waits for them, and re-layouts  0.73 us (2%)
    ppermute x17, waiting for transfers between devices, swapped(): return lax.ppermute(x, 'blk', [(i, i ^ bit) for i in range(count)])  20.1 us
    ppermute x17, starting transfers between devices, swapped(): return lax.ppermute(x, 'blk', [(i, i ^ bit) for i in range(count)])  19.8 us
    pallas_call x1, Pallas kernels, tile_call(): pl.pallas_call(functools.partial(tile_kernel, [len(block) for block in im...  2.59 us
    pallas_call x1, Pallas kernels, finish_first(): pl.pallas_call(finish_first_kernel, out_shape=(jax.ShapeDtypeStruct(value...  1.01 us
    pallas_call x1, Pallas kernels, finish_last(): pl.pallas_call(functools.partial(finish_last_kernel, pairs), out_shape=[j...  1.01 us
  transfers between devices with their start and end apart: 17, of which 7 were waited for; matrix products, arithmetic and copies ran while one was open for 0% of the time, Pallas kernels for 4%

profile of v16, /device:TPU:0, one launch (start us, length us, event | category | flops | bytes accessed | tf_op | source)
XLA Modules:
  0.0 48.1 jit_solution(10798352929634451483)
XLA Ops:
  0.6 0.0 copy-start.1
  0.6 3.0 %collective-permute-start = (bf16[128,1152]{1,0:T(8,128)(2,1)}, bf16[128,1152]{1,0:T(8,128)(2,1)S(1)}, u32[]{:S(2)}, u32[]{:S(2)}) collective-permute-start(bf16[128,1152]{1,0:T(8,128)(2,1)} %value.7), channel_id=1, source_target_pairs={{0,2},{1,3},{2,0},{3,1},{4,6},{5,7},{6,4},{7,5},{8,10},{9,11},{10,... | collective-permute-start | bytes 884744 | tf_op jit(solution)/shard_map/ppermute | solution.py:21
  3.6 1.6 %collective-permute-start.1 = (bf16[128,1152]{1,0:T(8,128)(2,1)}, bf16[128,1152]{1,0:T(8,128)(2,1)S(1)}, u32[]{:S(2)}, u32[]{:S(2)}) collective-permute-start(bf16[128,1152]{1,0:T(8,128)(2,1)} %value.7), channel_id=1, source_target_pairs={{0,4},{1,5},{2,6},{3,7},{4,0},{5,1},{6,2},{7,3},{8,12},{9,13},{10,... | collective-permute-start | bytes 884744 | tf_op jit(solution)/shard_map/ppermute | solution.py:21
  5.2 2.5 %collective-permute-start.4 = (bf16[128,1152]{1,0:T(8,128)(2,1)}, bf16[128,1152]{1,0:T(8,128)(2,1)S(1)}, u32[]{:S(2)}, u32[]{:S(2)}) collective-permute-start(bf16[128,1152]{1,0:T(8,128)(2,1)} %value.6), channel_id=1, source_target_pairs={{0,12},{1,13},{2,14},{3,15},{4,8},{5,9},{6,10},{7,11},{8,4},{9,5},... | collective-permute-start | bytes 884744 | tf_op jit(solution)/shard_map/ppermute | solution.py:21
  7.7 3.2 %collective-permute-done.value = bf16[128,1152]{1,0:T(8,128)(2,1)S(1)} collective-permute-done((bf16[128,1152]{1,0:T(8,128)(2,1)}, bf16[128,1152]{1,0:T(8,128)(2,1)S(1)}, u32[]{:S(2)}, u32[]{:S(2)}) %collective-permute-start) | collective-permute-done | bytes 294944 | tf_op jit(solution)/shard_map/ppermute | solution.py:21
  10.9 0.1 shard_map.75
  11.0 1.9 %collective-permute-start.3 = (bf16[64,1152]{1,0:T(8,128)(2,1)S(1)}, bf16[64,1152]{1,0:T(8,128)(2,1)S(1)}, u32[]{:S(2)}, u32[]{:S(2)}) collective-permute-start(bf16[64,1152]{1,0:T(8,128)(2,1)S(1)} %get-tuple-element.25.refs_4_), channel_id=1, source_target_pairs={{0,4},{1,5},{2,6},{3,7},{4,0},{5,1},{6,2},{7,3},{8,12},{9,13},{10,... | collective-permute-start | bytes 442376 | tf_op jit(solution)/shard_map/ppermute | solution.py:21
  14.2 0.0 copy-done.1
  14.2 0.0 copy-start
  14.2 0.1 shard_map.76.refs_0_.refs_7_
  14.4 0.1 collective-permute-start.5
  14.5 0.7 %copy-done = bf16[128,1152]{1,0:T(8,128)(2,1)S(1)} copy-done((bf16[128,1152]{1,0:T(8,128)(2,1)S(1)}, bf16[128,1152]{1,0:T(8,128)(2,1)}, u32[]{:S(2)}) %copy-start) | copy-done | bytes 294936
  15.2 0.1 shard_map.77.refs_0_
  15.3 0.0 collective-permute-done.1.value
  15.3 0.1 shard_map.78
  15.5 1.6 %collective-permute-start.2 = (bf16[64,1152]{1,0:T(8,128)(2,1)S(1)}, bf16[64,1152]{1,0:T(8,128)(2,1)S(1)}, u32[]{:S(2)}, u32[]{:S(2)}) collective-permute-start(bf16[64,1152]{1,0:T(8,128)(2,1)S(1)} %get-tuple-element.23.refs_0_.refs_1_), channel_id=1, source_target_pairs={{0,2},{1,3},{2,0},{3,1},{4,6},{5,7},{6,4},{7,5},{8,10},{9,11},{10,... | collective-permute-start | bytes 442376 | tf_op jit(solution)/shard_map/ppermute | solution.py:21
  17.0 5.1 %collective-permute-done.4.value = bf16[128,1152]{1,0:T(8,128)(2,1)S(1)} collective-permute-done((bf16[128,1152]{1,0:T(8,128)(2,1)}, bf16[128,1152]{1,0:T(8,128)(2,1)S(1)}, u32[]{:S(2)}, u32[]{:S(2)}) %collective-permute-start.4) | collective-permute-done | bytes 294944 | tf_op jit(solution)/shard_map/ppermute | solution.py:21
  22.2 0.1 shard_map.81.refs_8_
  22.3 0.1 collective-permute-start.6
  22.4 0.0 collective-permute-done.3.refs_0_
  22.4 0.0 collective-permute-done.2.refs_0_
  22.5 1.5 %collective-permute-done.6.refs_0_ = bf16[128,1152]{1,0:T(8,128)(2,1)S(1)} collective-permute-done((bf16[128,1152]{1,0:T(8,128)(2,1)S(1)}, bf16[128,1152]{1,0:T(8,128)(2,1)S(1)}, u32[]{:S(2)}, u32[]{:S(2)}) %collective-permute-start.6) | collective-permute-done | bytes 294944 | tf_op jit(solution)/shard_map/ppermute | solution.py:21
  24.0 0.0 collective-permute-done.5.refs_9_
  24.0 2.6 %shard_map.83 = (f32[128,1152]{1,0:T(8,128)S(1)}, f32[128,1152]{1,0:T(8,128)S(1)}, bf16[128,1152]{1,0:T(8,128)(2,1)S(1)}, bf16[128,1152]{1,0:T(8,128)(2,1)S(1)},...) custom-call(bf16[128,1152]{1,0:T(8,128)(2,1)S(1)} %shard_map.77.refs, ...), custom_call_target="tpu_custom_call" | custom-call | flops 1811939328 | tf_op jit(solution)/shard_map/pallas_call | solution.py:194
  26.6 0.2 collective-permute-start.8
  26.8 0.6 %collective-permute-start.14 = (bf16[128,1152]{1,0:T(8,128)(2,1)S(1)}, bf16[128,1152]{1,0:T(8,128)(2,1)S(1)}, u32[]{:S(2)}, u32[]{:S(2)}) collective-permute-start(bf16[128,1152]{1,0:T(8,128)(2,1)S(1)} %get-tuple-element.35), channel_id=1, source_target_pairs={{0,2},{1,3},{2,0},{3,1},{4,6},{5,7},{6,4},{7,5},{8,10},{9,11},{10,... | collective-permute-start | bytes 884744 | tf_op jit(solution)/shard_map/ppermute | solution.py:21
  27.3 0.0 collective-permute-start.10
  27.3 0.1 collective-permute-start.7
  27.4 0.8 %collective-permute-done.8.recv = bf16[128,1152]{1,0:T(8,128)(2,1)S(1)} collective-permute-done((bf16[128,1152]{1,0:T(8,128)(2,1)S(1)}, bf16[128,1152]{1,0:T(8,128)(2,1)S(1)}, u32[]{:S(2)}, u32[]{:S(2)}) %collective-permute-start.8) | collective-permute-done | bytes 294944 | tf_op jit(solution)/shard_map/ppermute | solution.py:21
  28.2 0.1 shard_map.84.refs_0_
  28.3 3.4 %collective-permute-start.9 = (bf16[128,1152]{1,0:T(8,128)(2,1)S(1)}, bf16[128,1152]{1,0:T(8,128)(2,1)S(1)}, u32[]{:S(2)}, u32[]{:S(2)}) collective-permute-start(bf16[128,1152]{1,0:T(8,128)(2,1)S(1)} %shard_map.84.refs_0_), channel_id=1, source_target_pairs={{0,12},{1,13},{2,14},{3,15},{4,8},{5,9},{6,10},{7,11},{8,4},{9,5},... | collective-permute-start | bytes 884744 | tf_op jit(solution)/shard_map/ppermute | solution.py:21
  31.7 0.0 collective-permute-done.10.second
  31.7 0.0 collective-permute-start.11
  31.7 1.2 %collective-permute-done.11.second = f32[16,128]{1,0:T(8,128)S(1)} collective-permute-done((f32[16,128]{1,0:T(8,128)S(1)}, f32[16,128]{1,0:T(8,128)S(1)}, u32[]{:S(2)}, u32[]{:S(2)}) %collective-permute-start.11) | collective-permute-done | bytes 8224 | tf_op jit(solution)/shard_map/ppermute | solution.py:21
  32.9 0.8 %collective-permute-start.12 = (f32[16,128]{1,0:T(8,128)S(1)}, f32[16,128]{1,0:T(8,128)S(1)}, u32[]{:S(2)}, u32[]{:S(2)}) collective-permute-start(f32[16,128]{1,0:T(8,128)S(1)} %shard_map.87.first), channel_id=1, source_target_pairs={{0,2},{1,3},{2,0},{3,1},{4,6},{5,7},{6,4},{7,5},{8,10},{9,11},{10,... | collective-permute-start | bytes 24584 | tf_op jit(solution)/shard_map/ppermute | solution.py:21
  33.7 2.9 %collective-permute-done.12.second = f32[16,128]{1,0:T(8,128)S(1)} collective-permute-done((f32[16,128]{1,0:T(8,128)S(1)}, f32[16,128]{1,0:T(8,128)S(1)}, u32[]{:S(2)}, u32[]{:S(2)}) %collective-permute-start.12) | collective-permute-done | bytes 8224 | tf_op jit(solution)/shard_map/ppermute | solution.py:21
  36.5 0.0 collective-permute-done.14.recv
  36.5 0.1 shard_map.89.refs_1_
  36.6 0.8 %collective-permute-start.15 = (bf16[128,1152]{1,0:T(8,128)(2,1)S(1)}, bf16[128,1152]{1,0:T(8,128)(2,1)S(1)}, u32[]{:S(2)}, u32[]{:S(2)}) collective-permute-start(bf16[128,1152]{1,0:T(8,128)(2,1)S(1)} %shard_map.90), channel_id=1, source_target_pairs={{0,2},{1,3},{2,0},{3,1},{4,6},{5,7},{6,4},{7,5},{8,10},{9,11},{10,... | collective-permute-start | bytes 884744 | tf_op jit(solution)/shard_map/ppermute | solution.py:21
  37.4 0.9 %collective-permute-start.16 = (bf16[128,1152]{1,0:T(8,128)(2,1)S(1)}, bf16[128,1152]{1,0:T(8,128)(2,1)S(1)}, u32[]{:S(2)}, u32[]{:S(2)}) collective-permute-start(bf16[128,1152]{1,0:T(8,128)(2,1)S(1)} %shard_map.89.refs_1_), channel_id=1, source_target_pairs={{0,4},{1,5},{2,6},{3,7},{4,0},{5,1},{6,2},{7,3},{8,12},{9,13},{10,... | collective-permute-start | bytes 884744 | tf_op jit(solution)/shard_map/ppermute | solution.py:21
  38.3 2.4 %collective-permute-start.13 = (f32[16,128]{1,0:T(8,128)S(1)}, f32[16,128]{1,0:T(8,128)S(1)}, u32[]{:S(2)}, u32[]{:S(2)}) collective-permute-start(f32[16,128]{1,0:T(8,128)S(1)} %shard_map.88.refs_1_.sums), channel_id=1, source_target_pairs={{0,12},{1,13},{2,14},{3,15},{4,8},{5,9},{6,10},{7,11},{8,4},{9,5},... | collective-permute-start | bytes 24584 | tf_op jit(solution)/shard_map/ppermute | solution.py:21
  40.7 0.0 collective-permute-done.7.refs_0_
  40.7 0.0 collective-permute-done.9.refs_1_
  40.7 1.0 %shard_map.85 = (bf16[128,1152]{1,0:T(8,128)(2,1)}, f32[8,128]{1,0:T(8,128)S(1)}) custom-call(bf16[128,1152]{1,0:T(8,128)(2,1)S(1)} %copy-done.1, f32[128,1152]{1,0:T(8,128)S(1)} %get-tuple-element.26.keep, bf16[128,1152]{1,0:T(8,128)(2,1)S(1)} %collective-permute-done.7.refs_0_, bf16[128,1152]{1,0:T(8,128)(2,1)S(1)} %collective-permute-done.9.refs_1_), custom_call_target="tpu_custom_call" | custom-call | flops 1000000000 | tf_op jit(solution)/shard_map/pallas_call | solution.py:237
  41.8 5.4 %collective-permute-done.13.sums_recv = f32[16,128]{1,0:T(8,128)S(1)} collective-permute-done((f32[16,128]{1,0:T(8,128)S(1)}, f32[16,128]{1,0:T(8,128)S(1)}, u32[]{:S(2)}, u32[]{:S(2)}) %collective-permute-start.13) | collective-permute-done | bytes 8224 | tf_op jit(solution)/shard_map/ppermute | solution.py:21
  47.1 0.0 collective-permute-done.15.refs_0_
  47.1 0.0 collective-permute-done.16.refs_1_
  47.1 1.0 %shard_map.91 = (bf16[128,1152]{1,0:T(8,128)(2,1)}, f32[1,1]{1,0:T(1,128)}, f32[1,1]{1,0:T(1,128)}) custom-call(f32[8,128]{1,0:T(8,128)S(1)} %get-tuple-element.30.token, f32[16,128]{1,0:T(8,128)S(1)} %shard_map.88.refs_1_.sums, f32[16,128]{1,0:T(8,128)S(1)} %collective-permute-done.13.sums_recv, bf16[128,1152]{1,0:T(8,128)(2,1)S(1)} %copy-done, ...), custom_call_target="tpu_custom_call" | custom-call | tf_op jit(solution)/shard_map/pallas_call | solution.py:259
  (7 shorter events, 0.0 us)
Async XLA Ops:
  0.6 13.6 %copy-start.1 = (bf16[128,1152]{1,0:T(8,128)(2,1)S(1)}, bf16[128,1152]{1,0:T(8,128)(2,1)}, u32[]{:S(2)}) copy-start(bf16[128,1152]{1,0:T(8,128)(2,1)} %value.6) | copy-start | bytes 884740
  0.6 10.2 %collective-permute-start = (bf16[128,1152]{1,0:T(8,128)(2,1)}, bf16[128,1152]{1,0:T(8,128)(2,1)S(1)}, u32[]{:S(2)}, u32[]{:S(2)}) collective-permute-start(bf16[128,1152]{1,0:T(8,128)(2,1)} %value.7), channel_id=1, source_target_pairs={{0,2},{1,3},{2,0},{3,1},{4,6},{5,7},{6,4},{7,5},{8,10},{9,11},{10,... | collective-permute-start | bytes 884744 | tf_op jit(solution)/shard_map/ppermute | solution.py:21
  3.6 11.7 %collective-permute-start.1 = (bf16[128,1152]{1,0:T(8,128)(2,1)}, bf16[128,1152]{1,0:T(8,128)(2,1)S(1)}, u32[]{:S(2)}, u32[]{:S(2)}) collective-permute-start(bf16[128,1152]{1,0:T(8,128)(2,1)} %value.7), channel_id=1, source_target_pairs={{0,4},{1,5},{2,6},{3,7},{4,0},{5,1},{6,2},{7,3},{8,12},{9,13},{10,... | collective-permute-start | bytes 884744 | tf_op jit(solution)/shard_map/ppermute | solution.py:21
  5.2 17.0 %collective-permute-start.4 = (bf16[128,1152]{1,0:T(8,128)(2,1)}, bf16[128,1152]{1,0:T(8,128)(2,1)S(1)}, u32[]{:S(2)}, u32[]{:S(2)}) collective-permute-start(bf16[128,1152]{1,0:T(8,128)(2,1)} %value.6), channel_id=1, source_target_pairs={{0,12},{1,13},{2,14},{3,15},{4,8},{5,9},{6,10},{7,11},{8,4},{9,5},... | collective-permute-start | bytes 884744 | tf_op jit(solution)/shard_map/ppermute | solution.py:21
  11.0 11.4 %collective-permute-start.3 = (bf16[64,1152]{1,0:T(8,128)(2,1)S(1)}, bf16[64,1152]{1,0:T(8,128)(2,1)S(1)}, u32[]{:S(2)}, u32[]{:S(2)}) collective-permute-start(bf16[64,1152]{1,0:T(8,128)(2,1)S(1)} %get-tuple-element.25.refs_4_), channel_id=1, source_target_pairs={{0,4},{1,5},{2,6},{3,7},{4,0},{5,1},{6,2},{7,3},{8,12},{9,13},{10,... | collective-permute-start | bytes 442376 | tf_op jit(solution)/shard_map/ppermute | solution.py:21
  14.2 1.0 %copy-start = (bf16[128,1152]{1,0:T(8,128)(2,1)S(1)}, bf16[128,1152]{1,0:T(8,128)(2,1)}, u32[]{:S(2)}) copy-start(bf16[128,1152]{1,0:T(8,128)(2,1)} %value.7) | copy-start | bytes 884740
  14.4 9.6 %collective-permute-start.5 = (bf16[128,1152]{1,0:T(8,128)(2,1)S(1)}, bf16[128,1152]{1,0:T(8,128)(2,1)S(1)}, u32[]{:S(2)}, u32[]{:S(2)}) collective-permute-start(bf16[128,1152]{1,0:T(8,128)(2,1)S(1)} %shard_map.76.refs_0_.refs_7_), channel_id=1, source_target_pairs={{0,1},{1,0},{2,3},{3,2},{4,5},{5,4},{6,7},{7,6},{8,9},{9,8},{10,11... | collective-permute-start | bytes 884744 | tf_op jit(solution)/shard_map/ppermute | solution.py:21
  15.5 6.9 %collective-permute-start.2 = (bf16[64,1152]{1,0:T(8,128)(2,1)S(1)}, bf16[64,1152]{1,0:T(8,128)(2,1)S(1)}, u32[]{:S(2)}, u32[]{:S(2)}) collective-permute-start(bf16[64,1152]{1,0:T(8,128)(2,1)S(1)} %get-tuple-element.23.refs_0_.refs_1_), channel_id=1, source_target_pairs={{0,2},{1,3},{2,0},{3,1},{4,6},{5,7},{6,4},{7,5},{8,10},{9,11},{10,... | collective-permute-start | bytes 442376 | tf_op jit(solution)/shard_map/ppermute | solution.py:21
  22.3 1.6 %collective-permute-start.6 = (bf16[128,1152]{1,0:T(8,128)(2,1)S(1)}, bf16[128,1152]{1,0:T(8,128)(2,1)S(1)}, u32[]{:S(2)}, u32[]{:S(2)}) collective-permute-start(bf16[128,1152]{1,0:T(8,128)(2,1)S(1)} %shard_map.81.refs_8_), channel_id=1, source_target_pairs={{0,1},{1,0},{2,3},{3,2},{4,5},{5,4},{6,7},{7,6},{8,9},{9,8},{10,11... | collective-permute-start | bytes 884744 | tf_op jit(solution)/shard_map/ppermute | solution.py:21
  26.6 1.6 %collective-permute-start.8 = (bf16[128,1152]{1,0:T(8,128)(2,1)S(1)}, bf16[128,1152]{1,0:T(8,128)(2,1)S(1)}, u32[]{:S(2)}, u32[]{:S(2)}) collective-permute-start(bf16[128,1152]{1,0:T(8,128)(2,1)S(1)} %get-tuple-element.29), channel_id=1, source_target_pairs={{0,1},{1,0},{2,3},{3,2},{4,5},{5,4},{6,7},{7,6},{8,9},{9,8},{10,11... | collective-permute-start | bytes 884744 | tf_op jit(solution)/shard_map/ppermute | solution.py:21
  26.8 9.8 %collective-permute-start.14 = (bf16[128,1152]{1,0:T(8,128)(2,1)S(1)}, bf16[128,1152]{1,0:T(8,128)(2,1)S(1)}, u32[]{:S(2)}, u32[]{:S(2)}) collective-permute-start(bf16[128,1152]{1,0:T(8,128)(2,1)S(1)} %get-tuple-element.35), channel_id=1, source_target_pairs={{0,2},{1,3},{2,0},{3,1},{4,6},{5,7},{6,4},{7,5},{8,10},{9,11},{10,... | collective-permute-start | bytes 884744 | tf_op jit(solution)/shard_map/ppermute | solution.py:21
  27.3 4.4 %collective-permute-start.10 = (f32[16,128]{1,0:T(8,128)S(1)}, f32[16,128]{1,0:T(8,128)S(1)}, u32[]{:S(2)}, u32[]{:S(2)}) collective-permute-start(f32[16,128]{1,0:T(8,128)S(1)} %get-tuple-element.31.first), channel_id=1, source_target_pairs={{0,4},{1,5},{2,6},{3,7},{4,0},{5,1},{6,2},{7,3},{8,12},{9,13},{10,... | collective-permute-start | bytes 24584 | tf_op jit(solution)/shard_map/ppermute | solution.py:21
  27.3 13.4 %collective-permute-start.7 = (bf16[128,1152]{1,0:T(8,128)(2,1)S(1)}, bf16[128,1152]{1,0:T(8,128)(2,1)S(1)}, u32[]{:S(2)}, u32[]{:S(2)}) collective-permute-start(bf16[128,1152]{1,0:T(8,128)(2,1)S(1)} %get-tuple-element.27), channel_id=1, source_target_pairs={{0,1},{1,0},{2,3},{3,2},{4,5},{5,4},{6,7},{7,6},{8,9},{9,8},{10,11... | collective-permute-start | bytes 884744 | tf_op jit(solution)/shard_map/ppermute | solution.py:21
  28.3 12.5 %collective-permute-start.9 = (bf16[128,1152]{1,0:T(8,128)(2,1)S(1)}, bf16[128,1152]{1,0:T(8,128)(2,1)S(1)}, u32[]{:S(2)}, u32[]{:S(2)}) collective-permute-start(bf16[128,1152]{1,0:T(8,128)(2,1)S(1)} %shard_map.84.refs_0_), channel_id=1, source_target_pairs={{0,12},{1,13},{2,14},{3,15},{4,8},{5,9},{6,10},{7,11},{8,4},{9,5},... | collective-permute-start | bytes 884744 | tf_op jit(solution)/shard_map/ppermute | solution.py:21
  31.7 1.2 %collective-permute-start.11 = (f32[16,128]{1,0:T(8,128)S(1)}, f32[16,128]{1,0:T(8,128)S(1)}, u32[]{:S(2)}, u32[]{:S(2)}) collective-permute-start(f32[16,128]{1,0:T(8,128)S(1)} %shard_map.86.first), channel_id=1, source_target_pairs={{0,1},{1,0},{2,3},{3,2},{4,5},{5,4},{6,7},{7,6},{8,9},{9,8},{10,11... | collective-permute-start | bytes 24584 | tf_op jit(solution)/shard_map/ppermute | solution.py:21
  32.9 3.7 %collective-permute-start.12 = (f32[16,128]{1,0:T(8,128)S(1)}, f32[16,128]{1,0:T(8,128)S(1)}, u32[]{:S(2)}, u32[]{:S(2)}) collective-permute-start(f32[16,128]{1,0:T(8,128)S(1)} %shard_map.87.first), channel_id=1, source_target_pairs={{0,2},{1,3},{2,0},{3,1},{4,6},{5,7},{6,4},{7,5},{8,10},{9,11},{10,... | collective-permute-start | bytes 24584 | tf_op jit(solution)/shard_map/ppermute | solution.py:21
  36.6 10.5 %collective-permute-start.15 = (bf16[128,1152]{1,0:T(8,128)(2,1)S(1)}, bf16[128,1152]{1,0:T(8,128)(2,1)S(1)}, u32[]{:S(2)}, u32[]{:S(2)}) collective-permute-start(bf16[128,1152]{1,0:T(8,128)(2,1)S(1)} %shard_map.90), channel_id=1, source_target_pairs={{0,2},{1,3},{2,0},{3,1},{4,6},{5,7},{6,4},{7,5},{8,10},{9,11},{10,... | collective-permute-start | bytes 884744 | tf_op jit(solution)/shard_map/ppermute | solution.py:21
  37.4 9.7 %collective-permute-start.16 = (bf16[128,1152]{1,0:T(8,128)(2,1)S(1)}, bf16[128,1152]{1,0:T(8,128)(2,1)S(1)}, u32[]{:S(2)}, u32[]{:S(2)}) collective-permute-start(bf16[128,1152]{1,0:T(8,128)(2,1)S(1)} %shard_map.89.refs_1_), channel_id=1, source_target_pairs={{0,4},{1,5},{2,6},{3,7},{4,0},{5,1},{6,2},{7,3},{8,12},{9,13},{10,... | collective-permute-start | bytes 884744 | tf_op jit(solution)/shard_map/ppermute | solution.py:21
  38.3 8.8 %collective-permute-start.13 = (f32[16,128]{1,0:T(8,128)S(1)}, f32[16,128]{1,0:T(8,128)S(1)}, u32[]{:S(2)}, u32[]{:S(2)}) collective-permute-start(f32[16,128]{1,0:T(8,128)S(1)} %shard_map.88.refs_1_.sums), channel_id=1, source_target_pairs={{0,12},{1,13},{2,14},{3,15},{4,8},{5,9},{6,10},{7,11},{8,4},{9,5},... | collective-permute-start | bytes 24584 | tf_op jit(solution)/shard_map/ppermute | solution.py:21

commit v17 on v16

--- a/solution.py
+++ b/solution.py
@@ -79,7 +79,7 @@
     img_raw = [swapped(image, bit) for bit in img_bits]
     txt_raw = swapped(text, txt_bits[0])
     rows = image.shape[0]
-    cuts = [rows // 2, rows // 2]
+    cuts = [rows * 3 // 8, rows * 5 // 8]
     imgs, txts = {}, {}
     others = []
     for place in reversed(range(1, len(img_bits))):

time: 48.3 us -> 47.9 us (level)
  transfers between devices with their start and end apart: 17 -> 17, of which waited for: 7 -> 8; matrix products, arithmetic and copies ran while one was open for 0% -> 0% of each run, Pallas kernels for 4% -> 4%
where the time goes in v17:
time: 47.9 us; the launch traced here: 47.7 us
  starting transfers between devices  19.8 us (41%)
  waiting for transfers between devices  19.7 us (41%)
  Pallas kernels  5.48 us (11%)
  between operations  2.04 us (4%)
  local copies, waits for them, and re-layouts  0.73 us (2%)
    ppermute x17, starting transfers between devices, swapped(): return lax.ppermute(x, 'blk', [(i, i ^ bit) for i in range(count)])  19.8 us
    ppermute x17, waiting for transfers between devices, swapped(): return lax.ppermute(x, 'blk', [(i, i ^ bit) for i in range(count)])  19.7 us
    pallas_call x1, Pallas kernels, tile_call(): pl.pallas_call(functools.partial(tile_kernel, [len(block) for block in im...  2.59 us
    pallas_call x1, Pallas kernels, finish_first(): pl.pallas_call(finish_first_kernel, out_shape=(jax.ShapeDtypeStruct(value...  1.01 us
    pallas_call x1, Pallas kernels, finish_last(): pl.pallas_call(functools.partial(finish_last_kernel, pairs), out_shape=[j...  1.01 us
  transfers between devices with their start and end apart: 17, of which 8 were waited for; matrix products, arithmetic and copies ran while one was open for 0% of the time, Pallas kernels for 4%

profile of v17, /device:TPU:0, one launch (start us, length us, event | category | flops | bytes accessed | tf_op | source)
XLA Modules:
  0.0 47.7 jit_solution(11845612685619286018)
XLA Ops:
  0.6 0.0 copy-start.1
  0.6 3.0 %collective-permute-start = (bf16[128,1152]{1,0:T(8,128)(2,1)}, bf16[128,1152]{1,0:T(8,128)(2,1)S(1)}, u32[]{:S(2)}, u32[]{:S(2)}) collective-permute-start(bf16[128,1152]{1,0:T(8,128)(2,1)} %value.7), channel_id=1, source_target_pairs={{0,2},{1,3},{2,0},{3,1},{4,6},{5,7},{6,4},{7,5},{8,10},{9,11},{10,... | collective-permute-start | bytes 884744 | tf_op jit(solution)/shard_map/ppermute | solution.py:21
  3.6 1.6 %collective-permute-start.1 = (bf16[128,1152]{1,0:T(8,128)(2,1)}, bf16[128,1152]{1,0:T(8,128)(2,1)S(1)}, u32[]{:S(2)}, u32[]{:S(2)}) collective-permute-start(bf16[128,1152]{1,0:T(8,128)(2,1)} %value.7), channel_id=1, source_target_pairs={{0,4},{1,5},{2,6},{3,7},{4,0},{5,1},{6,2},{7,3},{8,12},{9,13},{10,... | collective-permute-start | bytes 884744 | tf_op jit(solution)/shard_map/ppermute | solution.py:21
  5.2 2.5 %collective-permute-start.4 = (bf16[128,1152]{1,0:T(8,128)(2,1)}, bf16[128,1152]{1,0:T(8,128)(2,1)S(1)}, u32[]{:S(2)}, u32[]{:S(2)}) collective-permute-start(bf16[128,1152]{1,0:T(8,128)(2,1)} %value.6), channel_id=1, source_target_pairs={{0,12},{1,13},{2,14},{3,15},{4,8},{5,9},{6,10},{7,11},{8,4},{9,5},... | collective-permute-start | bytes 884744 | tf_op jit(solution)/shard_map/ppermute | solution.py:21
  7.7 3.2 %collective-permute-done.value = bf16[128,1152]{1,0:T(8,128)(2,1)S(1)} collective-permute-done((bf16[128,1152]{1,0:T(8,128)(2,1)}, bf16[128,1152]{1,0:T(8,128)(2,1)S(1)}, u32[]{:S(2)}, u32[]{:S(2)}) %collective-permute-start) | collective-permute-done | bytes 294944 | tf_op jit(solution)/shard_map/ppermute | solution.py:21
  10.9 0.1 shard_map.75
  11.0 1.9 %collective-permute-start.3 = (bf16[80,1152]{1,0:T(8,128)(2,1)S(1)}, bf16[80,1152]{1,0:T(8,128)(2,1)S(1)}, u32[]{:S(2)}, u32[]{:S(2)}) collective-permute-start(bf16[80,1152]{1,0:T(8,128)(2,1)S(1)} %get-tuple-element.25.refs_4_), channel_id=1, source_target_pairs={{0,4},{1,5},{2,6},{3,7},{4,0},{5,1},{6,2},{7,3},{8,12},{9,13},{10,... | collective-permute-start | bytes 552968 | tf_op jit(solution)/shard_map/ppermute | solution.py:21
  14.2 0.0 copy-done.1
  14.2 0.0 copy-start
  14.2 0.1 shard_map.76.refs_0_.refs_7_
  14.4 0.1 collective-permute-start.5
  14.5 0.7 %copy-done = bf16[128,1152]{1,0:T(8,128)(2,1)S(1)} copy-done((bf16[128,1152]{1,0:T(8,128)(2,1)S(1)}, bf16[128,1152]{1,0:T(8,128)(2,1)}, u32[]{:S(2)}) %copy-start) | copy-done | bytes 294936
  15.2 0.1 shard_map.77.refs_0_
  15.3 0.0 collective-permute-done.1.value
  15.3 0.1 shard_map.78
  15.5 1.6 %collective-permute-start.2 = (bf16[48,1152]{1,0:T(8,128)(2,1)S(1)}, bf16[48,1152]{1,0:T(8,128)(2,1)S(1)}, u32[]{:S(2)}, u32[]{:S(2)}) collective-permute-start(bf16[48,1152]{1,0:T(8,128)(2,1)S(1)} %get-tuple-element.23.refs_0_.refs_1_), channel_id=1, source_target_pairs={{0,2},{1,3},{2,0},{3,1},{4,6},{5,7},{6,4},{7,5},{8,10},{9,11},{10,... | collective-permute-start | bytes 331784 | tf_op jit(solution)/shard_map/ppermute | solution.py:21
  17.0 5.1 %collective-permute-done.4.value = bf16[128,1152]{1,0:T(8,128)(2,1)S(1)} collective-permute-done((bf16[128,1152]{1,0:T(8,128)(2,1)}, bf16[128,1152]{1,0:T(8,128)(2,1)S(1)}, u32[]{:S(2)}, u32[]{:S(2)}) %collective-permute-start.4) | collective-permute-done | bytes 294944 | tf_op jit(solution)/shard_map/ppermute | solution.py:21
  22.2 0.1 shard_map.81.refs_8_
  22.3 0.1 collective-permute-start.6
  22.4 0.8 %collective-permute-done.3.refs_0_ = bf16[80,1152]{1,0:T(8,128)(2,1)S(1)} collective-permute-done((bf16[80,1152]{1,0:T(8,128)(2,1)S(1)}, bf16[80,1152]{1,0:T(8,128)(2,1)S(1)}, u32[]{:S(2)}, u32[]{:S(2)}) %collective-permute-start.3) | collective-permute-done | bytes 184352 | tf_op jit(solution)/shard_map/ppermute | solution.py:21
  23.2 0.0 collective-permute-done.2.refs_0_
  23.2 0.8 %collective-permute-done.6.refs_0_ = bf16[128,1152]{1,0:T(8,128)(2,1)S(1)} collective-permute-done((bf16[128,1152]{1,0:T(8,128)(2,1)S(1)}, bf16[128,1152]{1,0:T(8,128)(2,1)S(1)}, u32[]{:S(2)}, u32[]{:S(2)}) %collective-permute-start.6) | collective-permute-done | bytes 294944 | tf_op jit(solution)/shard_map/ppermute | solution.py:21
  24.0 0.0 collective-permute-done.5.refs_9_
  24.0 2.6 %shard_map.83 = (f32[128,1152]{1,0:T(8,128)S(1)}, f32[128,1152]{1,0:T(8,128)S(1)}, bf16[128,1152]{1,0:T(8,128)(2,1)S(1)}, bf16[128,1152]{1,0:T(8,128)(2,1)S(1)},...) custom-call(bf16[128,1152]{1,0:T(8,128)(2,1)S(1)} %shard_map.77.refs, ...), custom_call_target="tpu_custom_call" | custom-call | flops 1811939328 | tf_op jit(solution)/shard_map/pallas_call | solution.py:194
  26.6 0.2 collective-permute-start.8
  26.8 0.5 %collective-permute-start.14 = (bf16[128,1152]{1,0:T(8,128)(2,1)S(1)}, bf16[128,1152]{1,0:T(8,128)(2,1)S(1)}, u32[]{:S(2)}, u32[]{:S(2)}) collective-permute-start(bf16[128,1152]{1,0:T(8,128)(2,1)S(1)} %get-tuple-element.35), channel_id=1, source_target_pairs={{0,2},{1,3},{2,0},{3,1},{4,6},{5,7},{6,4},{7,5},{8,10},{9,11},{10,... | collective-permute-start | bytes 884744 | tf_op jit(solution)/shard_map/ppermute | solution.py:21
  27.3 0.2 collective-permute-start.10
  27.5 0.0 collective-permute-start.7
  27.5 0.7 %collective-permute-done.8.recv = bf16[128,1152]{1,0:T(8,128)(2,1)S(1)} collective-permute-done((bf16[128,1152]{1,0:T(8,128)(2,1)S(1)}, bf16[128,1152]{1,0:T(8,128)(2,1)S(1)}, u32[]{:S(2)}, u32[]{:S(2)}) %collective-permute-start.8) | collective-permute-done | bytes 294944 | tf_op jit(solution)/shard_map/ppermute | solution.py:21
  28.2 0.1 shard_map.84.refs_0_
  28.3 3.0 %collective-permute-start.9 = (bf16[128,1152]{1,0:T(8,128)(2,1)S(1)}, bf16[128,1152]{1,0:T(8,128)(2,1)S(1)}, u32[]{:S(2)}, u32[]{:S(2)}) collective-permute-start(bf16[128,1152]{1,0:T(8,128)(2,1)S(1)} %shard_map.84.refs_0_), channel_id=1, source_target_pairs={{0,12},{1,13},{2,14},{3,15},{4,8},{5,9},{6,10},{7,11},{8,4},{9,5},... | collective-permute-start | bytes 884744 | tf_op jit(solution)/shard_map/ppermute | solution.py:21
  31.3 0.0 collective-permute-done.10.second
  31.3 0.0 collective-permute-start.11
  31.3 1.2 %collective-permute-done.11.second = f32[16,128]{1,0:T(8,128)S(1)} collective-permute-done((f32[16,128]{1,0:T(8,128)S(1)}, f32[16,128]{1,0:T(8,128)S(1)}, u32[]{:S(2)}, u32[]{:S(2)}) %collective-permute-start.11) | collective-permute-done | bytes 8224 | tf_op jit(solution)/shard_map/ppermute | solution.py:21
  32.5 1.2 %collective-permute-start.12 = (f32[16,128]{1,0:T(8,128)S(1)}, f32[16,128]{1,0:T(8,128)S(1)}, u32[]{:S(2)}, u32[]{:S(2)}) collective-permute-start(f32[16,128]{1,0:T(8,128)S(1)} %shard_map.87.first), channel_id=1, source_target_pairs={{0,2},{1,3},{2,0},{3,1},{4,6},{5,7},{6,4},{7,5},{8,10},{9,11},{10,... | collective-permute-start | bytes 24584 | tf_op jit(solution)/shard_map/ppermute | solution.py:21
  33.7 2.6 %collective-permute-done.12.second = f32[16,128]{1,0:T(8,128)S(1)} collective-permute-done((f32[16,128]{1,0:T(8,128)S(1)}, f32[16,128]{1,0:T(8,128)S(1)}, u32[]{:S(2)}, u32[]{:S(2)}) %collective-permute-start.12) | collective-permute-done | bytes 8224 | tf_op jit(solution)/shard_map/ppermute | solution.py:21
  36.3 0.0 collective-permute-done.14.recv
  36.3 0.1 shard_map.89.refs_1_
  36.3 1.1 %collective-permute-start.15 = (bf16[128,1152]{1,0:T(8,128)(2,1)S(1)}, bf16[128,1152]{1,0:T(8,128)(2,1)S(1)}, u32[]{:S(2)}, u32[]{:S(2)}) collective-permute-start(bf16[128,1152]{1,0:T(8,128)(2,1)S(1)} %shard_map.90), channel_id=1, source_target_pairs={{0,2},{1,3},{2,0},{3,1},{4,6},{5,7},{6,4},{7,5},{8,10},{9,11},{10,... | collective-permute-start | bytes 884744 | tf_op jit(solution)/shard_map/ppermute | solution.py:21
  37.5 0.5 %collective-permute-start.16 = (bf16[128,1152]{1,0:T(8,128)(2,1)S(1)}, bf16[128,1152]{1,0:T(8,128)(2,1)S(1)}, u32[]{:S(2)}, u32[]{:S(2)}) collective-permute-start(bf16[128,1152]{1,0:T(8,128)(2,1)S(1)} %shard_map.89.refs_1_), channel_id=1, source_target_pairs={{0,4},{1,5},{2,6},{3,7},{4,0},{5,1},{6,2},{7,3},{8,12},{9,13},{10,... | collective-permute-start | bytes 884744 | tf_op jit(solution)/shard_map/ppermute | solution.py:21
  37.9 2.4 %collective-permute-start.13 = (f32[16,128]{1,0:T(8,128)S(1)}, f32[16,128]{1,0:T(8,128)S(1)}, u32[]{:S(2)}, u32[]{:S(2)}) collective-permute-start(f32[16,128]{1,0:T(8,128)S(1)} %shard_map.88.refs_1_.sums), channel_id=1, source_target_pairs={{0,12},{1,13},{2,14},{3,15},{4,8},{5,9},{6,10},{7,11},{8,4},{9,5},... | collective-permute-start | bytes 24584 | tf_op jit(solution)/shard_map/ppermute | solution.py:21
  40.3 0.0 collective-permute-done.7.refs_0_
  40.3 0.0 collective-permute-done.9.refs_1_
  40.3 1.0 %shard_map.85 = (bf16[128,1152]{1,0:T(8,128)(2,1)}, f32[8,128]{1,0:T(8,128)S(1)}) custom-call(bf16[128,1152]{1,0:T(8,128)(2,1)S(1)} %copy-done.1, f32[128,1152]{1,0:T(8,128)S(1)} %get-tuple-element.26.keep, bf16[128,1152]{1,0:T(8,128)(2,1)S(1)} %collective-permute-done.7.refs_0_, bf16[128,1152]{1,0:T(8,128)(2,1)S(1)} %collective-permute-done.9.refs_1_), custom_call_target="tpu_custom_call" | custom-call | flops 1000000000 | tf_op jit(solution)/shard_map/pallas_call | solution.py:237
  41.4 5.4 %collective-permute-done.13.sums_recv = f32[16,128]{1,0:T(8,128)S(1)} collective-permute-done((f32[16,128]{1,0:T(8,128)S(1)}, f32[16,128]{1,0:T(8,128)S(1)}, u32[]{:S(2)}, u32[]{:S(2)}) %collective-permute-start.13) | collective-permute-done | bytes 8224 | tf_op jit(solution)/shard_map/ppermute | solution.py:21
  46.7 0.0 collective-permute-done.15.refs_0_
  46.7 0.0 collective-permute-done.16.refs_1_
  46.7 1.0 %shard_map.91 = (bf16[128,1152]{1,0:T(8,128)(2,1)}, f32[1,1]{1,0:T(1,128)}, f32[1,1]{1,0:T(1,128)}) custom-call(f32[8,128]{1,0:T(8,128)S(1)} %get-tuple-element.30.token, f32[16,128]{1,0:T(8,128)S(1)} %shard_map.88.refs_1_.sums, f32[16,128]{1,0:T(8,128)S(1)} %collective-permute-done.13.sums_recv, bf16[128,1152]{1,0:T(8,128)(2,1)S(1)} %copy-done, ...), custom_call_target="tpu_custom_call" | custom-call | tf_op jit(solution)/shard_map/pallas_call | solution.py:259
  (7 shorter events, 0.0 us)
Async XLA Ops:
  0.6 13.6 %copy-start.1 = (bf16[128,1152]{1,0:T(8,128)(2,1)S(1)}, bf16[128,1152]{1,0:T(8,128)(2,1)}, u32[]{:S(2)}) copy-start(bf16[128,1152]{1,0:T(8,128)(2,1)} %value.6) | copy-start | bytes 884740
  0.6 10.2 %collective-permute-start = (bf16[128,1152]{1,0:T(8,128)(2,1)}, bf16[128,1152]{1,0:T(8,128)(2,1)S(1)}, u32[]{:S(2)}, u32[]{:S(2)}) collective-permute-start(bf16[128,1152]{1,0:T(8,128)(2,1)} %value.7), channel_id=1, source_target_pairs={{0,2},{1,3},{2,0},{3,1},{4,6},{5,7},{6,4},{7,5},{8,10},{9,11},{10,... | collective-permute-start | bytes 884744 | tf_op jit(solution)/shard_map/ppermute | solution.py:21
  3.6 11.7 %collective-permute-start.1 = (bf16[128,1152]{1,0:T(8,128)(2,1)}, bf16[128,1152]{1,0:T(8,128)(2,1)S(1)}, u32[]{:S(2)}, u32[]{:S(2)}) collective-permute-start(bf16[128,1152]{1,0:T(8,128)(2,1)} %value.7), channel_id=1, source_target_pairs={{0,4},{1,5},{2,6},{3,7},{4,0},{5,1},{6,2},{7,3},{8,12},{9,13},{10,... | collective-permute-start | bytes 884744 | tf_op jit(solution)/shard_map/ppermute | solution.py:21
  5.2 17.0 %collective-permute-start.4 = (bf16[128,1152]{1,0:T(8,128)(2,1)}, bf16[128,1152]{1,0:T(8,128)(2,1)S(1)}, u32[]{:S(2)}, u32[]{:S(2)}) collective-permute-start(bf16[128,1152]{1,0:T(8,128)(2,1)} %value.6), channel_id=1, source_target_pairs={{0,12},{1,13},{2,14},{3,15},{4,8},{5,9},{6,10},{7,11},{8,4},{9,5},... | collective-permute-start | bytes 884744 | tf_op jit(solution)/shard_map/ppermute | solution.py:21
  11.0 12.2 %collective-permute-start.3 = (bf16[80,1152]{1,0:T(8,128)(2,1)S(1)}, bf16[80,1152]{1,0:T(8,128)(2,1)S(1)}, u32[]{:S(2)}, u32[]{:S(2)}) collective-permute-start(bf16[80,1152]{1,0:T(8,128)(2,1)S(1)} %get-tuple-element.25.refs_4_), channel_id=1, source_target_pairs={{0,4},{1,5},{2,6},{3,7},{4,0},{5,1},{6,2},{7,3},{8,12},{9,13},{10,... | collective-permute-start | bytes 552968 | tf_op jit(solution)/shard_map/ppermute | solution.py:21
  14.2 1.0 %copy-start = (bf16[128,1152]{1,0:T(8,128)(2,1)S(1)}, bf16[128,1152]{1,0:T(8,128)(2,1)}, u32[]{:S(2)}) copy-start(bf16[128,1152]{1,0:T(8,128)(2,1)} %value.7) | copy-start | bytes 884740
  14.4 9.6 %collective-permute-start.5 = (bf16[128,1152]{1,0:T(8,128)(2,1)S(1)}, bf16[128,1152]{1,0:T(8,128)(2,1)S(1)}, u32[]{:S(2)}, u32[]{:S(2)}) collective-permute-start(bf16[128,1152]{1,0:T(8,128)(2,1)S(1)} %shard_map.76.refs_0_.refs_7_), channel_id=1, source_target_pairs={{0,1},{1,0},{2,3},{3,2},{4,5},{5,4},{6,7},{7,6},{8,9},{9,8},{10,11... | collective-permute-start | bytes 884744 | tf_op jit(solution)/shard_map/ppermute | solution.py:21
  15.5 7.7 %collective-permute-start.2 = (bf16[48,1152]{1,0:T(8,128)(2,1)S(1)}, bf16[48,1152]{1,0:T(8,128)(2,1)S(1)}, u32[]{:S(2)}, u32[]{:S(2)}) collective-permute-start(bf16[48,1152]{1,0:T(8,128)(2,1)S(1)} %get-tuple-element.23.refs_0_.refs_1_), channel_id=1, source_target_pairs={{0,2},{1,3},{2,0},{3,1},{4,6},{5,7},{6,4},{7,5},{8,10},{9,11},{10,... | collective-permute-start | bytes 331784 | tf_op jit(solution)/shard_map/ppermute | solution.py:21
  22.3 1.6 %collective-permute-start.6 = (bf16[128,1152]{1,0:T(8,128)(2,1)S(1)}, bf16[128,1152]{1,0:T(8,128)(2,1)S(1)}, u32[]{:S(2)}, u32[]{:S(2)}) collective-permute-start(bf16[128,1152]{1,0:T(8,128)(2,1)S(1)} %shard_map.81.refs_8_), channel_id=1, source_target_pairs={{0,1},{1,0},{2,3},{3,2},{4,5},{5,4},{6,7},{7,6},{8,9},{9,8},{10,11... | collective-permute-start | bytes 884744 | tf_op jit(solution)/shard_map/ppermute | solution.py:21
  26.6 1.6 %collective-permute-start.8 = (bf16[128,1152]{1,0:T(8,128)(2,1)S(1)}, bf16[128,1152]{1,0:T(8,128)(2,1)S(1)}, u32[]{:S(2)}, u32[]{:S(2)}) collective-permute-start(bf16[128,1152]{1,0:T(8,128)(2,1)S(1)} %get-tuple-element.29), channel_id=1, source_target_pairs={{0,1},{1,0},{2,3},{3,2},{4,5},{5,4},{6,7},{7,6},{8,9},{9,8},{10,11... | collective-permute-start | bytes 884744 | tf_op jit(solution)/shard_map/ppermute | solution.py:21
  26.8 9.5 %collective-permute-start.14 = (bf16[128,1152]{1,0:T(8,128)(2,1)S(1)}, bf16[128,1152]{1,0:T(8,128)(2,1)S(1)}, u32[]{:S(2)}, u32[]{:S(2)}) collective-permute-start(bf16[128,1152]{1,0:T(8,128)(2,1)S(1)} %get-tuple-element.35), channel_id=1, source_target_pairs={{0,2},{1,3},{2,0},{3,1},{4,6},{5,7},{6,4},{7,5},{8,10},{9,11},{10,... | collective-permute-start | bytes 884744 | tf_op jit(solution)/shard_map/ppermute | solution.py:21
  27.3 4.0 %collective-permute-start.10 = (f32[16,128]{1,0:T(8,128)S(1)}, f32[16,128]{1,0:T(8,128)S(1)}, u32[]{:S(2)}, u32[]{:S(2)}) collective-permute-start(f32[16,128]{1,0:T(8,128)S(1)} %get-tuple-element.31.first), channel_id=1, source_target_pairs={{0,4},{1,5},{2,6},{3,7},{4,0},{5,1},{6,2},{7,3},{8,12},{9,13},{10,... | collective-permute-start | bytes 24584 | tf_op jit(solution)/shard_map/ppermute | solution.py:21
  27.5 12.8 %collective-permute-start.7 = (bf16[128,1152]{1,0:T(8,128)(2,1)S(1)}, bf16[128,1152]{1,0:T(8,128)(2,1)S(1)}, u32[]{:S(2)}, u32[]{:S(2)}) collective-permute-start(bf16[128,1152]{1,0:T(8,128)(2,1)S(1)} %get-tuple-element.27), channel_id=1, source_target_pairs={{0,1},{1,0},{2,3},{3,2},{4,5},{5,4},{6,7},{7,6},{8,9},{9,8},{10,11... | collective-permute-start | bytes 884744 | tf_op jit(solution)/shard_map/ppermute | solution.py:21
  28.3 12.1 %collective-permute-start.9 = (bf16[128,1152]{1,0:T(8,128)(2,1)S(1)}, bf16[128,1152]{1,0:T(8,128)(2,1)S(1)}, u32[]{:S(2)}, u32[]{:S(2)}) collective-permute-start(bf16[128,1152]{1,0:T(8,128)(2,1)S(1)} %shard_map.84.refs_0_), channel_id=1, source_target_pairs={{0,12},{1,13},{2,14},{3,15},{4,8},{5,9},{6,10},{7,11},{8,4},{9,5},... | collective-permute-start | bytes 884744 | tf_op jit(solution)/shard_map/ppermute | solution.py:21
  31.3 1.2 %collective-permute-start.11 = (f32[16,128]{1,0:T(8,128)S(1)}, f32[16,128]{1,0:T(8,128)S(1)}, u32[]{:S(2)}, u32[]{:S(2)}) collective-permute-start(f32[16,128]{1,0:T(8,128)S(1)} %shard_map.86.first), channel_id=1, source_target_pairs={{0,1},{1,0},{2,3},{3,2},{4,5},{5,4},{6,7},{7,6},{8,9},{9,8},{10,11... | collective-permute-start | bytes 24584 | tf_op jit(solution)/shard_map/ppermute | solution.py:21
  32.5 3.8 %collective-permute-start.12 = (f32[16,128]{1,0:T(8,128)S(1)}, f32[16,128]{1,0:T(8,128)S(1)}, u32[]{:S(2)}, u32[]{:S(2)}) collective-permute-start(f32[16,128]{1,0:T(8,128)S(1)} %shard_map.87.first), channel_id=1, source_target_pairs={{0,2},{1,3},{2,0},{3,1},{4,6},{5,7},{6,4},{7,5},{8,10},{9,11},{10,... | collective-permute-start | bytes 24584 | tf_op jit(solution)/shard_map/ppermute | solution.py:21
  36.3 10.4 %collective-permute-start.15 = (bf16[128,1152]{1,0:T(8,128)(2,1)S(1)}, bf16[128,1152]{1,0:T(8,128)(2,1)S(1)}, u32[]{:S(2)}, u32[]{:S(2)}) collective-permute-start(bf16[128,1152]{1,0:T(8,128)(2,1)S(1)} %shard_map.90), channel_id=1, source_target_pairs={{0,2},{1,3},{2,0},{3,1},{4,6},{5,7},{6,4},{7,5},{8,10},{9,11},{10,... | collective-permute-start | bytes 884744 | tf_op jit(solution)/shard_map/ppermute | solution.py:21
  37.5 9.3 %collective-permute-start.16 = (bf16[128,1152]{1,0:T(8,128)(2,1)S(1)}, bf16[128,1152]{1,0:T(8,128)(2,1)S(1)}, u32[]{:S(2)}, u32[]{:S(2)}) collective-permute-start(bf16[128,1152]{1,0:T(8,128)(2,1)S(1)} %shard_map.89.refs_1_), channel_id=1, source_target_pairs={{0,4},{1,5},{2,6},{3,7},{4,0},{5,1},{6,2},{7,3},{8,12},{9,13},{10,... | collective-permute-start | bytes 884744 | tf_op jit(solution)/shard_map/ppermute | solution.py:21
  37.9 8.8 %collective-permute-start.13 = (f32[16,128]{1,0:T(8,128)S(1)}, f32[16,128]{1,0:T(8,128)S(1)}, u32[]{:S(2)}, u32[]{:S(2)}) collective-permute-start(f32[16,128]{1,0:T(8,128)S(1)} %shard_map.88.refs_1_.sums), channel_id=1, source_target_pairs={{0,12},{1,13},{2,14},{3,15},{4,8},{5,9},{6,10},{7,11},{8,4},{9,5},... | collective-permute-start | bytes 24584 | tf_op jit(solution)/shard_map/ppermute | solution.py:21
